TPU v7x, 32 devices: a whole 2x2x4 slice. The times are simulated.
32 devices in a mesh: row: 4 (over y, x), col: 4 (over z), rep: 2 (over core).
Axes of the slice: x: 2, y: 2, z: 4, core: 2. Of those that a mesh axis runs over, the one named last changes fastest.
Arguments:
- queries: bfloat16 [2048, 4096], P(('rep', 'row'), 'col'), may hold values from -6 to 6
- key_vectors: bfloat16 [2048, 4096], P(('rep', 'row'), 'col'), may hold values from -6 to 6
- value_vectors: bfloat16 [2048, 4096], P(('rep', 'row'), 'col'), may hold values from -12 to 12
- cotangent: bfloat16 [2048, 6144], P(('rep', 'row'), 'col'), may hold values from -6 to 6
- out_weight: bfloat16 [4096, 6144], P('row', 'col'), may hold values from -0.09375 to 0.09375
Outputs:
- projected: bfloat16 [2048, 6144], P(('rep', 'row'), 'col')
- grad_query: bfloat16 [2048, 4096], P(('rep', 'row'), 'col')
- grad_key: bfloat16 [2048, 4096], P(('rep', 'row'), 'col')
- grad_value: bfloat16 [2048, 4096], P(('rep', 'row'), 'col')
- grad_weight: bfloat16 [4096, 6144], P('row', 'col')
All inputs are finite; a program needn't handle non-finite values.
Results may differ from a plain program's by a relative error of at most 0.011.
Values may be sent and summed in bfloat16 or wider, within the bound.
No kernel may reach another device: no remote copies, remote signals or barrier semaphores. Data moves between devices by JAX's collectives and lax.ppermute only.
A program may use at most 128 MiB of HBM per device.

v0:
```python
import jax
import jax.numpy as jnp
from jax import lax
from jax.sharding import PartitionSpec as P

HSZ = 128
PATCH = 256


def softmax_weights(query_blk, key_blk):
    scores = jnp.einsum(
        "bqhd,bkhd->bhqk", query_blk, key_blk, preferred_element_type=jnp.float32
    ) * HSZ ** (-0.5)
    peak = jnp.max(scores, axis=-1, keepdims=True)
    lifted = jnp.exp(scores - peak)
    return lifted / jnp.sum(lifted, axis=-1, keepdims=True)


def local(queries, key_vectors, value_vectors, cotangent, out_weight):
    tok_rows = queries.shape[0]
    features = queries.shape[1]
    shaped = (tok_rows // PATCH, PATCH, features // HSZ, HSZ)
    query_blk = queries.reshape(shaped)
    key_blk = key_vectors.reshape(shaped)
    value_blk = value_vectors.reshape(shaped)
    prob_full = softmax_weights(query_blk, key_blk)
    prob_low = prob_full.astype(jnp.bfloat16)
    head_out = jnp.einsum(
        "bhqk,bkhd->bqhd", prob_low, value_blk, preferred_element_type=jnp.float32
    )
    head_out = head_out.astype(jnp.bfloat16).reshape(tok_rows, features)
    gathered = lax.all_gather(head_out, "col", axis=1, tiled=True)
    column_panel = lax.all_gather(out_weight, "row", axis=0, tiled=True)
    projected = jnp.dot(gathered, column_panel, preferred_element_type=jnp.float32).astype(
        jnp.bfloat16
    )
    summed = lax.psum_scatter(
        lax.dot_general(
            column_panel, cotangent, (((1,), (1,)), ((), ())), preferred_element_type=jnp.float32
        ),
        "col",
        scatter_dimension=0,
        tiled=True,
    )
    grad_heads = summed.T.astype(jnp.bfloat16)
    grad_blk = grad_heads.reshape(shaped)
    grad_prob = jnp.einsum(
        "bqhd,bkhd->bhqk", grad_blk, value_blk, preferred_element_type=jnp.float32
    )
    row_delta = jnp.sum(prob_full * grad_prob, axis=-1, keepdims=True)
    grad_score = (prob_full * (grad_prob - row_delta) * HSZ ** (-0.5)).astype(jnp.bfloat16)
    grad_query = jnp.einsum(
        "bhqk,bkhd->bqhd", grad_score, key_blk, preferred_element_type=jnp.float32
    )
    grad_key = jnp.einsum(
        "bhqk,bqhd->bkhd", grad_score, query_blk, preferred_element_type=jnp.float32
    )
    grad_value = jnp.einsum(
        "bhqk,bqhd->bkhd", prob_low, grad_blk, preferred_element_type=jnp.float32
    )
    regrouped = lax.all_to_all(gathered, "row", split_axis=1, concat_axis=0, tiled=True)
    partial_value = lax.dot_general(
        regrouped,
        lax.all_gather(cotangent, "row", axis=0, tiled=True),
        (((0,), (0,)), ((), ())),
        preferred_element_type=jnp.float32,
    )
    replica_total = lax.psum(partial_value.astype(jnp.bfloat16), "rep").astype(jnp.float32)
    factor = float(tok_rows * lax.axis_size("row") * lax.axis_size("rep")) ** (-0.5)
    grad_weight = (replica_total * factor).astype(jnp.bfloat16)
    return (
        projected,
        grad_query.astype(jnp.bfloat16).reshape(tok_rows, features),
        grad_key.astype(jnp.bfloat16).reshape(tok_rows, features),
        grad_value.astype(jnp.bfloat16).reshape(tok_rows, features),
        grad_weight,
    )


def solution(mesh):
    placed = (
        P(("rep", "row"), "col"),
        P(("rep", "row"), "col"),
        P(("rep", "row"), "col"),
        P(("rep", "row"), "col"),
        P("row", "col"),
    )
    return jax.shard_map(
        local,
        mesh=mesh,
        in_specs=placed,
        out_specs=(
            P(("rep", "row"), "col"),
            P(("rep", "row"), "col"),
            P(("rep", "row"), "col"),
            P(("rep", "row"), "col"),
            P("row", "col"),
        ),
        check_vma=False,
    )
```

profile of v0, /device:TPU:0, one launch (start us, length us, event | category | flops | bytes accessed | tf_op | source)
XLA Modules:
  0.0 375.6 jit_solution(16406258679412441008)
XLA Ops:
  7.2 0.0 copy-start
  7.2 0.0 all-gather.4.cloned.1.call-start
  7.2 1.3 copy.58
  8.5 0.0 copy-start.4
  8.5 1.4 copy.59
  10.0 0.0 copy-start.3
  10.0 2.2 fusion.35
  12.2 0.0 copy-done.4
  12.2 0.0 copy-done
  12.2 2.8 convolution_convert_fusion.2
  14.9 0.0 copy-done.3
  14.9 0.0 all-gather.4.cloned.1.call-update
  15.0 0.0 all-gather.8.cloned.1.call-start
  15.0 0.7 all-gather.8.cloned.1.call-update
  15.7 0.0 all-gather.6.cloned.1.call-start
  15.8 0.7 all-gather.6.cloned.1.call-update
  16.5 0.0 all-reduce.2.cloned.1.call-start
  16.5 47.3 %all-gather.4.cloned.1.call-done = bf16[256,4096]{0,1:T(8,128)(2,1)} async-done(((bf16[256,1024]{0,1:T(8,128)(2,1)}), bf16[256,4096]{0,1:T(8,128)(2,1)}) %all-gather.4.cloned.1.call-update) | async-done | bytes 2097168 | tf_op jit(solution)/shard_map/all_gather | solution.py:32
  63.8 37.7 %all_to_all.19 = bf16[256,4,1024]{0,2,1:T(8,128)(2,1)S(1)} all-to-all(bf16[256,4,1024]{0,2,1:T(8,128)(2,1)} %bitcast.58), channel_id=1, replica_groups=mesh['row'=4,'col'=4,'rep'=2] {'row'}, dimensions={1} | all-to-all | bytes 4194304 | tf_op jit(solution)/shard_map/all_to_all | solution.py:61
  101.4 2.5 copy.49
  103.9 19.8 %all-gather.8.cloned.1.call-done = bf16[1024,1536]{1,0:T(8,128)(2,1)} async-done(((bf16[256,1536]{1,0:T(8,128)(2,1)}), bf16[1024,1536]{1,0:T(8,128)(2,1)}) %all-gather.8.cloned.1.call-update) | async-done | bytes 3145744 | tf_op jit(solution)/shard_map/all_gather | solution.py:64
  123.7 7.7 %convolution_convert_fusion = bf16[1024,1536]{1,0:T(8,128)(2,1)} fusion(bf16[1024,1024]{1,0:T(8,128)(2,1)} %bitcast.60, bf16[1024,1536]{1,0:T(8,128)(2,1)} %all-gather.8.cloned.1.call-done), kind=kOutput, calls=%fused_computation.3 | convolution fusion | flops 3222798336 | bytes 8388608 | tf_op jit(solution)/shard_map/dot_general | solution.py:62
  131.4 0.0 copy-start.2
  131.4 0.0 all-reduce.2.cloned.1.call-update
  131.4 0.2 reduce-scatter.2.cloned.1.call-start
  131.6 116.5 %all-gather.6.cloned.1.call-done = bf16[4096,1536]{1,0:T(8,128)(2,1)} async-done(((bf16[1024,1536]{1,0:T(8,128)(2,1)}), bf16[4096,1536]{1,0:T(8,128)(2,1)}) %all-gather.6.cloned.1.call-update) | async-done | bytes 12582928 | tf_op jit(solution)/shard_map/all_gather | solution.py:33
  248.1 0.0 copy-done.2
  248.1 10.2 %fusion.36 = f32[4096,256]{1,0:T(8,128)} fusion(bf16[4096,1536]{1,0:T(8,128)(2,1)} %all-gather.6.cloned.1.call-done, bf16[256,1536]{1,0:T(8,128)(2,1)S(1)} %copy-done.2), kind=kOutput, calls=%fused_computation.35 | convolution fusion | flops 3221225472 | bytes 17563648 | tf_op jit(solution)/shard_map/dot_general | solution.py:38
  258.3 0.0 reduce-scatter.2.cloned.1.call-update
  258.4 0.0 copy-start.1
  258.4 15.8 %all-reduce.2.cloned.1.call-done = bf16[1024,1536]{1,0:T(8,128)(2,1)} async-done(((bf16[1024,1536]{1,0:T(8,128)(2,1)}), bf16[1024,1536]{1,0:T(8,128)(2,1)}) %all-reduce.2.cloned.1.call-update) | async-done | bytes 3145744 | tf_op jit(solution)/shard_map/psum | solution.py:68
  274.1 4.1 %multiply_convert_fusion = bf16[1024,1536]{1,0:T(8,128)(2,1)} fusion(bf16[1024,1536]{1,0:T(8,128)(2,1)} %all-reduce.2.cloned.1.call-done), kind=kLoop, calls=%fused_computation.2 | loop fusion | flops 4718592 | bytes 6291456 | tf_op jit(solution)/shard_map/convert_element_type | solution.py:70
  278.3 0.0 copy-done.1
  278.3 7.4 %convolution_convert_fusion.1 = bf16[256,1536]{1,0:T(8,128)(2,1)} fusion(bf16[256,4096]{0,1:T(8,128)(2,1)S(1)} %copy-done.1, bf16[4096,1536]{1,0:T(8,128)(2,1)} %all-gather.6.cloned.1.call-done), kind=kOutput, calls=%fused_computation.4 | convolution fusion | flops 3221618688 | bytes 15466496 | tf_op jit(solution)/shard_map/dot_general | solution.py:34
  285.6 68.7 %reduce-scatter.2.cloned.1.call-done = f32[1024,256]{1,0:T(8,128)} async-done(((f32[4096,256]{1,0:T(8,128)}), f32[1024,256]{1,0:T(8,128)}) %reduce-scatter.2.cloned.1.call-update) | async-done | bytes 1048592 | tf_op jit(solution)/shard_map/reduce_scatter | solution.py:37
  354.3 1.3 convert_element_type.77
  355.6 0.4 fusion.22
  356.0 3.9 %fusion.15 = bf16[8,256,128]{1,2,0:T(8,128)(2,1)} fusion(bf16[256,8,128]{0,2,1:T(8,128)(2,1)} %bitcast.66, f32[8,256,256]{1,2,0:T(8,128)S(1)} %fusion.22, f32[8,256,256]{1,2,0:T(8,128)} %get-tuple-element.21, f32[8,256]{1,0:T(8,128)S(1)} %get-tuple-element.20), kind=kOutput, calls=%fused_computation.14 | convolution fusion | flops 138152192 | bytes 5251072 | tf_op jit(solution)/shard_map/bhqk,bqhd->bkhd/dot_general | solution.py:55
  359.9 3.9 %fusion.12 = bf16[8,256,128]{1,2,0:T(8,128)(2,1)} fusion(bf16[256,8,128]{0,2,1:T(8,128)(2,1)} %bitcast.64, f32[8,256,256]{1,2,0:T(8,128)S(1)} %fusion.22, f32[8,256,256]{1,2,0:T(8,128)} %get-tuple-element.21, f32[8,256]{1,0:T(8,128)S(1)} %get-tuple-element.20), kind=kOutput, calls=%fused_computation.13 | convolution fusion | flops 138152192 | bytes 5251072 | tf_op jit(solution)/shard_map/bhqk,bkhd->bqhd/dot_general | solution.py:52
  363.9 0.0 copy-start.5
  363.9 0.0 copy-start.6
  363.9 2.2 convolution_convert_fusion.3
  366.0 0.0 copy-done.5
  366.1 1.0 copy.51
  367.1 0.0 copy-done.6
  367.1 1.0 copy.50
  368.1 1.0 copy.52
Async XLA Ops:
  7.2 5.0 %copy-start = (bf16[256,1024]{1,0:T(8,128)(2,1)S(1)}, bf16[256,1024]{1,0:T(8,128)(2,1)}, u32[]{:S(2)}) copy-start(bf16[256,1024]{1,0:T(8,128)(2,1)} %param.7) | copy-start | bytes 1572868
  7.2 56.6 %all-gather.4.cloned.1.call-start = ((), (), s32[]{:S(2)}) async-start(), calls=%async_computation.2 | async-start | bytes 2621440 | tf_op jit(solution)/shard_map/all_gather | solution.py:32
  8.5 3.7 copy-start.4
  10.0 5.0 %copy-start.3 = (bf16[256,1024]{0,1:T(8,128)(2,1)}, bf16[256,1024]{0,1:T(8,128)(2,1)S(1)}, u32[]{:S(2)}) copy-start(bf16[256,1024]{0,1:T(8,128)(2,1)S(1)} %copy.59) | copy-start | bytes 1572868
  15.0 108.8 %all-gather.8.cloned.1.call-start = ((), (), s32[]{:S(2)}) async-start(), calls=%async_computation.5 | async-start | bytes 3932160 | tf_op jit(solution)/shard_map/all_gather | solution.py:64
  15.7 232.4 %all-gather.6.cloned.1.call-start = ((), (), s32[]{:S(2)}) async-start(), calls=%async_computation.3 | async-start | bytes 15728640 | tf_op jit(solution)/shard_map/all_gather | solution.py:33
  16.5 257.7 %all-reduce.2.cloned.1.call-start = ((), (), s32[]{:S(2)}) async-start(), calls=%async_computation.6 | async-start | bytes 6291456 | tf_op jit(solution)/shard_map/psum | solution.py:68
  131.4 116.7 %copy-start.2 = (bf16[256,1536]{1,0:T(8,128)(2,1)S(1)}, bf16[256,1536]{1,0:T(8,128)(2,1)}, u32[]{:S(2)}) copy-start(bf16[256,1536]{1,0:T(8,128)(2,1)} %param.8) | copy-start | bytes 2359300
  131.4 222.9 %reduce-scatter.2.cloned.1.call-start = ((), (), s32[]{:S(2)}) async-start(), calls=%async_computation.4 | async-start | bytes 5242880 | tf_op jit(solution)/shard_map/reduce_scatter | solution.py:37
  258.4 19.9 %copy-start.1 = (bf16[256,4096]{0,1:T(8,128)(2,1)S(1)}, bf16[256,4096]{0,1:T(8,128)(2,1)}, u32[]{:S(2)}) copy-start(bf16[256,4096]{0,1:T(8,128)(2,1)} %all-gather.4.cloned.1.call-done) | copy-start | bytes 6291460
  363.9 2.2 copy-start.5
  363.9 3.2 copy-start.6
Sparse Core Ops, SparseCore 0:
  15.1 48.6 all-gather.3
  65.6 58.0 all-gather.7
  125.6 122.5 all-gather.5
  250.9 23.2 all-reduce.1
  276.4 77.9 reduce-scatter.1
where the time goes:
time: 376 us
  waiting for transfers between devices  269 us (72%)
  matrix products  40.6 us (11%)
  blocking collectives  37.7 us (10%)
  between operations  13.9 us (4%)
  local copies, waits for them, and re-layouts  8.23 us (2%)
  other arithmetic  5.42 us (1%)
    all_gather x1, waiting for transfers between devices, local(): column_panel = lax.all_gather(out_weight, 'row', axis=0, tiled=True)  116 us
    reduce_scatter x1, waiting for transfers between devices, local(): lax.psum_scatter(lax.dot_general(column_panel, cotangent, (((1,), (1,)),...  68.7 us
    all_gather x1, waiting for transfers between devices, local(): gathered = lax.all_gather(head_out, 'col', axis=1, tiled=True)  47.3 us
    all_to_all x1, blocking collectives, local(): lax.all_to_all(gathered, 'row', split_axis=1, concat_axis=0, tiled=True)  37.7 us
    all_gather x1, waiting for transfers between devices, local(): lax.all_gather(cotangent, 'row', axis=0, tiled=True)  19.8 us
    psum x1, waiting for transfers between devices, local(): lax.psum(partial_value.astype(jnp.bfloat16), 'rep').astype(jnp.float32)  15.8 us
    dot_general x1, matrix products, local(): lax.dot_general(column_panel, cotangent, (((1,), (1,)), ((), ())), prefer...  10.2 us
    dot_general x1, matrix products, local(): lax.dot_general(regrouped, lax.all_gather(cotangent, 'row', axis=0, tiled...  7.65 us
  transfers between devices with their start and end apart: 5, of which 5 were waited for; matrix products, arithmetic and copies ran while one was open for 8% of the time, Pallas kernels for 0%

commit v1 on v0

v1 whole, which is shorter than its diff:
```python
import functools

import jax
import jax.numpy as jnp
from jax import lax
from jax.experimental import pallas as pl
from jax.experimental.pallas import tpu as pltpu
from jax.sharding import PartitionSpec as P

HSZ = 128
PATCH = 256
SCALE = HSZ ** (-0.5)

NT = (((1,), (1,)), ((), ()))
TN = (((0,), (0,)), ((), ()))


def dot(a, b, dims=(((1,), (0,)), ((), ()))):
    return lax.dot_general(a, b, dims, preferred_element_type=jnp.float32)


def softmax_block(q, k):
    scores = dot(q, k, NT) * SCALE
    lifted = jnp.exp(scores - jnp.max(scores, axis=-1, keepdims=True))
    return lifted / jnp.sum(lifted, axis=-1, keepdims=True)


def forward_kernel(q_ref, k_ref, v_ref, o_ref):
    for lo in range(0, q_ref.shape[1], HSZ):
        cols = slice(lo, lo + HSZ)
        prob = softmax_block(q_ref[:, cols], k_ref[:, cols]).astype(jnp.bfloat16)
        o_ref[:, cols] = dot(prob, v_ref[:, cols]).astype(jnp.bfloat16)


def backward_kernel(q_ref, k_ref, v_ref, g_ref, *refs):
    gq_ref, gk_ref, gv_ref = refs[-3:]
    for lo in range(0, q_ref.shape[1], HSZ):
        cols = slice(lo, lo + HSZ)
        q, k, v, g = q_ref[:, cols], k_ref[:, cols], v_ref[:, cols], g_ref[:, cols]
        prob = softmax_block(q, k)
        grad_prob = dot(g, v, NT)
        delta = jnp.sum(prob * grad_prob, axis=-1, keepdims=True)
        grad_score = (prob * (grad_prob - delta) * SCALE).astype(jnp.bfloat16)
        gq_ref[:, cols] = dot(grad_score, k).astype(jnp.bfloat16)
        gk_ref[:, cols] = dot(grad_score, q, TN).astype(jnp.bfloat16)
        gv_ref[:, cols] = dot(prob.astype(jnp.bfloat16), g, TN).astype(jnp.bfloat16)


def heads_per_step(width):
    return 2 if width % (2 * HSZ) == 0 else 1


def attention(q, k, v, at, width):
    wide = heads_per_step(width) * HSZ
    spec = pl.BlockSpec((PATCH, wide), lambda i, h: (i, h + at // wide))
    macs = 2 * q.shape[0] * PATCH * width
    return pl.pallas_call(
        forward_kernel,
        grid=(q.shape[0] // PATCH, width // wide),
        in_specs=[spec] * 3,
        out_specs=pl.BlockSpec((PATCH, wide), lambda i, h: (i, h)),
        out_shape=jax.ShapeDtypeStruct((q.shape[0], width), jnp.bfloat16),
        cost_estimate=pl.CostEstimate(
            flops=2 * macs, bytes_accessed=8 * q.shape[0] * width, transcendentals=macs // HSZ // 2
        ),
    )(q, k, v)


def attention_grads(q, k, v, g, at, before):
    width = g.shape[1]
    wide = heads_per_step(width) * HSZ
    spec = pl.BlockSpec((PATCH, wide), lambda i, h: (i, h + at // wide))
    macs = 5 * q.shape[0] * PATCH * width
    return pl.pallas_call(
        backward_kernel,
        grid=(q.shape[0] // PATCH, width // wide),
        in_specs=[spec] * 3
        + [pl.BlockSpec((PATCH, wide), lambda i, h: (i, h))]
        + [pl.BlockSpec(memory_space=pl.ANY)] * len(before),
        out_specs=[spec] * 3,
        out_shape=[jax.ShapeDtypeStruct(q.shape, jnp.bfloat16)] * 3,
        input_output_aliases={4 + i: i for i in range(len(before))},
        cost_estimate=pl.CostEstimate(
            flops=2 * macs, bytes_accessed=14 * q.shape[0] * width, transcendentals=macs // HSZ // 5
        ),
    )(q, k, v, g, *before)


def flip(x, axis, bit):
    return lax.ppermute(x, axis, [(i, i ^ bit) for i in range(lax.axis_size(axis))])


def xor_pick(blocks, m):
    odd, high = (m & 1) == 1, (m & 2) == 2
    a, b, c, d = blocks
    a, b, c, d = (
        jnp.where(odd, b, a),
        jnp.where(odd, a, b),
        jnp.where(odd, d, c),
        jnp.where(odd, c, d),
    )
    return [
        jnp.where(high, c, a),
        jnp.where(high, d, b),
        jnp.where(high, a, c),
        jnp.where(high, b, d),
    ]


def gather_line(own):
    near = flip(own, "col", 1)
    mid = lax.ppermute(own, "col", [(1, 2), (2, 1)])
    two_out = lax.ppermute(mid, "col", [(1, 0), (2, 3)])
    two_in = lax.ppermute(near, "col", [(1, 2), (2, 1)])
    three = lax.ppermute(two_in, "col", [(1, 0), (2, 3)])
    outer = (lax.axis_index("col") % 3) == 0
    return [own, near, jnp.where(outer, two_out, two_in), jnp.where(outer, three, mid)]


def scatter_line(parts):
    def plus(a, b):
        return (a.astype(jnp.float32) + b.astype(jnp.float32)).astype(jnp.bfloat16)

    far = lax.ppermute(parts[3], "col", [(0, 1), (3, 2)])
    second = plus(parts[2], far)
    out = lax.ppermute(second, "col", [(0, 1), (3, 2)])
    cross = lax.ppermute(second, "col", [(1, 2), (2, 1)])
    near = flip(plus(parts[1], cross), "col", 1)
    mid = lax.ppermute(plus(parts[3], out), "col", [(1, 2), (2, 1)])
    total = parts[0].astype(jnp.float32) + near.astype(jnp.float32) + mid.astype(jnp.float32)
    return total.astype(jnp.bfloat16)


def gather_heads(head_out):
    r, z = lax.axis_index("row"), lax.axis_index("col")
    if lax.axis_size("col") == 4:
        return xor_pick(gather_line(head_out), r ^ z)
    whole = lax.all_gather(head_out, "col", axis=1, tiled=True)
    width = whole.shape[1] // 4
    return [lax.dynamic_slice_in_dim(whole, (r ^ j) * width, width, 1) for j in range(4)]


def scatter_heads(parts):
    r, z = lax.axis_index("row"), lax.axis_index("col")
    if lax.axis_size("col") == 4:
        return scatter_line(xor_pick(parts, r ^ z))
    whole = jnp.concatenate(xor_pick(parts, r), axis=1).astype(jnp.float32)
    return lax.psum_scatter(whole, "col", scatter_dimension=1, tiled=True).astype(jnp.bfloat16)


def in_order(mine, other, axis):
    first = lax.axis_index("rep") == 0
    return jnp.where(
        first, jnp.concatenate([mine, other], axis), jnp.concatenate([other, mine], axis)
    )


def local(n_chunks, queries, key_vectors, value_vectors, cotangent, out_weight):
    tok_rows, features = queries.shape
    paired = lax.axis_size("rep") == 2
    me = lax.axis_index("rep")
    rows = out_weight.shape[0] // n_chunks
    width = features // n_chunks
    chunks = range(n_chunks)
    factor = float(tok_rows * lax.axis_size("row") * lax.axis_size("rep")) ** (-0.5)

    cot = jnp.concatenate([cotangent, flip(cotangent, "row", 2)], axis=0)
    weights, beside = [], []
    for h in chunks:
        block = lax.slice_in_dim(out_weight, h * rows, (h + 1) * rows, axis=0)
        if paired:
            half = flip(lax.dynamic_slice_in_dim(block, me * (rows // 2), rows // 2, 0), "row", 1)
            arrived = in_order(half, flip(half, "rep", 1), 0)
        else:
            arrived = flip(block, "row", 1)
        weights.append(block)
        beside.append(arrived)

    own, next_to = [], []
    for h in chunks:
        head_out = attention(queries, key_vectors, value_vectors, h * width, width)
        held = gather_heads(head_out)
        sent = flip(jnp.concatenate(held[2:], axis=1), "row", 2)
        own.append(jnp.concatenate([held[0], sent[:, :rows]], axis=0))
        next_to.append(jnp.concatenate([held[1], sent[:, rows:]], axis=0))

    grads = []
    for h in chunks:
        part = dot(cot, weights[h], NT).astype(jnp.bfloat16)
        part_beside = dot(cot, beside[h], NT).astype(jnp.bfloat16)
        sent = flip(
            jnp.concatenate([part[tok_rows:], part_beside[tok_rows:]], axis=1), "row", 2
        )
        summed = scatter_heads(
            [part[:tok_rows], part_beside[:tok_rows], sent[:, :rows], sent[:, rows:]]
        )
        grads = attention_grads(queries, key_vectors, value_vectors, summed, h * width, grads)

    grad_rows = []
    if paired:
        cot_both = jnp.concatenate([cot, flip(cot, "rep", 1)], axis=0)
    for h in chunks:
        if paired:
            half = rows // 2
            mine = [lax.dynamic_slice_in_dim(a, me * half, half, 1) for a in (own[h], next_to[h])]
            theirs = [
                lax.dynamic_slice_in_dim(a, (1 - me) * half, half, 1) for a in (own[h], next_to[h])
            ]
            got = flip(jnp.concatenate(theirs, axis=1), "rep", 1)
            left = jnp.concatenate([mine[0], got[:, :half]], axis=0)
            right = jnp.concatenate([mine[1], got[:, half:]], axis=0)
            away = flip(dot(right, cot_both, TN).astype(jnp.bfloat16), "row", 1)
            total = (dot(left, cot_both, TN) + away.astype(jnp.float32)) * factor
            total = total.astype(jnp.bfloat16)
            grad_rows.append(in_order(total, flip(total, "rep", 1), 0))
        else:
            away = flip(dot(next_to[h], cot, TN).astype(jnp.bfloat16), "row", 1)
            total = dot(own[h], cot, TN) + away.astype(jnp.float32)
            total = lax.psum(total.astype(jnp.bfloat16), "rep").astype(jnp.float32) * factor
            grad_rows.append(total.astype(jnp.bfloat16))
    grad_weight = jnp.concatenate(grad_rows, axis=0)

    every = jnp.concatenate([a for pair in zip(own, next_to) for a in pair], axis=1)
    every_weight = jnp.concatenate([a for pair in zip(weights, beside) for a in pair], axis=0)
    away = flip(dot(every[tok_rows:], every_weight).astype(jnp.bfloat16), "row", 2)
    projected = dot(every[:tok_rows], every_weight) + away.astype(jnp.float32)

    return (projected.astype(jnp.bfloat16), *grads, grad_weight)


def solution(mesh):
    placed = (P(("rep", "row"), "col"),) * 4 + (P("row", "col"),)
    n_chunks = 2 if mesh.shape["col"] == 4 else 1
    return jax.shard_map(
        functools.partial(local, n_chunks),
        mesh=mesh,
        in_specs=placed,
        out_specs=placed,
        check_vma=False,
    )
```

time: 376 us -> 182 us (0.48)
  waiting for transfers between devices: 269 us -> 60.2 us
  starting transfers between devices: 0.38 us -> 54.9 us
  blocking collectives: 37.7 us -> 0 us
  matrix products: 40.6 us -> 12.8 us
  other arithmetic: 5.42 us -> 28.3 us
  Pallas kernels: 0 us -> 15.9 us
  between operations: 13.9 us -> 1.31 us
    all_gather x3 -> x0, waiting for transfers between devices: 184 us -> none  [the longest x1 116 us: local(): column_panel = lax.all_gather(out_weight, 'row', axis=0, tiled=True)]
    reduce_scatter x1 -> x0, waiting for transfers between devices: 68.7 us -> none  [local(): lax.psum_scatter(lax.dot_general(column_panel, cotangent, (((1,), (1,)),...]
    ppermute x0 -> x37, waiting for transfers between devices: none -> 60.2 us  [the longest x21 45.8 us: flip(): lax.ppermute(x, axis, [(i, i ^ bit) for i in range(lax.axis_size(axis))])]
    ppermute x0 -> x37, starting transfers between devices: none -> 54.9 us  [the longest x21 20.9 us: flip(): lax.ppermute(x, axis, [(i, i ^ bit) for i in range(lax.axis_size(axis))])]
    all_to_all x1 -> x0, blocking collectives: 37.7 us -> none  [local(): lax.all_to_all(gathered, 'row', split_axis=1, concat_axis=0, tiled=True)]
    dot_general x8 -> x10, matrix products: 38.4 us -> 12.8 us  [dot(): return lax.dot_general(a, b, dims, preferred_element_type=jnp.float32)]
    pallas_call x0 -> x4, Pallas kernels: none -> 15.9 us  [the longest x2 8.77 us: attention_grads(): pl.pallas_call(backward_kernel, grid=(q.shape[0] // PATCH, width // wide)...]
    psum x1 -> x0, waiting for transfers between devices: 15.8 us -> none  [local(): lax.psum(partial_value.astype(jnp.bfloat16), 'rep').astype(jnp.float32)]
  transfers between devices with their start and end apart: 5 -> 37, of which waited for: 5 -> 11; matrix products, arithmetic and copies ran while one was open for 8% -> 25% of each run, Pallas kernels for 0% -> 7%
where the time goes in v1:
time: 182 us; the launch traced here: 181 us
  waiting for transfers between devices  60.2 us (33%)
  starting transfers between devices  54.9 us (30%)
  other arithmetic  28.3 us (16%)
  Pallas kernels  15.9 us (9%)
  matrix products  12.8 us (7%)
  local copies, waits for them, and re-layouts  7.62 us (4%)
    ppermute x21, waiting for transfers between devices, flip(): lax.ppermute(x, axis, [(i, i ^ bit) for i in range(lax.axis_size(axis))])  45.8 us
    ppermute x21, starting transfers between devices, flip(): lax.ppermute(x, axis, [(i, i ^ bit) for i in range(lax.axis_size(axis))])  20.9 us
    ppermute x2, starting transfers between devices, scatter_line(): out = lax.ppermute(second, 'col', [(0, 1), (3, 2)])  12.9 us
    dot_general x10, matrix products, dot(): return lax.dot_general(a, b, dims, preferred_element_type=jnp.float32)  12.8 us
    concatenate x1, other arithmetic, local(): jnp.concatenate([a for pair in zip(own, next_to) for a in pair], axis=1)  12.7 us
    pallas_call x2, Pallas kernels, attention_grads(): pl.pallas_call(backward_kernel, grid=(q.shape[0] // PATCH, width // wide)...  8.77 us
    ppermute x2, waiting for transfers between devices, gather_line(): two_out = lax.ppermute(mid, 'col', [(1, 0), (2, 3)])  8.59 us
    pallas_call x2, Pallas kernels, attention(): pl.pallas_call(forward_kernel, grid=(q.shape[0] // PATCH, width // wide),...  7.09 us
  transfers between devices with their start and end apart: 37, of which 11 were waited for; matrix products, arithmetic and copies ran while one was open for 25% of the time, Pallas kernels for 7%

profile of v1, /device:TPU:0, one launch (start us, length us, event | category | flops | bytes accessed | tf_op | source)
XLA Modules:
  0.0 181.0 jit_solution(12156115227172280036)
XLA Ops:
  0.6 3.6 %shard_map.92 = bf16[256,512]{1,0:T(8,128)(2,1)} custom-call(bf16[256,1024]{1,0:T(8,128)(2,1)} %q_ref.7, bf16[256,1024]{1,0:T(8,128)(2,1)} %k_ref.7, bf16[256,1024]{1,0:T(8,128)(2,1)} %v_ref.7), custom_call_target="tpu_custom_call" | custom-call | flops 134217728 | bytes 1048576 | tf_op jit(solution)/shard_map/pallas_call | solution.py:57
  4.2 3.0 %collective-permute-start = (bf16[256,512]{1,0:T(8,128)(2,1)}, bf16[256,512]{1,0:T(8,128)(2,1)}, u32[]{:S(2)}, u32[]{:S(2)}) collective-permute-start(bf16[256,512]{1,0:T(8,128)(2,1)} %shard_map.92), channel_id=1, source_target_pairs={{0,2},{2,0},{4,6},{6,4},{1,3},{3,1},{5,7},{7,5},{8,10},{10,8},{12,... | collective-permute-start | bytes 786440 | tf_op jit(solution)/shard_map/ppermute | solution.py:90
  7.2 1.4 collective-permute-start.3
  8.6 3.5 %shard_map.93 = bf16[256,512]{1,0:T(8,128)(2,1)} custom-call(bf16[256,1024]{1,0:T(8,128)(2,1)} %q_ref.7, bf16[256,1024]{1,0:T(8,128)(2,1)} %k_ref.7, bf16[256,1024]{1,0:T(8,128)(2,1)} %v_ref.7), custom_call_target="tpu_custom_call" | custom-call | flops 134217728 | bytes 1048576 | tf_op jit(solution)/shard_map/pallas_call | solution.py:57
  12.1 3.7 %collective-permute-start.6 = (bf16[256,512]{1,0:T(8,128)(2,1)}, bf16[256,512]{1,0:T(8,128)(2,1)}, u32[]{:S(2)}, u32[]{:S(2)}) collective-permute-start(bf16[256,512]{1,0:T(8,128)(2,1)} %shard_map.93), channel_id=1, source_target_pairs={{0,2},{2,0},{4,6},{6,4},{1,3},{3,1},{5,7},{7,5},{8,10},{10,8},{12,... | collective-permute-start | bytes 786440 | tf_op jit(solution)/shard_map/ppermute | solution.py:90
  15.8 1.4 collective-permute-start.9
  17.2 1.5 collective-permute-start.17
  18.7 2.1 %fusion.35 = (bf16[512,1536]{1,0:T(8,128)(2,1)S(1)}, bf16[512,1536]{1,0:T(8,128)(2,1)S(1)}) fusion(bf16[1024,1536]{1,0:T(8,128)(2,1)} %param.9), kind=kLoop, calls=%fused_computation.119 | loop fusion | bytes 6291456 | tf_op jit(solution)/shard_map/slice | solution.py:170
  20.9 1.4 collective-permute-start.1
  22.2 2.4 %constant_dynamic-update-slice_fusion.4 = (bf16[1024,1536]{1,0:T(8,128)(2,1)}, bf16[512,1536]{1,0:T(8,128)(2,1)}) fusion(bf16[256,1536]{1,0:T(8,128)(2,1)} %param.8), kind=kLoop, calls=%fused_computation.108 | loop fusion | bytes 2359296
  24.6 1.4 collective-permute-start.4
  26.1 1.4 collective-permute-start.7
  27.4 1.3 collective-permute-start.2
  29.8 1.6 collective-permute-start.12
  31.3 4.7 %collective-permute-done.4 = bf16[256,512]{1,0:T(8,128)(2,1)} collective-permute-done((bf16[256,512]{1,0:T(8,128)(2,1)}, bf16[256,512]{1,0:T(8,128)(2,1)}, u32[]{:S(2)}, u32[]{:S(2)}) %collective-permute-start.4) | collective-permute-done | bytes 262176 | tf_op jit(solution)/shard_map/ppermute | solution.py:113
  36.0 1.5 collective-permute-start.14
  37.5 1.3 collective-permute-start.10
  38.8 2.5 %collective-permute-done.2 = bf16[256,512]{1,0:T(8,128)(2,1)} collective-permute-done((bf16[256,512]{1,0:T(8,128)(2,1)}, bf16[256,512]{1,0:T(8,128)(2,1)}, u32[]{:S(2)}, u32[]{:S(2)}) %collective-permute-start.2) | collective-permute-done | bytes 262176 | tf_op jit(solution)/shard_map/ppermute | solution.py:115
  41.2 1.3 collective-permute-start.8
  42.5 1.1 broadcast_select_fusion.29
  43.7 1.0 broadcast_select_fusion.26
  44.8 3.9 %collective-permute-done.10 = bf16[256,512]{1,0:T(8,128)(2,1)S(1)} collective-permute-done((bf16[256,512]{1,0:T(8,128)(2,1)}, bf16[256,512]{1,0:T(8,128)(2,1)S(1)}, u32[]{:S(2)}, u32[]{:S(2)}) %collective-permute-start.10) | collective-permute-done | bytes 262176 | tf_op jit(solution)/shard_map/ppermute | solution.py:113
  48.7 2.9 %collective-permute-done.8 = bf16[256,512]{1,0:T(8,128)(2,1)S(1)} collective-permute-done((bf16[256,512]{1,0:T(8,128)(2,1)}, bf16[256,512]{1,0:T(8,128)(2,1)S(1)}, u32[]{:S(2)}, u32[]{:S(2)}) %collective-permute-start.8) | collective-permute-done | bytes 262176 | tf_op jit(solution)/shard_map/ppermute | solution.py:115
  51.7 1.0 broadcast_select_fusion.22
  52.9 1.4 constant_dynamic-update-slice_fusion.3
  57.1 8.0 %collective-permute-done.14 = bf16[256,1536]{1,0:T(8,128)(2,1)S(1)} collective-permute-done((bf16[256,1536]{1,0:T(8,128)(2,1)S(1)}, bf16[256,1536]{1,0:T(8,128)(2,1)S(1)}, u32[]{:S(2)}, u32[]{:S(2)}) %collective-permute-start.14) | collective-permute-done | bytes 786464 | tf_op jit(solution)/shard_map/ppermute | solution.py:90
  65.8 3.3 %collective-permute-done.11 = bf16[256,1024]{1,0:T(8,128)(2,1)S(1)} collective-permute-done((bf16[256,1024]{1,0:T(8,128)(2,1)S(1)}, bf16[256,1024]{1,0:T(8,128)(2,1)S(1)}, u32[]{:S(2)}, u32[]{:S(2)}) %collective-permute-start.11) | collective-permute-done | bytes 524320 | tf_op jit(solution)/shard_map/ppermute | solution.py:90
  69.2 12.7 %maximum_maximum_fusion = bf16[512,2048]{1,0:T(8,128)(2,1)S(1)} fusion(bf16[256,512]{1,0:T(8,128)(2,1)S(1)} %get-tuple-element.50, bf16[256,512]{1,0:T(8,128)(2,1)S(1)} %get-tuple-element.28, bf16[256,512]{1,0:T(8,128)(2,1)S(1)} %get-tuple-element.49, bf16[256,512]{1,0:T(8,128)(2,1)S(1)} %get-tuple-element.20, bf16[256,512]{1,0:T(8,128)(2,1)S(1)} %get-tuple-element.48, ...), kind=kLoop, calls=%fused_computation.11 | loop fusion | flops 16777216 | bytes 4194304 | tf_op jit(solution)/shard_map/concatenate | solution.py:223
  85.7 2.1 %collective-permute-start.18 = (bf16[256,1024]{1,0:T(8,128)(2,1)S(1)}, bf16[256,1024]{1,0:T(8,128)(2,1)S(1)}, u32[]{:S(2)}, u32[]{:S(2)}) collective-permute-start(bf16[256,1024]{1,0:T(8,128)(2,1)S(1)} %pad_maximum_fusion.8), channel_id=1, source_target_pairs={{0,16},{8,24},{16,0},{24,8},{1,17},{9,25},{17,1},{25,9},{2,18},{10... | collective-permute-start | bytes 1572872 | tf_op jit(solution)/shard_map/ppermute | solution.py:90
  87.8 2.0 %convolution_convert_fusion.2 = bf16[256,1536]{1,0:T(8,128)(2,1)S(1)} fusion(bf16[512,1536]{1,0:T(8,128)(2,1)S(1)} %maximum_select_fusion.1, bf16[512,1536]{1,0:T(8,128)(2,1)S(1)} %copy-done.1, bf16[512,1536]{1,0:T(8,128)(2,1)S(1)} %maximum_select_fusion, bf16[512,1536]{1,0:T(8,128)(2,1)S(1)} %get-tuple-element.23, ...), kind=kOutput, calls=%fused_computation.10 | convolution fusion | flops 1636171776 | bytes 8126464 | tf_op jit(solution)/shard_map/dot_general | solution.py:19
  90.3 8.4 %collective-permute-done.24 = bf16[256,1024]{1,0:T(8,128)(2,1)S(1)} collective-permute-done((bf16[256,1024]{1,0:T(8,128)(2,1)S(1)}, bf16[256,1024]{1,0:T(8,128)(2,1)S(1)}, u32[]{:S(2)}, u32[]{:S(2)}) %collective-permute-start.24) | collective-permute-done | bytes 524320 | tf_op jit(solution)/shard_map/ppermute | solution.py:90
  98.7 3.4 %collective-permute-start.25 = (bf16[256,512]{1,0:T(8,128)(2,1)S(1)}, bf16[256,512]{1,0:T(8,128)(2,1)S(1)}, u32[]{:S(2)}, u32[]{:S(2)}) collective-permute-start(bf16[256,512]{1,0:T(8,128)(2,1)S(1)} %broadcast_select_fusion.20), channel_id=1, source_target_pairs={{0,2},{6,4},{1,3},{7,5},{8,10},{14,12},{9,11},{15,13},{16,18},{22,... | collective-permute-start | bytes 786440 | tf_op jit(solution)/shard_map/ppermute | solution.py:124
  102.2 7.7 %collective-permute-done.18 = bf16[256,1024]{1,0:T(8,128)(2,1)S(1)} collective-permute-done((bf16[256,1024]{1,0:T(8,128)(2,1)S(1)}, bf16[256,1024]{1,0:T(8,128)(2,1)S(1)}, u32[]{:S(2)}, u32[]{:S(2)}) %collective-permute-start.18) | collective-permute-done | bytes 524320 | tf_op jit(solution)/shard_map/ppermute | solution.py:90
  109.9 3.4 %collective-permute-start.19 = (bf16[256,512]{1,0:T(8,128)(2,1)S(1)}, bf16[256,512]{1,0:T(8,128)(2,1)S(1)}, u32[]{:S(2)}, u32[]{:S(2)}) collective-permute-start(bf16[256,512]{1,0:T(8,128)(2,1)S(1)} %broadcast_select_fusion.21), channel_id=1, source_target_pairs={{0,2},{6,4},{1,3},{7,5},{8,10},{14,12},{9,11},{15,13},{16,18},{22,... | collective-permute-start | bytes 786440 | tf_op jit(solution)/shard_map/ppermute | solution.py:124
  114.3 4.3 %collective-permute-start.28 = (bf16[256,512]{1,0:T(8,128)(2,1)S(1)}, bf16[256,512]{1,0:T(8,128)(2,1)S(1)}, u32[]{:S(2)}, u32[]{:S(2)}) collective-permute-start(bf16[256,512]{1,0:T(8,128)(2,1)S(1)} %add_convert_fusion.4), channel_id=1, source_target_pairs={{0,2},{6,4},{1,3},{7,5},{8,10},{14,12},{9,11},{15,13},{16,18},{22,... | collective-permute-start | bytes 786440 | tf_op jit(solution)/shard_map/ppermute | solution.py:126
  119.9 8.7 %collective-permute-start.22 = (bf16[256,512]{1,0:T(8,128)(2,1)S(1)}, bf16[256,512]{1,0:T(8,128)(2,1)S(1)}, u32[]{:S(2)}, u32[]{:S(2)}) collective-permute-start(bf16[256,512]{1,0:T(8,128)(2,1)S(1)} %add_convert_fusion.8), channel_id=1, source_target_pairs={{0,2},{6,4},{1,3},{7,5},{8,10},{14,12},{9,11},{15,13},{16,18},{22,... | collective-permute-start | bytes 786440 | tf_op jit(solution)/shard_map/ppermute | solution.py:126
  129.7 1.6 collective-permute-start.32
  131.3 2.8 %add_convert_fusion = bf16[256,1536]{1,0:T(8,128)(2,1)} fusion(bf16[256,1536]{1,0:T(8,128)(2,1)S(1)} %collective-permute-done.16, bf16[512,1536]{1,0:T(8,128)(2,1)S(1)} %maximum_select_fusion.1, bf16[512,1536]{1,0:T(8,128)(2,1)S(1)} %copy-done.1, bf16[512,1536]{1,0:T(8,128)(2,1)S(1)} %maximum_select_fusion, bf16[512,1536]{1,0:T(8,128)(2,1)S(1)} %get-tuple-element.23, ...), kind=kOutput, calls=%fused_computation.16 | convolution fusion | flops 1636958208 | bytes 8912896 | tf_op jit(solution)/shard_map/dot_general | solution.py:19
  137.6 3.3 %collective-permute-start.21 = (bf16[256,512]{1,0:T(8,128)(2,1)}, bf16[256,512]{1,0:T(8,128)(2,1)S(1)}, u32[]{:S(2)}, u32[]{:S(2)}) collective-permute-start(bf16[256,512]{1,0:T(8,128)(2,1)} %add_convert_fusion.7), channel_id=1, source_target_pairs={{0,2},{2,0},{4,6},{6,4},{1,3},{3,1},{5,7},{7,5},{8,10},{10,8},{12,... | collective-permute-start | bytes 786440 | tf_op jit(solution)/shard_map/ppermute | solution.py:90
  141.6 8.7 %collective-permute-done.32 = bf16[256,1536]{1,0:T(8,128)(2,1)S(1)} collective-permute-done((bf16[256,1536]{1,0:T(8,128)(2,1)S(1)}, bf16[256,1536]{1,0:T(8,128)(2,1)S(1)}, u32[]{:S(2)}, u32[]{:S(2)}) %collective-permute-start.32) | collective-permute-done | bytes 786464 | tf_op jit(solution)/shard_map/ppermute | solution.py:90
  150.3 1.4 collective-permute-start.23
  152.6 9.7 %collective-permute-done.35 = bf16[256,1536]{1,0:T(8,128)(2,1)S(1)} collective-permute-done((bf16[256,1536]{1,0:T(8,128)(2,1)S(1)}, bf16[256,1536]{1,0:T(8,128)(2,1)S(1)}, u32[]{:S(2)}, u32[]{:S(2)}) %collective-permute-start.35) | collective-permute-done | bytes 786464 | tf_op jit(solution)/shard_map/ppermute | solution.py:90
  164.8 4.4 %shard_map.94 = (bf16[256,1024]{1,0:T(8,128)(2,1)}, bf16[256,1024]{1,0:T(8,128)(2,1)}, bf16[256,1024]{1,0:T(8,128)(2,1)}) custom-call(bf16[256,1024]{1,0:T(8,128)(2,1)} %q_ref.7, bf16[256,1024]{1,0:T(8,128)(2,1)} %k_ref.7, bf16[256,1024]{1,0:T(8,128)(2,1)} %v_ref.7, bf16[256,512]{1,0:T(8,128)(2,1)} %add_convert_fusion.1.g_ref), custom_call_target="tpu_custom_call" | custom-call | flops 335544320 | bytes 1835008 | tf_op jit(solution)/shard_map/pallas_call | solution.py:74
  169.2 1.9 %add_convert_fusion.5.g_ref = bf16[256,512]{1,0:T(8,128)(2,1)} fusion(bf16[256,512]{1,0:T(8,128)(2,1)} %collective-permute-done.23, bf16[256,512]{1,0:T(8,128)(2,1)S(1)} %collective-permute-done.21, pred[]{:T(512)S(6)} %eq.11, bf16[256,1024]{1,0:T(8,128)(2,1)S(1)} %collective-permute-done.18, pred[]{:T(512)S(6)} %eq.12, bf16[512,512]{1,0:T(8,128)(2,1)S(1)} %copy-done.3, ...), kind=kLoop, calls=%fused_computation.62 | loop fusion | flops 1179648 | bytes 1835010 | tf_op jit(solution)/shard_map/convert_element_type | solution.py:131
  171.1 4.4 %shard_map.95 = (bf16[256,1024]{1,0:T(8,128)(2,1)}, bf16[256,1024]{1,0:T(8,128)(2,1)}, bf16[256,1024]{1,0:T(8,128)(2,1)}) custom-call(bf16[256,1024]{1,0:T(8,128)(2,1)} %q_ref.7, bf16[256,1024]{1,0:T(8,128)(2,1)} %k_ref.7, bf16[256,1024]{1,0:T(8,128)(2,1)} %v_ref.7, ...), custom_call_target="tpu_custom_call", output_to_operand_aliasing={{0}: (4, {}), {1}: (5, {}), {2}: (6, {})} | custom-call | flops 335544320 | bytes 1835008 | tf_op jit(solution)/shard_map/pallas_call | solution.py:74
  175.5 1.8 maximum_select_fusion.2
  177.3 1.8 maximum_select_fusion.3
  179.1 1.9 %pad_maximum_fusion.1 = bf16[1024,1536]{1,0:T(8,128)(2,1)} fusion(bf16[512,1536]{1,0:T(8,128)(2,1)S(1)} %maximum_select_fusion.3, bf16[512,1536]{1,0:T(8,128)(2,1)S(1)} %maximum_select_fusion.2), kind=kLoop, calls=%fused_computation.1 | loop fusion | flops 6291456 | bytes 6291456 | tf_op jit(solution)/shard_map/concatenate | solution.py:221
  (106 shorter events, 20.1 us)
Async XLA Ops:
  4.2 16.7 %collective-permute-start = (bf16[256,512]{1,0:T(8,128)(2,1)}, bf16[256,512]{1,0:T(8,128)(2,1)}, u32[]{:S(2)}, u32[]{:S(2)}) collective-permute-start(bf16[256,512]{1,0:T(8,128)(2,1)} %shard_map.92), channel_id=1, source_target_pairs={{0,2},{2,0},{4,6},{6,4},{1,3},{3,1},{5,7},{7,5},{8,10},{10,8},{12,... | collective-permute-start | bytes 786440 | tf_op jit(solution)/shard_map/ppermute | solution.py:90
  7.2 17.4 %collective-permute-start.3 = (bf16[256,512]{1,0:T(8,128)(2,1)}, bf16[256,512]{1,0:T(8,128)(2,1)}, u32[]{:S(2)}, u32[]{:S(2)}) collective-permute-start(bf16[256,512]{1,0:T(8,128)(2,1)} %shard_map.92), channel_id=1, source_target_pairs={{2,4},{4,2},{3,5},{5,3},{10,12},{12,10},{11,13},{13,11},{18,20},{2... | collective-permute-start | bytes 786440 | tf_op jit(solution)/shard_map/ppermute | solution.py:112
  12.1 13.9 %collective-permute-start.6 = (bf16[256,512]{1,0:T(8,128)(2,1)}, bf16[256,512]{1,0:T(8,128)(2,1)}, u32[]{:S(2)}, u32[]{:S(2)}) collective-permute-start(bf16[256,512]{1,0:T(8,128)(2,1)} %shard_map.93), channel_id=1, source_target_pairs={{0,2},{2,0},{4,6},{6,4},{1,3},{3,1},{5,7},{7,5},{8,10},{10,8},{12,... | collective-permute-start | bytes 786440 | tf_op jit(solution)/shard_map/ppermute | solution.py:90
  15.8 13.9 %collective-permute-start.9 = (bf16[256,512]{1,0:T(8,128)(2,1)}, bf16[256,512]{1,0:T(8,128)(2,1)}, u32[]{:S(2)}, u32[]{:S(2)}) collective-permute-start(bf16[256,512]{1,0:T(8,128)(2,1)} %shard_map.93), channel_id=1, source_target_pairs={{2,4},{4,2},{3,5},{5,3},{10,12},{12,10},{11,13},{13,11},{18,20},{2... | collective-permute-start | bytes 786440 | tf_op jit(solution)/shard_map/ppermute | solution.py:112
  17.2 35.7 %collective-permute-start.17 = (bf16[256,1536]{1,0:T(8,128)(2,1)}, bf16[256,1536]{1,0:T(8,128)(2,1)}, u32[]{:S(2)}, u32[]{:S(2)}) collective-permute-start(bf16[256,1536]{1,0:T(8,128)(2,1)} %param.8), channel_id=1, source_target_pairs={{0,16},{8,24},{16,0},{24,8},{1,17},{9,25},{17,1},{25,9},{2,18},{10... | collective-permute-start | bytes 2359304 | tf_op jit(solution)/shard_map/ppermute | solution.py:90
  20.8 8.9 %copy-start = (bf16[512,1536]{1,0:T(8,128)(2,1)}, bf16[512,1536]{1,0:T(8,128)(2,1)S(1)}, u32[]{:S(2)}) copy-start(bf16[512,1536]{1,0:T(8,128)(2,1)S(1)} %get-tuple-element.24) | copy-start | bytes 4718596
  20.9 6.6 %collective-permute-start.1 = (bf16[256,512]{1,0:T(8,128)(2,1)}, bf16[256,512]{1,0:T(8,128)(2,1)}, u32[]{:S(2)}, u32[]{:S(2)}) collective-permute-start(bf16[256,512]{1,0:T(8,128)(2,1)} %collective-permute-done), channel_id=1, source_target_pairs={{2,4},{4,2},{3,5},{5,3},{10,12},{12,10},{11,13},{13,11},{18,20},{2... | collective-permute-start | bytes 786440 | tf_op jit(solution)/shard_map/ppermute | solution.py:114
  24.6 17.9 %copy-start.8 = (bf16[256,512]{1,0:T(8,128)(2,1)S(1)}, bf16[256,512]{1,0:T(8,128)(2,1)}, u32[]{:S(2)}) copy-start(bf16[256,512]{1,0:T(8,128)(2,1)} %shard_map.92) | copy-start | bytes 786436
  24.6 11.4 %collective-permute-start.4 = (bf16[256,512]{1,0:T(8,128)(2,1)}, bf16[256,512]{1,0:T(8,128)(2,1)}, u32[]{:S(2)}, u32[]{:S(2)}) collective-permute-start(bf16[256,512]{1,0:T(8,128)(2,1)} %collective-permute-done.3), channel_id=1, source_target_pairs={{2,0},{4,6},{3,1},{5,7},{10,8},{12,14},{11,9},{13,15},{18,16},{20,... | collective-permute-start | bytes 786440 | tf_op jit(solution)/shard_map/ppermute | solution.py:113
  26.1 11.4 %collective-permute-start.7 = (bf16[256,512]{1,0:T(8,128)(2,1)}, bf16[256,512]{1,0:T(8,128)(2,1)}, u32[]{:S(2)}, u32[]{:S(2)}) collective-permute-start(bf16[256,512]{1,0:T(8,128)(2,1)} %collective-permute-done.6), channel_id=1, source_target_pairs={{2,4},{4,2},{3,5},{5,3},{10,12},{12,10},{11,13},{13,11},{18,20},{2... | collective-permute-start | bytes 786440 | tf_op jit(solution)/shard_map/ppermute | solution.py:114
  27.4 13.8 %collective-permute-start.2 = (bf16[256,512]{1,0:T(8,128)(2,1)}, bf16[256,512]{1,0:T(8,128)(2,1)}, u32[]{:S(2)}, u32[]{:S(2)}) collective-permute-start(bf16[256,512]{1,0:T(8,128)(2,1)} %collective-permute-done.1), channel_id=1, source_target_pairs={{2,0},{4,6},{3,1},{5,7},{10,8},{12,14},{11,9},{13,15},{18,16},{20,... | collective-permute-start | bytes 786440 | tf_op jit(solution)/shard_map/ppermute | solution.py:115
  29.7 21.8 %copy-start.7 = (bf16[256,512]{1,0:T(8,128)(2,1)S(1)}, bf16[256,512]{1,0:T(8,128)(2,1)}, u32[]{:S(2)}) copy-start(bf16[256,512]{1,0:T(8,128)(2,1)} %shard_map.93) | copy-start | bytes 786436
  29.8 27.2 %collective-permute-start.12 = (bf16[256,1536]{1,0:T(8,128)(2,1)}, bf16[256,1536]{1,0:T(8,128)(2,1)S(1)}, u32[]{:S(2)}, u32[]{:S(2)}) collective-permute-start(bf16[256,1536]{1,0:T(8,128)(2,1)} %constant_dynamic-slice_fusion.1), channel_id=1, source_target_pairs={{0,8},{8,0},{16,24},{24,16},{1,9},{9,1},{17,25},{25,17},{2,10},{10... | collective-permute-start | bytes 2359304 | tf_op jit(solution)/shard_map/ppermute | solution.py:90
  36.0 29.1 %collective-permute-start.14 = (bf16[256,1536]{1,0:T(8,128)(2,1)S(1)}, bf16[256,1536]{1,0:T(8,128)(2,1)S(1)}, u32[]{:S(2)}, u32[]{:S(2)}) collective-permute-start(bf16[256,1536]{1,0:T(8,128)(2,1)S(1)} %constant_dynamic-slice_fusion), channel_id=1, source_target_pairs={{0,8},{8,0},{16,24},{24,16},{1,9},{9,1},{17,25},{25,17},{2,10},{10... | collective-permute-start | bytes 2359304 | tf_op jit(solution)/shard_map/ppermute | solution.py:90
  37.5 11.2 %collective-permute-start.10 = (bf16[256,512]{1,0:T(8,128)(2,1)}, bf16[256,512]{1,0:T(8,128)(2,1)S(1)}, u32[]{:S(2)}, u32[]{:S(2)}) collective-permute-start(bf16[256,512]{1,0:T(8,128)(2,1)} %collective-permute-done.9), channel_id=1, source_target_pairs={{2,0},{4,6},{3,1},{5,7},{10,8},{12,14},{11,9},{13,15},{18,16},{20,... | collective-permute-start | bytes 786440 | tf_op jit(solution)/shard_map/ppermute | solution.py:113
  41.2 10.3 %collective-permute-start.8 = (bf16[256,512]{1,0:T(8,128)(2,1)}, bf16[256,512]{1,0:T(8,128)(2,1)S(1)}, u32[]{:S(2)}, u32[]{:S(2)}) collective-permute-start(bf16[256,512]{1,0:T(8,128)(2,1)} %collective-permute-done.7), channel_id=1, source_target_pairs={{2,0},{4,6},{3,1},{5,7},{10,8},{12,14},{11,9},{13,15},{18,16},{20,... | collective-permute-start | bytes 786440 | tf_op jit(solution)/shard_map/ppermute | solution.py:115
  44.7 8.2 %copy-start.10 = (bf16[1024,1536]{1,0:T(8,128)(2,1)S(1)}, bf16[1024,1536]{1,0:T(8,128)(2,1)}, u32[]{:S(2)}) copy-start(bf16[1024,1536]{1,0:T(8,128)(2,1)} %get-tuple-element.33) | copy-start | bytes 9437188
  44.8 8.2 %copy-start.9 = (bf16[512,1536]{1,0:T(8,128)(2,1)S(1)}, bf16[512,1536]{1,0:T(8,128)(2,1)}, u32[]{:S(2)}) copy-start(bf16[512,1536]{1,0:T(8,128)(2,1)} %get-tuple-element.34) | copy-start | bytes 4718596
  48.7 16.4 %collective-permute-start.5 = (bf16[256,1024]{1,0:T(8,128)(2,1)S(1)}, bf16[256,1024]{1,0:T(8,128)(2,1)S(1)}, u32[]{:S(2)}, u32[]{:S(2)}) collective-permute-start(bf16[256,1024]{1,0:T(8,128)(2,1)S(1)} %pad_maximum_fusion.6), channel_id=1, source_target_pairs={{0,16},{8,24},{16,0},{24,8},{1,17},{9,25},{17,1},{25,9},{2,18},{10... | collective-permute-start | bytes 1572872 | tf_op jit(solution)/shard_map/ppermute | solution.py:90
  52.7 2.1 %copy-start.6 = (bf16[1024,1536]{1,0:T(8,128)(2,1)S(1)}, bf16[1024,1536]{1,0:T(8,128)(2,1)}, u32[]{:S(2)}) copy-start(bf16[1024,1536]{1,0:T(8,128)(2,1)} %param.9) | copy-start | bytes 9437188
  52.8 16.3 %collective-permute-start.11 = (bf16[256,1024]{1,0:T(8,128)(2,1)S(1)}, bf16[256,1024]{1,0:T(8,128)(2,1)S(1)}, u32[]{:S(2)}, u32[]{:S(2)}) collective-permute-start(bf16[256,1024]{1,0:T(8,128)(2,1)S(1)} %pad_maximum_fusion.7), channel_id=1, source_target_pairs={{0,16},{8,24},{16,0},{24,8},{1,17},{9,25},{17,1},{25,9},{2,18},{10... | collective-permute-start | bytes 1572872 | tf_op jit(solution)/shard_map/ppermute | solution.py:90
  54.4 65.5 %collective-permute-start.31 = (bf16[512,1536]{1,0:T(8,128)(2,1)S(1)}, bf16[512,1536]{1,0:T(8,128)(2,1)S(1)}, u32[]{:S(2)}, u32[]{:S(2)}) collective-permute-start(bf16[512,1536]{1,0:T(8,128)(2,1)S(1)} %get-tuple-element.32), channel_id=1, source_target_pairs={{0,1},{1,0},{2,3},{3,2},{4,5},{5,4},{6,7},{7,6},{8,9},{9,8},{10,11... | collective-permute-start | bytes 4718600 | tf_op jit(solution)/shard_map/ppermute | solution.py:90
  56.9 8.3 %copy-start.2 = (bf16[512,512]{1,0:T(8,128)(2,1)}, bf16[512,512]{1,0:T(8,128)(2,1)S(1)}, u32[]{:S(2)}) copy-start(bf16[512,512]{1,0:T(8,128)(2,1)S(1)} %convolution_convert_fusion.6) | copy-start | bytes 1572868
  56.9 25.2 %collective-permute-start.13 = (bf16[256,1536]{1,0:T(8,128)(2,1)S(1)}, bf16[256,1536]{1,0:T(8,128)(2,1)S(1)}, u32[]{:S(2)}, u32[]{:S(2)}) collective-permute-start(bf16[256,1536]{1,0:T(8,128)(2,1)S(1)} %collective-permute-done.12), channel_id=1, source_target_pairs={{0,1},{1,0},{2,3},{3,2},{4,5},{5,4},{6,7},{7,6},{8,9},{9,8},{10,11... | collective-permute-start | bytes 2359304 | tf_op jit(solution)/shard_map/ppermute | solution.py:90
  65.0 18.9 %collective-permute-start.15 = (bf16[256,1536]{1,0:T(8,128)(2,1)S(1)}, bf16[256,1536]{1,0:T(8,128)(2,1)S(1)}, u32[]{:S(2)}, u32[]{:S(2)}) collective-permute-start(bf16[256,1536]{1,0:T(8,128)(2,1)S(1)} %collective-permute-done.14), channel_id=1, source_target_pairs={{0,1},{1,0},{2,3},{3,2},{4,5},{5,4},{6,7},{7,6},{8,9},{9,8},{10,11... | collective-permute-start | bytes 2359304 | tf_op jit(solution)/shard_map/ppermute | solution.py:90
  65.2 24.6 %collective-permute-start.30 = (bf16[512,512]{1,0:T(8,128)(2,1)S(1)}, bf16[512,512]{1,0:T(8,128)(2,1)S(1)}, u32[]{:S(2)}, u32[]{:S(2)}) collective-permute-start(bf16[512,512]{1,0:T(8,128)(2,1)S(1)} %pad_maximum_fusion.10), channel_id=1, source_target_pairs={{0,1},{1,0},{2,3},{3,2},{4,5},{5,4},{6,7},{7,6},{8,9},{9,8},{10,11... | collective-permute-start | bytes 1572872 | tf_op jit(solution)/shard_map/ppermute | solution.py:90
  82.0 31.4 %collective-permute-start.34 = (bf16[512,512]{1,0:T(8,128)(2,1)S(1)}, bf16[512,512]{1,0:T(8,128)(2,1)S(1)}, u32[]{:S(2)}, u32[]{:S(2)}) collective-permute-start(bf16[512,512]{1,0:T(8,128)(2,1)S(1)} %pad_maximum_fusion.11), channel_id=1, source_target_pairs={{0,1},{1,0},{2,3},{3,2},{4,5},{5,4},{6,7},{7,6},{8,9},{9,8},{10,11... | collective-permute-start | bytes 1572872 | tf_op jit(solution)/shard_map/ppermute | solution.py:90
  83.9 14.8 %collective-permute-start.24 = (bf16[256,1024]{1,0:T(8,128)(2,1)S(1)}, bf16[256,1024]{1,0:T(8,128)(2,1)S(1)}, u32[]{:S(2)}, u32[]{:S(2)}) collective-permute-start(bf16[256,1024]{1,0:T(8,128)(2,1)S(1)} %pad_maximum_fusion.9), channel_id=1, source_target_pairs={{0,16},{8,24},{16,0},{24,8},{1,17},{9,25},{17,1},{25,9},{2,18},{10... | collective-permute-start | bytes 1572872 | tf_op jit(solution)/shard_map/ppermute | solution.py:90
  84.6 1.1 slice-start
  84.6 3.2 %copy-start.1 = (bf16[512,1536]{1,0:T(8,128)(2,1)S(1)}, bf16[512,1536]{1,0:T(8,128)(2,1)}, u32[]{:S(2)}) copy-start(bf16[512,1536]{1,0:T(8,128)(2,1)} %copy-done) | copy-start | bytes 4718596
  85.7 12.9 %copy-start.5 = (bf16[512,512]{1,0:T(8,128)(2,1)S(1)}, bf16[512,512]{1,0:T(8,128)(2,1)}, u32[]{:S(2)}) copy-start(bf16[512,512]{1,0:T(8,128)(2,1)} %copy-done.4) | copy-start | bytes 1572868
  85.7 24.2 %collective-permute-start.18 = (bf16[256,1024]{1,0:T(8,128)(2,1)S(1)}, bf16[256,1024]{1,0:T(8,128)(2,1)S(1)}, u32[]{:S(2)}, u32[]{:S(2)}) collective-permute-start(bf16[256,1024]{1,0:T(8,128)(2,1)S(1)} %pad_maximum_fusion.8), channel_id=1, source_target_pairs={{0,16},{8,24},{16,0},{24,8},{1,17},{9,25},{17,1},{25,9},{2,18},{10... | collective-permute-start | bytes 1572872 | tf_op jit(solution)/shard_map/ppermute | solution.py:90
  89.8 20.1 %copy-start.3 = (bf16[512,512]{1,0:T(8,128)(2,1)S(1)}, bf16[512,512]{1,0:T(8,128)(2,1)}, u32[]{:S(2)}) copy-start(bf16[512,512]{1,0:T(8,128)(2,1)} %copy-done.2) | copy-start | bytes 1572868
  89.9 39.9 %collective-permute-start.16 = (bf16[256,1536]{1,0:T(8,128)(2,1)S(1)}, bf16[256,1536]{1,0:T(8,128)(2,1)S(1)}, u32[]{:S(2)}, u32[]{:S(2)}) collective-permute-start(bf16[256,1536]{1,0:T(8,128)(2,1)S(1)} %convolution_convert_fusion.2), channel_id=1, source_target_pairs={{0,16},{8,24},{16,0},{24,8},{1,17},{9,25},{17,1},{25,9},{2,18},{10... | collective-permute-start | bytes 2359304 | tf_op jit(solution)/shard_map/ppermute | solution.py:90
  98.7 14.7 %collective-permute-start.25 = (bf16[256,512]{1,0:T(8,128)(2,1)S(1)}, bf16[256,512]{1,0:T(8,128)(2,1)S(1)}, u32[]{:S(2)}, u32[]{:S(2)}) collective-permute-start(bf16[256,512]{1,0:T(8,128)(2,1)S(1)} %broadcast_select_fusion.20), channel_id=1, source_target_pairs={{0,2},{6,4},{1,3},{7,5},{8,10},{14,12},{9,11},{15,13},{16,18},{22,... | collective-permute-start | bytes 786440 | tf_op jit(solution)/shard_map/ppermute | solution.py:124
  109.9 9.1 %collective-permute-start.19 = (bf16[256,512]{1,0:T(8,128)(2,1)S(1)}, bf16[256,512]{1,0:T(8,128)(2,1)S(1)}, u32[]{:S(2)}, u32[]{:S(2)}) collective-permute-start(bf16[256,512]{1,0:T(8,128)(2,1)S(1)} %broadcast_select_fusion.21), channel_id=1, source_target_pairs={{0,2},{6,4},{1,3},{7,5},{8,10},{14,12},{9,11},{15,13},{16,18},{22,... | collective-permute-start | bytes 786440 | tf_op jit(solution)/shard_map/ppermute | solution.py:124
  113.6 21.4 %collective-permute-start.26 = (bf16[256,512]{1,0:T(8,128)(2,1)S(1)}, bf16[256,512]{1,0:T(8,128)(2,1)S(1)}, u32[]{:S(2)}, u32[]{:S(2)}) collective-permute-start(bf16[256,512]{1,0:T(8,128)(2,1)S(1)} %add_convert_fusion.4), channel_id=1, source_target_pairs={{2,4},{4,2},{3,5},{5,3},{10,12},{12,10},{11,13},{13,11},{18,20},{2... | collective-permute-start | bytes 786440 | tf_op jit(solution)/shard_map/ppermute | solution.py:127
  114.3 21.5 %collective-permute-start.28 = (bf16[256,512]{1,0:T(8,128)(2,1)S(1)}, bf16[256,512]{1,0:T(8,128)(2,1)S(1)}, u32[]{:S(2)}, u32[]{:S(2)}) collective-permute-start(bf16[256,512]{1,0:T(8,128)(2,1)S(1)} %add_convert_fusion.4), channel_id=1, source_target_pairs={{0,2},{6,4},{1,3},{7,5},{8,10},{14,12},{9,11},{15,13},{16,18},{22,... | collective-permute-start | bytes 786440 | tf_op jit(solution)/shard_map/ppermute | solution.py:126
  119.2 16.8 %collective-permute-start.20 = (bf16[256,512]{1,0:T(8,128)(2,1)S(1)}, bf16[256,512]{1,0:T(8,128)(2,1)S(1)}, u32[]{:S(2)}, u32[]{:S(2)}) collective-permute-start(bf16[256,512]{1,0:T(8,128)(2,1)S(1)} %add_convert_fusion.8), channel_id=1, source_target_pairs={{2,4},{4,2},{3,5},{5,3},{10,12},{12,10},{11,13},{13,11},{18,20},{2... | collective-permute-start | bytes 786440 | tf_op jit(solution)/shard_map/ppermute | solution.py:127
  119.9 17.7 %collective-permute-start.22 = (bf16[256,512]{1,0:T(8,128)(2,1)S(1)}, bf16[256,512]{1,0:T(8,128)(2,1)S(1)}, u32[]{:S(2)}, u32[]{:S(2)}) collective-permute-start(bf16[256,512]{1,0:T(8,128)(2,1)S(1)} %add_convert_fusion.8), channel_id=1, source_target_pairs={{0,2},{6,4},{1,3},{7,5},{8,10},{14,12},{9,11},{15,13},{16,18},{22,... | collective-permute-start | bytes 786440 | tf_op jit(solution)/shard_map/ppermute | solution.py:126
  129.7 20.5 %collective-permute-start.32 = (bf16[256,1536]{1,0:T(8,128)(2,1)S(1)}, bf16[256,1536]{1,0:T(8,128)(2,1)S(1)}, u32[]{:S(2)}, u32[]{:S(2)}) collective-permute-start(bf16[256,1536]{1,0:T(8,128)(2,1)S(1)} %convolution_convert_fusion.1), channel_id=1, source_target_pairs={{0,8},{8,0},{16,24},{24,16},{1,9},{9,1},{17,25},{25,17},{2,10},{10... | collective-permute-start | bytes 2359304 | tf_op jit(solution)/shard_map/ppermute | solution.py:90
  135.0 27.3 %collective-permute-start.35 = (bf16[256,1536]{1,0:T(8,128)(2,1)S(1)}, bf16[256,1536]{1,0:T(8,128)(2,1)S(1)}, u32[]{:S(2)}, u32[]{:S(2)}) collective-permute-start(bf16[256,1536]{1,0:T(8,128)(2,1)S(1)} %convolution_convert_fusion), channel_id=1, source_target_pairs={{0,8},{8,0},{16,24},{24,16},{1,9},{9,1},{17,25},{25,17},{2,10},{10... | collective-permute-start | bytes 2359304 | tf_op jit(solution)/shard_map/ppermute | solution.py:90
  135.8 27.5 %collective-permute-start.27 = (bf16[256,512]{1,0:T(8,128)(2,1)S(1)}, bf16[256,512]{1,0:T(8,128)(2,1)S(1)}, u32[]{:S(2)}, u32[]{:S(2)}) collective-permute-start(bf16[256,512]{1,0:T(8,128)(2,1)S(1)} %add_convert_fusion.3), channel_id=1, source_target_pairs={{0,2},{2,0},{4,6},{6,4},{1,3},{3,1},{5,7},{7,5},{8,10},{10,8},{12,... | collective-permute-start | bytes 786440 | tf_op jit(solution)/shard_map/ppermute | solution.py:90
  136.0 28.0 %collective-permute-start.29 = (bf16[256,512]{1,0:T(8,128)(2,1)S(1)}, bf16[256,512]{1,0:T(8,128)(2,1)S(1)}, u32[]{:S(2)}, u32[]{:S(2)}) collective-permute-start(bf16[256,512]{1,0:T(8,128)(2,1)S(1)} %add_convert_fusion.2), channel_id=1, source_target_pairs={{2,4},{4,2},{3,5},{5,3},{10,12},{12,10},{11,13},{13,11},{18,20},{2... | collective-permute-start | bytes 786440 | tf_op jit(solution)/shard_map/ppermute | solution.py:129
  137.6 31.7 %collective-permute-start.21 = (bf16[256,512]{1,0:T(8,128)(2,1)}, bf16[256,512]{1,0:T(8,128)(2,1)S(1)}, u32[]{:S(2)}, u32[]{:S(2)}) collective-permute-start(bf16[256,512]{1,0:T(8,128)(2,1)} %add_convert_fusion.7), channel_id=1, source_target_pairs={{0,2},{2,0},{4,6},{6,4},{1,3},{3,1},{5,7},{7,5},{8,10},{10,8},{12,... | collective-permute-start | bytes 786440 | tf_op jit(solution)/shard_map/ppermute | solution.py:90
  150.3 19.0 %collective-permute-start.23 = (bf16[256,512]{1,0:T(8,128)(2,1)}, bf16[256,512]{1,0:T(8,128)(2,1)}, u32[]{:S(2)}, u32[]{:S(2)}) collective-permute-start(bf16[256,512]{1,0:T(8,128)(2,1)} %add_convert_fusion.6), channel_id=1, source_target_pairs={{2,4},{4,2},{3,5},{5,3},{10,12},{12,10},{11,13},{13,11},{18,20},{2... | collective-permute-start | bytes 786440 | tf_op jit(solution)/shard_map/ppermute | solution.py:129
  162.3 13.1 %collective-permute-start.33 = (bf16[256,1536]{1,0:T(8,128)(2,1)S(1)}, bf16[256,1536]{1,0:T(8,128)(2,1)}, u32[]{:S(2)}, u32[]{:S(2)}) collective-permute-start(bf16[256,1536]{1,0:T(8,128)(2,1)S(1)} %fusion.3), channel_id=1, source_target_pairs={{0,1},{1,0},{2,3},{3,2},{4,5},{5,4},{6,7},{7,6},{8,9},{9,8},{10,11... | collective-permute-start | bytes 2359304 | tf_op jit(solution)/shard_map/ppermute | solution.py:90
  163.4 13.9 %collective-permute-start.36 = (bf16[256,1536]{1,0:T(8,128)(2,1)S(1)}, bf16[256,1536]{1,0:T(8,128)(2,1)}, u32[]{:S(2)}, u32[]{:S(2)}) collective-permute-start(bf16[256,1536]{1,0:T(8,128)(2,1)S(1)} %fusion.2), channel_id=1, source_target_pairs={{0,1},{1,0},{2,3},{3,2},{4,5},{5,4},{6,7},{7,6},{8,9},{9,8},{10,11... | collective-permute-start | bytes 2359304 | tf_op jit(solution)/shard_map/ppermute | solution.py:90
  (2 other events, 2.1 us)

commit v2 on v0

v2 whole, which is shorter than its diff:
```python
import functools

import jax
import jax.numpy as jnp
from jax import lax
from jax.experimental import pallas as pl
from jax.experimental.pallas import tpu as pltpu
from jax.sharding import PartitionSpec as P

HSZ = 128
PATCH = 256
SCALE = HSZ ** (-0.5)
BF16, F32 = jnp.bfloat16, jnp.float32

NN = (((1,), (0,)), ((), ()))
NT = (((1,), (1,)), ((), ()))
TN = (((0,), (0,)), ((), ()))
VMEM = pl.BlockSpec(memory_space=pltpu.VMEM)
ANY = pl.BlockSpec(memory_space=pl.ANY)
HBM = pl.BlockSpec(memory_space=pltpu.HBM)
PARAMS = pltpu.CompilerParams(vmem_limit_bytes=40 * 2**20)


def dot(a, b, dims=NN):
    return lax.dot_general(a, b, dims, preferred_element_type=F32)


def cost(macs, moved, exps=0):
    return pl.CostEstimate(flops=2 * macs, bytes_accessed=moved, transcendentals=exps)


def like(shape, dtype=BF16):
    return jax.ShapeDtypeStruct(shape, dtype)


def call(kernel, arrays, in_specs, after, prefetch=0, **options):
    n = len(arrays)

    def body(*refs):
        kernel(*refs[:n], *refs[n + len(after) :])

    in_specs = list(in_specs) + [ANY] * len(after)
    if prefetch:
        options["grid_spec"] = pltpu.PrefetchScalarGridSpec(
            num_scalar_prefetch=prefetch,
            grid=options.pop("grid"),
            in_specs=in_specs,
            out_specs=options.pop("out_specs"),
        )
    else:
        options["in_specs"] = in_specs
    return pl.pallas_call(body, compiler_params=PARAMS, **options)(*arrays, *after)


def position():
    z = lax.axis_index("col")
    return lax.axis_index("row") ^ z, lax.axis_index("rep"), lax.rem(z, 3) == 0


def tie(x, after):
    return call(
        lambda *refs: None,
        (x,),
        [ANY],
        after,
        out_specs=ANY,
        out_shape=like(x.shape, x.dtype),
        input_output_aliases={0: 0},
        cost_estimate=cost(0, 0),
        name="tie",
    )


def plus_kernel(a_ref, b_ref, out_ref):
    out_ref[...] = (a_ref[...].astype(F32) + b_ref[...].astype(F32)).astype(out_ref.dtype)


def plus(a, b, after=()):
    spec = pl.BlockSpec(a.shape, lambda i: (0, 0))
    return call(
        plus_kernel,
        (a, b),
        [spec] * 2,
        after,
        grid=(1,),
        out_specs=spec,
        out_shape=like(a.shape),
        cost_estimate=cost(0, 6 * a.size),
        name="plus",
    )


def copies(pairs, sems):
    started = [pltpu.make_async_copy(a, b, sems.at[i]) for i, (a, b) in enumerate(pairs)]
    for copy in started:
        copy.start()
    return started


def softmax_t(q, k):
    scores = dot(k, q, NT)
    lifted = jnp.exp((scores - jnp.max(scores, axis=0, keepdims=True)) * SCALE)
    return lifted * (1.0 / jnp.sum(lifted, axis=0, keepdims=True))


def forward_kernel(q_ref, k_ref, v_ref, o_ref):
    for lo in range(0, q_ref.shape[1], HSZ):
        cols = slice(lo, lo + HSZ)
        prob = softmax_t(q_ref[:, cols], k_ref[:, cols]).astype(BF16)
        o_ref[:, cols] = dot(prob, v_ref[:, cols], TN).astype(BF16)


def backward_head(q, k, v, g):
    prob = softmax_t(q, k)
    grad_prob = dot(v, g, NT)
    delta = jnp.sum(prob * grad_prob, axis=0, keepdims=True)
    grad_score = (prob * (grad_prob - delta) * SCALE).astype(BF16)
    return (
        dot(grad_score, k, TN).astype(BF16),
        dot(grad_score, q).astype(BF16),
        dot(prob.astype(BF16), g).astype(BF16),
    )


def backward_kernel(q_ref, k_ref, v_ref, g_ref, *grads):
    for lo in range(0, q_ref.shape[1], HSZ):
        cols = slice(lo, lo + HSZ)
        got = backward_head(q_ref[:, cols], k_ref[:, cols], v_ref[:, cols], g_ref[:, cols])
        for ref, value in zip(grads, got):
            ref[:, cols] = value


def backward_sum_kernel(at, q_ref, k_ref, v_ref, *refs):
    outs, (gq, gk, gv, sems) = refs[-7:-4], refs[-4:]
    for lo in range(0, q_ref.shape[1], HSZ):
        cols = slice(lo, lo + HSZ)
        g = sum(ref[:, cols].astype(F32) for ref in refs[:4]).astype(BF16)
        got = backward_head(q_ref[:, cols], k_ref[:, cols], v_ref[:, cols], g)
        for ref, value in zip((gq, gk, gv), got):
            ref[:, cols] = value
    stores = [(a, out.at[:, pl.ds(at, a.shape[1])]) for a, out in zip((gq, gk, gv), outs)]
    for copy in copies(stores, sems):
        copy.wait()


def head_width(width):
    return (2 if width % (2 * HSZ) == 0 else 1) * HSZ


def attention(q, k, v, at, width, after=()):
    wide = head_width(width)
    spec = pl.BlockSpec((PATCH, wide), lambda i, h: (i, h + at // wide))
    tokens = q.shape[0]
    return call(
        forward_kernel,
        (q, k, v),
        [spec] * 3,
        after,
        grid=(tokens // PATCH, width // wide),
        out_specs=pl.BlockSpec((PATCH, wide), lambda i, h: (i, h)),
        out_shape=like((tokens, width)),
        cost_estimate=cost(2 * tokens * PATCH * width, 8 * tokens * width),
        name="attention",
    )


def attention_grads(q, k, v, g):
    wide = head_width(q.shape[1])
    spec = pl.BlockSpec((PATCH, wide), lambda i, h: (i, h))
    tokens, width = q.shape
    return pl.pallas_call(
        backward_kernel,
        grid=(tokens // PATCH, width // wide),
        in_specs=[spec] * 4,
        out_specs=[spec] * 3,
        out_shape=[like(q.shape)] * 3,
        cost_estimate=cost(5 * tokens * PATCH * width, 14 * tokens * width),
        name="attention_grads",
    )(q, k, v, g)


def attention_grads_sum(q, k, v, terms, h, before, after):
    tokens, width = terms[0].shape
    spec = pl.BlockSpec((tokens, width), lambda i: (0, h))
    part = pl.BlockSpec((tokens, width), lambda i: (0, 0))
    return call(
        functools.partial(backward_sum_kernel, h * width),
        (q, k, v, *terms, *before),
        [spec] * 3 + [part] * 4 + [HBM] * len(before),
        after,
        grid=(1,),
        out_specs=[HBM] * 3,
        out_shape=[like(q.shape)] * 3,
        scratch_shapes=[pltpu.VMEM((tokens, width), BF16)] * 3 + [pltpu.SemaphoreType.DMA((3,))],
        input_output_aliases={7 + i: i for i in range(len(before))},
        cost_estimate=cost(5 * tokens * PATCH * width, 20 * tokens * width),
        name="attention_grads",
    )


def fetch_halves_kernel(weight_ref, *refs):
    outs, sems = refs[:-1], refs[-1]
    half, me = outs[0].shape[0], position()[1]
    for copy in copies(
        [
            (weight_ref.at[pl.ds(pl.multiple_of((2 * h + me) * half, half), half)], out)
            for h, out in enumerate(outs)
        ],
        sems,
    ):
        copy.wait()


def fetch_halves(weight):
    rows, depth = weight.shape
    return call(
        fetch_halves_kernel,
        (weight,),
        [HBM],
        (),
        out_specs=[ANY] * 2,
        out_shape=[like((rows // 4, depth))] * 2,
        scratch_shapes=[pltpu.SemaphoreType.DMA((2,))],
        cost_estimate=cost(0, 2 * rows * depth),
        name="fetch_halves",
    )


def route_heads_kernel(*refs):
    m = position()[0]
    sources, (keep_ref, send_ref, sems) = refs[:4], refs[4:]
    targets = [keep_ref.at[0], keep_ref.at[1], send_ref.at[0], send_ref.at[1]]
    for j, target in enumerate(targets):
        for step, source in enumerate(sources):

            @pl.when((m ^ j) == step)
            def _(target=target, j=j, source=source):
                pltpu.make_async_copy(source, target, sems.at[j]).start()

    for j, target in enumerate(targets):
        pltpu.make_async_copy(sources[0], target, sems.at[j]).wait()


def route_heads(sources, after):
    shape = (2, *sources[0].shape)
    return call(
        route_heads_kernel,
        sources,
        [ANY] * 4,
        after,
        out_specs=[ANY] * 2,
        out_shape=[like(shape)] * 2,
        scratch_shapes=[pltpu.SemaphoreType.DMA((4,))],
        cost_estimate=cost(0, 16 * sources[0].size),
        name="route_heads",
    )


def head_parts_kernel(at, cot_ref, far_ref, mine_ref, other_ref, w_ref, keep_ref, send_ref, w, sems):
    (load,) = copies([(w_ref.at[pl.ds(at, w.shape[0])], w)], sems)
    m, me, _ = position()
    low, half = m & 1, mine_ref.shape[0]
    sides = ((far_ref, send_ref), (cot_ref, keep_ref))
    for source, target in sides:
        for ref, i in ((mine_ref, me), (other_ref, 1 - me)):
            cols = pl.ds(pl.multiple_of(i * half, half), half)
            target[1 - low, :, cols] = dot(source[...], ref[...], NT).astype(BF16)
    load.wait()
    for source, target in sides:
        target[low] = dot(source[...], w[...], NT).astype(BF16)


def head_parts(cot, cot_far, weight, mine, other, h, after):
    tokens, depth = cot.shape
    rows = 2 * mine.shape[0]
    whole = lambda a: pl.BlockSpec(a.shape, lambda i: (0, 0))
    out = pl.BlockSpec((2, tokens, rows), lambda i: (0, 0, 0))
    return call(
        functools.partial(head_parts_kernel, h * rows),
        (cot, cot_far, mine, other, weight),
        [whole(cot)] * 2 + [whole(mine)] * 2 + [HBM],
        after,
        grid=(1,),
        out_specs=[out] * 2,
        out_shape=[like((2, tokens, rows))] * 2,
        scratch_shapes=[pltpu.VMEM((rows, depth), BF16), pltpu.SemaphoreType.DMA((1,))],
        cost_estimate=cost(4 * tokens * depth * rows, 4 * (tokens + rows) * depth + 8 * tokens * rows),
        name="head_parts",
    )


def route_parts_kernel(keep_ref, recv_ref, *refs):
    targets, sems = refs[:4], refs[4]
    m = position()[0]
    for step, target in enumerate(targets):
        for high, source in ((step >> 1, keep_ref), (1 - (step >> 1), recv_ref)):

            @pl.when(m >> 1 == high)
            def _(target=target, step=step, source=source):
                pltpu.make_async_copy(source.at[step & 1], target, sems.at[step]).start()

    for step, target in enumerate(targets):
        pltpu.make_async_copy(keep_ref.at[0], target, sems.at[step]).wait()


def route_parts(keep, recv, after):
    shape = keep.shape[1:]
    return call(
        route_parts_kernel,
        (keep, recv),
        [ANY] * 2,
        after,
        out_specs=[ANY] * 4,
        out_shape=[like(shape)] * 4,
        scratch_shapes=[pltpu.SemaphoreType.DMA((4,))],
        cost_estimate=cost(0, 8 * keep.size),
        name="route_parts",
    )


def weight_parts_kernel(*refs):
    heads, cots, (away_ref, own_ref) = refs[:4], refs[4:8], refs[8:]
    half, me = heads[0].shape[2] // 2, position()[1]
    cols = pl.ds(pl.multiple_of(me * half, half), half)
    for j, target in ((1, away_ref), (0, own_ref)):
        left = jnp.concatenate([ref[j, :, cols] for ref in heads], axis=0)
        right = jnp.concatenate([ref[...] for ref in cots], axis=0)
        target[...] = dot(left, right, TN).astype(target.dtype)


def weight_parts(heads, cots, after):
    _, tokens, rows = heads[0].shape
    depth = cots[0].shape[1]
    wide = depth // 3 if depth % 384 == 0 else depth
    whole = pl.BlockSpec(heads[0].shape, lambda i: (0, 0, 0))
    cot = pl.BlockSpec((tokens, wide), lambda i: (0, i))
    out = pl.BlockSpec((rows // 2, wide), lambda i: (0, i))
    return call(
        weight_parts_kernel,
        (*heads, *cots),
        [whole] * 4 + [cot] * 4,
        after,
        grid=(depth // wide,),
        out_specs=[out] * 2,
        out_shape=[like((rows // 2, depth)), like((rows // 2, depth), F32)],
        cost_estimate=cost(4 * tokens * rows * depth, 16 * tokens * rows + 8 * tokens * depth + 3 * rows * depth),
        name="weight_parts",
    )


def weight_total(own, away, factor, h, before, rows, after):
    half, depth = own.shape

    def kernel(own_ref, away_ref, *refs):
        *_, total_ref, out_ref, own, away, total, sems = refs
        me = position()[1]
        at = pl.multiple_of((2 * h + me) * half, half)
        for copy in copies([(own_ref, own), (away_ref, away)], sems):
            copy.wait()
        total[...] = ((own[...] + away[...].astype(F32)) * factor).astype(BF16)
        for copy in copies([(total, total_ref), (total, out_ref.at[pl.ds(at, half)])], sems):
            copy.wait()

    return call(
        kernel,
        (own, away, *before),
        [ANY] * (2 + len(before)),
        after,
        out_specs=[ANY] * 2,
        out_shape=[like((half, depth)), like((rows, depth))],
        scratch_shapes=[
            pltpu.VMEM((half, depth), F32),
            pltpu.VMEM((half, depth), BF16),
            pltpu.VMEM((half, depth), BF16),
            pltpu.SemaphoreType.DMA((2,)),
        ],
        input_output_aliases={2: 1} if before else {},
        cost_estimate=cost(0, 10 * half * depth),
        name="weight_total",
    )


def weight_fill_kernel(first_ref, second_ref, held_ref, out_ref, sems):
    half, me = first_ref.shape[0], position()[1]
    for copy in copies(
        [
            (ref, out_ref.at[pl.ds(pl.multiple_of((2 * h + 1 - me) * half, half), half)])
            for h, ref in enumerate((first_ref, second_ref))
        ],
        sems,
    ):
        copy.wait()


def weight_fill(first, second, held, after=()):
    return call(
        weight_fill_kernel,
        (first, second, held),
        [ANY] * 3,
        after,
        out_specs=ANY,
        out_shape=like(held.shape),
        scratch_shapes=[pltpu.SemaphoreType.DMA((2,))],
        input_output_aliases={2: 0},
        cost_estimate=cost(0, 8 * first.size),
        name="weight_fill",
    )


def project_kernel(*refs):
    heads, besides, weight_ref, out_ref, weight, total, sems = refs[:2], refs[2:6], *refs[6:]
    (load,) = copies([(weight_ref, weight)], sems)
    me = position()[1]
    rows, half = heads[0].shape[2], besides[0].shape[0]
    for h in (0, 1):
        for ref, at in ((besides[2 * h], me), (besides[2 * h + 1], 1 - me)):
            cols = pl.ds(pl.multiple_of(at * half, half), half)
            term = dot(heads[h][1, :, cols], ref[...])
            total[...] = term if h == 0 and at is me else total[...] + term
    load.wait()
    for h in (0, 1):
        total[...] += dot(heads[h][0], weight[h * rows : (h + 1) * rows, :])
    out_ref[...] = total[...].astype(out_ref.dtype)


def project(heads, weight, besides, dtype, after):
    _, tokens, _ = heads[0].shape
    rows, depth = weight.shape
    whole = lambda a: pl.BlockSpec(a.shape, lambda i: (0,) * a.ndim)
    return call(
        project_kernel,
        (*heads, *besides, weight),
        [whole(a) for a in (*heads, *besides)] + [HBM],
        after,
        grid=(1,),
        out_specs=pl.BlockSpec((tokens, depth), lambda i: (0, 0)),
        out_shape=like((tokens, depth), dtype),
        scratch_shapes=[
            pltpu.VMEM((rows, depth), BF16),
            pltpu.VMEM((tokens, depth), F32),
            pltpu.SemaphoreType.DMA((1,)),
        ],
        cost_estimate=cost(2 * tokens * rows * depth, 4 * (tokens + rows) * depth),
        name="project",
    )


def flip(x, axis, bit):
    return lax.ppermute(x, axis, [(i, i ^ bit) for i in range(lax.axis_size(axis))])


def local_grid(queries, key_vectors, value_vectors, cotangent, out_weight):
    tok_rows, features = queries.shape
    width = features // 2
    factor = float(tok_rows * lax.axis_size("row") * lax.axis_size("rep")) ** (-0.5)
    rows = out_weight.shape[0]

    def grads(terms, h, before, after):
        return attention_grads_sum(queries, key_vectors, value_vectors, terms, h, before, after)

    def parts(h, beside, after):
        return head_parts(cotangent, cot_far, out_weight, *beside, h, after)

    def across(blocks):
        return flip(blocks[3], "col", 3), flip(blocks[1], "col", 1), flip(blocks[2], "col", 2)

    halves = fetch_halves(out_weight)
    cot_far = flip(cotangent, "row", 2)
    mine0, mine1 = [flip(a, "row", 1) for a in halves]
    own0 = attention(queries, key_vectors, value_vectors, 0, width, halves)
    own1 = attention(queries, key_vectors, value_vectors, width, width, [own0])
    three, one, two = across([own0] * 4)

    held0, send_h0 = route_heads((own0, one, two, three), [own1])
    got_h0 = flip(send_h0, "row", 2)
    own1 = tie(own1, [held0])
    three, one, two = across([own1] * 4)
    mine0 = tie(mine0, [cot_far, held0])
    beside0 = (mine0, flip(mine0, "rep", 1))
    held0_core = flip(held0, "rep", 1)
    keep0, send0 = parts(0, beside0, [held0])
    cots = [cotangent, cot_far, flip(cotangent, "rep", 1), flip(tie(cot_far, [held0]), "rep", 1)]

    got_h0 = tie(got_h0, [send0, three, one])
    got0 = flip(tie(send0, [got_h0]), "row", 2)
    mine1 = tie(mine1, [got_h0])
    beside1 = (mine1, flip(mine1, "rep", 1))
    heads0 = [held0, got_h0, held0_core, flip(got_h0, "rep", 1)]
    away0, total0 = weight_parts(heads0, cots, [mine1])
    away0 = flip(away0, "row", 1)
    keep1, send1 = parts(1, beside1, [total0])

    got0 = tie(got0, [send1])
    held1, send_h1 = route_heads((own1, one, two, three), [got0])
    got_h1 = flip(send_h1, "row", 2)
    terms0 = route_parts(keep0, got0, [held1])
    three, one, two = across(terms0)
    held1_core = flip(held1, "rep", 1)

    got_h1 = tie(got_h1, [three, one])
    got1 = flip(tie(send1, [got_h1]), "row", 2)
    heads1 = [held1, got_h1, held1_core, flip(got_h1, "rep", 1)]
    total0, held = weight_total(total0, away0, factor, 0, (), rows, [got_h1])
    total0 = flip(total0, "rep", 1)
    away1, total1 = weight_parts(heads1, cots, [held])
    away1 = flip(away1, "row", 1)
    besides = [*beside0, *beside1]
    sent = project([got_h0, got_h1], out_weight, besides, BF16, [total1])

    got1 = tie(got1, [sent, two])
    terms1 = route_parts(keep1, got1, [sent])
    from_far = flip(tie(sent, [terms1[0]]), "row", 2)
    some = grads((terms0[0], one, two, three), 0, (), [terms1[0]])
    three, one, _ = across(terms1)
    projected = project([held0, held1], out_weight, besides, F32, [some[0]])
    two = flip(tie(terms1[2], [three, one]), "col", 2)

    away1 = tie(away1, [projected, three, one])
    total1, held = weight_total(total1, away1, factor, 1, (held,), rows, [projected])
    grad_weight = weight_fill(total0, flip(total1, "rep", 1), held)
    projected = plus(projected, from_far, [held])
    full = grads((terms1[0], one, two, three), 1, some, [projected])
    return (projected, *full, grad_weight)


def local_any(queries, key_vectors, value_vectors, cotangent, out_weight):
    tok_rows, features = queries.shape
    rows = out_weight.shape[0]
    r = lax.axis_index("row")
    cot = jnp.concatenate([cotangent, flip(cotangent, "row", 2)], axis=0)
    beside = flip(out_weight, "row", 1)

    head_out = attention(queries, key_vectors, value_vectors, 0, features)
    whole = lax.all_gather(head_out, "col", axis=1, tiled=True)
    held = [lax.dynamic_slice_in_dim(whole, (r ^ j) * rows, rows, 1) for j in range(4)]
    sent = flip(jnp.concatenate(held[2:], axis=1), "row", 2)
    own = jnp.concatenate([held[0], sent[:, :rows]], axis=0)
    next_to = jnp.concatenate([held[1], sent[:, rows:]], axis=0)

    part, part_beside = dot(cot, out_weight, NT), dot(cot, beside, NT)
    sent = flip(
        jnp.concatenate([part[tok_rows:], part_beside[tok_rows:]], axis=1).astype(BF16), "row", 2
    ).astype(F32)
    parts = jnp.stack([part[:tok_rows], part_beside[:tok_rows], sent[:, :rows], sent[:, rows:]])
    whole = jnp.concatenate([parts[r ^ j] for j in range(4)], axis=1)
    summed = lax.psum_scatter(whole, "col", scatter_dimension=1, tiled=True)
    grads = attention_grads(queries, key_vectors, value_vectors, summed.astype(BF16))

    factor = float(tok_rows * lax.axis_size("row") * lax.axis_size("rep")) ** (-0.5)
    away = flip(dot(next_to, cot, TN).astype(BF16), "row", 1)
    total = dot(own, cot, TN) + away.astype(F32)
    total = lax.psum(total.astype(BF16), "rep").astype(F32) * factor

    away = dot(own[tok_rows:], out_weight) + dot(next_to[tok_rows:], beside)
    away = flip(away.astype(BF16), "row", 2)
    projected = dot(own[:tok_rows], out_weight) + dot(next_to[:tok_rows], beside)
    projected = projected + away.astype(F32)
    return (projected.astype(BF16), *grads, total.astype(BF16))


def solution(mesh):
    placed = (P(("rep", "row"), "col"),) * 4 + (P("row", "col"),)
    grid = mesh.shape["col"] == 4 and mesh.shape["rep"] == 2
    return jax.shard_map(
        local_grid if grid else local_any,
        mesh=mesh,
        in_specs=placed,
        out_specs=placed,
        check_vma=False,
    )
```

time: 376 us -> 150 us (0.40)
  waiting for transfers between devices: 269 us -> 83.5 us
  matrix products: 40.6 us -> 0 us
  blocking collectives: 37.7 us -> 0 us
  Pallas kernels: 0 us -> 29.5 us
  starting transfers between devices: 0.38 us -> 26.1 us
  between operations: 13.9 us -> 1.18 us
  other arithmetic: 5.42 us -> 0 us
    all_gather x3 -> x0, waiting for transfers between devices: 184 us -> none  [the longest x1 116 us: local(): column_panel = lax.all_gather(out_weight, 'row', axis=0, tiled=True)]
    ppermute x0 -> x32, waiting for transfers between devices: none -> 83.5 us  [flip(): lax.ppermute(x, axis, [(i, i ^ bit) for i in range(lax.axis_size(axis))])]
    reduce_scatter x1 -> x0, waiting for transfers between devices: 68.7 us -> none  [local(): lax.psum_scatter(lax.dot_general(column_panel, cotangent, (((1,), (1,)),...]
    dot_general x8 -> x0, matrix products: 38.4 us -> none  [the longest x1 10.2 us: local(): lax.dot_general(column_panel, cotangent, (((1,), (1,)), ((), ())), prefer...]
    all_to_all x1 -> x0, blocking collectives: 37.7 us -> none  [local(): lax.all_to_all(gathered, 'row', split_axis=1, concat_axis=0, tiled=True)]
    pallas_call x0 -> x32, Pallas kernels: none -> 29.5 us  [call(): pl.pallas_call(body, compiler_params=PARAMS, **options)(*arrays, *after)]
    ppermute x0 -> x32, starting transfers between devices: none -> 26.1 us  [flip(): lax.ppermute(x, axis, [(i, i ^ bit) for i in range(lax.axis_size(axis))])]
    psum x1 -> x0, waiting for transfers between devices: 15.8 us -> none  [local(): lax.psum(partial_value.astype(jnp.bfloat16), 'rep').astype(jnp.float32)]
  transfers between devices with their start and end apart: 5 -> 32, of which waited for: 5 -> 14; matrix products, arithmetic and copies ran while one was open for 8% -> 0% of each run, Pallas kernels for 0% -> 19%
where the time goes in v2:
time: 150 us; the launch traced here: 149 us
  waiting for transfers between devices  83.5 us (56%)
  Pallas kernels  29.5 us (20%)
  starting transfers between devices  26.1 us (17%)
  local copies, waits for them, and re-layouts  8.98 us (6%)
    ppermute x32, waiting for transfers between devices, flip(): lax.ppermute(x, axis, [(i, i ^ bit) for i in range(lax.axis_size(axis))])  83.5 us
    pallas_call x32, Pallas kernels, call(): pl.pallas_call(body, compiler_params=PARAMS, **options)(*arrays, *after)  29.5 us
    ppermute x32, starting transfers between devices, flip(): lax.ppermute(x, axis, [(i, i ^ bit) for i in range(lax.axis_size(axis))])  26.1 us
    unnamed x29, local copies, waits for them, and re-layouts  8.98 us
  transfers between devices with their start and end apart: 32, of which 14 were waited for; matrix products, arithmetic and copies ran while one was open for 0% of the time, Pallas kernels for 19%

profile of v2, /device:TPU:0, one launch (start us, length us, event | category | flops | bytes accessed | tf_op | source)
XLA Modules:
  0.0 149.2 jit_solution(15255181829810260633)
XLA Ops:
  0.6 3.0 %collective-permute-start.6 = (bf16[256,1536]{1,0:T(8,128)(2,1)}, bf16[256,1536]{1,0:T(8,128)(2,1)S(1)}, u32[]{:S(2)}, u32[]{:S(2)}) collective-permute-start(bf16[256,1536]{1,0:T(8,128)(2,1)} %refs_4_.7), channel_id=1, source_target_pairs={{0,16},{8,24},{16,0},{24,8},{1,17},{9,25},{17,1},{25,9},{2,18},{10... | collective-permute-start | bytes 2359304 | tf_op jit(solution)/shard_map/ppermute | solution.py:449
  3.7 1.9 %copy-done = bf16[1024,1536]{1,0:T(8,128)(2,1)S(1)} copy-done((bf16[1024,1536]{1,0:T(8,128)(2,1)S(1)}, bf16[1024,1536]{1,0:T(8,128)(2,1)}, u32[]{:S(2)}) %copy-start) | copy-done | bytes 3145752
  5.7 1.6 %collective-permute-start.7 = (bf16[256,1536]{1,0:T(8,128)(2,1)S(1)}, bf16[256,1536]{1,0:T(8,128)(2,1)S(1)}, u32[]{:S(2)}, u32[]{:S(2)}) collective-permute-start(bf16[256,1536]{1,0:T(8,128)(2,1)S(1)} %get-tuple-element.37.refs_3_), channel_id=1, source_target_pairs={{0,8},{8,0},{16,24},{24,16},{1,9},{9,1},{17,25},{25,17},{2,10},{10... | collective-permute-start | bytes 2359304 | tf_op jit(solution)/shard_map/ppermute | solution.py:449
  7.3 1.9 %attention.2.refs_3_.refs_0_ = bf16[256,512]{1,0:T(8,128)(2,1)S(1)} custom-call(bf16[256,1024]{1,0:T(8,128)(2,1)S(1)} %copy-done.5, bf16[256,1024]{1,0:T(8,128)(2,1)S(1)} %copy-done.6, bf16[256,1024]{1,0:T(8,128)(2,1)S(1)} %copy-done.7, bf16[256,1536]{1,0:T(8,128)(2,1)S(1)} %get-tuple-element.37.refs_3_, bf16[256,1536]{1,0:T(8,128)(2,1)S(1)} %get-tuple-element.38.refs_4_), custom_call_target="tpu_custom_call" | custom-call | flops 134217728 | bytes 1048576 | tf_op jit(solution)/shard_map/attention/pallas_call | solution.py:52
  9.2 3.7 %collective-permute-start.2 = (bf16[256,512]{1,0:T(8,128)(2,1)S(1)}, bf16[256,512]{1,0:T(8,128)(2,1)S(1)}, u32[]{:S(2)}, u32[]{:S(2)}) collective-permute-start(bf16[256,512]{1,0:T(8,128)(2,1)S(1)} %attention.2.refs_3_.refs_0_), channel_id=1, source_target_pairs={{0,6},{2,4},{4,2},{6,0},{1,7},{3,5},{5,3},{7,1},{8,14},{10,12},{12... | collective-permute-start | bytes 786440 | tf_op jit(solution)/shard_map/ppermute | solution.py:449
  12.9 0.8 collective-permute-start
  13.7 1.9 %attention.3.refs_4_.refs_0_ = bf16[256,512]{1,0:T(8,128)(2,1)S(1)} custom-call(bf16[256,1024]{1,0:T(8,128)(2,1)S(1)} %copy-done.5, bf16[256,1024]{1,0:T(8,128)(2,1)S(1)} %copy-done.6, bf16[256,1024]{1,0:T(8,128)(2,1)S(1)} %copy-done.7, bf16[256,512]{1,0:T(8,128)(2,1)S(1)} %attention.2.refs_3_.refs_0_), custom_call_target="tpu_custom_call" | custom-call | flops 134217728 | bytes 1048576 | tf_op jit(solution)/shard_map/attention/pallas_call | solution.py:52
  15.6 4.8 %collective-permute-done.2.refs_3_ = bf16[256,512]{1,0:T(8,128)(2,1)S(1)} collective-permute-done((bf16[256,512]{1,0:T(8,128)(2,1)S(1)}, bf16[256,512]{1,0:T(8,128)(2,1)S(1)}, u32[]{:S(2)}, u32[]{:S(2)}) %collective-permute-start.2) | collective-permute-done | bytes 262176 | tf_op jit(solution)/shard_map/ppermute | solution.py:449
  20.4 14.2 %collective-permute-done.1.refs_2_ = bf16[256,512]{1,0:T(8,128)(2,1)S(1)} collective-permute-done((bf16[256,512]{1,0:T(8,128)(2,1)S(1)}, bf16[256,512]{1,0:T(8,128)(2,1)S(1)}, u32[]{:S(2)}, u32[]{:S(2)}) %collective-permute-start.1) | collective-permute-done | bytes 262176 | tf_op jit(solution)/shard_map/ppermute | solution.py:449
  35.0 1.5 collective-permute-start.11
  36.9 2.5 %collective-permute-start.5 = (bf16[256,512]{1,0:T(8,128)(2,1)S(1)}, bf16[256,512]{1,0:T(8,128)(2,1)S(1)}, u32[]{:S(2)}, u32[]{:S(2)}) collective-permute-start(bf16[256,512]{1,0:T(8,128)(2,1)S(1)} %tie.13.refs_0_), channel_id=1, source_target_pairs={{0,6},{2,4},{4,2},{6,0},{1,7},{3,5},{5,3},{7,1},{8,14},{10,12},{12... | collective-permute-start | bytes 786440 | tf_op jit(solution)/shard_map/ppermute | solution.py:449
  39.5 8.5 %collective-permute-done.5.refs_2_.refs_3_ = bf16[256,512]{1,0:T(8,128)(2,1)S(1)} collective-permute-done((bf16[256,512]{1,0:T(8,128)(2,1)S(1)}, bf16[256,512]{1,0:T(8,128)(2,1)S(1)}, u32[]{:S(2)}, u32[]{:S(2)}) %collective-permute-start.5) | collective-permute-done | bytes 262176 | tf_op jit(solution)/shard_map/ppermute | solution.py:449
  48.0 4.6 %collective-permute-done.3.refs_3_.refs_1_ = bf16[256,512]{1,0:T(8,128)(2,1)S(1)} collective-permute-done((bf16[256,512]{1,0:T(8,128)(2,1)S(1)}, bf16[256,512]{1,0:T(8,128)(2,1)S(1)}, u32[]{:S(2)}, u32[]{:S(2)}) %collective-permute-start.3) | collective-permute-done | bytes 262176 | tf_op jit(solution)/shard_map/ppermute | solution.py:449
  53.1 2.1 %head_parts.2 = (bf16[2,256,512]{2,1,0:T(8,128)(2,1)S(1)}, bf16[2,256,512]{2,1,0:T(8,128)(2,1)S(1)}) custom-call(bf16[256,1536]{1,0:T(8,128)(2,1)S(1)} %copy-done.4, bf16[256,1536]{1,0:T(8,128)(2,1)S(1)} %collective-permute-done.6.refs_1_.refs_5_, bf16[256,1536]{1,0:T(8,128)(2,1)S(1)} %tie.14.refs_2_, bf16[256,1536]{1,0:T(8,128)(2,1)S(1)} %collective-permute-done.8.refs_3_, ...), custom_call_target="tpu_custom_call" | custom-call | flops 1610612736 | bytes 5767168 | tf_op jit(solution)/shard_map/head_parts/pallas_call | solution.py:52
  55.8 1.5 %collective-permute-start.10 = (bf16[2,256,512]{2,1,0:T(8,128)(2,1)S(1)}, bf16[2,256,512]{2,1,0:T(8,128)(2,1)S(1)}, u32[]{:S(2)}, u32[]{:S(2)}) collective-permute-start(bf16[2,256,512]{2,1,0:T(8,128)(2,1)S(1)} %tie.16), channel_id=1, source_target_pairs={{0,16},{8,24},{16,0},{24,8},{1,17},{9,25},{17,1},{25,9},{2,18},{10... | collective-permute-start | bytes 1572872 | tf_op jit(solution)/shard_map/ppermute | solution.py:449
  58.4 2.6 %weight_parts.2 = (bf16[256,1536]{1,0:T(8,128)(2,1)S(1)}, f32[256,1536]{1,0:T(8,128)S(1)}) custom-call(bf16[2,256,512]{2,1,0:T(8,128)(2,1)S(1)} %get-tuple-element.39.refs_1_.refs_2_.refs_5_.refs_0_, bf16[2,256,512]{2,1,0:T(8,128)(2,1)S(1)} %tie.15.refs_1_.refs_0_, bf16[2,256,512]{2,1,0:T(8,128)(2,1)S(1)} %collective-permute-done.13.refs_2_, ...), custom_call_target="tpu_custom_call" | custom-call | flops 1610612736 | bytes 7602176 | tf_op jit(solution)/shard_map/weight_parts/pallas_call | solution.py:52
  61.0 2.5 %head_parts.3 = (bf16[2,256,512]{2,1,0:T(8,128)(2,1)S(1)}, bf16[2,256,512]{2,1,0:T(8,128)(2,1)}) custom-call(bf16[256,1536]{1,0:T(8,128)(2,1)S(1)} %copy-done.4, bf16[256,1536]{1,0:T(8,128)(2,1)S(1)} %collective-permute-done.6.refs_1_.refs_5_, bf16[256,1536]{1,0:T(8,128)(2,1)S(1)} %tie.17.refs_8_.refs_2_.refs_4_, ...), custom_call_target="tpu_custom_call" | custom-call | flops 1610612736 | bytes 5767168 | tf_op jit(solution)/shard_map/head_parts/pallas_call | solution.py:52
  63.5 0.8 copy-done.10
  64.3 5.4 %collective-permute-done.10.refs_0_ = bf16[2,256,512]{2,1,0:T(8,128)(2,1)S(1)} collective-permute-done((bf16[2,256,512]{2,1,0:T(8,128)(2,1)S(1)}, bf16[2,256,512]{2,1,0:T(8,128)(2,1)S(1)}, u32[]{:S(2)}, u32[]{:S(2)}) %collective-permute-start.10) | collective-permute-done | bytes 524320 | tf_op jit(solution)/shard_map/ppermute | solution.py:449
  69.7 2.1 %collective-permute-done.4.refs_2_ = bf16[256,512]{1,0:T(8,128)(2,1)S(1)} collective-permute-done((bf16[256,512]{1,0:T(8,128)(2,1)S(1)}, bf16[256,512]{1,0:T(8,128)(2,1)S(1)}, u32[]{:S(2)}, u32[]{:S(2)}) %collective-permute-start.4) | collective-permute-done | bytes 262176 | tf_op jit(solution)/shard_map/ppermute | solution.py:449
  72.1 0.6 collective-permute-start.20
  72.6 0.8 collective-permute-start.24
  73.6 1.4 collective-permute-start.19
  75.1 11.8 %collective-permute-done.17.refs_2_.refs_4_ = bf16[256,512]{1,0:T(8,128)(2,1)S(1)} collective-permute-done((bf16[256,512]{1,0:T(8,128)(2,1)S(1)}, bf16[256,512]{1,0:T(8,128)(2,1)S(1)}, u32[]{:S(2)}, u32[]{:S(2)}) %collective-permute-start.17) | collective-permute-done | bytes 262176 | tf_op jit(solution)/shard_map/ppermute | solution.py:449
  87.0 1.4 collective-permute-start.21
  88.4 3.4 %collective-permute-done.24.refs_1_ = bf16[256,1536]{1,0:T(8,128)(2,1)S(1)} collective-permute-done((bf16[256,1536]{1,0:T(8,128)(2,1)S(1)}, bf16[256,1536]{1,0:T(8,128)(2,1)S(1)}, u32[]{:S(2)}, u32[]{:S(2)}) %collective-permute-start.24) | collective-permute-done | bytes 786464 | tf_op jit(solution)/shard_map/ppermute | solution.py:449
  91.8 1.3 weight_total.2
  93.1 2.2 %copy-done.2 = bf16[1024,1536]{1,0:T(8,128)(2,1)S(1)} copy-done((bf16[1024,1536]{1,0:T(8,128)(2,1)S(1)}, bf16[1024,1536]{1,0:T(8,128)(2,1)}, u32[]{:S(2)}) %copy-start.2) | copy-done | bytes 3145752
  95.2 3.0 %weight_parts.3 = (bf16[256,1536]{1,0:T(8,128)(2,1)}, f32[256,1536]{1,0:T(8,128)S(1)}) custom-call(bf16[2,256,512]{2,1,0:T(8,128)(2,1)S(1)} %get-tuple-element.44.refs_2_.refs_0_.refs_1_, bf16[2,256,512]{2,1,0:T(8,128)(2,1)S(1)} %tie.20.refs_1_.refs_2_, bf16[2,256,512]{2,1,0:T(8,128)(2,1)S(1)} %collective-permute-done.22.refs_2_, ...), custom_call_target="tpu_custom_call" | custom-call | flops 1610612736 | bytes 7602176 | tf_op jit(solution)/shard_map/weight_parts/pallas_call | solution.py:52
  98.3 0.8 collective-permute-start.26
  99.1 2.1 %project.2.refs_1_.refs_2_.refs_0_ = bf16[256,1536]{1,0:T(8,128)(2,1)S(1)} custom-call(bf16[2,256,512]{2,1,0:T(8,128)(2,1)S(1)} %tie.15.refs_1_.refs_0_, bf16[2,256,512]{2,1,0:T(8,128)(2,1)S(1)} %tie.20.refs_1_.refs_2_, bf16[256,1536]{1,0:T(8,128)(2,1)S(1)} %tie.14.refs_2_, bf16[256,1536]{1,0:T(8,128)(2,1)S(1)} %collective-permute-done.8.refs_3_, ...), custom_call_target="tpu_custom_call" | custom-call | flops 1610612736 | bytes 7864320 | tf_op jit(solution)/shard_map/project/pallas_call | solution.py:52
  101.2 10.9 %collective-permute-done.18.refs_2_.refs_5_ = bf16[256,512]{1,0:T(8,128)(2,1)S(1)} collective-permute-done((bf16[256,512]{1,0:T(8,128)(2,1)S(1)}, bf16[256,512]{1,0:T(8,128)(2,1)S(1)}, u32[]{:S(2)}, u32[]{:S(2)}) %collective-permute-start.18) | collective-permute-done | bytes 262176 | tf_op jit(solution)/shard_map/ppermute | solution.py:449
  112.4 1.6 %collective-permute-start.27 = (bf16[256,512]{1,0:T(8,128)(2,1)S(1)}, bf16[256,512]{1,0:T(8,128)(2,1)S(1)}, u32[]{:S(2)}, u32[]{:S(2)}) collective-permute-start(bf16[256,512]{1,0:T(8,128)(2,1)S(1)} %get-tuple-element.58), channel_id=1, source_target_pairs={{0,6},{2,4},{4,2},{6,0},{1,7},{3,5},{5,3},{7,1},{8,14},{10,12},{12... | collective-permute-start | bytes 786440 | tf_op jit(solution)/shard_map/ppermute | solution.py:449
  114.0 1.4 collective-permute-start.25
  115.4 2.7 %attention_grads.2 = (bf16[256,1024]{1,0:T(8,128)(2,1)}, bf16[256,1024]{1,0:T(8,128)(2,1)}, bf16[256,1024]{1,0:T(8,128)(2,1)}) custom-call(bf16[256,1024]{1,0:T(8,128)(2,1)S(1)} %copy-done.5, bf16[256,1024]{1,0:T(8,128)(2,1)S(1)} %copy-done.6, bf16[256,1024]{1,0:T(8,128)(2,1)S(1)} %copy-done.7, bf16[256,512]{1,0:T(8,128)(2,1)S(1)} %get-tuple-element.46.refs_3_, ...), custom_call_target="tpu_custom_call" | custom-call | flops 335544320 | bytes 2621440 | tf_op jit(solution)/shard_map/attention_grads/pallas_call | solution.py:52
  118.1 1.0 copy-done.9
  119.2 2.1 %project.3.refs_1_.refs_3_.refs_0_ = f32[256,1536]{1,0:T(8,128)S(1)} custom-call(bf16[2,256,512]{2,1,0:T(8,128)(2,1)S(1)} %get-tuple-element.39.refs_1_.refs_2_.refs_5_.refs_0_, bf16[2,256,512]{2,1,0:T(8,128)(2,1)S(1)} %get-tuple-element.44.refs_2_.refs_0_.refs_1_, bf16[256,1536]{1,0:T(8,128)(2,1)S(1)} %tie.14.refs_2_, ...), custom_call_target="tpu_custom_call" | custom-call | flops 1610612736 | bytes 7864320 | tf_op jit(solution)/shard_map/project/pallas_call | solution.py:52
  121.2 2.2 %collective-permute-done.27.refs_2_.refs_1_.refs_6_ = bf16[256,512]{1,0:T(8,128)(2,1)S(1)} collective-permute-done((bf16[256,512]{1,0:T(8,128)(2,1)S(1)}, bf16[256,512]{1,0:T(8,128)(2,1)S(1)}, u32[]{:S(2)}, u32[]{:S(2)}) %collective-permute-start.27) | collective-permute-done | bytes 262176 | tf_op jit(solution)/shard_map/ppermute | solution.py:449
  123.5 4.1 %collective-permute-done.28.refs_3_.refs_2_.refs_4_ = bf16[256,512]{1,0:T(8,128)(2,1)S(1)} collective-permute-done((bf16[256,512]{1,0:T(8,128)(2,1)S(1)}, bf16[256,512]{1,0:T(8,128)(2,1)S(1)}, u32[]{:S(2)}, u32[]{:S(2)}) %collective-permute-start.28) | collective-permute-done | bytes 262176 | tf_op jit(solution)/shard_map/ppermute | solution.py:449
  127.6 1.3 weight_total.3
  129.0 1.2 collective-permute-start.29
  130.2 3.8 %collective-permute-done.25.refs_1_ = bf16[256,1536]{1,0:T(8,128)(2,1)S(1)} collective-permute-done((bf16[256,1536]{1,0:T(8,128)(2,1)S(1)}, bf16[256,1536]{1,0:T(8,128)(2,1)S(1)}, u32[]{:S(2)}, u32[]{:S(2)}) %collective-permute-start.25) | collective-permute-done | bytes 786464 | tf_op jit(solution)/shard_map/ppermute | solution.py:449
  134.0 1.9 %copy-done.3 = bf16[1024,1536]{1,0:T(8,128)(2,1)S(1)} copy-done((bf16[1024,1536]{1,0:T(8,128)(2,1)S(1)}, bf16[1024,1536]{1,0:T(8,128)(2,1)}, u32[]{:S(2)}) %copy-start.3) | copy-done | bytes 3145752
  135.9 1.0 plus.1.refs_10_
  136.9 7.1 %collective-permute-done.29.refs_5_ = bf16[256,512]{1,0:T(8,128)(2,1)S(1)} collective-permute-done((bf16[256,512]{1,0:T(8,128)(2,1)S(1)}, bf16[256,512]{1,0:T(8,128)(2,1)S(1)}, u32[]{:S(2)}, u32[]{:S(2)}) %collective-permute-start.29) | collective-permute-done | bytes 262176 | tf_op jit(solution)/shard_map/ppermute | solution.py:449
  144.0 1.1 copy-done.8
  145.1 2.7 %attention_grads.3 = (bf16[256,1024]{1,0:T(8,128)(2,1)}, bf16[256,1024]{1,0:T(8,128)(2,1)}, bf16[256,1024]{1,0:T(8,128)(2,1)}) custom-call(bf16[256,1024]{1,0:T(8,128)(2,1)S(1)} %copy-done.5, bf16[256,1024]{1,0:T(8,128)(2,1)S(1)} %copy-done.6, bf16[256,1024]{1,0:T(8,128)(2,1)S(1)} %copy-done.7, ...), custom_call_target="tpu_custom_call", output_to_operand_aliasing={{0}: (7, {}), {1}: (8, {}), {2}: (9, {})} | custom-call | flops 335544320 | bytes 2621440 | tf_op jit(solution)/shard_map/attention_grads/pallas_call | solution.py:52
  147.9 1.2 weight_fill.1
  (77 shorter events, 4.0 us)
Async XLA Ops:
  0.6 34.2 %collective-permute-start.6 = (bf16[256,1536]{1,0:T(8,128)(2,1)}, bf16[256,1536]{1,0:T(8,128)(2,1)S(1)}, u32[]{:S(2)}, u32[]{:S(2)}) collective-permute-start(bf16[256,1536]{1,0:T(8,128)(2,1)} %refs_4_.7), channel_id=1, source_target_pairs={{0,16},{8,24},{16,0},{24,8},{1,17},{9,25},{17,1},{25,9},{2,18},{10... | collective-permute-start | bytes 2359304 | tf_op jit(solution)/shard_map/ppermute | solution.py:449
  3.7 1.9 %copy-start = (bf16[1024,1536]{1,0:T(8,128)(2,1)S(1)}, bf16[1024,1536]{1,0:T(8,128)(2,1)}, u32[]{:S(2)}) copy-start(bf16[1024,1536]{1,0:T(8,128)(2,1)} %refs_6_.3) | copy-start | bytes 9437188
  5.6 1.7 %copy-start.5 = (bf16[256,1024]{1,0:T(8,128)(2,1)S(1)}, bf16[256,1024]{1,0:T(8,128)(2,1)}, u32[]{:S(2)}) copy-start(bf16[256,1024]{1,0:T(8,128)(2,1)} %refs_0_.13) | copy-start | bytes 1572868
  5.6 1.7 %copy-start.6 = (bf16[256,1024]{1,0:T(8,128)(2,1)S(1)}, bf16[256,1024]{1,0:T(8,128)(2,1)}, u32[]{:S(2)}) copy-start(bf16[256,1024]{1,0:T(8,128)(2,1)} %refs_1_.7) | copy-start | bytes 1572868
  5.6 1.7 %copy-start.7 = (bf16[256,1024]{1,0:T(8,128)(2,1)S(1)}, bf16[256,1024]{1,0:T(8,128)(2,1)}, u32[]{:S(2)}) copy-start(bf16[256,1024]{1,0:T(8,128)(2,1)} %refs_2_.7) | copy-start | bytes 1572868
  5.7 29.1 %collective-permute-start.7 = (bf16[256,1536]{1,0:T(8,128)(2,1)S(1)}, bf16[256,1536]{1,0:T(8,128)(2,1)S(1)}, u32[]{:S(2)}, u32[]{:S(2)}) collective-permute-start(bf16[256,1536]{1,0:T(8,128)(2,1)S(1)} %get-tuple-element.37.refs_3_), channel_id=1, source_target_pairs={{0,8},{8,0},{16,24},{24,16},{1,9},{9,1},{17,25},{25,17},{2,10},{10... | collective-permute-start | bytes 2359304 | tf_op jit(solution)/shard_map/ppermute | solution.py:449
  9.2 11.2 %collective-permute-start.2 = (bf16[256,512]{1,0:T(8,128)(2,1)S(1)}, bf16[256,512]{1,0:T(8,128)(2,1)S(1)}, u32[]{:S(2)}, u32[]{:S(2)}) collective-permute-start(bf16[256,512]{1,0:T(8,128)(2,1)S(1)} %attention.2.refs_3_.refs_0_), channel_id=1, source_target_pairs={{0,6},{2,4},{4,2},{6,0},{1,7},{3,5},{5,3},{7,1},{8,14},{10,12},{12... | collective-permute-start | bytes 786440 | tf_op jit(solution)/shard_map/ppermute | solution.py:449
  12.9 21.7 %collective-permute-start.1 = (bf16[256,512]{1,0:T(8,128)(2,1)S(1)}, bf16[256,512]{1,0:T(8,128)(2,1)S(1)}, u32[]{:S(2)}, u32[]{:S(2)}) collective-permute-start(bf16[256,512]{1,0:T(8,128)(2,1)S(1)} %attention.2.refs_3_.refs_0_), channel_id=1, source_target_pairs={{0,4},{2,6},{4,0},{6,2},{1,5},{3,7},{5,1},{7,3},{8,12},{10,14},{12... | collective-permute-start | bytes 786440 | tf_op jit(solution)/shard_map/ppermute | solution.py:449
  12.9 21.7 %collective-permute-start = (bf16[256,512]{1,0:T(8,128)(2,1)S(1)}, bf16[256,512]{1,0:T(8,128)(2,1)S(1)}, u32[]{:S(2)}, u32[]{:S(2)}) collective-permute-start(bf16[256,512]{1,0:T(8,128)(2,1)S(1)} %attention.2.refs_3_.refs_0_), channel_id=1, source_target_pairs={{0,2},{2,0},{4,6},{6,4},{1,3},{3,1},{5,7},{7,5},{8,10},{10,8},{12,... | collective-permute-start | bytes 786440 | tf_op jit(solution)/shard_map/ppermute | solution.py:449
  34.9 13.1 %copy-start.4 = (bf16[256,1536]{1,0:T(8,128)(2,1)S(1)}, bf16[256,1536]{1,0:T(8,128)(2,1)}, u32[]{:S(2)}) copy-start(bf16[256,1536]{1,0:T(8,128)(2,1)} %refs_4_.7) | copy-start | bytes 2359300
  34.9 18.2 %copy-start.1 = (bf16[1024,1536]{1,0:T(8,128)(2,1)S(1)}, bf16[1024,1536]{1,0:T(8,128)(2,1)}, u32[]{:S(2)}) copy-start(bf16[1024,1536]{1,0:T(8,128)(2,1)} %refs_6_.3) | copy-start | bytes 9437188
  34.9 17.7 %collective-permute-start.8 = (bf16[256,1536]{1,0:T(8,128)(2,1)S(1)}, bf16[256,1536]{1,0:T(8,128)(2,1)S(1)}, u32[]{:S(2)}, u32[]{:S(2)}) collective-permute-start(bf16[256,1536]{1,0:T(8,128)(2,1)S(1)} %tie.14.refs_2_), channel_id=1, source_target_pairs={{0,1},{1,0},{2,3},{3,2},{4,5},{5,4},{6,7},{7,6},{8,9},{9,8},{10,11... | collective-permute-start | bytes 2359304 | tf_op jit(solution)/shard_map/ppermute | solution.py:449
  35.0 20.3 %collective-permute-start.11 = (bf16[256,1536]{1,0:T(8,128)(2,1)S(1)}, bf16[256,1536]{1,0:T(8,128)(2,1)S(1)}, u32[]{:S(2)}, u32[]{:S(2)}) collective-permute-start(bf16[256,1536]{1,0:T(8,128)(2,1)S(1)} %get-tuple-element.38.refs_4_), channel_id=1, source_target_pairs={{0,8},{8,0},{16,24},{24,16},{1,9},{9,1},{17,25},{25,17},{2,10},{10... | collective-permute-start | bytes 2359304 | tf_op jit(solution)/shard_map/ppermute | solution.py:449
  36.4 18.8 %collective-permute-start.9 = (bf16[2,256,512]{2,1,0:T(8,128)(2,1)S(1)}, bf16[2,256,512]{2,1,0:T(8,128)(2,1)S(1)}, u32[]{:S(2)}, u32[]{:S(2)}) collective-permute-start(bf16[2,256,512]{2,1,0:T(8,128)(2,1)S(1)} %get-tuple-element.41), channel_id=1, source_target_pairs={{0,16},{8,24},{16,0},{24,8},{1,17},{9,25},{17,1},{25,9},{2,18},{10... | collective-permute-start | bytes 1572872 | tf_op jit(solution)/shard_map/ppermute | solution.py:449
  36.9 11.0 %collective-permute-start.5 = (bf16[256,512]{1,0:T(8,128)(2,1)S(1)}, bf16[256,512]{1,0:T(8,128)(2,1)S(1)}, u32[]{:S(2)}, u32[]{:S(2)}) collective-permute-start(bf16[256,512]{1,0:T(8,128)(2,1)S(1)} %tie.13.refs_0_), channel_id=1, source_target_pairs={{0,6},{2,4},{4,2},{6,0},{1,7},{3,5},{5,3},{7,1},{8,14},{10,12},{12... | collective-permute-start | bytes 786440 | tf_op jit(solution)/shard_map/ppermute | solution.py:449
  39.4 13.1 %collective-permute-start.3 = (bf16[256,512]{1,0:T(8,128)(2,1)S(1)}, bf16[256,512]{1,0:T(8,128)(2,1)S(1)}, u32[]{:S(2)}, u32[]{:S(2)}) collective-permute-start(bf16[256,512]{1,0:T(8,128)(2,1)S(1)} %tie.13.refs_0_), channel_id=1, source_target_pairs={{0,2},{2,0},{4,6},{6,4},{1,3},{3,1},{5,7},{7,5},{8,10},{10,8},{12,... | collective-permute-start | bytes 786440 | tf_op jit(solution)/shard_map/ppermute | solution.py:449
  48.0 9.4 %collective-permute-start.15 = (bf16[256,1536]{1,0:T(8,128)(2,1)S(1)}, bf16[256,1536]{1,0:T(8,128)(2,1)S(1)}, u32[]{:S(2)}, u32[]{:S(2)}) collective-permute-start(bf16[256,1536]{1,0:T(8,128)(2,1)S(1)} %copy-done.4), channel_id=1, source_target_pairs={{0,1},{1,0},{2,3},{3,2},{4,5},{5,4},{6,7},{7,6},{8,9},{9,8},{10,11... | collective-permute-start | bytes 2359304 | tf_op jit(solution)/shard_map/ppermute | solution.py:449
  52.6 3.3 %collective-permute-start.13 = (bf16[2,256,512]{2,1,0:T(8,128)(2,1)S(1)}, bf16[2,256,512]{2,1,0:T(8,128)(2,1)S(1)}, u32[]{:S(2)}, u32[]{:S(2)}) collective-permute-start(bf16[2,256,512]{2,1,0:T(8,128)(2,1)S(1)} %get-tuple-element.39.refs_1_.refs_2_.refs_5_.refs_0_), channel_id=1, source_target_pairs={{0,1},{1,0},{2,3},{3,2},{4,5},{5,4},{6,7},{7,6},{8,9},{9,8},{10,11... | collective-permute-start | bytes 1572872 | tf_op jit(solution)/shard_map/ppermute | solution.py:449
  52.6 5.3 %collective-permute-start.16 = (bf16[256,1536]{1,0:T(8,128)(2,1)S(1)}, bf16[256,1536]{1,0:T(8,128)(2,1)S(1)}, u32[]{:S(2)}, u32[]{:S(2)}) collective-permute-start(bf16[256,1536]{1,0:T(8,128)(2,1)S(1)} %tie.18), channel_id=1, source_target_pairs={{0,1},{1,0},{2,3},{3,2},{4,5},{5,4},{6,7},{7,6},{8,9},{9,8},{10,11... | collective-permute-start | bytes 2359304 | tf_op jit(solution)/shard_map/ppermute | solution.py:449
  55.3 5.7 %collective-permute-start.12 = (bf16[256,1536]{1,0:T(8,128)(2,1)S(1)}, bf16[256,1536]{1,0:T(8,128)(2,1)S(1)}, u32[]{:S(2)}, u32[]{:S(2)}) collective-permute-start(bf16[256,1536]{1,0:T(8,128)(2,1)S(1)} %tie.17.refs_8_.refs_2_.refs_4_), channel_id=1, source_target_pairs={{0,1},{1,0},{2,3},{3,2},{4,5},{5,4},{6,7},{7,6},{8,9},{9,8},{10,11... | collective-permute-start | bytes 2359304 | tf_op jit(solution)/shard_map/ppermute | solution.py:449
  55.3 3.0 %collective-permute-start.14 = (bf16[2,256,512]{2,1,0:T(8,128)(2,1)S(1)}, bf16[2,256,512]{2,1,0:T(8,128)(2,1)S(1)}, u32[]{:S(2)}, u32[]{:S(2)}) collective-permute-start(bf16[2,256,512]{2,1,0:T(8,128)(2,1)S(1)} %tie.15.refs_1_.refs_0_), channel_id=1, source_target_pairs={{0,1},{1,0},{2,3},{3,2},{4,5},{5,4},{6,7},{7,6},{8,9},{9,8},{10,11... | collective-permute-start | bytes 1572872 | tf_op jit(solution)/shard_map/ppermute | solution.py:449
  55.8 13.9 %collective-permute-start.10 = (bf16[2,256,512]{2,1,0:T(8,128)(2,1)S(1)}, bf16[2,256,512]{2,1,0:T(8,128)(2,1)S(1)}, u32[]{:S(2)}, u32[]{:S(2)}) collective-permute-start(bf16[2,256,512]{2,1,0:T(8,128)(2,1)S(1)} %tie.16), channel_id=1, source_target_pairs={{0,16},{8,24},{16,0},{24,8},{1,17},{9,25},{17,1},{25,9},{2,18},{10... | collective-permute-start | bytes 1572872 | tf_op jit(solution)/shard_map/ppermute | solution.py:449
  57.4 14.5 %collective-permute-start.4 = (bf16[256,512]{1,0:T(8,128)(2,1)S(1)}, bf16[256,512]{1,0:T(8,128)(2,1)S(1)}, u32[]{:S(2)}, u32[]{:S(2)}) collective-permute-start(bf16[256,512]{1,0:T(8,128)(2,1)S(1)} %tie.13.refs_0_), channel_id=1, source_target_pairs={{0,4},{2,6},{4,0},{6,2},{1,5},{3,7},{5,1},{7,3},{8,12},{10,14},{12... | collective-permute-start | bytes 786440 | tf_op jit(solution)/shard_map/ppermute | solution.py:449
  63.5 0.8 copy-start.10
  72.1 14.8 %collective-permute-start.20 = (bf16[2,256,512]{2,1,0:T(8,128)(2,1)S(1)}, bf16[2,256,512]{2,1,0:T(8,128)(2,1)S(1)}, u32[]{:S(2)}, u32[]{:S(2)}) collective-permute-start(bf16[2,256,512]{2,1,0:T(8,128)(2,1)S(1)} %get-tuple-element.51), channel_id=1, source_target_pairs={{0,16},{8,24},{16,0},{24,8},{1,17},{9,25},{17,1},{25,9},{2,18},{10... | collective-permute-start | bytes 1572872 | tf_op jit(solution)/shard_map/ppermute | solution.py:449
  72.6 19.1 %collective-permute-start.24 = (bf16[256,1536]{1,0:T(8,128)(2,1)S(1)}, bf16[256,1536]{1,0:T(8,128)(2,1)S(1)}, u32[]{:S(2)}, u32[]{:S(2)}) collective-permute-start(bf16[256,1536]{1,0:T(8,128)(2,1)S(1)} %get-tuple-element.52), channel_id=1, source_target_pairs={{0,8},{8,0},{16,24},{24,16},{1,9},{9,1},{17,25},{25,17},{2,10},{10... | collective-permute-start | bytes 2359304 | tf_op jit(solution)/shard_map/ppermute | solution.py:449
  73.5 13.4 %collective-permute-start.17 = (bf16[256,512]{1,0:T(8,128)(2,1)S(1)}, bf16[256,512]{1,0:T(8,128)(2,1)S(1)}, u32[]{:S(2)}, u32[]{:S(2)}) collective-permute-start(bf16[256,512]{1,0:T(8,128)(2,1)S(1)} %get-tuple-element.47), channel_id=1, source_target_pairs={{0,2},{2,0},{4,6},{6,4},{1,3},{3,1},{5,7},{7,5},{8,10},{10,8},{12,... | collective-permute-start | bytes 786440 | tf_op jit(solution)/shard_map/ppermute | solution.py:449
  73.6 13.3 %collective-permute-start.19 = (bf16[256,512]{1,0:T(8,128)(2,1)S(1)}, bf16[256,512]{1,0:T(8,128)(2,1)S(1)}, u32[]{:S(2)}, u32[]{:S(2)}) collective-permute-start(bf16[256,512]{1,0:T(8,128)(2,1)S(1)} %get-tuple-element.49), channel_id=1, source_target_pairs={{0,6},{2,4},{4,2},{6,0},{1,7},{3,5},{5,3},{7,1},{8,14},{10,12},{12... | collective-permute-start | bytes 786440 | tf_op jit(solution)/shard_map/ppermute | solution.py:449
  75.0 18.0 %collective-permute-start.22 = (bf16[2,256,512]{2,1,0:T(8,128)(2,1)S(1)}, bf16[2,256,512]{2,1,0:T(8,128)(2,1)S(1)}, u32[]{:S(2)}, u32[]{:S(2)}) collective-permute-start(bf16[2,256,512]{2,1,0:T(8,128)(2,1)S(1)} %get-tuple-element.44.refs_2_.refs_0_.refs_1_), channel_id=1, source_target_pairs={{0,1},{1,0},{2,3},{3,2},{4,5},{5,4},{6,7},{7,6},{8,9},{9,8},{10,11... | collective-permute-start | bytes 1572872 | tf_op jit(solution)/shard_map/ppermute | solution.py:449
  86.9 6.2 %collective-permute-start.23 = (bf16[2,256,512]{2,1,0:T(8,128)(2,1)S(1)}, bf16[2,256,512]{2,1,0:T(8,128)(2,1)S(1)}, u32[]{:S(2)}, u32[]{:S(2)}) collective-permute-start(bf16[2,256,512]{2,1,0:T(8,128)(2,1)S(1)} %tie.20.refs_1_.refs_2_), channel_id=1, source_target_pairs={{0,1},{1,0},{2,3},{3,2},{4,5},{5,4},{6,7},{7,6},{8,9},{9,8},{10,11... | collective-permute-start | bytes 1572872 | tf_op jit(solution)/shard_map/ppermute | solution.py:449
  87.0 25.1 %collective-permute-start.21 = (bf16[2,256,512]{2,1,0:T(8,128)(2,1)}, bf16[2,256,512]{2,1,0:T(8,128)(2,1)S(1)}, u32[]{:S(2)}, u32[]{:S(2)}) collective-permute-start(bf16[2,256,512]{2,1,0:T(8,128)(2,1)} %tie.21), channel_id=1, source_target_pairs={{0,16},{8,24},{16,0},{24,8},{1,17},{9,25},{17,1},{25,9},{2,18},{10... | collective-permute-start | bytes 1572872 | tf_op jit(solution)/shard_map/ppermute | solution.py:449
  93.1 5.2 %copy-start.12 = (bf16[256,1536]{1,0:T(8,128)(2,1)}, bf16[256,1536]{1,0:T(8,128)(2,1)S(1)}, u32[]{:S(2)}) copy-start(bf16[256,1536]{1,0:T(8,128)(2,1)S(1)} %get-tuple-element.67) | copy-start | bytes 2359300
  93.1 2.2 %copy-start.2 = (bf16[1024,1536]{1,0:T(8,128)(2,1)S(1)}, bf16[1024,1536]{1,0:T(8,128)(2,1)}, u32[]{:S(2)}) copy-start(bf16[1024,1536]{1,0:T(8,128)(2,1)} %get-tuple-element.53.refs_8_.refs_2_) | copy-start | bytes 9437188
  98.3 29.3 %collective-permute-start.26 = (bf16[256,1536]{1,0:T(8,128)(2,1)}, bf16[256,1536]{1,0:T(8,128)(2,1)S(1)}, u32[]{:S(2)}, u32[]{:S(2)}) collective-permute-start(bf16[256,1536]{1,0:T(8,128)(2,1)} %get-tuple-element.57), channel_id=1, source_target_pairs={{0,8},{8,0},{16,24},{24,16},{1,9},{9,1},{17,25},{25,17},{2,10},{10... | collective-permute-start | bytes 2359304 | tf_op jit(solution)/shard_map/ppermute | solution.py:449
  99.1 12.9 %collective-permute-start.18 = (bf16[256,512]{1,0:T(8,128)(2,1)S(1)}, bf16[256,512]{1,0:T(8,128)(2,1)S(1)}, u32[]{:S(2)}, u32[]{:S(2)}) collective-permute-start(bf16[256,512]{1,0:T(8,128)(2,1)S(1)} %get-tuple-element.48), channel_id=1, source_target_pairs={{0,4},{2,6},{4,0},{6,2},{1,5},{3,7},{5,1},{7,3},{8,12},{10,14},{12... | collective-permute-start | bytes 786440 | tf_op jit(solution)/shard_map/ppermute | solution.py:449
  99.1 12.9 %copy-start.11 = (bf16[2,256,512]{2,1,0:T(8,128)(2,1)S(1)}, bf16[2,256,512]{2,1,0:T(8,128)(2,1)}, u32[]{:S(2)}) copy-start(bf16[2,256,512]{2,1,0:T(8,128)(2,1)} %copy-done.10) | copy-start | bytes 1572868
  101.2 12.8 %copy-start.13 = (bf16[256,1536]{1,0:T(8,128)(2,1)S(1)}, bf16[256,1536]{1,0:T(8,128)(2,1)}, u32[]{:S(2)}) copy-start(bf16[256,1536]{1,0:T(8,128)(2,1)} %copy-done.12) | copy-start | bytes 2359300
  112.4 11.1 %collective-permute-start.27 = (bf16[256,512]{1,0:T(8,128)(2,1)S(1)}, bf16[256,512]{1,0:T(8,128)(2,1)S(1)}, u32[]{:S(2)}, u32[]{:S(2)}) collective-permute-start(bf16[256,512]{1,0:T(8,128)(2,1)S(1)} %get-tuple-element.58), channel_id=1, source_target_pairs={{0,6},{2,4},{4,2},{6,0},{1,7},{3,5},{5,3},{7,1},{8,14},{10,12},{12... | collective-permute-start | bytes 786440 | tf_op jit(solution)/shard_map/ppermute | solution.py:449
  114.0 13.6 %collective-permute-start.28 = (bf16[256,512]{1,0:T(8,128)(2,1)S(1)}, bf16[256,512]{1,0:T(8,128)(2,1)S(1)}, u32[]{:S(2)}, u32[]{:S(2)}) collective-permute-start(bf16[256,512]{1,0:T(8,128)(2,1)S(1)} %get-tuple-element.59), channel_id=1, source_target_pairs={{0,2},{2,0},{4,6},{6,4},{1,3},{3,1},{5,7},{7,5},{8,10},{10,8},{12,... | collective-permute-start | bytes 786440 | tf_op jit(solution)/shard_map/ppermute | solution.py:449
  114.0 33.8 %collective-permute-start.30 = (bf16[256,1536]{1,0:T(8,128)(2,1)S(1)}, bf16[256,1536]{1,0:T(8,128)(2,1)S(1)}, u32[]{:S(2)}, u32[]{:S(2)}) collective-permute-start(bf16[256,1536]{1,0:T(8,128)(2,1)S(1)} %copy-done.13), channel_id=1, source_target_pairs={{0,1},{1,0},{2,3},{3,2},{4,5},{5,4},{6,7},{7,6},{8,9},{9,8},{10,11... | collective-permute-start | bytes 2359304 | tf_op jit(solution)/shard_map/ppermute | solution.py:449
  114.0 20.0 %collective-permute-start.25 = (bf16[256,1536]{1,0:T(8,128)(2,1)S(1)}, bf16[256,1536]{1,0:T(8,128)(2,1)S(1)}, u32[]{:S(2)}, u32[]{:S(2)}) collective-permute-start(bf16[256,1536]{1,0:T(8,128)(2,1)S(1)} %tie.23), channel_id=1, source_target_pairs={{0,16},{8,24},{16,0},{24,8},{1,17},{9,25},{17,1},{25,9},{2,18},{10... | collective-permute-start | bytes 2359304 | tf_op jit(solution)/shard_map/ppermute | solution.py:449
  118.1 1.0 copy-start.9
  128.9 19.0 %collective-permute-start.31 = (bf16[256,1536]{1,0:T(8,128)(2,1)S(1)}, bf16[256,1536]{1,0:T(8,128)(2,1)S(1)}, u32[]{:S(2)}, u32[]{:S(2)}) collective-permute-start(bf16[256,1536]{1,0:T(8,128)(2,1)S(1)} %get-tuple-element.68), channel_id=1, source_target_pairs={{0,1},{1,0},{2,3},{3,2},{4,5},{5,4},{6,7},{7,6},{8,9},{9,8},{10,11... | collective-permute-start | bytes 2359304 | tf_op jit(solution)/shard_map/ppermute | solution.py:449
  129.0 15.0 %collective-permute-start.29 = (bf16[256,512]{1,0:T(8,128)(2,1)S(1)}, bf16[256,512]{1,0:T(8,128)(2,1)S(1)}, u32[]{:S(2)}, u32[]{:S(2)}) collective-permute-start(bf16[256,512]{1,0:T(8,128)(2,1)S(1)} %tie.25), channel_id=1, source_target_pairs={{0,4},{2,6},{4,0},{6,2},{1,5},{3,7},{5,1},{7,3},{8,12},{10,14},{12... | collective-permute-start | bytes 786440 | tf_op jit(solution)/shard_map/ppermute | solution.py:449
  134.0 1.9 %copy-start.3 = (bf16[1024,1536]{1,0:T(8,128)(2,1)S(1)}, bf16[1024,1536]{1,0:T(8,128)(2,1)}, u32[]{:S(2)}) copy-start(bf16[1024,1536]{1,0:T(8,128)(2,1)} %get-tuple-element.60.refs_2_) | copy-start | bytes 9437188
  144.0 1.1 copy-start.8

commit v3 on v2

v3 whole, which is shorter than its diff:
```python
import functools

import jax
import jax.numpy as jnp
from jax import lax
from jax.experimental import pallas as pl
from jax.experimental.pallas import tpu as pltpu
from jax.sharding import PartitionSpec as P

HSZ = 128
PATCH = 256
SCALE = HSZ ** (-0.5)
BF16, F32 = jnp.bfloat16, jnp.float32

NN = (((1,), (0,)), ((), ()))
NT = (((1,), (1,)), ((), ()))
TN = (((0,), (0,)), ((), ()))
VMEM = pl.BlockSpec(memory_space=pltpu.VMEM)
ANY = pl.BlockSpec(memory_space=pl.ANY)
HBM = pl.BlockSpec(memory_space=pltpu.HBM)
PARAMS = pltpu.CompilerParams(vmem_limit_bytes=24 * 2**20)


def dot(a, b, dims=NN):
    return lax.dot_general(a, b, dims, preferred_element_type=F32)


def cost(macs, moved, exps=0):
    return pl.CostEstimate(flops=2 * macs, bytes_accessed=moved, transcendentals=exps)


def like(shape, dtype=BF16):
    return jax.ShapeDtypeStruct(shape, dtype)


def call(kernel, arrays, in_specs, after, out_specs, out_shape, **options):
    n, many = len(arrays), isinstance(out_shape, list)
    shapes, specs = (out_shape, out_specs) if many else ([out_shape], [out_specs])
    first = n + len(after)

    def body(*refs):
        kernel(*refs[:n], *refs[first : first + len(shapes)], *refs[first + len(shapes) + 1 :])

    *outs, mark = pl.pallas_call(
        body,
        in_specs=[*in_specs, *[ANY] * len(after)],
        out_specs=[*specs, ANY],
        out_shape=[*shapes, like((8, 128), F32)],
        compiler_params=PARAMS,
        **options,
    )(*arrays, *after)
    return (outs if many else outs[0]), mark


def tie(x, *after):
    return call(
        lambda *refs: None,
        (x,),
        [ANY],
        after,
        ANY,
        like(x.shape, x.dtype),
        input_output_aliases={0: 0},
        cost_estimate=cost(0, 0),
        name="tie",
    )[0]


def position():
    z = lax.axis_index("col")
    return lax.axis_index("row") ^ z, lax.axis_index("rep"), lax.rem(z, 3) == 0


def plus_kernel(a_ref, b_ref, out_ref):
    out_ref[...] = (a_ref[...].astype(F32) + b_ref[...].astype(F32)).astype(out_ref.dtype)


def plus(a, b, after=()):
    spec = pl.BlockSpec(a.shape, lambda i: (0, 0))
    return call(
        plus_kernel,
        (a, b),
        [spec] * 2,
        after,
        grid=(1,),
        out_specs=spec,
        out_shape=like(a.shape),
        cost_estimate=cost(0, 6 * a.size),
        name="plus",
    )


def copies(pairs, sems):
    started = [pltpu.make_async_copy(a, b, sems.at[i]) for i, (a, b) in enumerate(pairs)]
    for copy in started:
        copy.start()
    return started


def softmax_t(q, k):
    scores = dot(k, q, NT)
    lifted = jnp.exp((scores - jnp.max(scores, axis=0, keepdims=True)) * SCALE)
    return lifted * (1.0 / jnp.sum(lifted, axis=0, keepdims=True))


def forward_kernel(q_ref, k_ref, v_ref, o_ref):
    for lo in range(0, q_ref.shape[1], HSZ):
        cols = slice(lo, lo + HSZ)
        prob = softmax_t(q_ref[:, cols], k_ref[:, cols]).astype(BF16)
        o_ref[:, cols] = dot(prob, v_ref[:, cols], TN).astype(BF16)


def backward_head(q, k, v, g):
    prob = softmax_t(q, k)
    grad_prob = dot(v, g, NT)
    delta = jnp.sum(prob * grad_prob, axis=0, keepdims=True)
    grad_score = (prob * (grad_prob - delta) * SCALE).astype(BF16)
    return (
        dot(grad_score, k, TN).astype(BF16),
        dot(grad_score, q).astype(BF16),
        dot(prob.astype(BF16), g).astype(BF16),
    )


def backward_kernel(q_ref, k_ref, v_ref, g_ref, *grads):
    for lo in range(0, q_ref.shape[1], HSZ):
        cols = slice(lo, lo + HSZ)
        got = backward_head(q_ref[:, cols], k_ref[:, cols], v_ref[:, cols], g_ref[:, cols])
        for ref, value in zip(grads, got):
            ref[:, cols] = value


def backward_sum_kernel(q_ref, k_ref, v_ref, *refs):
    for lo in range(0, q_ref.shape[1], HSZ):
        cols = slice(lo, lo + HSZ)
        g = sum(ref[:, cols].astype(F32) for ref in refs[:-3]).astype(BF16)
        got = backward_head(q_ref[:, cols], k_ref[:, cols], v_ref[:, cols], g)
        for ref, value in zip(refs[-3:], got):
            ref[:, cols] = value


def head_width(width):
    return (2 if width % (2 * HSZ) == 0 else 1) * HSZ


def attention(q, k, v, at, width, after=()):
    wide = head_width(width)
    spec = pl.BlockSpec((PATCH, wide), lambda i, h: (i, h + at // wide))
    tokens = q.shape[0]
    return call(
        forward_kernel,
        (q, k, v),
        [spec] * 3,
        after,
        grid=(tokens // PATCH, width // wide),
        out_specs=pl.BlockSpec((PATCH, wide), lambda i, h: (i, h)),
        out_shape=like((tokens, width)),
        cost_estimate=cost(2 * tokens * PATCH * width, 8 * tokens * width),
        name="attention",
    )


def attention_grads(q, k, v, g):
    wide = head_width(q.shape[1])
    spec = pl.BlockSpec((PATCH, wide), lambda i, h: (i, h))
    tokens, width = q.shape
    return pl.pallas_call(
        backward_kernel,
        grid=(tokens // PATCH, width // wide),
        in_specs=[spec] * 4,
        out_specs=[spec] * 3,
        out_shape=[like(q.shape)] * 3,
        cost_estimate=cost(5 * tokens * PATCH * width, 14 * tokens * width),
        name="attention_grads",
    )(q, k, v, g)


def attention_grads_sum(q, k, v, terms, after):
    tokens, width = q.shape
    wide = head_width(width)
    spec = pl.BlockSpec((PATCH, wide), lambda i, h: (i, h))
    return call(
        backward_sum_kernel,
        (q, k, v, *terms),
        [spec] * (3 + len(terms)),
        after,
        grid=(tokens // PATCH, width // wide),
        out_specs=[spec] * 3,
        out_shape=[like(q.shape)] * 3,
        cost_estimate=cost(5 * tokens * PATCH * width, 18 * tokens * width),
        name="attention_grads",
    )


def fetch_halves_kernel(weight_ref, *refs):
    outs, sems = refs[:-1], refs[-1]
    half, me = outs[0].shape[0], position()[1]
    for copy in copies(
        [
            (weight_ref.at[pl.ds(pl.multiple_of((2 * h + me) * half, half), half)], out)
            for h, out in enumerate(outs)
        ],
        sems,
    ):
        copy.wait()


def fetch_halves(weight, after):
    rows, depth = weight.shape
    return call(
        fetch_halves_kernel,
        (weight,),
        [HBM],
        after,
        out_specs=[ANY] * 2,
        out_shape=[like((rows // 4, depth))] * 2,
        scratch_shapes=[pltpu.SemaphoreType.DMA((2,))],
        cost_estimate=cost(0, 2 * rows * depth),
        name="fetch_halves",
    )


def route_heads_kernel(*refs):
    m, _, outer = position()
    sources, (keep_ref, two_ref, three_ref, sems) = refs[:6], refs[6:]
    steps = ((0, None), (1, None), (2, True), (2, False), (3, True), (3, False))
    targets = [keep_ref.at[0], keep_ref.at[1], two_ref, three_ref]
    for j, target in enumerate(targets):
        for source, (step, at_ends) in zip(sources, steps):
            here = (m ^ j) == step

            @pl.when(here if at_ends is None else here & (outer == at_ends))
            def _(target=target, j=j, source=source):
                pltpu.make_async_copy(source, target, sems.at[j]).start()

    for j, target in enumerate(targets):
        pltpu.make_async_copy(sources[0], target, sems.at[j]).wait()


def route_heads(sources, after):
    shape = sources[0].shape
    return call(
        route_heads_kernel,
        sources,
        [ANY] * 6,
        after,
        out_specs=[ANY] * 3,
        out_shape=[like((2, *shape)), like(shape), like(shape)],
        scratch_shapes=[pltpu.SemaphoreType.DMA((4,))],
        cost_estimate=cost(0, 16 * sources[0].size),
        name="route_heads",
    )


def head_parts_kernel(at, cot_ref, far_ref, mine_ref, other_ref, w_ref, keep_ref, send_ref, w, sems):
    (load,) = copies([(w_ref.at[pl.ds(at, w.shape[0])], w)], sems)
    m, me, _ = position()
    low, half = m & 1, mine_ref.shape[0]
    sides = ((far_ref, send_ref), (cot_ref, keep_ref))
    for source, target in sides:
        for ref, i in ((mine_ref, me), (other_ref, 1 - me)):
            cols = pl.ds(pl.multiple_of(i * half, half), half)
            target[1 - low, :, cols] = dot(source[...], ref[...], NT).astype(BF16)
    load.wait()
    for source, target in sides:
        target[low] = dot(source[...], w[...], NT).astype(BF16)


def head_parts(cot, cot_far, weight, mine, other, h, after):
    tokens, depth = cot.shape
    rows = 2 * mine.shape[0]
    whole = lambda a: pl.BlockSpec(a.shape, lambda i: (0, 0))
    out = pl.BlockSpec((2, tokens, rows), lambda i: (0, 0, 0))
    return call(
        functools.partial(head_parts_kernel, h * rows),
        (cot, cot_far, mine, other, weight),
        [whole(cot)] * 2 + [whole(mine)] * 2 + [HBM],
        after,
        grid=(1,),
        out_specs=[out] * 2,
        out_shape=[like((2, tokens, rows))] * 2,
        scratch_shapes=[pltpu.VMEM((rows, depth), BF16), pltpu.SemaphoreType.DMA((1,))],
        cost_estimate=cost(4 * tokens * depth * rows, 4 * (tokens + rows) * depth + 8 * tokens * rows),
        name="head_parts",
    )


def route_parts_kernel(*refs):
    parts, targets, sems = refs[:4], refs[4:8], refs[8]
    m = position()[0]
    width = parts[0].shape[2]
    views = [target.at[:, pl.ds(h * width, width)] for target in targets for h in (0, 1)]
    for i, view in enumerate(views):
        step, h = i // 2, i % 2
        for high, source in ((step >> 1, parts[2 * h]), (1 - (step >> 1), parts[2 * h + 1])):

            @pl.when(m >> 1 == high)
            def _(view=view, i=i, source=source.at[step & 1]):
                pltpu.make_async_copy(source, view, sems.at[i]).start()

    for i, view in enumerate(views):
        pltpu.make_async_copy(parts[0].at[0], view, sems.at[i]).wait()


def route_parts(parts, after):
    _, tokens, width = parts[0].shape
    return call(
        route_parts_kernel,
        parts,
        [ANY] * 4,
        after,
        out_specs=[ANY] * 4,
        out_shape=[like((tokens, 2 * width))] * 4,
        scratch_shapes=[pltpu.SemaphoreType.DMA((8,))],
        cost_estimate=cost(0, 16 * parts[0].size),
        name="route_parts",
    )


def weight_parts_kernel(*refs):
    heads, cots, out_ref = refs[:4], refs[4:8], refs[8]
    half = out_ref.shape[0]
    cols = pl.ds(pl.multiple_of(position()[1] * half, half), half)
    left = jnp.concatenate([ref.at[0][:, cols] if len(ref.shape) == 3 else ref[:, cols] for ref in heads], axis=0)
    right = jnp.concatenate([ref[...] for ref in cots], axis=0)
    out_ref[...] = dot(left, right, TN).astype(out_ref.dtype)


def weight_parts(j, heads, cots, dtype, after):
    tokens, rows = heads[1].shape
    depth = cots[0].shape[1]
    wide = depth // 3 if depth % 384 == 0 else depth
    pair = pl.BlockSpec((1, tokens, rows), lambda i: (j, 0, 0))
    whole = pl.BlockSpec((tokens, rows), lambda i: (0, 0))
    return call(
        weight_parts_kernel,
        (*heads, *cots),
        [pair, whole] * 2 + [pl.BlockSpec((tokens, wide), lambda i: (0, i))] * 4,
        after,
        grid=(depth // wide,),
        out_specs=pl.BlockSpec((rows // 2, wide), lambda i: (0, i)),
        out_shape=like((rows // 2, depth), dtype),
        cost_estimate=cost(2 * tokens * rows * depth, 8 * tokens * (rows + depth) + rows * depth),
        name="weight_parts",
    )


def weight_total(own, away, factor, rows, after):
    half, depth = own.shape
    cut = half // 2

    def kernel(own_ref, away_ref, total_ref, out_ref, own, away, total, sems):
        at = position()[1] * half
        loads, stores = [], []
        for i in (0, 1):
            part = pl.ds(i * cut, cut)
            loads.append(
                copies([(own_ref.at[part], own.at[part]), (away_ref.at[part], away.at[part])], sems.at[i])
            )
        for i, load in enumerate(loads):
            part = pl.ds(i * cut, cut)
            for copy in load:
                copy.wait()
            total[part] = ((own[part] + away[part].astype(F32)) * factor).astype(BF16)
            place = out_ref.at[pl.ds(pl.multiple_of(at + i * cut, cut), cut)]
            stores += copies([(total.at[part], total_ref.at[part]), (total.at[part], place)], sems.at[2 + i])
        for copy in stores:
            copy.wait()

    return call(
        kernel,
        (own, away),
        [ANY] * 2,
        after,
        out_specs=[ANY] * 2,
        out_shape=[like((half, depth)), like((rows, depth))],
        scratch_shapes=[
            pltpu.VMEM((half, depth), F32),
            pltpu.VMEM((half, depth), BF16),
            pltpu.VMEM((half, depth), BF16),
            pltpu.SemaphoreType.DMA((4, 2)),
        ],
        cost_estimate=cost(0, 10 * half * depth),
        name="weight_total",
    )


def weight_fill_kernel(other_ref, held_ref, out_ref, sems):
    half = other_ref.shape[0]
    at = pl.multiple_of((1 - position()[1]) * half, half)
    for copy in copies([(other_ref, out_ref.at[pl.ds(at, half)])], sems):
        copy.wait()


def weight_fill(other, held, after=()):
    return call(
        weight_fill_kernel,
        (other, held),
        [ANY] * 2,
        after,
        out_specs=ANY,
        out_shape=like(held.shape),
        scratch_shapes=[pltpu.SemaphoreType.DMA((1,))],
        input_output_aliases={1: 0},
        cost_estimate=cost(0, 4 * other.size),
        name="weight_fill",
    )


def project_kernel(own_ref, beside_ref, *refs):
    besides, weight_ref, out_ref, weight, total, sems = refs[:4], *refs[4:]
    (load,) = copies([(weight_ref, weight)], sems)
    me = position()[1]
    half = besides[0].shape[0]
    for i, ref in enumerate(besides):
        at = i // 2 * 2 + (1 - me if i % 2 else me)
        cols = pl.ds(pl.multiple_of(at * half, half), half)
        block = beside_ref[0, :, cols] if len(beside_ref.shape) == 3 else beside_ref[:, cols]
        term = dot(block, ref[...])
        total[...] = term if i == 0 else total[...] + term
    load.wait()
    total[...] += dot(own_ref[0] if len(own_ref.shape) == 3 else own_ref[...], weight[...])
    out_ref[...] = total[...].astype(out_ref.dtype)


def project(heads, weight, besides, dtype, after):
    rows, depth = weight.shape
    tokens = heads[0].shape[-2]
    whole = lambda a: pl.BlockSpec(a.shape, lambda i: (0,) * a.ndim)
    if heads[0].ndim == 3:
        specs = [pl.BlockSpec((1, tokens, rows), lambda i, j=j: (j, 0, 0)) for j in (0, 1)]
    else:
        specs = [whole(a) for a in heads]
    return call(
        project_kernel,
        (*heads, *besides, weight),
        specs + [whole(a) for a in besides] + [HBM],
        after,
        grid=(1,),
        out_specs=pl.BlockSpec((tokens, depth), lambda i: (0, 0)),
        out_shape=like((tokens, depth), dtype),
        scratch_shapes=[
            pltpu.VMEM((rows, depth), BF16),
            pltpu.VMEM((tokens, depth), F32),
            pltpu.SemaphoreType.DMA((1,)),
        ],
        cost_estimate=cost(2 * tokens * rows * depth, 4 * (tokens + rows) * depth),
        name="project",
    )


def flip(x, axis, bit):
    return lax.ppermute(x, axis, [(i, i ^ bit) for i in range(lax.axis_size(axis))])


def line(x, *pairs):
    return lax.ppermute(x, "col", pairs)


def local_grid(queries, key_vectors, value_vectors, cotangent, out_weight):
    tok_rows, features = queries.shape
    width = features // 2
    factor = float(tok_rows * lax.axis_size("row") * lax.axis_size("rep")) ** (-0.5)
    rows = out_weight.shape[0]

    def parts(h, beside, after):
        return head_parts(cotangent, cot_far, out_weight, *beside, h, after)

    own, done = attention(queries, key_vectors, value_vectors, 0, features)
    near, mid = flip(own, "col", 1), line(own, (1, 2), (2, 1))

    (half0, half1), _ = fetch_halves(out_weight, [])
    mine0, mine1 = flip(half0, "row", 1), flip(half1, "row", 1)
    cot_far = flip(cotangent, "row", 2)
    two_out, two_in = line(mid, (1, 0), (2, 3)), line(near, (1, 2), (2, 1))
    mine0 = tie(mine0, near, mid)
    beside0 = mine0, flip(mine0, "rep", 1)
    (keep0, send0), done = parts(0, beside0, [])
    got0 = flip(send0, "row", 2)
    two_in, two_out = tie(two_in, got0), tie(two_out, got0)
    three = line(two_in, (1, 0), (2, 3))
    mine1 = tie(mine1, two_in, two_out)
    beside1 = mine1, flip(mine1, "rep", 1)
    (keep1, send1), done = parts(1, beside1, [])
    got1 = flip(send1, "row", 2)
    (held, away_two, away_three), done = route_heads((own, near, two_out, two_in, three, mid), [done, got0])
    got_three = flip(away_three, "row", 2)

    (p0, p1, p2, p3), done = route_parts((keep0, got0, keep1, got1), [done])
    far = line(p3, (0, 1), (3, 2))
    held_core = flip(held, "rep", 1)
    cots = [cotangent, cot_far, flip(cotangent, "rep", 1), flip(tie(cot_far, done), "rep", 1)]
    got_three = tie(got_three, done)
    second, done = plus(p2, far, [got_three])
    out, cross = line(second, (0, 1), (3, 2)), line(second, (1, 2), (2, 1))
    got_two = flip(tie(away_two, done), "row", 2)
    heads = [held, got_three, held_core, flip(got_three, "rep", 1)]
    away, done = weight_parts(1, heads, cots, BF16, [done])
    away = flip(away, "row", 1)
    near, done = plus(p1, cross, [done])
    mid, done = plus(p3, out, [done])
    near, mid = flip(near, "col", 1), line(mid, (1, 2), (2, 1))

    besides = [*beside0, *beside1]
    sent, done = project([got_two, got_three], out_weight, besides, BF16, [done])
    from_far = flip(sent, "row", 2)
    heads = [held, got_two, held_core, flip(got_two, "rep", 1)]
    total, done = weight_parts(0, heads, cots, F32, [done])
    projected, done = project([held, held], out_weight, besides, F32, [done])
    grads, done = attention_grads_sum(queries, key_vectors, value_vectors, (p0, near, mid), [done])
    projected, done = plus(projected, from_far, [done])
    (total, grad_weight), done = weight_total(total, away, factor, rows, [done])
    grad_weight, _ = weight_fill(flip(total, "rep", 1), grad_weight)
    return (projected, *grads, grad_weight)


def local_any(queries, key_vectors, value_vectors, cotangent, out_weight):
    tok_rows, features = queries.shape
    rows = out_weight.shape[0]
    r = lax.axis_index("row")
    cot = jnp.concatenate([cotangent, flip(cotangent, "row", 2)], axis=0)
    beside = flip(out_weight, "row", 1)

    head_out, _ = attention(queries, key_vectors, value_vectors, 0, features)
    whole = lax.all_gather(head_out, "col", axis=1, tiled=True)
    held = [lax.dynamic_slice_in_dim(whole, (r ^ j) * rows, rows, 1) for j in range(4)]
    sent = flip(jnp.concatenate(held[2:], axis=1), "row", 2)
    own = jnp.concatenate([held[0], sent[:, :rows]], axis=0)
    next_to = jnp.concatenate([held[1], sent[:, rows:]], axis=0)

    part, part_beside = dot(cot, out_weight, NT), dot(cot, beside, NT)
    sent = flip(
        jnp.concatenate([part[tok_rows:], part_beside[tok_rows:]], axis=1).astype(BF16), "row", 2
    ).astype(F32)
    parts = jnp.stack([part[:tok_rows], part_beside[:tok_rows], sent[:, :rows], sent[:, rows:]])
    whole = jnp.concatenate([parts[r ^ j] for j in range(4)], axis=1)
    summed = lax.psum_scatter(whole, "col", scatter_dimension=1, tiled=True)
    grads = attention_grads(queries, key_vectors, value_vectors, summed.astype(BF16))

    factor = float(tok_rows * lax.axis_size("row") * lax.axis_size("rep")) ** (-0.5)
    away = flip(dot(next_to, cot, TN).astype(BF16), "row", 1)
    total = dot(own, cot, TN) + away.astype(F32)
    total = lax.psum(total.astype(BF16), "rep").astype(F32) * factor

    away = dot(own[tok_rows:], out_weight) + dot(next_to[tok_rows:], beside)
    away = flip(away.astype(BF16), "row", 2)
    projected = dot(own[:tok_rows], out_weight) + dot(next_to[:tok_rows], beside)
    projected = projected + away.astype(F32)
    return (projected.astype(BF16), *grads, total.astype(BF16))


def solution(mesh):
    placed = (P(("rep", "row"), "col"),) * 4 + (P("row", "col"),)
    grid = mesh.shape["col"] == 4 and mesh.shape["rep"] == 2
    return jax.shard_map(
        local_grid if grid else local_any,
        mesh=mesh,
        in_specs=placed,
        out_specs=placed,
        check_vma=False,
    )
```

time: 150 us -> 140 us (0.933)
  waiting for transfers between devices: 83.5 us -> 69.9 us
  starting transfers between devices: 26.1 us -> 38.9 us
  local copies, waits for them, and re-layouts: 8.98 us -> 1.96 us
    ppermute x32 -> x19, waiting for transfers between devices: 83.5 us -> 46.6 us  [flip(): lax.ppermute(x, axis, [(i, i ^ bit) for i in range(lax.axis_size(axis))])]
    ppermute x0 -> x8, waiting for transfers between devices: none -> 23.3 us  [line(): return lax.ppermute(x, 'col', pairs)]
    ppermute x0 -> x8, starting transfers between devices: none -> 16 us  [line(): return lax.ppermute(x, 'col', pairs)]
    unnamed x29 -> x13, local copies, waits for them, and re-layouts: 8.98 us -> 1.96 us
    ppermute x32 -> x19, starting transfers between devices: 26.1 us -> 22.9 us  [flip(): lax.ppermute(x, axis, [(i, i ^ bit) for i in range(lax.axis_size(axis))])]
    pallas_call x32 -> x24, Pallas kernels: 29.5 us -> 28.1 us  [call(): pl.pallas_call(body, in_specs=[*in_specs, *[ANY] * len(after)], out_specs...]
  transfers between devices with their start and end apart: 32 -> 27, of which waited for: 14 -> 13; matrix products, arithmetic and copies ran while one was open for 0% -> 0% of each run, Pallas kernels for 19% -> 16%
where the time goes in v3:
time: 140 us
  waiting for transfers between devices  69.9 us (50%)
  starting transfers between devices  38.9 us (28%)
  Pallas kernels  28.1 us (20%)
  local copies, waits for them, and re-layouts  1.96 us (1%)
    ppermute x19, waiting for transfers between devices, flip(): lax.ppermute(x, axis, [(i, i ^ bit) for i in range(lax.axis_size(axis))])  46.6 us
    pallas_call x24, Pallas kernels, call(): pl.pallas_call(body, in_specs=[*in_specs, *[ANY] * len(after)], out_specs...  28.1 us
    ppermute x8, waiting for transfers between devices, line(): return lax.ppermute(x, 'col', pairs)  23.3 us
    ppermute x19, starting transfers between devices, flip(): lax.ppermute(x, axis, [(i, i ^ bit) for i in range(lax.axis_size(axis))])  22.9 us
    ppermute x8, starting transfers between devices, line(): return lax.ppermute(x, 'col', pairs)  16 us
  transfers between devices with their start and end apart: 27, of which 13 were waited for; matrix products, arithmetic and copies ran while one was open for 0% of the time, Pallas kernels for 16%

profile of v3, /device:TPU:0, one launch (start us, length us, event | category | flops | bytes accessed | tf_op | source)
XLA Modules:
  0.0 140.0 jit_solution(16396230801485904482)
XLA Ops:
  0.6 1.9 %copy-done = bf16[1024,1536]{1,0:T(8,128)(2,1)S(1)} copy-done((bf16[1024,1536]{1,0:T(8,128)(2,1)S(1)}, bf16[1024,1536]{1,0:T(8,128)(2,1)}, u32[]{:S(2)}) %copy-start) | copy-done | bytes 3145752
  2.5 0.1 fetch_halves.1
  2.7 3.0 %collective-permute-start.4 = (bf16[256,1536]{1,0:T(8,128)(2,1)S(1)}, bf16[256,1536]{1,0:T(8,128)(2,1)S(1)}, u32[]{:S(2)}, u32[]{:S(2)}) collective-permute-start(bf16[256,1536]{1,0:T(8,128)(2,1)S(1)} %get-tuple-element.53), channel_id=1, source_target_pairs={{0,8},{8,0},{16,24},{24,16},{1,9},{9,1},{17,25},{25,17},{2,10},{10... | collective-permute-start | bytes 2359304 | tf_op jit(solution)/shard_map/ppermute | solution.py:453
  5.7 3.9 %attention.1 = (bf16[256,1024]{1,0:T(8,128)(2,1)S(1)}, f32[8,128]{1,0:T(8,128)}) custom-call(bf16[256,1024]{1,0:T(8,128)(2,1)S(1)} %copy-done.3, bf16[256,1024]{1,0:T(8,128)(2,1)S(1)} %copy-done.4, bf16[256,1024]{1,0:T(8,128)(2,1)S(1)} %copy-done.5), custom_call_target="tpu_custom_call" | custom-call | flops 268435456 | bytes 2097152 | tf_op jit(solution)/shard_map/attention/pallas_call | solution.py:44
  9.6 0.7 collective-permute-start.1
  10.3 4.4 %collective-permute-start = (bf16[256,1024]{1,0:T(8,128)(2,1)S(1)}, bf16[256,1024]{1,0:T(8,128)(2,1)S(1)}, u32[]{:S(2)}, u32[]{:S(2)}) collective-permute-start(bf16[256,1024]{1,0:T(8,128)(2,1)S(1)} %get-tuple-element.52.refs_0_), channel_id=1, source_target_pairs={{0,2},{2,0},{4,6},{6,4},{1,3},{3,1},{5,7},{7,5},{8,10},{10,8},{12,... | collective-permute-start | bytes 1572872 | tf_op jit(solution)/shard_map/ppermute | solution.py:453
  14.7 1.5 %collective-permute-start.3 = (bf16[256,1536]{1,0:T(8,128)(2,1)S(1)}, bf16[256,1536]{1,0:T(8,128)(2,1)S(1)}, u32[]{:S(2)}, u32[]{:S(2)}) collective-permute-start(bf16[256,1536]{1,0:T(8,128)(2,1)S(1)} %copy-done.2), channel_id=1, source_target_pairs={{0,16},{8,24},{16,0},{24,8},{1,17},{9,25},{17,1},{25,9},{2,18},{10... | collective-permute-start | bytes 2359304 | tf_op jit(solution)/shard_map/ppermute | solution.py:453
  16.2 9.8 %collective-permute-done.refs_1_ = bf16[256,1024]{1,0:T(8,128)(2,1)S(1)} collective-permute-done((bf16[256,1024]{1,0:T(8,128)(2,1)S(1)}, bf16[256,1024]{1,0:T(8,128)(2,1)S(1)}, u32[]{:S(2)}, u32[]{:S(2)}) %collective-permute-start) | collective-permute-done | bytes 524320 | tf_op jit(solution)/shard_map/ppermute | solution.py:453
  26.1 1.4 %collective-permute-start.9 = (bf16[256,1536]{1,0:T(8,128)(2,1)S(1)}, bf16[256,1536]{1,0:T(8,128)(2,1)S(1)}, u32[]{:S(2)}, u32[]{:S(2)}) collective-permute-start(bf16[256,1536]{1,0:T(8,128)(2,1)S(1)} %get-tuple-element.58), channel_id=1, source_target_pairs={{0,8},{8,0},{16,24},{24,16},{1,9},{9,1},{17,25},{25,17},{2,10},{10... | collective-permute-start | bytes 2359304 | tf_op jit(solution)/shard_map/ppermute | solution.py:453
  27.5 0.7 collective-permute-start.7
  28.2 4.9 %collective-permute-done.3.refs_1_.refs_5_ = bf16[256,1536]{1,0:T(8,128)(2,1)S(1)} collective-permute-done((bf16[256,1536]{1,0:T(8,128)(2,1)S(1)}, bf16[256,1536]{1,0:T(8,128)(2,1)S(1)}, u32[]{:S(2)}, u32[]{:S(2)}) %collective-permute-start.3) | collective-permute-done | bytes 786464 | tf_op jit(solution)/shard_map/ppermute | solution.py:453
  33.2 2.1 %head_parts.2 = (bf16[2,256,512]{2,1,0:T(8,128)(2,1)S(1)}, bf16[2,256,512]{2,1,0:T(8,128)(2,1)S(1)}, f32[8,128]{1,0:T(8,128)}) custom-call(bf16[256,1536]{1,0:T(8,128)(2,1)S(1)} %copy-done.2, bf16[256,1536]{1,0:T(8,128)(2,1)S(1)} %collective-permute-done.3.refs_1_.refs_5_, bf16[256,1536]{1,0:T(8,128)(2,1)S(1)} %get-tuple-element.54.refs_2_, ...), custom_call_target="tpu_custom_call" | custom-call | flops 1610612736 | bytes 5767168 | tf_op jit(solution)/shard_map/head_parts/pallas_call | solution.py:44
  35.3 1.6 %collective-permute-start.6 = (bf16[2,256,512]{2,1,0:T(8,128)(2,1)S(1)}, bf16[2,256,512]{2,1,0:T(8,128)(2,1)S(1)}, u32[]{:S(2)}, u32[]{:S(2)}) collective-permute-start(bf16[2,256,512]{2,1,0:T(8,128)(2,1)S(1)} %get-tuple-element.55), channel_id=1, source_target_pairs={{0,16},{8,24},{16,0},{24,8},{1,17},{9,25},{17,1},{25,9},{2,18},{10... | collective-permute-start | bytes 1572872 | tf_op jit(solution)/shard_map/ppermute | solution.py:453
  36.9 1.3 collective-permute-start.2
  38.2 9.1 %collective-permute-done.6.refs_1_.refs_7_ = bf16[2,256,512]{2,1,0:T(8,128)(2,1)S(1)} collective-permute-done((bf16[2,256,512]{2,1,0:T(8,128)(2,1)S(1)}, bf16[2,256,512]{2,1,0:T(8,128)(2,1)S(1)}, u32[]{:S(2)}, u32[]{:S(2)}) %collective-permute-start.6) | collective-permute-done | bytes 524320 | tf_op jit(solution)/shard_map/ppermute | solution.py:453
  47.3 3.1 %collective-permute-done.2.refs_0_ = bf16[256,1024]{1,0:T(8,128)(2,1)S(1)} collective-permute-done((bf16[256,1024]{1,0:T(8,128)(2,1)S(1)}, bf16[256,1024]{1,0:T(8,128)(2,1)S(1)}, u32[]{:S(2)}, u32[]{:S(2)}) %collective-permute-start.2) | collective-permute-done | bytes 524320 | tf_op jit(solution)/shard_map/ppermute | solution.py:457
  50.4 1.3 collective-permute-start.8
  51.7 1.0 collective-permute-done.10.refs_3_.refs_5_
  52.7 2.1 %head_parts.3 = (bf16[2,256,512]{2,1,0:T(8,128)(2,1)S(1)}, bf16[2,256,512]{2,1,0:T(8,128)(2,1)S(1)}, f32[8,128]{1,0:T(8,128)S(1)}) custom-call(bf16[256,1536]{1,0:T(8,128)(2,1)S(1)} %copy-done.2, bf16[256,1536]{1,0:T(8,128)(2,1)S(1)} %collective-permute-done.3.refs_1_.refs_5_, bf16[256,1536]{1,0:T(8,128)(2,1)S(1)} %get-tuple-element.59.refs_2_.refs_4_, ...), custom_call_target="tpu_custom_call" | custom-call | flops 1610612736 | bytes 5767168 | tf_op jit(solution)/shard_map/head_parts/pallas_call | solution.py:44
  54.8 0.6 collective-permute-start.11
  55.4 11.2 %collective-permute-done.8.refs_4_ = bf16[256,1024]{1,0:T(8,128)(2,1)S(1)} collective-permute-done((bf16[256,1024]{1,0:T(8,128)(2,1)S(1)}, bf16[256,1024]{1,0:T(8,128)(2,1)S(1)}, u32[]{:S(2)}, u32[]{:S(2)}) %collective-permute-start.8) | collective-permute-done | bytes 524320 | tf_op jit(solution)/shard_map/ppermute | solution.py:457
  66.6 0.3 route_heads.1
  66.9 0.6 collective-permute-start.13
  67.5 0.5 collective-permute-start.17
  68.1 0.8 collective-permute-done.11.refs_3_
  68.9 0.3 route_parts.1
  69.2 4.4 %collective-permute-start.12 = (bf16[256,1024]{1,0:T(8,128)(2,1)S(1)}, bf16[256,1024]{1,0:T(8,128)(2,1)S(1)}, u32[]{:S(2)}, u32[]{:S(2)}) collective-permute-start(bf16[256,1024]{1,0:T(8,128)(2,1)S(1)} %get-tuple-element.68.refs_0_), channel_id=1, source_target_pairs={{0,2},{6,4},{1,3},{7,5},{8,10},{14,12},{9,11},{15,13},{16,18},{22,... | collective-permute-start | bytes 1572872 | tf_op jit(solution)/shard_map/ppermute | solution.py:457
  73.7 6.9 %collective-permute-done.13.refs_0_ = bf16[256,1024]{1,0:T(8,128)(2,1)S(1)} collective-permute-done((bf16[256,1024]{1,0:T(8,128)(2,1)S(1)}, bf16[256,1024]{1,0:T(8,128)(2,1)S(1)}, u32[]{:S(2)}, u32[]{:S(2)}) %collective-permute-start.13) | collective-permute-done | bytes 524320 | tf_op jit(solution)/shard_map/ppermute | solution.py:453
  80.5 4.9 %collective-permute-done.12.refs_1_ = bf16[256,1024]{1,0:T(8,128)(2,1)S(1)} collective-permute-done((bf16[256,1024]{1,0:T(8,128)(2,1)S(1)}, bf16[256,1024]{1,0:T(8,128)(2,1)S(1)}, u32[]{:S(2)}, u32[]{:S(2)}) %collective-permute-start.12) | collective-permute-done | bytes 524320 | tf_op jit(solution)/shard_map/ppermute | solution.py:457
  85.6 2.6 %weight_parts.2 = (bf16[512,1536]{1,0:T(8,128)(2,1)S(1)}, f32[8,128]{1,0:T(8,128)S(1)}) custom-call(bf16[2,256,1024]{2,1,0:T(8,128)(2,1)S(1)} %get-tuple-element.61.refs_0_.refs_1_, bf16[256,1024]{1,0:T(8,128)(2,1)S(1)} %get-tuple-element.71.refs_2_.refs_1_, bf16[2,256,1024]{2,1,0:T(8,128)(2,1)S(1)} %collective-permute-done.15.refs_2_, ...), custom_call_target="tpu_custom_call" | custom-call | flops 1610612736 | bytes 6815744 | tf_op jit(solution)/shard_map/weight_parts/pallas_call | solution.py:44
  88.2 1.7 %collective-permute-start.25 = (bf16[512,1536]{1,0:T(8,128)(2,1)S(1)}, bf16[512,1536]{1,0:T(8,128)(2,1)S(1)}, u32[]{:S(2)}, u32[]{:S(2)}) collective-permute-start(bf16[512,1536]{1,0:T(8,128)(2,1)S(1)} %get-tuple-element.94), channel_id=1, source_target_pairs={{0,8},{8,0},{16,24},{24,16},{1,9},{9,1},{17,25},{25,17},{2,10},{10... | collective-permute-start | bytes 4718600 | tf_op jit(solution)/shard_map/ppermute | solution.py:453
  90.0 0.5 collective-permute-start.14
  90.5 0.7 collective-permute-start.20
  91.2 6.1 %collective-permute-start.19 = (bf16[256,1024]{1,0:T(8,128)(2,1)S(1)}, bf16[256,1024]{1,0:T(8,128)(2,1)S(1)}, u32[]{:S(2)}, u32[]{:S(2)}) collective-permute-start(bf16[256,1024]{1,0:T(8,128)(2,1)S(1)} %get-tuple-element.75), channel_id=1, source_target_pairs={{0,2},{6,4},{1,3},{7,5},{8,10},{14,12},{9,11},{15,13},{16,18},{22,... | collective-permute-start | bytes 1572872 | tf_op jit(solution)/shard_map/ppermute | solution.py:457
  97.3 6.0 %collective-permute-done.14.refs_0_.refs_1_ = bf16[256,1024]{1,0:T(8,128)(2,1)S(1)} collective-permute-done((bf16[256,1024]{1,0:T(8,128)(2,1)S(1)}, bf16[256,1024]{1,0:T(8,128)(2,1)S(1)}, u32[]{:S(2)}, u32[]{:S(2)}) %collective-permute-start.14) | collective-permute-done | bytes 524320 | tf_op jit(solution)/shard_map/ppermute | solution.py:453
  103.3 4.1 %collective-permute-done.19.refs_1_ = bf16[256,1024]{1,0:T(8,128)(2,1)S(1)} collective-permute-done((bf16[256,1024]{1,0:T(8,128)(2,1)S(1)}, bf16[256,1024]{1,0:T(8,128)(2,1)S(1)}, u32[]{:S(2)}, u32[]{:S(2)}) %collective-permute-start.19) | collective-permute-done | bytes 524320 | tf_op jit(solution)/shard_map/ppermute | solution.py:457
  107.5 2.1 %project.2 = (bf16[256,1536]{1,0:T(8,128)(2,1)S(1)}, f32[8,128]{1,0:T(8,128)S(1)}) custom-call(bf16[256,1024]{1,0:T(8,128)(2,1)S(1)} %collective-permute-done.14.refs_0_.refs_1_, bf16[256,1024]{1,0:T(8,128)(2,1)S(1)} %get-tuple-element.71.refs_2_.refs_1_, bf16[256,1536]{1,0:T(8,128)(2,1)S(1)} %get-tuple-element.54.refs_2_, ...), custom_call_target="tpu_custom_call" | custom-call | flops 1610612736 | bytes 7864320 | tf_op jit(solution)/shard_map/project/pallas_call | solution.py:44
  109.6 1.6 %collective-permute-start.22 = (bf16[256,1536]{1,0:T(8,128)(2,1)S(1)}, bf16[256,1536]{1,0:T(8,128)(2,1)S(1)}, u32[]{:S(2)}, u32[]{:S(2)}) collective-permute-start(bf16[256,1536]{1,0:T(8,128)(2,1)S(1)} %get-tuple-element.83), channel_id=1, source_target_pairs={{0,16},{8,24},{16,0},{24,8},{1,17},{9,25},{17,1},{25,9},{2,18},{10... | collective-permute-start | bytes 2359304 | tf_op jit(solution)/shard_map/ppermute | solution.py:453
  111.2 0.9 collective-permute-start.24
  112.1 5.3 %collective-permute-start.23 = (bf16[256,1024]{1,0:T(8,128)(2,1)S(1)}, bf16[256,1024]{1,0:T(8,128)(2,1)S(1)}, u32[]{:S(2)}, u32[]{:S(2)}) collective-permute-start(bf16[256,1024]{1,0:T(8,128)(2,1)S(1)} %get-tuple-element.85), channel_id=1, source_target_pairs={{0,2},{2,0},{4,6},{6,4},{1,3},{3,1},{5,7},{7,5},{8,10},{10,8},{12,... | collective-permute-start | bytes 1572872 | tf_op jit(solution)/shard_map/ppermute | solution.py:453
  117.4 2.7 %weight_parts.3 = (f32[512,1536]{1,0:T(8,128)S(1)}, f32[8,128]{1,0:T(8,128)S(1)}) custom-call(bf16[2,256,1024]{2,1,0:T(8,128)(2,1)S(1)} %get-tuple-element.61.refs_0_.refs_1_, bf16[256,1024]{1,0:T(8,128)(2,1)S(1)} %collective-permute-done.14.refs_0_.refs_1_, bf16[2,256,1024]{2,1,0:T(8,128)(2,1)S(1)} %collective-permute-done.15.refs_2_, ...), custom_call_target="tpu_custom_call" | custom-call | flops 1610612736 | bytes 6815744 | tf_op jit(solution)/shard_map/weight_parts/pallas_call | solution.py:44
  120.1 2.1 %project.3 = (f32[256,1536]{1,0:T(8,128)S(1)}, f32[8,128]{1,0:T(8,128)S(1)}) custom-call(bf16[2,256,1024]{2,1,0:T(8,128)(2,1)S(1)} %get-tuple-element.61.refs_0_.refs_1_, bf16[2,256,1024]{2,1,0:T(8,128)(2,1)S(1)} %get-tuple-element.61.refs_0_.refs_1_, bf16[256,1536]{1,0:T(8,128)(2,1)S(1)} %get-tuple-element.54.refs_2_, ...), custom_call_target="tpu_custom_call" | custom-call | flops 1610612736 | bytes 7864320 | tf_op jit(solution)/shard_map/project/pallas_call | solution.py:44
  122.2 4.7 %collective-permute-done.23.refs_4_ = bf16[256,1024]{1,0:T(8,128)(2,1)S(1)} collective-permute-done((bf16[256,1024]{1,0:T(8,128)(2,1)S(1)}, bf16[256,1024]{1,0:T(8,128)(2,1)S(1)}, u32[]{:S(2)}, u32[]{:S(2)}) %collective-permute-start.23) | collective-permute-done | bytes 524320 | tf_op jit(solution)/shard_map/ppermute | solution.py:453
  126.9 5.4 %attention_grads.1 = (bf16[256,1024]{1,0:T(8,128)(2,1)}, bf16[256,1024]{1,0:T(8,128)(2,1)}, bf16[256,1024]{1,0:T(8,128)(2,1)}, f32[8,128]{1,0:T(8,128)S(1)}) custom-call(bf16[256,1024]{1,0:T(8,128)(2,1)S(1)} %copy-done.3, bf16[256,1024]{1,0:T(8,128)(2,1)S(1)} %copy-done.4, bf16[256,1024]{1,0:T(8,128)(2,1)S(1)} %copy-done.5, ...), custom_call_target="tpu_custom_call" | custom-call | flops 671088640 | bytes 4718592 | tf_op jit(solution)/shard_map/attention_grads/pallas_call | solution.py:44
  132.3 1.1 plus.7
  133.4 1.8 %weight_total.1 = (bf16[512,1536]{1,0:T(8,128)(2,1)S(1)}, bf16[1024,1536]{1,0:T(8,128)(2,1)}, f32[8,128]{1,0:T(8,128)}) custom-call(f32[512,1536]{1,0:T(8,128)S(1)} %get-tuple-element.93.refs_0_, bf16[512,1536]{1,0:T(8,128)(2,1)S(1)} %collective-permute-done.25.refs_1_, f32[8,128]{1,0:T(8,128)S(1)} %get-tuple-element.95.refs_2_), custom_call_target="tpu_custom_call" | custom-call | bytes 7864320 | tf_op jit(solution)/shard_map/weight_total/pallas_call | solution.py:44
  135.2 3.4 %collective-permute-done.26.refs_0_ = bf16[512,1536]{1,0:T(8,128)(2,1)S(1)} collective-permute-done((bf16[512,1536]{1,0:T(8,128)(2,1)S(1)}, bf16[512,1536]{1,0:T(8,128)(2,1)S(1)}, u32[]{:S(2)}, u32[]{:S(2)}) %collective-permute-start.26) | collective-permute-done | bytes 1572896 | tf_op jit(solution)/shard_map/ppermute | solution.py:453
  138.6 1.1 weight_fill.1
  (43 shorter events, 0.6 us)
Async XLA Ops:
  0.6 1.9 %copy-start = (bf16[1024,1536]{1,0:T(8,128)(2,1)S(1)}, bf16[1024,1536]{1,0:T(8,128)(2,1)}, u32[]{:S(2)}) copy-start(bf16[1024,1536]{1,0:T(8,128)(2,1)} %refs_6_.3) | copy-start | bytes 9437188
  2.5 3.2 %copy-start.3 = (bf16[256,1024]{1,0:T(8,128)(2,1)S(1)}, bf16[256,1024]{1,0:T(8,128)(2,1)}, u32[]{:S(2)}) copy-start(bf16[256,1024]{1,0:T(8,128)(2,1)} %refs_0_.9) | copy-start | bytes 1572868
  2.5 3.2 %copy-start.4 = (bf16[256,1024]{1,0:T(8,128)(2,1)S(1)}, bf16[256,1024]{1,0:T(8,128)(2,1)}, u32[]{:S(2)}) copy-start(bf16[256,1024]{1,0:T(8,128)(2,1)} %refs_1_.3) | copy-start | bytes 1572868
  2.5 3.2 %copy-start.5 = (bf16[256,1024]{1,0:T(8,128)(2,1)S(1)}, bf16[256,1024]{1,0:T(8,128)(2,1)}, u32[]{:S(2)}) copy-start(bf16[256,1024]{1,0:T(8,128)(2,1)} %refs_2_.3) | copy-start | bytes 1572868
  2.5 12.2 %copy-start.2 = (bf16[256,1536]{1,0:T(8,128)(2,1)S(1)}, bf16[256,1536]{1,0:T(8,128)(2,1)}, u32[]{:S(2)}) copy-start(bf16[256,1536]{1,0:T(8,128)(2,1)} %refs_4_.7) | copy-start | bytes 2359300
  2.7 30.5 %copy-start.1 = (bf16[1024,1536]{1,0:T(8,128)(2,1)S(1)}, bf16[1024,1536]{1,0:T(8,128)(2,1)}, u32[]{:S(2)}) copy-start(bf16[1024,1536]{1,0:T(8,128)(2,1)} %refs_6_.3) | copy-start | bytes 9437188
  2.7 23.4 %collective-permute-start.4 = (bf16[256,1536]{1,0:T(8,128)(2,1)S(1)}, bf16[256,1536]{1,0:T(8,128)(2,1)S(1)}, u32[]{:S(2)}, u32[]{:S(2)}) collective-permute-start(bf16[256,1536]{1,0:T(8,128)(2,1)S(1)} %get-tuple-element.53), channel_id=1, source_target_pairs={{0,8},{8,0},{16,24},{24,16},{1,9},{9,1},{17,25},{25,17},{2,10},{10... | collective-permute-start | bytes 2359304 | tf_op jit(solution)/shard_map/ppermute | solution.py:453
  9.6 6.7 %collective-permute-start.1 = (bf16[256,1024]{1,0:T(8,128)(2,1)S(1)}, bf16[256,1024]{1,0:T(8,128)(2,1)S(1)}, u32[]{:S(2)}, u32[]{:S(2)}) collective-permute-start(bf16[256,1024]{1,0:T(8,128)(2,1)S(1)} %get-tuple-element.52.refs_0_), channel_id=1, source_target_pairs={{2,4},{4,2},{3,5},{5,3},{10,12},{12,10},{11,13},{13,11},{18,20},{2... | collective-permute-start | bytes 1572872 | tf_op jit(solution)/shard_map/ppermute | solution.py:457
  10.3 15.8 %collective-permute-start = (bf16[256,1024]{1,0:T(8,128)(2,1)S(1)}, bf16[256,1024]{1,0:T(8,128)(2,1)S(1)}, u32[]{:S(2)}, u32[]{:S(2)}) collective-permute-start(bf16[256,1024]{1,0:T(8,128)(2,1)S(1)} %get-tuple-element.52.refs_0_), channel_id=1, source_target_pairs={{0,2},{2,0},{4,6},{6,4},{1,3},{3,1},{5,7},{7,5},{8,10},{10,8},{12,... | collective-permute-start | bytes 1572872 | tf_op jit(solution)/shard_map/ppermute | solution.py:453
  14.7 18.4 %collective-permute-start.3 = (bf16[256,1536]{1,0:T(8,128)(2,1)S(1)}, bf16[256,1536]{1,0:T(8,128)(2,1)S(1)}, u32[]{:S(2)}, u32[]{:S(2)}) collective-permute-start(bf16[256,1536]{1,0:T(8,128)(2,1)S(1)} %copy-done.2), channel_id=1, source_target_pairs={{0,16},{8,24},{16,0},{24,8},{1,17},{9,25},{17,1},{25,9},{2,18},{10... | collective-permute-start | bytes 2359304 | tf_op jit(solution)/shard_map/ppermute | solution.py:453
  26.1 7.1 %collective-permute-start.5 = (bf16[256,1536]{1,0:T(8,128)(2,1)S(1)}, bf16[256,1536]{1,0:T(8,128)(2,1)S(1)}, u32[]{:S(2)}, u32[]{:S(2)}) collective-permute-start(bf16[256,1536]{1,0:T(8,128)(2,1)S(1)} %get-tuple-element.54.refs_2_), channel_id=1, source_target_pairs={{0,1},{1,0},{2,3},{3,2},{4,5},{5,4},{6,7},{7,6},{8,9},{9,8},{10,11... | collective-permute-start | bytes 2359304 | tf_op jit(solution)/shard_map/ppermute | solution.py:453
  26.1 24.3 %collective-permute-start.9 = (bf16[256,1536]{1,0:T(8,128)(2,1)S(1)}, bf16[256,1536]{1,0:T(8,128)(2,1)S(1)}, u32[]{:S(2)}, u32[]{:S(2)}) collective-permute-start(bf16[256,1536]{1,0:T(8,128)(2,1)S(1)} %get-tuple-element.58), channel_id=1, source_target_pairs={{0,8},{8,0},{16,24},{24,16},{1,9},{9,1},{17,25},{25,17},{2,10},{10... | collective-permute-start | bytes 2359304 | tf_op jit(solution)/shard_map/ppermute | solution.py:453
  27.5 10.7 %collective-permute-start.7 = (bf16[256,1024]{1,0:T(8,128)(2,1)S(1)}, bf16[256,1024]{1,0:T(8,128)(2,1)S(1)}, u32[]{:S(2)}, u32[]{:S(2)}) collective-permute-start(bf16[256,1024]{1,0:T(8,128)(2,1)S(1)} %collective-permute-done.refs_1_), channel_id=1, source_target_pairs={{2,4},{4,2},{3,5},{5,3},{10,12},{12,10},{11,13},{13,11},{18,20},{2... | collective-permute-start | bytes 1572872 | tf_op jit(solution)/shard_map/ppermute | solution.py:457
  35.3 12.0 %collective-permute-start.6 = (bf16[2,256,512]{2,1,0:T(8,128)(2,1)S(1)}, bf16[2,256,512]{2,1,0:T(8,128)(2,1)S(1)}, u32[]{:S(2)}, u32[]{:S(2)}) collective-permute-start(bf16[2,256,512]{2,1,0:T(8,128)(2,1)S(1)} %get-tuple-element.55), channel_id=1, source_target_pairs={{0,16},{8,24},{16,0},{24,8},{1,17},{9,25},{17,1},{25,9},{2,18},{10... | collective-permute-start | bytes 1572872 | tf_op jit(solution)/shard_map/ppermute | solution.py:453
  36.9 13.5 %collective-permute-start.2 = (bf16[256,1024]{1,0:T(8,128)(2,1)S(1)}, bf16[256,1024]{1,0:T(8,128)(2,1)S(1)}, u32[]{:S(2)}, u32[]{:S(2)}) collective-permute-start(bf16[256,1024]{1,0:T(8,128)(2,1)S(1)} %collective-permute-done.1.refs_2_.refs_5_), channel_id=1, source_target_pairs={{2,0},{4,6},{3,1},{5,7},{10,8},{12,14},{11,9},{13,15},{18,16},{20,... | collective-permute-start | bytes 1572872 | tf_op jit(solution)/shard_map/ppermute | solution.py:457
  50.4 2.3 %collective-permute-start.10 = (bf16[256,1536]{1,0:T(8,128)(2,1)S(1)}, bf16[256,1536]{1,0:T(8,128)(2,1)S(1)}, u32[]{:S(2)}, u32[]{:S(2)}) collective-permute-start(bf16[256,1536]{1,0:T(8,128)(2,1)S(1)} %get-tuple-element.59.refs_2_.refs_4_), channel_id=1, source_target_pairs={{0,1},{1,0},{2,3},{3,2},{4,5},{5,4},{6,7},{7,6},{8,9},{9,8},{10,11... | collective-permute-start | bytes 2359304 | tf_op jit(solution)/shard_map/ppermute | solution.py:453
  50.4 16.2 %collective-permute-start.8 = (bf16[256,1024]{1,0:T(8,128)(2,1)S(1)}, bf16[256,1024]{1,0:T(8,128)(2,1)S(1)}, u32[]{:S(2)}, u32[]{:S(2)}) collective-permute-start(bf16[256,1024]{1,0:T(8,128)(2,1)S(1)} %get-tuple-element.57.refs_1_.refs_3_), channel_id=1, source_target_pairs={{2,0},{4,6},{3,1},{5,7},{10,8},{12,14},{11,9},{13,15},{18,16},{20,... | collective-permute-start | bytes 1572872 | tf_op jit(solution)/shard_map/ppermute | solution.py:457
  54.8 14.0 %collective-permute-start.11 = (bf16[2,256,512]{2,1,0:T(8,128)(2,1)S(1)}, bf16[2,256,512]{2,1,0:T(8,128)(2,1)S(1)}, u32[]{:S(2)}, u32[]{:S(2)}) collective-permute-start(bf16[2,256,512]{2,1,0:T(8,128)(2,1)S(1)} %get-tuple-element.65), channel_id=1, source_target_pairs={{0,16},{8,24},{16,0},{24,8},{1,17},{9,25},{17,1},{25,9},{2,18},{10... | collective-permute-start | bytes 1572872 | tf_op jit(solution)/shard_map/ppermute | solution.py:453
  66.9 13.6 %collective-permute-start.13 = (bf16[256,1024]{1,0:T(8,128)(2,1)S(1)}, bf16[256,1024]{1,0:T(8,128)(2,1)S(1)}, u32[]{:S(2)}, u32[]{:S(2)}) collective-permute-start(bf16[256,1024]{1,0:T(8,128)(2,1)S(1)} %get-tuple-element.69), channel_id=1, source_target_pairs={{0,16},{8,24},{16,0},{24,8},{1,17},{9,25},{17,1},{25,9},{2,18},{10... | collective-permute-start | bytes 1572872 | tf_op jit(solution)/shard_map/ppermute | solution.py:453
  67.5 18.1 %collective-permute-start.15 = (bf16[2,256,1024]{2,1,0:T(8,128)(2,1)S(1)}, bf16[2,256,1024]{2,1,0:T(8,128)(2,1)S(1)}, u32[]{:S(2)}, u32[]{:S(2)}) collective-permute-start(bf16[2,256,1024]{2,1,0:T(8,128)(2,1)S(1)} %get-tuple-element.61.refs_0_.refs_1_), channel_id=1, source_target_pairs={{0,1},{1,0},{2,3},{3,2},{4,5},{5,4},{6,7},{7,6},{8,9},{9,8},{10,11... | collective-permute-start | bytes 3145736 | tf_op jit(solution)/shard_map/ppermute | solution.py:453
  67.5 18.1 %collective-permute-start.17 = (bf16[256,1536]{1,0:T(8,128)(2,1)S(1)}, bf16[256,1536]{1,0:T(8,128)(2,1)S(1)}, u32[]{:S(2)}, u32[]{:S(2)}) collective-permute-start(bf16[256,1536]{1,0:T(8,128)(2,1)S(1)} %copy-done.2), channel_id=1, source_target_pairs={{0,1},{1,0},{2,3},{3,2},{4,5},{5,4},{6,7},{7,6},{8,9},{9,8},{10,11... | collective-permute-start | bytes 2359304 | tf_op jit(solution)/shard_map/ppermute | solution.py:453
  69.1 16.5 %collective-permute-start.18 = (bf16[256,1536]{1,0:T(8,128)(2,1)S(1)}, bf16[256,1536]{1,0:T(8,128)(2,1)S(1)}, u32[]{:S(2)}, u32[]{:S(2)}) collective-permute-start(bf16[256,1536]{1,0:T(8,128)(2,1)S(1)} %get-tuple-element.74), channel_id=1, source_target_pairs={{0,1},{1,0},{2,3},{3,2},{4,5},{5,4},{6,7},{7,6},{8,9},{9,8},{10,11... | collective-permute-start | bytes 2359304 | tf_op jit(solution)/shard_map/ppermute | solution.py:453
  69.2 16.2 %collective-permute-start.12 = (bf16[256,1024]{1,0:T(8,128)(2,1)S(1)}, bf16[256,1024]{1,0:T(8,128)(2,1)S(1)}, u32[]{:S(2)}, u32[]{:S(2)}) collective-permute-start(bf16[256,1024]{1,0:T(8,128)(2,1)S(1)} %get-tuple-element.68.refs_0_), channel_id=1, source_target_pairs={{0,2},{6,4},{1,3},{7,5},{8,10},{14,12},{9,11},{15,13},{16,18},{22,... | collective-permute-start | bytes 1572872 | tf_op jit(solution)/shard_map/ppermute | solution.py:457
  80.5 5.0 %collective-permute-start.21 = (bf16[256,1024]{1,0:T(8,128)(2,1)S(1)}, bf16[256,1024]{1,0:T(8,128)(2,1)S(1)}, u32[]{:S(2)}, u32[]{:S(2)}) collective-permute-start(bf16[256,1024]{1,0:T(8,128)(2,1)S(1)} %get-tuple-element.71.refs_2_.refs_1_), channel_id=1, source_target_pairs={{0,1},{1,0},{2,3},{3,2},{4,5},{5,4},{6,7},{7,6},{8,9},{9,8},{10,11... | collective-permute-start | bytes 1572872 | tf_op jit(solution)/shard_map/ppermute | solution.py:453
  88.2 45.2 %collective-permute-start.25 = (bf16[512,1536]{1,0:T(8,128)(2,1)S(1)}, bf16[512,1536]{1,0:T(8,128)(2,1)S(1)}, u32[]{:S(2)}, u32[]{:S(2)}) collective-permute-start(bf16[512,1536]{1,0:T(8,128)(2,1)S(1)} %get-tuple-element.94), channel_id=1, source_target_pairs={{0,8},{8,0},{16,24},{24,16},{1,9},{9,1},{17,25},{25,17},{2,10},{10... | collective-permute-start | bytes 4718600 | tf_op jit(solution)/shard_map/ppermute | solution.py:453
  90.0 13.3 %collective-permute-start.14 = (bf16[256,1024]{1,0:T(8,128)(2,1)S(1)}, bf16[256,1024]{1,0:T(8,128)(2,1)S(1)}, u32[]{:S(2)}, u32[]{:S(2)}) collective-permute-start(bf16[256,1024]{1,0:T(8,128)(2,1)S(1)} %get-tuple-element.73), channel_id=1, source_target_pairs={{0,16},{8,24},{16,0},{24,8},{1,17},{9,25},{17,1},{25,9},{2,18},{10... | collective-permute-start | bytes 1572872 | tf_op jit(solution)/shard_map/ppermute | solution.py:453
  90.5 12.8 %collective-permute-start.20 = (bf16[256,1024]{1,0:T(8,128)(2,1)S(1)}, bf16[256,1024]{1,0:T(8,128)(2,1)S(1)}, u32[]{:S(2)}, u32[]{:S(2)}) collective-permute-start(bf16[256,1024]{1,0:T(8,128)(2,1)S(1)} %get-tuple-element.75), channel_id=1, source_target_pairs={{2,4},{4,2},{3,5},{5,3},{10,12},{12,10},{11,13},{13,11},{18,20},{2... | collective-permute-start | bytes 1572872 | tf_op jit(solution)/shard_map/ppermute | solution.py:457
  91.2 16.3 %collective-permute-start.19 = (bf16[256,1024]{1,0:T(8,128)(2,1)S(1)}, bf16[256,1024]{1,0:T(8,128)(2,1)S(1)}, u32[]{:S(2)}, u32[]{:S(2)}) collective-permute-start(bf16[256,1024]{1,0:T(8,128)(2,1)S(1)} %get-tuple-element.75), channel_id=1, source_target_pairs={{0,2},{6,4},{1,3},{7,5},{8,10},{14,12},{9,11},{15,13},{16,18},{22,... | collective-permute-start | bytes 1572872 | tf_op jit(solution)/shard_map/ppermute | solution.py:457
  103.2 14.2 %collective-permute-start.16 = (bf16[256,1024]{1,0:T(8,128)(2,1)S(1)}, bf16[256,1024]{1,0:T(8,128)(2,1)S(1)}, u32[]{:S(2)}, u32[]{:S(2)}) collective-permute-start(bf16[256,1024]{1,0:T(8,128)(2,1)S(1)} %collective-permute-done.14.refs_0_.refs_1_), channel_id=1, source_target_pairs={{0,1},{1,0},{2,3},{3,2},{4,5},{5,4},{6,7},{7,6},{8,9},{9,8},{10,11... | collective-permute-start | bytes 1572872 | tf_op jit(solution)/shard_map/ppermute | solution.py:453
  109.6 22.7 %collective-permute-start.22 = (bf16[256,1536]{1,0:T(8,128)(2,1)S(1)}, bf16[256,1536]{1,0:T(8,128)(2,1)S(1)}, u32[]{:S(2)}, u32[]{:S(2)}) collective-permute-start(bf16[256,1536]{1,0:T(8,128)(2,1)S(1)} %get-tuple-element.83), channel_id=1, source_target_pairs={{0,16},{8,24},{16,0},{24,8},{1,17},{9,25},{17,1},{25,9},{2,18},{10... | collective-permute-start | bytes 2359304 | tf_op jit(solution)/shard_map/ppermute | solution.py:453
  111.2 11.0 %collective-permute-start.24 = (bf16[256,1024]{1,0:T(8,128)(2,1)S(1)}, bf16[256,1024]{1,0:T(8,128)(2,1)S(1)}, u32[]{:S(2)}, u32[]{:S(2)}) collective-permute-start(bf16[256,1024]{1,0:T(8,128)(2,1)S(1)} %get-tuple-element.86), channel_id=1, source_target_pairs={{2,4},{4,2},{3,5},{5,3},{10,12},{12,10},{11,13},{13,11},{18,20},{2... | collective-permute-start | bytes 1572872 | tf_op jit(solution)/shard_map/ppermute | solution.py:457
  112.1 14.8 %collective-permute-start.23 = (bf16[256,1024]{1,0:T(8,128)(2,1)S(1)}, bf16[256,1024]{1,0:T(8,128)(2,1)S(1)}, u32[]{:S(2)}, u32[]{:S(2)}) collective-permute-start(bf16[256,1024]{1,0:T(8,128)(2,1)S(1)} %get-tuple-element.85), channel_id=1, source_target_pairs={{0,2},{2,0},{4,6},{6,4},{1,3},{3,1},{5,7},{7,5},{8,10},{10,8},{12,... | collective-permute-start | bytes 1572872 | tf_op jit(solution)/shard_map/ppermute | solution.py:453
  135.2 3.5 %collective-permute-start.26 = (bf16[512,1536]{1,0:T(8,128)(2,1)S(1)}, bf16[512,1536]{1,0:T(8,128)(2,1)S(1)}, u32[]{:S(2)}, u32[]{:S(2)}) collective-permute-start(bf16[512,1536]{1,0:T(8,128)(2,1)S(1)} %get-tuple-element.96), channel_id=1, source_target_pairs={{0,1},{1,0},{2,3},{3,2},{4,5},{5,4},{6,7},{7,6},{8,9},{9,8},{10,11... | collective-permute-start | bytes 4718600 | tf_op jit(solution)/shard_map/ppermute | solution.py:453

commit v4 on v3

--- a/solution.py
+++ b/solution.py
@@ -221,9 +221,11 @@
 
 
 def route_heads_kernel(*refs):
-    m, _, outer = position()
-    sources, (keep_ref, two_ref, three_ref, sems) = refs[:6], refs[6:]
+    m, me, outer = position()
+    sources, (keep_ref, two_ref, three_ref, core_ref, sems) = refs[:6], refs[6:]
     steps = ((0, None), (1, None), (2, True), (2, False), (3, True), (3, False))
+    half = core_ref.shape[2]
+    cols = pl.ds(pl.multiple_of((1 - me) * half, half), half)
     targets = [keep_ref.at[0], keep_ref.at[1], two_ref, three_ref]
     for j, target in enumerate(targets):
         for source, (step, at_ends) in zip(sources, steps):
@@ -232,23 +234,50 @@
             @pl.when(here if at_ends is None else here & (outer == at_ends))
             def _(target=target, j=j, source=source):
                 pltpu.make_async_copy(source, target, sems.at[j]).start()
+                if j < 2:
+                    pltpu.make_async_copy(source.at[:, cols], core_ref.at[j], sems.at[4 + j]).start()
 
     for j, target in enumerate(targets):
         pltpu.make_async_copy(sources[0], target, sems.at[j]).wait()
+        if j < 2:
+            pltpu.make_async_copy(sources[0].at[:, cols], core_ref.at[j], sems.at[4 + j]).wait()
 
 
 def route_heads(sources, after):
-    shape = sources[0].shape
+    tokens, width = sources[0].shape
     return call(
         route_heads_kernel,
         sources,
         [ANY] * 6,
         after,
-        out_specs=[ANY] * 3,
-        out_shape=[like((2, *shape)), like(shape), like(shape)],
-        scratch_shapes=[pltpu.SemaphoreType.DMA((4,))],
-        cost_estimate=cost(0, 16 * sources[0].size),
+        out_specs=[ANY] * 4,
+        out_shape=[like((2, tokens, width)), like((tokens, width)), like((tokens, width))]
+        + [like((2, tokens, width // 2))],
+        scratch_shapes=[pltpu.SemaphoreType.DMA((6,))],
+        cost_estimate=cost(0, 20 * sources[0].size),
         name="route_heads",
+    )
+
+
+def core_half_kernel(whole_ref, half_ref, sems):
+    half = half_ref.shape[1]
+    cols = pl.ds(pl.multiple_of((1 - position()[1]) * half, half), half)
+    for copy in copies([(whole_ref.at[:, cols], half_ref)], sems):
+        copy.wait()
+
+
+def core_half(whole, after=()):
+    tokens, width = whole.shape
+    return call(
+        core_half_kernel,
+        (whole,),
+        [ANY],
+        after,
+        out_specs=ANY,
+        out_shape=like((tokens, width // 2)),
+        scratch_shapes=[pltpu.SemaphoreType.DMA((1,))],
+        cost_estimate=cost(0, 2 * whole.size),
+        name="core_half",
     )
 
 
@@ -317,25 +346,26 @@
     )
 
 
-def weight_parts_kernel(*refs):
-    heads, cots, out_ref = refs[:4], refs[4:8], refs[8]
+def weight_parts_kernel(held_ref, got_ref, held_core_ref, got_core_ref, *refs):
+    cots, out_ref = refs[:4], refs[4]
     half = out_ref.shape[0]
     cols = pl.ds(pl.multiple_of(position()[1] * half, half), half)
-    left = jnp.concatenate([ref.at[0][:, cols] if len(ref.shape) == 3 else ref[:, cols] for ref in heads], axis=0)
+    left = [held_ref[0, :, cols], got_ref[:, cols], held_core_ref[0], got_core_ref[...]]
     right = jnp.concatenate([ref[...] for ref in cots], axis=0)
-    out_ref[...] = dot(left, right, TN).astype(out_ref.dtype)
+    out_ref[...] = dot(jnp.concatenate(left, axis=0), right, TN).astype(out_ref.dtype)
 
 
 def weight_parts(j, heads, cots, dtype, after):
     tokens, rows = heads[1].shape
     depth = cots[0].shape[1]
     wide = depth // 3 if depth % 384 == 0 else depth
-    pair = pl.BlockSpec((1, tokens, rows), lambda i: (j, 0, 0))
-    whole = pl.BlockSpec((tokens, rows), lambda i: (0, 0))
+    pair = lambda width: pl.BlockSpec((1, tokens, width), lambda i: (j, 0, 0))
+    whole = lambda width: pl.BlockSpec((tokens, width), lambda i: (0, 0))
     return call(
         weight_parts_kernel,
         (*heads, *cots),
-        [pair, whole] * 2 + [pl.BlockSpec((tokens, wide), lambda i: (0, i))] * 4,
+        [pair(rows), whole(rows), pair(rows // 2), whole(rows // 2)]
+        + [pl.BlockSpec((tokens, wide), lambda i: (0, i))] * 4,
         after,
         grid=(depth // wide,),
         out_specs=pl.BlockSpec((rows // 2, wide), lambda i: (0, i)),
@@ -473,9 +503,11 @@
     mine0, mine1 = flip(half0, "row", 1), flip(half1, "row", 1)
     cot_far = flip(cotangent, "row", 2)
     two_out, two_in = line(mid, (1, 0), (2, 3)), line(near, (1, 2), (2, 1))
-    mine0 = tie(mine0, near, mid)
+    cot_core = flip(cotangent, "rep", 1)
+    mine0 = tie(mine0, near, mid, cot_far, cot_core)
     beside0 = mine0, flip(mine0, "rep", 1)
     (keep0, send0), done = parts(0, beside0, [])
+    far_core = flip(tie(cot_far, done), "rep", 1)
     got0 = flip(send0, "row", 2)
     two_in, two_out = tie(two_in, got0), tie(two_out, got0)
     three = line(two_in, (1, 0), (2, 3))
@@ -483,34 +515,35 @@
     beside1 = mine1, flip(mine1, "rep", 1)
     (keep1, send1), done = parts(1, beside1, [])
     got1 = flip(send1, "row", 2)
-    (held, away_two, away_three), done = route_heads((own, near, two_out, two_in, three, mid), [done, got0])
+    (held, away_two, away_three, core), done = route_heads(
+        (own, near, two_out, two_in, three, mid), [done, got0, far_core]
+    )
     got_three = flip(away_three, "row", 2)
 
     (p0, p1, p2, p3), done = route_parts((keep0, got0, keep1, got1), [done])
     far = line(p3, (0, 1), (3, 2))
-    held_core = flip(held, "rep", 1)
-    cots = [cotangent, cot_far, flip(cotangent, "rep", 1), flip(tie(cot_far, done), "rep", 1)]
+    held_core = flip(core, "rep", 1)
+    cots = [cotangent, cot_far, cot_core, far_core]
     got_three = tie(got_three, done)
-    second, done = plus(p2, far, [got_three])
+    got_two = flip(tie(away_two, got_three), "row", 2)
+    half, done = core_half(got_three)
+    second, done = plus(p2, far, [done])
     out, cross = line(second, (0, 1), (3, 2)), line(second, (1, 2), (2, 1))
-    got_two = flip(tie(away_two, done), "row", 2)
-    heads = [held, got_three, held_core, flip(got_three, "rep", 1)]
-    away, done = weight_parts(1, heads, cots, BF16, [done])
+    away, done = weight_parts(1, [held, got_three, held_core, flip(half, "rep", 1)], cots, BF16, [done])
     away = flip(away, "row", 1)
+    besides = [*beside0, *beside1]
+    projected, done = project([held, held], out_weight, besides, F32, [done])
+    sent, done = project([got_two, got_three], out_weight, besides, BF16, [done])
+    from_far = flip(sent, "row", 2)
     near, done = plus(p1, cross, [done])
     mid, done = plus(p3, out, [done])
     near, mid = flip(near, "col", 1), line(mid, (1, 2), (2, 1))
-
-    besides = [*beside0, *beside1]
-    sent, done = project([got_two, got_three], out_weight, besides, BF16, [done])
-    from_far = flip(sent, "row", 2)
-    heads = [held, got_two, held_core, flip(got_two, "rep", 1)]
-    total, done = weight_parts(0, heads, cots, F32, [done])
-    projected, done = project([held, held], out_weight, besides, F32, [done])
+    half, done = core_half(got_two, [done])
+    total, done = weight_parts(0, [held, got_two, held_core, flip(half, "rep", 1)], cots, F32, [done])
+    projected, done = plus(projected, from_far, [done])
+    (total, grad_weight), done = weight_total(total, away, factor, rows, [done, near, mid])
     grads, done = attention_grads_sum(queries, key_vectors, value_vectors, (p0, near, mid), [done])
-    projected, done = plus(projected, from_far, [done])
-    (total, grad_weight), done = weight_total(total, away, factor, rows, [done])
-    grad_weight, _ = weight_fill(flip(total, "rep", 1), grad_weight)
+    grad_weight, _ = weight_fill(flip(total, "rep", 1), grad_weight, [done])
     return (projected, *grads, grad_weight)
 
 

time: 140 us -> 128 us (0.914)
  waiting for transfers between devices: 69.9 us -> 63.8 us
  starting transfers between devices: 38.9 us -> 33 us
    ppermute x19, waiting for transfers between devices: 46.6 us -> 32.7 us  [flip(): lax.ppermute(x, axis, [(i, i ^ bit) for i in range(lax.axis_size(axis))])]
    ppermute x8, waiting for transfers between devices: 23.3 us -> 31.1 us  [line(): return lax.ppermute(x, 'col', pairs)]
    ppermute x19, starting transfers between devices: 22.9 us -> 17.9 us  [flip(): lax.ppermute(x, axis, [(i, i ^ bit) for i in range(lax.axis_size(axis))])]
    pallas_call x24 -> x26, Pallas kernels: 28.1 us -> 28.2 us  [call(): pl.pallas_call(body, in_specs=[*in_specs, *[ANY] * len(after)], out_specs...]
  transfers between devices with their start and end apart: 27 -> 27, of which waited for: 13 -> 11; matrix products, arithmetic and copies ran while one was open for 0% -> 0% of each run, Pallas kernels for 16% -> 18%
where the time goes in v4:
time: 128 us
  waiting for transfers between devices  63.8 us (50%)
  starting transfers between devices  33 us (26%)
  Pallas kernels  28.2 us (22%)
  local copies, waits for them, and re-layouts  1.96 us (2%)
    ppermute x19, waiting for transfers between devices, flip(): lax.ppermute(x, axis, [(i, i ^ bit) for i in range(lax.axis_size(axis))])  32.7 us
    ppermute x8, waiting for transfers between devices, line(): return lax.ppermute(x, 'col', pairs)  31.1 us
    pallas_call x26, Pallas kernels, call(): pl.pallas_call(body, in_specs=[*in_specs, *[ANY] * len(after)], out_specs...  28.2 us
    ppermute x19, starting transfers between devices, flip(): lax.ppermute(x, axis, [(i, i ^ bit) for i in range(lax.axis_size(axis))])  17.9 us
    ppermute x8, starting transfers between devices, line(): return lax.ppermute(x, 'col', pairs)  15.1 us
  transfers between devices with their start and end apart: 27, of which 11 were waited for; matrix products, arithmetic and copies ran while one was open for 0% of the time, Pallas kernels for 18%

profile of v4, /device:TPU:0, one launch (start us, length us, event | category | flops | bytes accessed | tf_op | source)
XLA Modules:
  0.0 128.0 jit_solution(11241094585540287290)
XLA Ops:
  0.6 3.0 %collective-permute-start.3 = (bf16[256,1536]{1,0:T(8,128)(2,1)}, bf16[256,1536]{1,0:T(8,128)(2,1)S(1)}, u32[]{:S(2)}, u32[]{:S(2)}) collective-permute-start(bf16[256,1536]{1,0:T(8,128)(2,1)} %refs_4_.7), channel_id=1, source_target_pairs={{0,16},{8,24},{16,0},{24,8},{1,17},{9,25},{17,1},{25,9},{2,18},{10... | collective-permute-start | bytes 2359304 | tf_op jit(solution)/shard_map/ppermute | solution.py:483
  3.7 1.9 %copy-done = bf16[1024,1536]{1,0:T(8,128)(2,1)S(1)} copy-done((bf16[1024,1536]{1,0:T(8,128)(2,1)S(1)}, bf16[1024,1536]{1,0:T(8,128)(2,1)}, u32[]{:S(2)}) %copy-start) | copy-done | bytes 3145752
  5.6 0.1 fetch_halves.1
  5.7 1.6 %collective-permute-start.4 = (bf16[256,1536]{1,0:T(8,128)(2,1)S(1)}, bf16[256,1536]{1,0:T(8,128)(2,1)S(1)}, u32[]{:S(2)}, u32[]{:S(2)}) collective-permute-start(bf16[256,1536]{1,0:T(8,128)(2,1)S(1)} %get-tuple-element.60), channel_id=1, source_target_pairs={{0,8},{8,0},{16,24},{24,16},{1,9},{9,1},{17,25},{25,17},{2,10},{10... | collective-permute-start | bytes 2359304 | tf_op jit(solution)/shard_map/ppermute | solution.py:483
  7.3 3.9 %attention.1 = (bf16[256,1024]{1,0:T(8,128)(2,1)S(1)}, f32[8,128]{1,0:T(8,128)}) custom-call(bf16[256,1024]{1,0:T(8,128)(2,1)S(1)} %copy-done.3, bf16[256,1024]{1,0:T(8,128)(2,1)S(1)} %copy-done.4, bf16[256,1024]{1,0:T(8,128)(2,1)S(1)} %copy-done.5), custom_call_target="tpu_custom_call" | custom-call | flops 268435456 | bytes 2097152 | tf_op jit(solution)/shard_map/attention/pallas_call | solution.py:44
  11.2 1.6 %collective-permute-start = (bf16[256,1024]{1,0:T(8,128)(2,1)S(1)}, bf16[256,1024]{1,0:T(8,128)(2,1)S(1)}, u32[]{:S(2)}, u32[]{:S(2)}) collective-permute-start(bf16[256,1024]{1,0:T(8,128)(2,1)S(1)} %get-tuple-element.59.refs_0_), channel_id=1, source_target_pairs={{0,2},{2,0},{4,6},{6,4},{1,3},{3,1},{5,7},{7,5},{8,10},{10,8},{12,... | collective-permute-start | bytes 1572872 | tf_op jit(solution)/shard_map/ppermute | solution.py:483
  12.8 0.7 collective-permute-start.1
  13.5 12.0 %collective-permute-done.refs_1_ = bf16[256,1024]{1,0:T(8,128)(2,1)S(1)} collective-permute-done((bf16[256,1024]{1,0:T(8,128)(2,1)S(1)}, bf16[256,1024]{1,0:T(8,128)(2,1)S(1)}, u32[]{:S(2)}, u32[]{:S(2)}) %collective-permute-start) | collective-permute-done | bytes 524320 | tf_op jit(solution)/shard_map/ppermute | solution.py:483
  25.7 1.0 collective-permute-start.10
  26.7 1.3 collective-permute-start.2
  28.0 2.1 %head_parts.2 = (bf16[2,256,512]{2,1,0:T(8,128)(2,1)S(1)}, bf16[2,256,512]{2,1,0:T(8,128)(2,1)S(1)}, f32[8,128]{1,0:T(8,128)S(1)}) custom-call(bf16[256,1536]{1,0:T(8,128)(2,1)S(1)} %copy-done.2, bf16[256,1536]{1,0:T(8,128)(2,1)S(1)} %collective-permute-done.3.refs_3_.refs_1_.refs_5_, bf16[256,1536]{1,0:T(8,128)(2,1)S(1)} %get-tuple-element.61.refs_2_, ...), custom_call_target="tpu_custom_call" | custom-call | flops 1610612736 | bytes 5767168 | tf_op jit(solution)/shard_map/head_parts/pallas_call | solution.py:44
  30.1 0.6 collective-permute-start.7
  30.7 0.7 collective-permute-start.8
  31.4 13.4 %collective-permute-done.2.refs_0_ = bf16[256,1024]{1,0:T(8,128)(2,1)S(1)} collective-permute-done((bf16[256,1024]{1,0:T(8,128)(2,1)S(1)}, bf16[256,1024]{1,0:T(8,128)(2,1)S(1)}, u32[]{:S(2)}, u32[]{:S(2)}) %collective-permute-start.2) | collective-permute-done | bytes 524320 | tf_op jit(solution)/shard_map/ppermute | solution.py:487
  44.8 0.9 collective-permute-done.10.refs_0_
  45.7 0.6 collective-permute-start.12
  46.3 1.3 collective-permute-start.9
  47.6 0.4 collective-permute-done.11.refs_3_.refs_5_
  47.9 2.1 %head_parts.3 = (bf16[2,256,512]{2,1,0:T(8,128)(2,1)S(1)}, bf16[2,256,512]{2,1,0:T(8,128)(2,1)S(1)}, f32[8,128]{1,0:T(8,128)S(1)}) custom-call(bf16[256,1536]{1,0:T(8,128)(2,1)S(1)} %copy-done.2, bf16[256,1536]{1,0:T(8,128)(2,1)S(1)} %collective-permute-done.3.refs_3_.refs_1_.refs_5_, bf16[256,1536]{1,0:T(8,128)(2,1)S(1)} %get-tuple-element.66.refs_2_.refs_4_, ...), custom_call_target="tpu_custom_call" | custom-call | flops 1610612736 | bytes 5767168 | tf_op jit(solution)/shard_map/head_parts/pallas_call | solution.py:44
  50.1 0.6 collective-permute-start.14
  50.7 14.3 %collective-permute-done.9.refs_4_ = bf16[256,1024]{1,0:T(8,128)(2,1)S(1)} collective-permute-done((bf16[256,1024]{1,0:T(8,128)(2,1)S(1)}, bf16[256,1024]{1,0:T(8,128)(2,1)S(1)}, u32[]{:S(2)}, u32[]{:S(2)}) %collective-permute-start.9) | collective-permute-done | bytes 524320 | tf_op jit(solution)/shard_map/ppermute | solution.py:487
  64.9 0.4 route_heads.1
  65.3 1.6 %collective-permute-start.13 = (bf16[256,1024]{1,0:T(8,128)(2,1)S(1)}, bf16[256,1024]{1,0:T(8,128)(2,1)S(1)}, u32[]{:S(2)}, u32[]{:S(2)}) collective-permute-start(bf16[256,1024]{1,0:T(8,128)(2,1)S(1)} %get-tuple-element.71), channel_id=1, source_target_pairs={{0,16},{8,24},{16,0},{24,8},{1,17},{9,25},{17,1},{25,9},{2,18},{10... | collective-permute-start | bytes 1572872 | tf_op jit(solution)/shard_map/ppermute | solution.py:483
  66.9 0.3 route_parts.1
  67.1 5.2 %collective-permute-start.17 = (bf16[256,1024]{1,0:T(8,128)(2,1)S(1)}, bf16[256,1024]{1,0:T(8,128)(2,1)S(1)}, u32[]{:S(2)}, u32[]{:S(2)}) collective-permute-start(bf16[256,1024]{1,0:T(8,128)(2,1)S(1)} %get-tuple-element.81.refs_0_), channel_id=1, source_target_pairs={{0,2},{6,4},{1,3},{7,5},{8,10},{14,12},{9,11},{15,13},{16,18},{22,... | collective-permute-start | bytes 1572872 | tf_op jit(solution)/shard_map/ppermute | solution.py:487
  72.5 6.2 %collective-permute-done.13.refs_0_ = bf16[256,1024]{1,0:T(8,128)(2,1)S(1)} collective-permute-done((bf16[256,1024]{1,0:T(8,128)(2,1)S(1)}, bf16[256,1024]{1,0:T(8,128)(2,1)S(1)}, u32[]{:S(2)}, u32[]{:S(2)}) %collective-permute-start.13) | collective-permute-done | bytes 524320 | tf_op jit(solution)/shard_map/ppermute | solution.py:483
  78.8 3.4 %collective-permute-done.17.refs_1_ = bf16[256,1024]{1,0:T(8,128)(2,1)S(1)} collective-permute-done((bf16[256,1024]{1,0:T(8,128)(2,1)S(1)}, bf16[256,1024]{1,0:T(8,128)(2,1)S(1)}, u32[]{:S(2)}, u32[]{:S(2)}) %collective-permute-start.17) | collective-permute-done | bytes 524320 | tf_op jit(solution)/shard_map/ppermute | solution.py:487
  82.2 0.1 plus.4
  82.3 2.6 %weight_parts.2 = (bf16[512,1536]{1,0:T(8,128)(2,1)S(1)}, f32[8,128]{1,0:T(8,128)S(1)}) custom-call(bf16[2,256,1024]{2,1,0:T(8,128)(2,1)S(1)} %get-tuple-element.70.refs_0_.refs_1_, bf16[256,1024]{1,0:T(8,128)(2,1)S(1)} %get-tuple-element.77.refs_0_.refs_1_, bf16[2,256,512]{2,1,0:T(8,128)(2,1)S(1)} %collective-permute-done.15.refs_2_, ...), custom_call_target="tpu_custom_call" | custom-call | flops 1610612736 | bytes 6815744 | tf_op jit(solution)/shard_map/weight_parts/pallas_call | solution.py:44
  85.0 1.2 collective-permute-start.25
  86.1 1.5 %collective-permute-start.18 = (bf16[256,1024]{1,0:T(8,128)(2,1)S(1)}, bf16[256,1024]{1,0:T(8,128)(2,1)S(1)}, u32[]{:S(2)}, u32[]{:S(2)}) collective-permute-start(bf16[256,1024]{1,0:T(8,128)(2,1)S(1)} %get-tuple-element.87), channel_id=1, source_target_pairs={{0,16},{8,24},{16,0},{24,8},{1,17},{9,25},{17,1},{25,9},{2,18},{10... | collective-permute-start | bytes 1572872 | tf_op jit(solution)/shard_map/ppermute | solution.py:483
  87.6 4.4 %collective-permute-start.20 = (bf16[256,1024]{1,0:T(8,128)(2,1)S(1)}, bf16[256,1024]{1,0:T(8,128)(2,1)S(1)}, u32[]{:S(2)}, u32[]{:S(2)}) collective-permute-start(bf16[256,1024]{1,0:T(8,128)(2,1)S(1)} %get-tuple-element.90), channel_id=1, source_target_pairs={{0,2},{6,4},{1,3},{7,5},{8,10},{14,12},{9,11},{15,13},{16,18},{22,... | collective-permute-start | bytes 1572872 | tf_op jit(solution)/shard_map/ppermute | solution.py:487
  92.1 0.7 collective-permute-start.21
  92.8 2.1 %project.2 = (f32[256,1536]{1,0:T(8,128)S(1)}, f32[8,128]{1,0:T(8,128)S(1)}) custom-call(bf16[2,256,1024]{2,1,0:T(8,128)(2,1)S(1)} %get-tuple-element.70.refs_0_.refs_1_, bf16[2,256,1024]{2,1,0:T(8,128)(2,1)S(1)} %get-tuple-element.70.refs_0_.refs_1_, bf16[256,1536]{1,0:T(8,128)(2,1)S(1)} %get-tuple-element.61.refs_2_, ...), custom_call_target="tpu_custom_call" | custom-call | flops 1610612736 | bytes 7864320 | tf_op jit(solution)/shard_map/project/pallas_call | solution.py:44
  94.8 2.9 %collective-permute-done.18.refs_0_.refs_1_ = bf16[256,1024]{1,0:T(8,128)(2,1)S(1)} collective-permute-done((bf16[256,1024]{1,0:T(8,128)(2,1)S(1)}, bf16[256,1024]{1,0:T(8,128)(2,1)S(1)}, u32[]{:S(2)}, u32[]{:S(2)}) %collective-permute-start.18) | collective-permute-done | bytes 524320 | tf_op jit(solution)/shard_map/ppermute | solution.py:483
  97.8 2.1 %project.3 = (bf16[256,1536]{1,0:T(8,128)(2,1)S(1)}, f32[8,128]{1,0:T(8,128)S(1)}) custom-call(bf16[256,1024]{1,0:T(8,128)(2,1)S(1)} %collective-permute-done.18.refs_0_.refs_1_, bf16[256,1024]{1,0:T(8,128)(2,1)S(1)} %get-tuple-element.77.refs_0_.refs_1_, bf16[256,1536]{1,0:T(8,128)(2,1)S(1)} %get-tuple-element.61.refs_2_, ...), custom_call_target="tpu_custom_call" | custom-call | flops 1610612736 | bytes 7864320 | tf_op jit(solution)/shard_map/project/pallas_call | solution.py:44
  99.9 1.6 %collective-permute-start.19 = (bf16[256,1536]{1,0:T(8,128)(2,1)S(1)}, bf16[256,1536]{1,0:T(8,128)(2,1)S(1)}, u32[]{:S(2)}, u32[]{:S(2)}) collective-permute-start(bf16[256,1536]{1,0:T(8,128)(2,1)S(1)} %get-tuple-element.89), channel_id=1, source_target_pairs={{0,16},{8,24},{16,0},{24,8},{1,17},{9,25},{17,1},{25,9},{2,18},{10... | collective-permute-start | bytes 2359304 | tf_op jit(solution)/shard_map/ppermute | solution.py:483
  101.4 0.1 plus.5
  101.6 2.8 %collective-permute-start.23 = (bf16[256,1024]{1,0:T(8,128)(2,1)S(1)}, bf16[256,1024]{1,0:T(8,128)(2,1)S(1)}, u32[]{:S(2)}, u32[]{:S(2)}) collective-permute-start(bf16[256,1024]{1,0:T(8,128)(2,1)S(1)} %get-tuple-element.100), channel_id=1, source_target_pairs={{0,2},{2,0},{4,6},{6,4},{1,3},{3,1},{5,7},{7,5},{8,10},{10,8},{12,... | collective-permute-start | bytes 1572872 | tf_op jit(solution)/shard_map/ppermute | solution.py:483
  104.5 0.9 collective-permute-start.24
  105.5 1.5 %collective-permute-done.22.refs_3_ = bf16[256,512]{1,0:T(8,128)(2,1)S(1)} collective-permute-done((bf16[256,512]{1,0:T(8,128)(2,1)S(1)}, bf16[256,512]{1,0:T(8,128)(2,1)S(1)}, u32[]{:S(2)}, u32[]{:S(2)}) %collective-permute-start.22) | collective-permute-done | bytes 262176 | tf_op jit(solution)/shard_map/ppermute | solution.py:483
  107.0 2.7 %weight_parts.3 = (f32[512,1536]{1,0:T(8,128)S(1)}, f32[8,128]{1,0:T(8,128)S(1)}) custom-call(bf16[2,256,1024]{2,1,0:T(8,128)(2,1)S(1)} %get-tuple-element.70.refs_0_.refs_1_, bf16[256,1024]{1,0:T(8,128)(2,1)S(1)} %collective-permute-done.18.refs_0_.refs_1_, bf16[2,256,512]{2,1,0:T(8,128)(2,1)S(1)} %collective-permute-done.15.refs_2_, ...), custom_call_target="tpu_custom_call" | custom-call | flops 1610612736 | bytes 6815744 | tf_op jit(solution)/shard_map/weight_parts/pallas_call | solution.py:44
  109.7 6.6 %collective-permute-done.19.refs_1_ = bf16[256,1536]{1,0:T(8,128)(2,1)S(1)} collective-permute-done((bf16[256,1536]{1,0:T(8,128)(2,1)S(1)}, bf16[256,1536]{1,0:T(8,128)(2,1)S(1)}, u32[]{:S(2)}, u32[]{:S(2)}) %collective-permute-start.19) | collective-permute-done | bytes 786464 | tf_op jit(solution)/shard_map/ppermute | solution.py:483
  116.3 1.0 plus.7
  117.3 2.1 %collective-permute-done.25.refs_1_ = bf16[512,1536]{1,0:T(8,128)(2,1)S(1)} collective-permute-done((bf16[512,1536]{1,0:T(8,128)(2,1)S(1)}, bf16[512,1536]{1,0:T(8,128)(2,1)S(1)}, u32[]{:S(2)}, u32[]{:S(2)}) %collective-permute-start.25) | collective-permute-done | bytes 1572896 | tf_op jit(solution)/shard_map/ppermute | solution.py:483
  119.4 1.8 %weight_total.1 = (bf16[512,1536]{1,0:T(8,128)(2,1)S(1)}, bf16[1024,1536]{1,0:T(8,128)(2,1)}, f32[8,128]{1,0:T(8,128)S(1)}) custom-call(f32[512,1536]{1,0:T(8,128)S(1)} %get-tuple-element.102.refs_0_, bf16[512,1536]{1,0:T(8,128)(2,1)S(1)} %collective-permute-done.25.refs_1_, f32[8,128]{1,0:T(8,128)S(1)} %get-tuple-element.104.refs_2_, ...), custom_call_target="tpu_custom_call" | custom-call | bytes 7864320 | tf_op jit(solution)/shard_map/weight_total/pallas_call | solution.py:44
  121.3 5.4 %attention_grads.1 = (bf16[256,1024]{1,0:T(8,128)(2,1)}, bf16[256,1024]{1,0:T(8,128)(2,1)}, bf16[256,1024]{1,0:T(8,128)(2,1)}, f32[8,128]{1,0:T(8,128)S(1)}) custom-call(bf16[256,1024]{1,0:T(8,128)(2,1)S(1)} %copy-done.3, bf16[256,1024]{1,0:T(8,128)(2,1)S(1)} %copy-done.4, bf16[256,1024]{1,0:T(8,128)(2,1)S(1)} %copy-done.5, ...), custom_call_target="tpu_custom_call" | custom-call | flops 671088640 | bytes 4718592 | tf_op jit(solution)/shard_map/attention_grads/pallas_call | solution.py:44
  126.7 1.2 weight_fill.1
  (45 shorter events, 0.7 us)
Async XLA Ops:
  0.6 25.0 %collective-permute-start.3 = (bf16[256,1536]{1,0:T(8,128)(2,1)}, bf16[256,1536]{1,0:T(8,128)(2,1)S(1)}, u32[]{:S(2)}, u32[]{:S(2)}) collective-permute-start(bf16[256,1536]{1,0:T(8,128)(2,1)} %refs_4_.7), channel_id=1, source_target_pairs={{0,16},{8,24},{16,0},{24,8},{1,17},{9,25},{17,1},{25,9},{2,18},{10... | collective-permute-start | bytes 2359304 | tf_op jit(solution)/shard_map/ppermute | solution.py:483
  3.7 1.9 %copy-start = (bf16[1024,1536]{1,0:T(8,128)(2,1)S(1)}, bf16[1024,1536]{1,0:T(8,128)(2,1)}, u32[]{:S(2)}) copy-start(bf16[1024,1536]{1,0:T(8,128)(2,1)} %refs_6_.3) | copy-start | bytes 9437188
  5.6 1.7 %copy-start.2 = (bf16[256,1536]{1,0:T(8,128)(2,1)S(1)}, bf16[256,1536]{1,0:T(8,128)(2,1)}, u32[]{:S(2)}) copy-start(bf16[256,1536]{1,0:T(8,128)(2,1)} %refs_4_.7) | copy-start | bytes 2359300
  5.6 1.7 %copy-start.3 = (bf16[256,1024]{1,0:T(8,128)(2,1)S(1)}, bf16[256,1024]{1,0:T(8,128)(2,1)}, u32[]{:S(2)}) copy-start(bf16[256,1024]{1,0:T(8,128)(2,1)} %refs_0_.9) | copy-start | bytes 1572868
  5.6 1.7 %copy-start.4 = (bf16[256,1024]{1,0:T(8,128)(2,1)S(1)}, bf16[256,1024]{1,0:T(8,128)(2,1)}, u32[]{:S(2)}) copy-start(bf16[256,1024]{1,0:T(8,128)(2,1)} %refs_1_.3) | copy-start | bytes 1572868
  5.6 1.7 %copy-start.5 = (bf16[256,1024]{1,0:T(8,128)(2,1)S(1)}, bf16[256,1024]{1,0:T(8,128)(2,1)}, u32[]{:S(2)}) copy-start(bf16[256,1024]{1,0:T(8,128)(2,1)} %refs_2_.3) | copy-start | bytes 1572868
  5.7 19.9 %collective-permute-start.4 = (bf16[256,1536]{1,0:T(8,128)(2,1)S(1)}, bf16[256,1536]{1,0:T(8,128)(2,1)S(1)}, u32[]{:S(2)}, u32[]{:S(2)}) collective-permute-start(bf16[256,1536]{1,0:T(8,128)(2,1)S(1)} %get-tuple-element.60), channel_id=1, source_target_pairs={{0,8},{8,0},{16,24},{24,16},{1,9},{9,1},{17,25},{25,17},{2,10},{10... | collective-permute-start | bytes 2359304 | tf_op jit(solution)/shard_map/ppermute | solution.py:483
  7.3 18.3 %collective-permute-start.5 = (bf16[256,1536]{1,0:T(8,128)(2,1)S(1)}, bf16[256,1536]{1,0:T(8,128)(2,1)S(1)}, u32[]{:S(2)}, u32[]{:S(2)}) collective-permute-start(bf16[256,1536]{1,0:T(8,128)(2,1)S(1)} %copy-done.2), channel_id=1, source_target_pairs={{0,1},{1,0},{2,3},{3,2},{4,5},{5,4},{6,7},{7,6},{8,9},{9,8},{10,11... | collective-permute-start | bytes 2359304 | tf_op jit(solution)/shard_map/ppermute | solution.py:483
  11.2 16.8 %copy-start.1 = (bf16[1024,1536]{1,0:T(8,128)(2,1)S(1)}, bf16[1024,1536]{1,0:T(8,128)(2,1)}, u32[]{:S(2)}) copy-start(bf16[1024,1536]{1,0:T(8,128)(2,1)} %refs_6_.3) | copy-start | bytes 9437188
  11.2 14.4 %collective-permute-start = (bf16[256,1024]{1,0:T(8,128)(2,1)S(1)}, bf16[256,1024]{1,0:T(8,128)(2,1)S(1)}, u32[]{:S(2)}, u32[]{:S(2)}) collective-permute-start(bf16[256,1024]{1,0:T(8,128)(2,1)S(1)} %get-tuple-element.59.refs_0_), channel_id=1, source_target_pairs={{0,2},{2,0},{4,6},{6,4},{1,3},{3,1},{5,7},{7,5},{8,10},{10,8},{12,... | collective-permute-start | bytes 1572872 | tf_op jit(solution)/shard_map/ppermute | solution.py:483
  12.8 12.7 %collective-permute-start.1 = (bf16[256,1024]{1,0:T(8,128)(2,1)S(1)}, bf16[256,1024]{1,0:T(8,128)(2,1)S(1)}, u32[]{:S(2)}, u32[]{:S(2)}) collective-permute-start(bf16[256,1024]{1,0:T(8,128)(2,1)S(1)} %get-tuple-element.59.refs_0_), channel_id=1, source_target_pairs={{2,4},{4,2},{3,5},{5,3},{10,12},{12,10},{11,13},{13,11},{18,20},{2... | collective-permute-start | bytes 1572872 | tf_op jit(solution)/shard_map/ppermute | solution.py:487
  25.6 2.4 %collective-permute-start.6 = (bf16[256,1536]{1,0:T(8,128)(2,1)S(1)}, bf16[256,1536]{1,0:T(8,128)(2,1)S(1)}, u32[]{:S(2)}, u32[]{:S(2)}) collective-permute-start(bf16[256,1536]{1,0:T(8,128)(2,1)S(1)} %get-tuple-element.61.refs_2_), channel_id=1, source_target_pairs={{0,1},{1,0},{2,3},{3,2},{4,5},{5,4},{6,7},{7,6},{8,9},{9,8},{10,11... | collective-permute-start | bytes 2359304 | tf_op jit(solution)/shard_map/ppermute | solution.py:483
  25.7 20.0 %collective-permute-start.10 = (bf16[256,1536]{1,0:T(8,128)(2,1)S(1)}, bf16[256,1536]{1,0:T(8,128)(2,1)S(1)}, u32[]{:S(2)}, u32[]{:S(2)}) collective-permute-start(bf16[256,1536]{1,0:T(8,128)(2,1)S(1)} %get-tuple-element.65), channel_id=1, source_target_pairs={{0,8},{8,0},{16,24},{24,16},{1,9},{9,1},{17,25},{25,17},{2,10},{10... | collective-permute-start | bytes 2359304 | tf_op jit(solution)/shard_map/ppermute | solution.py:483
  26.7 18.1 %collective-permute-start.2 = (bf16[256,1024]{1,0:T(8,128)(2,1)S(1)}, bf16[256,1024]{1,0:T(8,128)(2,1)S(1)}, u32[]{:S(2)}, u32[]{:S(2)}) collective-permute-start(bf16[256,1024]{1,0:T(8,128)(2,1)S(1)} %collective-permute-done.1.refs_2_.refs_5_), channel_id=1, source_target_pairs={{2,0},{4,6},{3,1},{5,7},{10,8},{12,14},{11,9},{13,15},{18,16},{20,... | collective-permute-start | bytes 1572872 | tf_op jit(solution)/shard_map/ppermute | solution.py:487
  30.1 14.6 %collective-permute-start.7 = (bf16[2,256,512]{2,1,0:T(8,128)(2,1)S(1)}, bf16[2,256,512]{2,1,0:T(8,128)(2,1)S(1)}, u32[]{:S(2)}, u32[]{:S(2)}) collective-permute-start(bf16[2,256,512]{2,1,0:T(8,128)(2,1)S(1)} %get-tuple-element.62), channel_id=1, source_target_pairs={{0,16},{8,24},{16,0},{24,8},{1,17},{9,25},{17,1},{25,9},{2,18},{10... | collective-permute-start | bytes 1572872 | tf_op jit(solution)/shard_map/ppermute | solution.py:483
  30.7 14.1 %collective-permute-start.8 = (bf16[256,1024]{1,0:T(8,128)(2,1)S(1)}, bf16[256,1024]{1,0:T(8,128)(2,1)S(1)}, u32[]{:S(2)}, u32[]{:S(2)}) collective-permute-start(bf16[256,1024]{1,0:T(8,128)(2,1)S(1)} %collective-permute-done.refs_1_), channel_id=1, source_target_pairs={{2,4},{4,2},{3,5},{5,3},{10,12},{12,10},{11,13},{13,11},{18,20},{2... | collective-permute-start | bytes 1572872 | tf_op jit(solution)/shard_map/ppermute | solution.py:487
  45.6 2.3 %collective-permute-start.11 = (bf16[256,1536]{1,0:T(8,128)(2,1)S(1)}, bf16[256,1536]{1,0:T(8,128)(2,1)S(1)}, u32[]{:S(2)}, u32[]{:S(2)}) collective-permute-start(bf16[256,1536]{1,0:T(8,128)(2,1)S(1)} %get-tuple-element.66.refs_2_.refs_4_), channel_id=1, source_target_pairs={{0,1},{1,0},{2,3},{3,2},{4,5},{5,4},{6,7},{7,6},{8,9},{9,8},{10,11... | collective-permute-start | bytes 2359304 | tf_op jit(solution)/shard_map/ppermute | solution.py:483
  45.7 4.9 %collective-permute-start.12 = (bf16[256,1536]{1,0:T(8,128)(2,1)S(1)}, bf16[256,1536]{1,0:T(8,128)(2,1)S(1)}, u32[]{:S(2)}, u32[]{:S(2)}) collective-permute-start(bf16[256,1536]{1,0:T(8,128)(2,1)S(1)} %get-tuple-element.69), channel_id=1, source_target_pairs={{0,1},{1,0},{2,3},{3,2},{4,5},{5,4},{6,7},{7,6},{8,9},{9,8},{10,11... | collective-permute-start | bytes 2359304 | tf_op jit(solution)/shard_map/ppermute | solution.py:483
  46.3 18.6 %collective-permute-start.9 = (bf16[256,1024]{1,0:T(8,128)(2,1)S(1)}, bf16[256,1024]{1,0:T(8,128)(2,1)S(1)}, u32[]{:S(2)}, u32[]{:S(2)}) collective-permute-start(bf16[256,1024]{1,0:T(8,128)(2,1)S(1)} %get-tuple-element.64.refs_1_.refs_3_), channel_id=1, source_target_pairs={{2,0},{4,6},{3,1},{5,7},{10,8},{12,14},{11,9},{13,15},{18,16},{20,... | collective-permute-start | bytes 1572872 | tf_op jit(solution)/shard_map/ppermute | solution.py:487
  50.1 16.8 %collective-permute-start.14 = (bf16[2,256,512]{2,1,0:T(8,128)(2,1)S(1)}, bf16[2,256,512]{2,1,0:T(8,128)(2,1)S(1)}, u32[]{:S(2)}, u32[]{:S(2)}) collective-permute-start(bf16[2,256,512]{2,1,0:T(8,128)(2,1)S(1)} %get-tuple-element.74), channel_id=1, source_target_pairs={{0,16},{8,24},{16,0},{24,8},{1,17},{9,25},{17,1},{25,9},{2,18},{10... | collective-permute-start | bytes 1572872 | tf_op jit(solution)/shard_map/ppermute | solution.py:483
  65.3 13.4 %collective-permute-start.13 = (bf16[256,1024]{1,0:T(8,128)(2,1)S(1)}, bf16[256,1024]{1,0:T(8,128)(2,1)S(1)}, u32[]{:S(2)}, u32[]{:S(2)}) collective-permute-start(bf16[256,1024]{1,0:T(8,128)(2,1)S(1)} %get-tuple-element.71), channel_id=1, source_target_pairs={{0,16},{8,24},{16,0},{24,8},{1,17},{9,25},{17,1},{25,9},{2,18},{10... | collective-permute-start | bytes 1572872 | tf_op jit(solution)/shard_map/ppermute | solution.py:483
  67.1 15.0 %collective-permute-start.17 = (bf16[256,1024]{1,0:T(8,128)(2,1)S(1)}, bf16[256,1024]{1,0:T(8,128)(2,1)S(1)}, u32[]{:S(2)}, u32[]{:S(2)}) collective-permute-start(bf16[256,1024]{1,0:T(8,128)(2,1)S(1)} %get-tuple-element.81.refs_0_), channel_id=1, source_target_pairs={{0,2},{6,4},{1,3},{7,5},{8,10},{14,12},{9,11},{15,13},{16,18},{22,... | collective-permute-start | bytes 1572872 | tf_op jit(solution)/shard_map/ppermute | solution.py:487
  72.4 9.9 %collective-permute-start.15 = (bf16[2,256,512]{2,1,0:T(8,128)(2,1)S(1)}, bf16[2,256,512]{2,1,0:T(8,128)(2,1)S(1)}, u32[]{:S(2)}, u32[]{:S(2)}) collective-permute-start(bf16[2,256,512]{2,1,0:T(8,128)(2,1)S(1)} %get-tuple-element.78), channel_id=1, source_target_pairs={{0,1},{1,0},{2,3},{3,2},{4,5},{5,4},{6,7},{7,6},{8,9},{9,8},{10,11... | collective-permute-start | bytes 1572872 | tf_op jit(solution)/shard_map/ppermute | solution.py:483
  78.7 3.6 %collective-permute-start.16 = (bf16[256,512]{1,0:T(8,128)(2,1)S(1)}, bf16[256,512]{1,0:T(8,128)(2,1)S(1)}, u32[]{:S(2)}, u32[]{:S(2)}) collective-permute-start(bf16[256,512]{1,0:T(8,128)(2,1)S(1)} %get-tuple-element.79), channel_id=1, source_target_pairs={{0,1},{1,0},{2,3},{3,2},{4,5},{5,4},{6,7},{7,6},{8,9},{9,8},{10,11... | collective-permute-start | bytes 786440 | tf_op jit(solution)/shard_map/ppermute | solution.py:483
  85.0 34.5 %collective-permute-start.25 = (bf16[512,1536]{1,0:T(8,128)(2,1)S(1)}, bf16[512,1536]{1,0:T(8,128)(2,1)S(1)}, u32[]{:S(2)}, u32[]{:S(2)}) collective-permute-start(bf16[512,1536]{1,0:T(8,128)(2,1)S(1)} %get-tuple-element.103), channel_id=1, source_target_pairs={{0,8},{8,0},{16,24},{24,16},{1,9},{9,1},{17,25},{25,17},{2,10},{10... | collective-permute-start | bytes 4718600 | tf_op jit(solution)/shard_map/ppermute | solution.py:483
  86.1 11.6 %collective-permute-start.18 = (bf16[256,1024]{1,0:T(8,128)(2,1)S(1)}, bf16[256,1024]{1,0:T(8,128)(2,1)S(1)}, u32[]{:S(2)}, u32[]{:S(2)}) collective-permute-start(bf16[256,1024]{1,0:T(8,128)(2,1)S(1)} %get-tuple-element.87), channel_id=1, source_target_pairs={{0,16},{8,24},{16,0},{24,8},{1,17},{9,25},{17,1},{25,9},{2,18},{10... | collective-permute-start | bytes 1572872 | tf_op jit(solution)/shard_map/ppermute | solution.py:483
  87.6 16.7 %collective-permute-start.20 = (bf16[256,1024]{1,0:T(8,128)(2,1)S(1)}, bf16[256,1024]{1,0:T(8,128)(2,1)S(1)}, u32[]{:S(2)}, u32[]{:S(2)}) collective-permute-start(bf16[256,1024]{1,0:T(8,128)(2,1)S(1)} %get-tuple-element.90), channel_id=1, source_target_pairs={{0,2},{6,4},{1,3},{7,5},{8,10},{14,12},{9,11},{15,13},{16,18},{22,... | collective-permute-start | bytes 1572872 | tf_op jit(solution)/shard_map/ppermute | solution.py:487
  92.1 9.4 %collective-permute-start.21 = (bf16[256,1024]{1,0:T(8,128)(2,1)S(1)}, bf16[256,1024]{1,0:T(8,128)(2,1)S(1)}, u32[]{:S(2)}, u32[]{:S(2)}) collective-permute-start(bf16[256,1024]{1,0:T(8,128)(2,1)S(1)} %get-tuple-element.90), channel_id=1, source_target_pairs={{2,4},{4,2},{3,5},{5,3},{10,12},{12,10},{11,13},{13,11},{18,20},{2... | collective-permute-start | bytes 1572872 | tf_op jit(solution)/shard_map/ppermute | solution.py:487
  99.9 16.4 %collective-permute-start.19 = (bf16[256,1536]{1,0:T(8,128)(2,1)S(1)}, bf16[256,1536]{1,0:T(8,128)(2,1)S(1)}, u32[]{:S(2)}, u32[]{:S(2)}) collective-permute-start(bf16[256,1536]{1,0:T(8,128)(2,1)S(1)} %get-tuple-element.89), channel_id=1, source_target_pairs={{0,16},{8,24},{16,0},{24,8},{1,17},{9,25},{17,1},{25,9},{2,18},{10... | collective-permute-start | bytes 2359304 | tf_op jit(solution)/shard_map/ppermute | solution.py:483
  101.6 15.7 %collective-permute-start.23 = (bf16[256,1024]{1,0:T(8,128)(2,1)S(1)}, bf16[256,1024]{1,0:T(8,128)(2,1)S(1)}, u32[]{:S(2)}, u32[]{:S(2)}) collective-permute-start(bf16[256,1024]{1,0:T(8,128)(2,1)S(1)} %get-tuple-element.100), channel_id=1, source_target_pairs={{0,2},{2,0},{4,6},{6,4},{1,3},{3,1},{5,7},{7,5},{8,10},{10,8},{12,... | collective-permute-start | bytes 1572872 | tf_op jit(solution)/shard_map/ppermute | solution.py:483
  104.5 12.8 %collective-permute-start.24 = (bf16[256,1024]{1,0:T(8,128)(2,1)S(1)}, bf16[256,1024]{1,0:T(8,128)(2,1)S(1)}, u32[]{:S(2)}, u32[]{:S(2)}) collective-permute-start(bf16[256,1024]{1,0:T(8,128)(2,1)S(1)} %get-tuple-element.101), channel_id=1, source_target_pairs={{2,4},{4,2},{3,5},{5,3},{10,12},{12,10},{11,13},{13,11},{18,20},{2... | collective-permute-start | bytes 1572872 | tf_op jit(solution)/shard_map/ppermute | solution.py:487
  105.4 1.6 %collective-permute-start.22 = (bf16[256,512]{1,0:T(8,128)(2,1)S(1)}, bf16[256,512]{1,0:T(8,128)(2,1)S(1)}, u32[]{:S(2)}, u32[]{:S(2)}) collective-permute-start(bf16[256,512]{1,0:T(8,128)(2,1)S(1)} %get-tuple-element.95), channel_id=1, source_target_pairs={{0,1},{1,0},{2,3},{3,2},{4,5},{5,4},{6,7},{7,6},{8,9},{9,8},{10,11... | collective-permute-start | bytes 786440 | tf_op jit(solution)/shard_map/ppermute | solution.py:483
  121.2 5.5 %collective-permute-start.26 = (bf16[512,1536]{1,0:T(8,128)(2,1)S(1)}, bf16[512,1536]{1,0:T(8,128)(2,1)S(1)}, u32[]{:S(2)}, u32[]{:S(2)}) collective-permute-start(bf16[512,1536]{1,0:T(8,128)(2,1)S(1)} %get-tuple-element.109), channel_id=1, source_target_pairs={{0,1},{1,0},{2,3},{3,2},{4,5},{5,4},{6,7},{7,6},{8,9},{9,8},{10,11... | collective-permute-start | bytes 4718600 | tf_op jit(solution)/shard_map/ppermute | solution.py:483

commit v5 on v4

--- a/solution.py
+++ b/solution.py
@@ -140,7 +140,7 @@
 
 
 def head_width(width):
-    return (2 if width % (2 * HSZ) == 0 else 1) * HSZ
+    return next(n for n in (8, 4, 2, 1) if width % (n * HSZ) == 0) * HSZ
 
 
 def attention(q, k, v, at, width, after=()):
@@ -192,34 +192,6 @@
     )
 
 
-def fetch_halves_kernel(weight_ref, *refs):
-    outs, sems = refs[:-1], refs[-1]
-    half, me = outs[0].shape[0], position()[1]
-    for copy in copies(
-        [
-            (weight_ref.at[pl.ds(pl.multiple_of((2 * h + me) * half, half), half)], out)
-            for h, out in enumerate(outs)
-        ],
-        sems,
-    ):
-        copy.wait()
-
-
-def fetch_halves(weight, after):
-    rows, depth = weight.shape
-    return call(
-        fetch_halves_kernel,
-        (weight,),
-        [HBM],
-        after,
-        out_specs=[ANY] * 2,
-        out_shape=[like((rows // 4, depth))] * 2,
-        scratch_shapes=[pltpu.SemaphoreType.DMA((2,))],
-        cost_estimate=cost(0, 2 * rows * depth),
-        name="fetch_halves",
-    )
-
-
 def route_heads_kernel(*refs):
     m, me, outer = position()
     sources, (keep_ref, two_ref, three_ref, core_ref, sems) = refs[:6], refs[6:]
@@ -281,67 +253,105 @@
     )
 
 
-def head_parts_kernel(at, cot_ref, far_ref, mine_ref, other_ref, w_ref, keep_ref, send_ref, w, sems):
-    (load,) = copies([(w_ref.at[pl.ds(at, w.shape[0])], w)], sems)
-    m, me, _ = position()
-    low, half = m & 1, mine_ref.shape[0]
+def head_parts_kernel(n_other, cot_ref, far_ref, mine_ref, *refs):
+    others, refs = refs[:n_other], refs[n_other:]
+    half, me = mine_ref.shape[0], position()[1]
+    whole = len(refs) > 2
+    keep_ref, send_ref = refs[1:3] if whole else refs
+    if whole:
+        w, sems = refs[3:]
+        (load,) = copies([(refs[0], w)], sems)
+    rows = keep_ref.shape[1] - 2 * half
     sides = ((far_ref, send_ref), (cot_ref, keep_ref))
+    pieces = [(mine_ref, rows + me * half)]
+    for i, ref in enumerate(others):
+        pieces.append((ref, rows + (1 - me) * half + i * ref.shape[0]))
     for source, target in sides:
-        for ref, i in ((mine_ref, me), (other_ref, 1 - me)):
-            cols = pl.ds(pl.multiple_of(i * half, half), half)
-            target[1 - low, :, cols] = dot(source[...], ref[...], NT).astype(BF16)
-    load.wait()
-    for source, target in sides:
-        target[low] = dot(source[...], w[...], NT).astype(BF16)
-
-
-def head_parts(cot, cot_far, weight, mine, other, h, after):
+        for ref, at in pieces:
+            cols = pl.ds(pl.multiple_of(at, HSZ), ref.shape[0])
+            target[:, cols] = dot(source[...], ref[...], NT).astype(BF16)
+    if whole:
+        load.wait()
+        for source, target in sides:
+            target[:, :rows] = dot(source[...], w[...], NT).astype(BF16)
+
+
+def head_parts(cot, cot_far, mine, others, weight, after):
     tokens, depth = cot.shape
-    rows = 2 * mine.shape[0]
+    width = 2 * mine.shape[0] + sum(a.shape[0] for a in weight)
     whole = lambda a: pl.BlockSpec(a.shape, lambda i: (0, 0))
-    out = pl.BlockSpec((2, tokens, rows), lambda i: (0, 0, 0))
-    return call(
-        functools.partial(head_parts_kernel, h * rows),
-        (cot, cot_far, mine, other, weight),
-        [whole(cot)] * 2 + [whole(mine)] * 2 + [HBM],
+    out = pl.BlockSpec((tokens, width), lambda i: (0, 0))
+    return call(
+        functools.partial(head_parts_kernel, len(others)),
+        (cot, cot_far, mine, *others, *weight),
+        [whole(a) for a in (cot, cot_far, mine, *others)] + [HBM] * len(weight),
         after,
         grid=(1,),
         out_specs=[out] * 2,
-        out_shape=[like((2, tokens, rows))] * 2,
-        scratch_shapes=[pltpu.VMEM((rows, depth), BF16), pltpu.SemaphoreType.DMA((1,))],
-        cost_estimate=cost(4 * tokens * depth * rows, 4 * (tokens + rows) * depth + 8 * tokens * rows),
+        out_shape=[like((tokens, width))] * 2,
+        scratch_shapes=[b for a in weight for b in (pltpu.VMEM(a.shape, BF16), pltpu.SemaphoreType.DMA((1,)))],
+        cost_estimate=cost(2 * tokens * depth * width, 2 * (2 * tokens + width) * depth + 4 * tokens * width),
         name="head_parts",
     )
 
 
+def split_kernel(whole_ref, *refs):
+    outs, sems = refs[:-1], refs[-1]
+    rows = outs[0].shape[0]
+    for copy in copies([(whole_ref.at[pl.ds(i * rows, rows)], out) for i, out in enumerate(outs)], sems):
+        copy.wait()
+
+
+def split(whole, after):
+    rows, depth = whole.shape
+    return call(
+        split_kernel,
+        (whole,),
+        [ANY],
+        after,
+        out_specs=[ANY] * 2,
+        out_shape=[like((rows // 2, depth))] * 2,
+        scratch_shapes=[pltpu.SemaphoreType.DMA((2,))],
+        cost_estimate=cost(0, 4 * whole.size),
+        name="split",
+    )[0]
+
+
 def route_parts_kernel(*refs):
-    parts, targets, sems = refs[:4], refs[4:8], refs[8]
-    m = position()[0]
-    width = parts[0].shape[2]
-    views = [target.at[:, pl.ds(h * width, width)] for target in targets for h in (0, 1)]
-    for i, view in enumerate(views):
-        step, h = i // 2, i % 2
-        for high, source in ((step >> 1, parts[2 * h]), (1 - (step >> 1), parts[2 * h + 1])):
-
-            @pl.when(m >> 1 == high)
-            def _(view=view, i=i, source=source.at[step & 1]):
-                pltpu.make_async_copy(source, view, sems.at[i]).start()
-
-    for i, view in enumerate(views):
-        pltpu.make_async_copy(parts[0].at[0], view, sems.at[i]).wait()
+    (keep0, got0, keep1, got1), targets, sems = refs[:4], refs[4:8], refs[8]
+    m, width = position()[0], targets[0].shape[1]
+    first = keep0.shape[1] - width
+    moves = []
+    for j in range(4):
+        big, small = (keep0, keep1) if j < 2 else (got0, got1)
+        if j % 2 == 0:
+            moves.append((j, big.at[:, pl.ds(0, width)], pl.ds(0, width)))
+        else:
+            moves.append((j, big.at[:, pl.ds(width, first)], pl.ds(0, first)))
+            moves.append((j, small, pl.ds(first, width - first)))
+    for i, (j, view, place) in enumerate(moves):
+        for step, target in enumerate(targets):
+
+            @pl.when((m ^ j) == step)
+            def _(view=view, target=target.at[:, place], i=i):
+                pltpu.make_async_copy(view, target, sems.at[i]).start()
+
+    for i, (_, view, place) in enumerate(moves):
+        pltpu.make_async_copy(view, targets[0].at[:, place], sems.at[i]).wait()
 
 
 def route_parts(parts, after):
-    _, tokens, width = parts[0].shape
+    tokens = parts[0].shape[0]
+    width = (parts[0].shape[1] + parts[2].shape[1]) // 2
     return call(
         route_parts_kernel,
         parts,
         [ANY] * 4,
         after,
         out_specs=[ANY] * 4,
-        out_shape=[like((tokens, 2 * width))] * 4,
-        scratch_shapes=[pltpu.SemaphoreType.DMA((8,))],
-        cost_estimate=cost(0, 16 * parts[0].size),
+        out_shape=[like((tokens, width))] * 4,
+        scratch_shapes=[pltpu.SemaphoreType.DMA((6,))],
+        cost_estimate=cost(0, 16 * tokens * width),
         name="route_parts",
     )
 
@@ -438,13 +448,14 @@
 
 
 def project_kernel(own_ref, beside_ref, *refs):
-    besides, weight_ref, out_ref, weight, total, sems = refs[:4], *refs[4:]
+    besides, weight_ref, out_ref, weight, total, sems = refs[:-5], *refs[-5:]
     (load,) = copies([(weight_ref, weight)], sems)
     me = position()[1]
     half = besides[0].shape[0]
+    starts = [me * half, (1 - me) * half, (2 + me) * half]
     for i, ref in enumerate(besides):
-        at = i // 2 * 2 + (1 - me if i % 2 else me)
-        cols = pl.ds(pl.multiple_of(at * half, half), half)
+        at = starts[i] if i < 3 else (3 - me) * half + (i - 3) * ref.shape[0]
+        cols = pl.ds(pl.multiple_of(at, HSZ), ref.shape[0])
         block = beside_ref[0, :, cols] if len(beside_ref.shape) == 3 else beside_ref[:, cols]
         term = dot(block, ref[...])
         total[...] = term if i == 0 else total[...] + term
@@ -493,30 +504,31 @@
     factor = float(tok_rows * lax.axis_size("row") * lax.axis_size("rep")) ** (-0.5)
     rows = out_weight.shape[0]
 
-    def parts(h, beside, after):
-        return head_parts(cotangent, cot_far, out_weight, *beside, h, after)
+    def parts(beside, weight, after):
+        return head_parts(cotangent, cot_far, beside[0], beside[1:], weight, after)
 
     own, done = attention(queries, key_vectors, value_vectors, 0, features)
     near, mid = flip(own, "col", 1), line(own, (1, 2), (2, 1))
 
-    (half0, half1), _ = fetch_halves(out_weight, [])
+    me, cut = lax.axis_index("rep"), rows // 4
+    half0, half1 = [lax.dynamic_slice_in_dim(out_weight, (2 * h + me) * cut, cut, 0) for h in (0, 1)]
     mine0, mine1 = flip(half0, "row", 1), flip(half1, "row", 1)
     cot_far = flip(cotangent, "row", 2)
     two_out, two_in = line(mid, (1, 0), (2, 3)), line(near, (1, 2), (2, 1))
     cot_core = flip(cotangent, "rep", 1)
     mine0 = tie(mine0, near, mid, cot_far, cot_core)
     beside0 = mine0, flip(mine0, "rep", 1)
-    (keep0, send0), done = parts(0, beside0, [])
+    (keep0, send0), done = parts(beside0, [out_weight], [])
     far_core = flip(tie(cot_far, done), "rep", 1)
     got0 = flip(send0, "row", 2)
-    two_in, two_out = tie(two_in, got0), tie(two_out, got0)
+    two_in = tie(two_in, done)
     three = line(two_in, (1, 0), (2, 3))
     mine1 = tie(mine1, two_in, two_out)
-    beside1 = mine1, flip(mine1, "rep", 1)
-    (keep1, send1), done = parts(1, beside1, [])
+    beside1 = mine1, *(flip(a, "rep", 1) for a in split(mine1, []))
+    (keep1, send1), done = parts(beside1, [], [])
     got1 = flip(send1, "row", 2)
     (held, away_two, away_three, core), done = route_heads(
-        (own, near, two_out, two_in, three, mid), [done, got0, far_core]
+        (own, near, two_out, two_in, three, mid), [done, got0, got1]
     )
     got_three = flip(away_three, "row", 2)
 

time: 128 us -> 124 us (0.969)
  starting transfers between devices: 33 us -> 29.7 us
  Pallas kernels: 28.2 us -> 25.7 us
  waiting for transfers between devices: 63.8 us -> 65.9 us
    ppermute x19 -> x20, waiting for transfers between devices: 32.7 us -> 52.1 us  [flip(): lax.ppermute(x, axis, [(i, i ^ bit) for i in range(lax.axis_size(axis))])]
    ppermute x8, waiting for transfers between devices: 31.1 us -> 13.8 us  [line(): return lax.ppermute(x, 'col', pairs)]
    ppermute x8, starting transfers between devices: 15.1 us -> 11.4 us  [line(): return lax.ppermute(x, 'col', pairs)]
    pallas_call x26 -> x25, Pallas kernels: 28.2 us -> 25.7 us  [call(): pl.pallas_call(body, in_specs=[*in_specs, *[ANY] * len(after)], out_specs...]
    unnamed x13 -> x11, local copies, waits for them, and re-layouts: 1.96 us -> 0.07 us
    dynamic_slice x0 -> x1, local copies, waits for them, and re-layouts: none -> 1.47 us  [local_grid(): lax.dynamic_slice_in_dim(out_weight, (2 * h + me) * cut, cut, 0)]
    ppermute x19 -> x20, starting transfers between devices: 17.9 us -> 18.4 us  [flip(): lax.ppermute(x, axis, [(i, i ^ bit) for i in range(lax.axis_size(axis))])]
  transfers between devices with their start and end apart: 27 -> 28, of which waited for: 11 -> 12; matrix products, arithmetic and copies ran while one was open for 0% -> 1% of each run, Pallas kernels for 18% -> 16%
where the time goes in v5:
time: 124 us
  waiting for transfers between devices  65.9 us (53%)
  starting transfers between devices  29.7 us (24%)
  Pallas kernels  25.7 us (21%)
  local copies, waits for them, and re-layouts  1.55 us (1%)
    ppermute x20, waiting for transfers between devices, flip(): lax.ppermute(x, axis, [(i, i ^ bit) for i in range(lax.axis_size(axis))])  52.1 us
    pallas_call x25, Pallas kernels, call(): pl.pallas_call(body, in_specs=[*in_specs, *[ANY] * len(after)], out_specs...  25.7 us
    ppermute x20, starting transfers between devices, flip(): lax.ppermute(x, axis, [(i, i ^ bit) for i in range(lax.axis_size(axis))])  18.4 us
    ppermute x8, waiting for transfers between devices, line(): return lax.ppermute(x, 'col', pairs)  13.8 us
    ppermute x8, starting transfers between devices, line(): return lax.ppermute(x, 'col', pairs)  11.4 us
  transfers between devices with their start and end apart: 28, of which 12 were waited for; matrix products, arithmetic and copies ran while one was open for 1% of the time, Pallas kernels for 16%

profile of v5, /device:TPU:0, one launch (start us, length us, event | category | flops | bytes accessed | tf_op | source)
XLA Modules:
  0.0 124.1 jit_solution(6727641378263317667)
XLA Ops:
  0.7 3.0 %collective-permute-start.4 = (bf16[256,1536]{1,0:T(8,128)(2,1)}, bf16[256,1536]{1,0:T(8,128)(2,1)S(1)}, u32[]{:S(2)}, u32[]{:S(2)}) collective-permute-start(bf16[256,1536]{1,0:T(8,128)(2,1)} %refs_4_.5), channel_id=1, source_target_pairs={{0,16},{8,24},{16,0},{24,8},{1,17},{9,25},{17,1},{25,9},{2,18},{10... | collective-permute-start | bytes 2359304 | tf_op jit(solution)/shard_map/ppermute | solution.py:494
  3.7 1.5 %constant_dynamic-slice_fusion = (bf16[256,1536]{1,0:T(8,128)(2,1)S(1)}, bf16[256,1536]{1,0:T(8,128)(2,1)S(1)}) fusion(bf16[1024,1536]{1,0:T(8,128)(2,1)} %refs_7_.3, s32[]{:T(128)S(6)} %select_n.7, s32[]{:T(128)S(6)} %select_n.6), kind=kLoop, calls=%fused_computation | loop fusion | bytes 3145736 | tf_op jit(solution)/shard_map/dynamic_slice | solution.py:514
  5.2 1.6 %collective-permute-start.5 = (bf16[256,1536]{1,0:T(8,128)(2,1)S(1)}, bf16[256,1536]{1,0:T(8,128)(2,1)S(1)}, u32[]{:S(2)}, u32[]{:S(2)}) collective-permute-start(bf16[256,1536]{1,0:T(8,128)(2,1)S(1)} %get-tuple-element.112), channel_id=1, source_target_pairs={{0,8},{8,0},{16,24},{24,16},{1,9},{9,1},{17,25},{25,17},{2,10},{10... | collective-permute-start | bytes 2359304 | tf_op jit(solution)/shard_map/ppermute | solution.py:494
  6.8 1.4 %attention.1 = (bf16[256,1024]{1,0:T(8,128)(2,1)S(1)}, f32[8,128]{1,0:T(8,128)}) custom-call(bf16[256,1024]{1,0:T(8,128)(2,1)S(1)} %copy-done.1, bf16[256,1024]{1,0:T(8,128)(2,1)S(1)} %copy-done.2, bf16[256,1024]{1,0:T(8,128)(2,1)S(1)} %copy-done.3), custom_call_target="tpu_custom_call" | custom-call | flops 268435456 | bytes 2097152 | tf_op jit(solution)/shard_map/attention/pallas_call | solution.py:44
  8.2 1.6 %collective-permute-start = (bf16[256,1024]{1,0:T(8,128)(2,1)S(1)}, bf16[256,1024]{1,0:T(8,128)(2,1)S(1)}, u32[]{:S(2)}, u32[]{:S(2)}) collective-permute-start(bf16[256,1024]{1,0:T(8,128)(2,1)S(1)} %get-tuple-element.58.refs_0_), channel_id=1, source_target_pairs={{0,2},{2,0},{4,6},{6,4},{1,3},{3,1},{5,7},{7,5},{8,10},{10,8},{12,... | collective-permute-start | bytes 1572872 | tf_op jit(solution)/shard_map/ppermute | solution.py:494
  9.9 0.7 collective-permute-start.1
  10.6 12.1 %collective-permute-done.refs_1_ = bf16[256,1024]{1,0:T(8,128)(2,1)S(1)} collective-permute-done((bf16[256,1024]{1,0:T(8,128)(2,1)S(1)}, bf16[256,1024]{1,0:T(8,128)(2,1)S(1)}, u32[]{:S(2)}, u32[]{:S(2)}) %collective-permute-start) | collective-permute-done | bytes 524320 | tf_op jit(solution)/shard_map/ppermute | solution.py:494
  22.6 1.6 %collective-permute-done.5.refs_0_ = bf16[256,1536]{1,0:T(8,128)(2,1)S(1)} collective-permute-done((bf16[256,1536]{1,0:T(8,128)(2,1)S(1)}, bf16[256,1536]{1,0:T(8,128)(2,1)S(1)}, u32[]{:S(2)}, u32[]{:S(2)}) %collective-permute-start.5) | collective-permute-done | bytes 786464 | tf_op jit(solution)/shard_map/ppermute | solution.py:494
  24.3 1.6 %collective-permute-start.9 = (bf16[256,1536]{1,0:T(8,128)(2,1)S(1)}, bf16[256,1536]{1,0:T(8,128)(2,1)S(1)}, u32[]{:S(2)}, u32[]{:S(2)}) collective-permute-start(bf16[256,1536]{1,0:T(8,128)(2,1)S(1)} %get-tuple-element.111), channel_id=1, source_target_pairs={{0,8},{8,0},{16,24},{24,16},{1,9},{9,1},{17,25},{25,17},{2,10},{10... | collective-permute-start | bytes 2359304 | tf_op jit(solution)/shard_map/ppermute | solution.py:494
  25.8 0.7 collective-permute-start.3
  26.5 1.3 %collective-permute-start.2 = (bf16[256,1024]{1,0:T(8,128)(2,1)S(1)}, bf16[256,1024]{1,0:T(8,128)(2,1)S(1)}, u32[]{:S(2)}, u32[]{:S(2)}) collective-permute-start(bf16[256,1024]{1,0:T(8,128)(2,1)S(1)} %collective-permute-done.1.refs_2_.refs_5_), channel_id=1, source_target_pairs={{2,0},{4,6},{3,1},{5,7},{10,8},{12,14},{11,9},{13,15},{18,16},{20,... | collective-permute-start | bytes 1572872 | tf_op jit(solution)/shard_map/ppermute | solution.py:498
  27.8 3.1 %head_parts.2 = (bf16[256,1536]{1,0:T(8,128)(2,1)S(1)}, bf16[256,1536]{1,0:T(8,128)(2,1)S(1)}, f32[8,128]{1,0:T(8,128)S(1)}) custom-call(bf16[256,1536]{1,0:T(8,128)(2,1)S(1)} %copy-done.4, bf16[256,1536]{1,0:T(8,128)(2,1)S(1)} %collective-permute-done.4.refs_3_.refs_1_.refs_5_, bf16[256,1536]{1,0:T(8,128)(2,1)S(1)} %get-tuple-element.59.refs_2_, ...), custom_call_target="tpu_custom_call" | custom-call | flops 2415919104 | bytes 7864320 | tf_op jit(solution)/shard_map/head_parts/pallas_call | solution.py:44
  30.9 0.7 collective-permute-start.12
  31.6 12.6 %collective-permute-done.9.refs_0_ = bf16[256,1536]{1,0:T(8,128)(2,1)S(1)} collective-permute-done((bf16[256,1536]{1,0:T(8,128)(2,1)S(1)}, bf16[256,1536]{1,0:T(8,128)(2,1)S(1)}, u32[]{:S(2)}, u32[]{:S(2)}) %collective-permute-start.9) | collective-permute-done | bytes 786464 | tf_op jit(solution)/shard_map/ppermute | solution.py:494
  44.2 0.6 collective-permute-done.2.refs_2_
  44.8 0.4 split.1
  45.3 0.5 collective-permute-start.11
  45.8 1.3 %collective-permute-start.8 = (bf16[256,1024]{1,0:T(8,128)(2,1)S(1)}, bf16[256,1024]{1,0:T(8,128)(2,1)S(1)}, u32[]{:S(2)}, u32[]{:S(2)}) collective-permute-start(bf16[256,1024]{1,0:T(8,128)(2,1)S(1)} %get-tuple-element.61.refs_1_.refs_3_), channel_id=1, source_target_pairs={{2,0},{4,6},{3,1},{5,7},{10,8},{12,14},{11,9},{13,15},{18,16},{20,... | collective-permute-start | bytes 1572872 | tf_op jit(solution)/shard_map/ppermute | solution.py:498
  47.1 0.5 collective-permute-done.11.refs_4_.refs_6_
  47.6 1.4 %head_parts.3 = (bf16[256,512]{1,0:T(8,128)(2,1)S(1)}, bf16[256,512]{1,0:T(8,128)(2,1)S(1)}, f32[8,128]{1,0:T(8,128)S(1)}) custom-call(bf16[256,1536]{1,0:T(8,128)(2,1)S(1)} %copy-done.4, bf16[256,1536]{1,0:T(8,128)(2,1)S(1)} %collective-permute-done.4.refs_3_.refs_1_.refs_5_, bf16[256,1536]{1,0:T(8,128)(2,1)S(1)} %get-tuple-element.62.refs_0_.refs_2_.refs_4_, ...), custom_call_target="tpu_custom_call" | custom-call | flops 805306368 | bytes 3670016 | tf_op jit(solution)/shard_map/head_parts/pallas_call | solution.py:44
  48.9 0.7 collective-permute-start.13
  49.6 12.1 %collective-permute-done.8.refs_4_ = bf16[256,1024]{1,0:T(8,128)(2,1)S(1)} collective-permute-done((bf16[256,1024]{1,0:T(8,128)(2,1)S(1)}, bf16[256,1024]{1,0:T(8,128)(2,1)S(1)}, u32[]{:S(2)}, u32[]{:S(2)}) %collective-permute-start.8) | collective-permute-done | bytes 524320 | tf_op jit(solution)/shard_map/ppermute | solution.py:498
  61.7 0.4 route_heads.1
  62.1 0.7 collective-permute-start.14
  62.9 0.3 route_parts.1
  63.2 1.5 %collective-permute-start.18 = (bf16[256,1024]{1,0:T(8,128)(2,1)S(1)}, bf16[256,1024]{1,0:T(8,128)(2,1)S(1)}, u32[]{:S(2)}, u32[]{:S(2)}) collective-permute-start(bf16[256,1024]{1,0:T(8,128)(2,1)S(1)} %get-tuple-element.79.refs_0_), channel_id=1, source_target_pairs={{0,2},{6,4},{1,3},{7,5},{8,10},{14,12},{9,11},{15,13},{16,18},{22,... | collective-permute-start | bytes 1572872 | tf_op jit(solution)/shard_map/ppermute | solution.py:498
  64.7 0.4 collective-permute-start.15
  65.1 10.3 %collective-permute-done.14.refs_0_ = bf16[256,1024]{1,0:T(8,128)(2,1)S(1)} collective-permute-done((bf16[256,1024]{1,0:T(8,128)(2,1)S(1)}, bf16[256,1024]{1,0:T(8,128)(2,1)S(1)}, u32[]{:S(2)}, u32[]{:S(2)}) %collective-permute-start.14) | collective-permute-done | bytes 524320 | tf_op jit(solution)/shard_map/ppermute | solution.py:494
  75.5 1.1 collective-permute-done.18.refs_1_
  76.7 0.2 collective-permute-done.16.refs_3_
  77.0 2.6 %weight_parts.2 = (bf16[512,1536]{1,0:T(8,128)(2,1)S(1)}, f32[8,128]{1,0:T(8,128)S(1)}) custom-call(bf16[2,256,1024]{2,1,0:T(8,128)(2,1)S(1)} %get-tuple-element.68.refs_0_.refs_1_, bf16[256,1024]{1,0:T(8,128)(2,1)S(1)} %get-tuple-element.74.refs_0_.refs_1_, bf16[2,256,512]{2,1,0:T(8,128)(2,1)S(1)} %collective-permute-done.15.refs_2_, ...), custom_call_target="tpu_custom_call" | custom-call | flops 1610612736 | bytes 6815744 | tf_op jit(solution)/shard_map/weight_parts/pallas_call | solution.py:44
  79.6 1.3 %collective-permute-start.26 = (bf16[512,1536]{1,0:T(8,128)(2,1)S(1)}, bf16[512,1536]{1,0:T(8,128)(2,1)S(1)}, u32[]{:S(2)}, u32[]{:S(2)}) collective-permute-start(bf16[512,1536]{1,0:T(8,128)(2,1)S(1)} %get-tuple-element.101), channel_id=1, source_target_pairs={{0,8},{8,0},{16,24},{24,16},{1,9},{9,1},{17,25},{25,17},{2,10},{10... | collective-permute-start | bytes 4718600 | tf_op jit(solution)/shard_map/ppermute | solution.py:494
  80.9 1.3 %collective-permute-start.19 = (bf16[256,1024]{1,0:T(8,128)(2,1)S(1)}, bf16[256,1024]{1,0:T(8,128)(2,1)S(1)}, u32[]{:S(2)}, u32[]{:S(2)}) collective-permute-start(bf16[256,1024]{1,0:T(8,128)(2,1)S(1)} %get-tuple-element.85), channel_id=1, source_target_pairs={{0,16},{8,24},{16,0},{24,8},{1,17},{9,25},{17,1},{25,9},{2,18},{10... | collective-permute-start | bytes 1572872 | tf_op jit(solution)/shard_map/ppermute | solution.py:494
  82.2 4.4 %collective-permute-start.21 = (bf16[256,1024]{1,0:T(8,128)(2,1)S(1)}, bf16[256,1024]{1,0:T(8,128)(2,1)S(1)}, u32[]{:S(2)}, u32[]{:S(2)}) collective-permute-start(bf16[256,1024]{1,0:T(8,128)(2,1)S(1)} %get-tuple-element.88), channel_id=1, source_target_pairs={{0,2},{6,4},{1,3},{7,5},{8,10},{14,12},{9,11},{15,13},{16,18},{22,... | collective-permute-start | bytes 1572872 | tf_op jit(solution)/shard_map/ppermute | solution.py:498
  86.6 0.7 collective-permute-start.22
  87.3 2.3 %project.2 = (f32[256,1536]{1,0:T(8,128)S(1)}, f32[8,128]{1,0:T(8,128)S(1)}) custom-call(bf16[2,256,1024]{2,1,0:T(8,128)(2,1)S(1)} %get-tuple-element.68.refs_0_.refs_1_, bf16[2,256,1024]{2,1,0:T(8,128)(2,1)S(1)} %get-tuple-element.68.refs_0_.refs_1_, bf16[256,1536]{1,0:T(8,128)(2,1)S(1)} %get-tuple-element.59.refs_2_, ...), custom_call_target="tpu_custom_call" | custom-call | flops 1610612736 | bytes 7864320 | tf_op jit(solution)/shard_map/project/pallas_call | solution.py:44
  89.6 5.0 %collective-permute-done.19.refs_0_.refs_1_ = bf16[256,1024]{1,0:T(8,128)(2,1)S(1)} collective-permute-done((bf16[256,1024]{1,0:T(8,128)(2,1)S(1)}, bf16[256,1024]{1,0:T(8,128)(2,1)S(1)}, u32[]{:S(2)}, u32[]{:S(2)}) %collective-permute-start.19) | collective-permute-done | bytes 524320 | tf_op jit(solution)/shard_map/ppermute | solution.py:494
  94.6 2.3 %project.3 = (bf16[256,1536]{1,0:T(8,128)(2,1)S(1)}, f32[8,128]{1,0:T(8,128)S(1)}) custom-call(bf16[256,1024]{1,0:T(8,128)(2,1)S(1)} %collective-permute-done.19.refs_0_.refs_1_, bf16[256,1024]{1,0:T(8,128)(2,1)S(1)} %get-tuple-element.74.refs_0_.refs_1_, bf16[256,1536]{1,0:T(8,128)(2,1)S(1)} %get-tuple-element.59.refs_2_, ...), custom_call_target="tpu_custom_call" | custom-call | flops 1610612736 | bytes 7864320 | tf_op jit(solution)/shard_map/project/pallas_call | solution.py:44
  96.8 1.1 collective-permute-start.20
  98.0 3.5 %collective-permute-start.24 = (bf16[256,1024]{1,0:T(8,128)(2,1)S(1)}, bf16[256,1024]{1,0:T(8,128)(2,1)S(1)}, u32[]{:S(2)}, u32[]{:S(2)}) collective-permute-start(bf16[256,1024]{1,0:T(8,128)(2,1)S(1)} %get-tuple-element.98), channel_id=1, source_target_pairs={{0,2},{2,0},{4,6},{6,4},{1,3},{3,1},{5,7},{7,5},{8,10},{10,8},{12,... | collective-permute-start | bytes 1572872 | tf_op jit(solution)/shard_map/ppermute | solution.py:494
  101.7 0.9 collective-permute-start.25
  102.7 1.5 %collective-permute-done.23.refs_3_ = bf16[256,512]{1,0:T(8,128)(2,1)S(1)} collective-permute-done((bf16[256,512]{1,0:T(8,128)(2,1)S(1)}, bf16[256,512]{1,0:T(8,128)(2,1)S(1)}, u32[]{:S(2)}, u32[]{:S(2)}) %collective-permute-start.23) | collective-permute-done | bytes 262176 | tf_op jit(solution)/shard_map/ppermute | solution.py:494
  104.2 2.7 %weight_parts.3 = (f32[512,1536]{1,0:T(8,128)S(1)}, f32[8,128]{1,0:T(8,128)S(1)}) custom-call(bf16[2,256,1024]{2,1,0:T(8,128)(2,1)S(1)} %get-tuple-element.68.refs_0_.refs_1_, bf16[256,1024]{1,0:T(8,128)(2,1)S(1)} %collective-permute-done.19.refs_0_.refs_1_, bf16[2,256,512]{2,1,0:T(8,128)(2,1)S(1)} %collective-permute-done.15.refs_2_, ...), custom_call_target="tpu_custom_call" | custom-call | flops 1610612736 | bytes 6815744 | tf_op jit(solution)/shard_map/weight_parts/pallas_call | solution.py:44
  106.9 8.4 %collective-permute-done.20.refs_1_ = bf16[256,1536]{1,0:T(8,128)(2,1)S(1)} collective-permute-done((bf16[256,1536]{1,0:T(8,128)(2,1)S(1)}, bf16[256,1536]{1,0:T(8,128)(2,1)S(1)}, u32[]{:S(2)}, u32[]{:S(2)}) %collective-permute-start.20) | collective-permute-done | bytes 786464 | tf_op jit(solution)/shard_map/ppermute | solution.py:494
  115.3 1.0 plus.7
  116.4 1.8 %weight_total.1 = (bf16[512,1536]{1,0:T(8,128)(2,1)S(1)}, bf16[1024,1536]{1,0:T(8,128)(2,1)}, f32[8,128]{1,0:T(8,128)S(1)}) custom-call(f32[512,1536]{1,0:T(8,128)S(1)} %get-tuple-element.100.refs_0_, bf16[512,1536]{1,0:T(8,128)(2,1)S(1)} %collective-permute-done.26.refs_1_, f32[8,128]{1,0:T(8,128)S(1)} %get-tuple-element.102.refs_2_, ...), custom_call_target="tpu_custom_call" | custom-call | bytes 7864320 | tf_op jit(solution)/shard_map/weight_total/pallas_call | solution.py:44
  118.2 4.5 %attention_grads.1 = (bf16[256,1024]{1,0:T(8,128)(2,1)}, bf16[256,1024]{1,0:T(8,128)(2,1)}, bf16[256,1024]{1,0:T(8,128)(2,1)}, f32[8,128]{1,0:T(8,128)S(1)}) custom-call(bf16[256,1024]{1,0:T(8,128)(2,1)S(1)} %copy-done.1, bf16[256,1024]{1,0:T(8,128)(2,1)S(1)} %copy-done.2, bf16[256,1024]{1,0:T(8,128)(2,1)S(1)} %copy-done.3, ...), custom_call_target="tpu_custom_call" | custom-call | flops 671088640 | bytes 4718592 | tf_op jit(solution)/shard_map/attention_grads/pallas_call | solution.py:44
  122.8 1.2 weight_fill.1
  (45 shorter events, 0.9 us)
Async XLA Ops:
  0.6 6.1 %copy-start.4 = (bf16[256,1536]{1,0:T(8,128)(2,1)S(1)}, bf16[256,1536]{1,0:T(8,128)(2,1)}, u32[]{:S(2)}) copy-start(bf16[256,1536]{1,0:T(8,128)(2,1)} %refs_4_.5) | copy-start | bytes 2359300
  0.6 6.1 %copy-start.1 = (bf16[256,1024]{1,0:T(8,128)(2,1)S(1)}, bf16[256,1024]{1,0:T(8,128)(2,1)}, u32[]{:S(2)}) copy-start(bf16[256,1024]{1,0:T(8,128)(2,1)} %refs_0_.7) | copy-start | bytes 1572868
  0.7 6.1 %copy-start.2 = (bf16[256,1024]{1,0:T(8,128)(2,1)S(1)}, bf16[256,1024]{1,0:T(8,128)(2,1)}, u32[]{:S(2)}) copy-start(bf16[256,1024]{1,0:T(8,128)(2,1)} %refs_1_.3) | copy-start | bytes 1572868
  0.7 6.1 %copy-start.3 = (bf16[256,1024]{1,0:T(8,128)(2,1)S(1)}, bf16[256,1024]{1,0:T(8,128)(2,1)}, u32[]{:S(2)}) copy-start(bf16[256,1024]{1,0:T(8,128)(2,1)} %refs_2_.3) | copy-start | bytes 1572868
  0.7 22.0 %collective-permute-start.4 = (bf16[256,1536]{1,0:T(8,128)(2,1)}, bf16[256,1536]{1,0:T(8,128)(2,1)S(1)}, u32[]{:S(2)}, u32[]{:S(2)}) collective-permute-start(bf16[256,1536]{1,0:T(8,128)(2,1)} %refs_4_.5), channel_id=1, source_target_pairs={{0,16},{8,24},{16,0},{24,8},{1,17},{9,25},{17,1},{25,9},{2,18},{10... | collective-permute-start | bytes 2359304 | tf_op jit(solution)/shard_map/ppermute | solution.py:494
  5.2 22.6 %copy-start = (bf16[1024,1536]{1,0:T(8,128)(2,1)S(1)}, bf16[1024,1536]{1,0:T(8,128)(2,1)}, u32[]{:S(2)}) copy-start(bf16[1024,1536]{1,0:T(8,128)(2,1)} %refs_7_.3) | copy-start | bytes 9437188
  5.2 19.1 %collective-permute-start.5 = (bf16[256,1536]{1,0:T(8,128)(2,1)S(1)}, bf16[256,1536]{1,0:T(8,128)(2,1)S(1)}, u32[]{:S(2)}, u32[]{:S(2)}) collective-permute-start(bf16[256,1536]{1,0:T(8,128)(2,1)S(1)} %get-tuple-element.112), channel_id=1, source_target_pairs={{0,8},{8,0},{16,24},{24,16},{1,9},{9,1},{17,25},{25,17},{2,10},{10... | collective-permute-start | bytes 2359304 | tf_op jit(solution)/shard_map/ppermute | solution.py:494
  6.8 17.5 %collective-permute-start.6 = (bf16[256,1536]{1,0:T(8,128)(2,1)S(1)}, bf16[256,1536]{1,0:T(8,128)(2,1)S(1)}, u32[]{:S(2)}, u32[]{:S(2)}) collective-permute-start(bf16[256,1536]{1,0:T(8,128)(2,1)S(1)} %copy-done.4), channel_id=1, source_target_pairs={{0,1},{1,0},{2,3},{3,2},{4,5},{5,4},{6,7},{7,6},{8,9},{9,8},{10,11... | collective-permute-start | bytes 2359304 | tf_op jit(solution)/shard_map/ppermute | solution.py:494
  8.2 14.4 %collective-permute-start = (bf16[256,1024]{1,0:T(8,128)(2,1)S(1)}, bf16[256,1024]{1,0:T(8,128)(2,1)S(1)}, u32[]{:S(2)}, u32[]{:S(2)}) collective-permute-start(bf16[256,1024]{1,0:T(8,128)(2,1)S(1)} %get-tuple-element.58.refs_0_), channel_id=1, source_target_pairs={{0,2},{2,0},{4,6},{6,4},{1,3},{3,1},{5,7},{7,5},{8,10},{10,8},{12,... | collective-permute-start | bytes 1572872 | tf_op jit(solution)/shard_map/ppermute | solution.py:494
  9.9 12.7 %collective-permute-start.1 = (bf16[256,1024]{1,0:T(8,128)(2,1)S(1)}, bf16[256,1024]{1,0:T(8,128)(2,1)S(1)}, u32[]{:S(2)}, u32[]{:S(2)}) collective-permute-start(bf16[256,1024]{1,0:T(8,128)(2,1)S(1)} %get-tuple-element.58.refs_0_), channel_id=1, source_target_pairs={{2,4},{4,2},{3,5},{5,3},{10,12},{12,10},{11,13},{13,11},{18,20},{2... | collective-permute-start | bytes 1572872 | tf_op jit(solution)/shard_map/ppermute | solution.py:498
  24.3 3.5 %collective-permute-start.7 = (bf16[256,1536]{1,0:T(8,128)(2,1)S(1)}, bf16[256,1536]{1,0:T(8,128)(2,1)S(1)}, u32[]{:S(2)}, u32[]{:S(2)}) collective-permute-start(bf16[256,1536]{1,0:T(8,128)(2,1)S(1)} %get-tuple-element.59.refs_2_), channel_id=1, source_target_pairs={{0,1},{1,0},{2,3},{3,2},{4,5},{5,4},{6,7},{7,6},{8,9},{9,8},{10,11... | collective-permute-start | bytes 2359304 | tf_op jit(solution)/shard_map/ppermute | solution.py:494
  24.3 20.0 %collective-permute-start.9 = (bf16[256,1536]{1,0:T(8,128)(2,1)S(1)}, bf16[256,1536]{1,0:T(8,128)(2,1)S(1)}, u32[]{:S(2)}, u32[]{:S(2)}) collective-permute-start(bf16[256,1536]{1,0:T(8,128)(2,1)S(1)} %get-tuple-element.111), channel_id=1, source_target_pairs={{0,8},{8,0},{16,24},{24,16},{1,9},{9,1},{17,25},{25,17},{2,10},{10... | collective-permute-start | bytes 2359304 | tf_op jit(solution)/shard_map/ppermute | solution.py:494
  25.8 5.8 %collective-permute-start.3 = (bf16[256,1024]{1,0:T(8,128)(2,1)S(1)}, bf16[256,1024]{1,0:T(8,128)(2,1)S(1)}, u32[]{:S(2)}, u32[]{:S(2)}) collective-permute-start(bf16[256,1024]{1,0:T(8,128)(2,1)S(1)} %collective-permute-done.refs_1_), channel_id=1, source_target_pairs={{2,4},{4,2},{3,5},{5,3},{10,12},{12,10},{11,13},{13,11},{18,20},{2... | collective-permute-start | bytes 1572872 | tf_op jit(solution)/shard_map/ppermute | solution.py:498
  26.5 18.3 %collective-permute-start.2 = (bf16[256,1024]{1,0:T(8,128)(2,1)S(1)}, bf16[256,1024]{1,0:T(8,128)(2,1)S(1)}, u32[]{:S(2)}, u32[]{:S(2)}) collective-permute-start(bf16[256,1024]{1,0:T(8,128)(2,1)S(1)} %collective-permute-done.1.refs_2_.refs_5_), channel_id=1, source_target_pairs={{2,0},{4,6},{3,1},{5,7},{10,8},{12,14},{11,9},{13,15},{18,16},{20,... | collective-permute-start | bytes 1572872 | tf_op jit(solution)/shard_map/ppermute | solution.py:498
  30.9 30.8 %collective-permute-start.12 = (bf16[256,1536]{1,0:T(8,128)(2,1)S(1)}, bf16[256,1536]{1,0:T(8,128)(2,1)S(1)}, u32[]{:S(2)}, u32[]{:S(2)}) collective-permute-start(bf16[256,1536]{1,0:T(8,128)(2,1)S(1)} %get-tuple-element.66), channel_id=1, source_target_pairs={{0,16},{8,24},{16,0},{24,8},{1,17},{9,25},{17,1},{25,9},{2,18},{10... | collective-permute-start | bytes 2359304 | tf_op jit(solution)/shard_map/ppermute | solution.py:494
  45.2 1.9 %collective-permute-start.10 = (bf16[128,1536]{1,0:T(8,128)(2,1)S(1)}, bf16[128,1536]{1,0:T(8,128)(2,1)S(1)}, u32[]{:S(2)}, u32[]{:S(2)}) collective-permute-start(bf16[128,1536]{1,0:T(8,128)(2,1)S(1)} %get-tuple-element.63), channel_id=1, source_target_pairs={{0,1},{1,0},{2,3},{3,2},{4,5},{5,4},{6,7},{7,6},{8,9},{9,8},{10,11... | collective-permute-start | bytes 1179656 | tf_op jit(solution)/shard_map/ppermute | solution.py:494
  45.3 2.3 %collective-permute-start.11 = (bf16[128,1536]{1,0:T(8,128)(2,1)S(1)}, bf16[128,1536]{1,0:T(8,128)(2,1)S(1)}, u32[]{:S(2)}, u32[]{:S(2)}) collective-permute-start(bf16[128,1536]{1,0:T(8,128)(2,1)S(1)} %get-tuple-element.64), channel_id=1, source_target_pairs={{0,1},{1,0},{2,3},{3,2},{4,5},{5,4},{6,7},{7,6},{8,9},{9,8},{10,11... | collective-permute-start | bytes 1179656 | tf_op jit(solution)/shard_map/ppermute | solution.py:494
  45.8 15.9 %collective-permute-start.8 = (bf16[256,1024]{1,0:T(8,128)(2,1)S(1)}, bf16[256,1024]{1,0:T(8,128)(2,1)S(1)}, u32[]{:S(2)}, u32[]{:S(2)}) collective-permute-start(bf16[256,1024]{1,0:T(8,128)(2,1)S(1)} %get-tuple-element.61.refs_1_.refs_3_), channel_id=1, source_target_pairs={{2,0},{4,6},{3,1},{5,7},{10,8},{12,14},{11,9},{13,15},{18,16},{20,... | collective-permute-start | bytes 1572872 | tf_op jit(solution)/shard_map/ppermute | solution.py:498
  48.9 12.8 %collective-permute-start.13 = (bf16[256,512]{1,0:T(8,128)(2,1)S(1)}, bf16[256,512]{1,0:T(8,128)(2,1)S(1)}, u32[]{:S(2)}, u32[]{:S(2)}) collective-permute-start(bf16[256,512]{1,0:T(8,128)(2,1)S(1)} %get-tuple-element.67), channel_id=1, source_target_pairs={{0,16},{8,24},{16,0},{24,8},{1,17},{9,25},{17,1},{25,9},{2,18},{10... | collective-permute-start | bytes 786440 | tf_op jit(solution)/shard_map/ppermute | solution.py:494
  62.1 13.3 %collective-permute-start.14 = (bf16[256,1024]{1,0:T(8,128)(2,1)S(1)}, bf16[256,1024]{1,0:T(8,128)(2,1)S(1)}, u32[]{:S(2)}, u32[]{:S(2)}) collective-permute-start(bf16[256,1024]{1,0:T(8,128)(2,1)S(1)} %get-tuple-element.69), channel_id=1, source_target_pairs={{0,16},{8,24},{16,0},{24,8},{1,17},{9,25},{17,1},{25,9},{2,18},{10... | collective-permute-start | bytes 1572872 | tf_op jit(solution)/shard_map/ppermute | solution.py:494
  62.8 13.9 %collective-permute-start.17 = (bf16[256,1536]{1,0:T(8,128)(2,1)S(1)}, bf16[256,1536]{1,0:T(8,128)(2,1)S(1)}, u32[]{:S(2)}, u32[]{:S(2)}) collective-permute-start(bf16[256,1536]{1,0:T(8,128)(2,1)S(1)} %get-tuple-element.77), channel_id=1, source_target_pairs={{0,1},{1,0},{2,3},{3,2},{4,5},{5,4},{6,7},{7,6},{8,9},{9,8},{10,11... | collective-permute-start | bytes 2359304 | tf_op jit(solution)/shard_map/ppermute | solution.py:494
  63.2 13.4 %collective-permute-start.18 = (bf16[256,1024]{1,0:T(8,128)(2,1)S(1)}, bf16[256,1024]{1,0:T(8,128)(2,1)S(1)}, u32[]{:S(2)}, u32[]{:S(2)}) collective-permute-start(bf16[256,1024]{1,0:T(8,128)(2,1)S(1)} %get-tuple-element.79.refs_0_), channel_id=1, source_target_pairs={{0,2},{6,4},{1,3},{7,5},{8,10},{14,12},{9,11},{15,13},{16,18},{22,... | collective-permute-start | bytes 1572872 | tf_op jit(solution)/shard_map/ppermute | solution.py:498
  64.7 12.1 %collective-permute-start.15 = (bf16[2,256,512]{2,1,0:T(8,128)(2,1)S(1)}, bf16[2,256,512]{2,1,0:T(8,128)(2,1)S(1)}, u32[]{:S(2)}, u32[]{:S(2)}) collective-permute-start(bf16[2,256,512]{2,1,0:T(8,128)(2,1)S(1)} %get-tuple-element.75), channel_id=1, source_target_pairs={{0,1},{1,0},{2,3},{3,2},{4,5},{5,4},{6,7},{7,6},{8,9},{9,8},{10,11... | collective-permute-start | bytes 1572872 | tf_op jit(solution)/shard_map/ppermute | solution.py:494
  75.4 1.6 %collective-permute-start.16 = (bf16[256,512]{1,0:T(8,128)(2,1)S(1)}, bf16[256,512]{1,0:T(8,128)(2,1)S(1)}, u32[]{:S(2)}, u32[]{:S(2)}) collective-permute-start(bf16[256,512]{1,0:T(8,128)(2,1)S(1)} %get-tuple-element.76), channel_id=1, source_target_pairs={{0,1},{1,0},{2,3},{3,2},{4,5},{5,4},{6,7},{7,6},{8,9},{9,8},{10,11... | collective-permute-start | bytes 786440 | tf_op jit(solution)/shard_map/ppermute | solution.py:494
  79.6 36.8 %collective-permute-start.26 = (bf16[512,1536]{1,0:T(8,128)(2,1)S(1)}, bf16[512,1536]{1,0:T(8,128)(2,1)S(1)}, u32[]{:S(2)}, u32[]{:S(2)}) collective-permute-start(bf16[512,1536]{1,0:T(8,128)(2,1)S(1)} %get-tuple-element.101), channel_id=1, source_target_pairs={{0,8},{8,0},{16,24},{24,16},{1,9},{9,1},{17,25},{25,17},{2,10},{10... | collective-permute-start | bytes 4718600 | tf_op jit(solution)/shard_map/ppermute | solution.py:494
  80.9 13.7 %collective-permute-start.19 = (bf16[256,1024]{1,0:T(8,128)(2,1)S(1)}, bf16[256,1024]{1,0:T(8,128)(2,1)S(1)}, u32[]{:S(2)}, u32[]{:S(2)}) collective-permute-start(bf16[256,1024]{1,0:T(8,128)(2,1)S(1)} %get-tuple-element.85), channel_id=1, source_target_pairs={{0,16},{8,24},{16,0},{24,8},{1,17},{9,25},{17,1},{25,9},{2,18},{10... | collective-permute-start | bytes 1572872 | tf_op jit(solution)/shard_map/ppermute | solution.py:494
  82.2 19.4 %collective-permute-start.21 = (bf16[256,1024]{1,0:T(8,128)(2,1)S(1)}, bf16[256,1024]{1,0:T(8,128)(2,1)S(1)}, u32[]{:S(2)}, u32[]{:S(2)}) collective-permute-start(bf16[256,1024]{1,0:T(8,128)(2,1)S(1)} %get-tuple-element.88), channel_id=1, source_target_pairs={{0,2},{6,4},{1,3},{7,5},{8,10},{14,12},{9,11},{15,13},{16,18},{22,... | collective-permute-start | bytes 1572872 | tf_op jit(solution)/shard_map/ppermute | solution.py:498
  86.6 11.3 %collective-permute-start.22 = (bf16[256,1024]{1,0:T(8,128)(2,1)S(1)}, bf16[256,1024]{1,0:T(8,128)(2,1)S(1)}, u32[]{:S(2)}, u32[]{:S(2)}) collective-permute-start(bf16[256,1024]{1,0:T(8,128)(2,1)S(1)} %get-tuple-element.88), channel_id=1, source_target_pairs={{2,4},{4,2},{3,5},{5,3},{10,12},{12,10},{11,13},{13,11},{18,20},{2... | collective-permute-start | bytes 1572872 | tf_op jit(solution)/shard_map/ppermute | solution.py:498
  96.8 18.5 %collective-permute-start.20 = (bf16[256,1536]{1,0:T(8,128)(2,1)S(1)}, bf16[256,1536]{1,0:T(8,128)(2,1)S(1)}, u32[]{:S(2)}, u32[]{:S(2)}) collective-permute-start(bf16[256,1536]{1,0:T(8,128)(2,1)S(1)} %get-tuple-element.87), channel_id=1, source_target_pairs={{0,16},{8,24},{16,0},{24,8},{1,17},{9,25},{17,1},{25,9},{2,18},{10... | collective-permute-start | bytes 2359304 | tf_op jit(solution)/shard_map/ppermute | solution.py:494
  98.0 18.3 %collective-permute-start.24 = (bf16[256,1024]{1,0:T(8,128)(2,1)S(1)}, bf16[256,1024]{1,0:T(8,128)(2,1)S(1)}, u32[]{:S(2)}, u32[]{:S(2)}) collective-permute-start(bf16[256,1024]{1,0:T(8,128)(2,1)S(1)} %get-tuple-element.98), channel_id=1, source_target_pairs={{0,2},{2,0},{4,6},{6,4},{1,3},{3,1},{5,7},{7,5},{8,10},{10,8},{12,... | collective-permute-start | bytes 1572872 | tf_op jit(solution)/shard_map/ppermute | solution.py:494
  101.7 14.6 %collective-permute-start.25 = (bf16[256,1024]{1,0:T(8,128)(2,1)S(1)}, bf16[256,1024]{1,0:T(8,128)(2,1)S(1)}, u32[]{:S(2)}, u32[]{:S(2)}) collective-permute-start(bf16[256,1024]{1,0:T(8,128)(2,1)S(1)} %get-tuple-element.99), channel_id=1, source_target_pairs={{2,4},{4,2},{3,5},{5,3},{10,12},{12,10},{11,13},{13,11},{18,20},{2... | collective-permute-start | bytes 1572872 | tf_op jit(solution)/shard_map/ppermute | solution.py:498
  102.6 1.6 %collective-permute-start.23 = (bf16[256,512]{1,0:T(8,128)(2,1)S(1)}, bf16[256,512]{1,0:T(8,128)(2,1)S(1)}, u32[]{:S(2)}, u32[]{:S(2)}) collective-permute-start(bf16[256,512]{1,0:T(8,128)(2,1)S(1)} %get-tuple-element.93), channel_id=1, source_target_pairs={{0,1},{1,0},{2,3},{3,2},{4,5},{5,4},{6,7},{7,6},{8,9},{9,8},{10,11... | collective-permute-start | bytes 786440 | tf_op jit(solution)/shard_map/ppermute | solution.py:494
  118.1 4.6 %collective-permute-start.27 = (bf16[512,1536]{1,0:T(8,128)(2,1)S(1)}, bf16[512,1536]{1,0:T(8,128)(2,1)S(1)}, u32[]{:S(2)}, u32[]{:S(2)}) collective-permute-start(bf16[512,1536]{1,0:T(8,128)(2,1)S(1)} %get-tuple-element.107), channel_id=1, source_target_pairs={{0,1},{1,0},{2,3},{3,2},{4,5},{5,4},{6,7},{7,6},{8,9},{9,8},{10,11... | collective-permute-start | bytes 4718600 | tf_op jit(solution)/shard_map/ppermute | solution.py:494

commit v6 on v5

--- a/solution.py
+++ b/solution.py
@@ -110,8 +110,7 @@
         o_ref[:, cols] = dot(prob, v_ref[:, cols], TN).astype(BF16)
 
 
-def backward_head(q, k, v, g):
-    prob = softmax_t(q, k)
+def backward_head(q, k, v, g, prob):
     grad_prob = dot(v, g, NT)
     delta = jnp.sum(prob * grad_prob, axis=0, keepdims=True)
     grad_score = (prob * (grad_prob - delta) * SCALE).astype(BF16)
@@ -125,16 +124,17 @@
 def backward_kernel(q_ref, k_ref, v_ref, g_ref, *grads):
     for lo in range(0, q_ref.shape[1], HSZ):
         cols = slice(lo, lo + HSZ)
-        got = backward_head(q_ref[:, cols], k_ref[:, cols], v_ref[:, cols], g_ref[:, cols])
+        q, k = q_ref[:, cols], k_ref[:, cols]
+        got = backward_head(q, k, v_ref[:, cols], g_ref[:, cols], softmax_t(q, k))
         for ref, value in zip(grads, got):
             ref[:, cols] = value
 
 
-def backward_sum_kernel(q_ref, k_ref, v_ref, *refs):
+def backward_sum_kernel(q_ref, k_ref, v_ref, prob_ref, *refs):
     for lo in range(0, q_ref.shape[1], HSZ):
         cols = slice(lo, lo + HSZ)
         g = sum(ref[:, cols].astype(F32) for ref in refs[:-3]).astype(BF16)
-        got = backward_head(q_ref[:, cols], k_ref[:, cols], v_ref[:, cols], g)
+        got = backward_head(q_ref[:, cols], k_ref[:, cols], v_ref[:, cols], g, prob_ref[lo // HSZ])
         for ref, value in zip(refs[-3:], got):
             ref[:, cols] = value
 
@@ -175,17 +175,35 @@
     )(q, k, v, g)
 
 
-def attention_grads_sum(q, k, v, terms, after):
+def weights_kernel(q_ref, k_ref, out_ref):
+    for i in range(out_ref.shape[0]):
+        cols = slice(i * HSZ, (i + 1) * HSZ)
+        out_ref[i] = softmax_t(q_ref[:, cols], k_ref[:, cols])
+
+
+def softmax_weights(q, k, after):
     tokens, width = q.shape
-    wide = head_width(width)
-    spec = pl.BlockSpec((PATCH, wide), lambda i, h: (i, h))
+    return call(
+        weights_kernel,
+        (q, k),
+        [VMEM] * 2,
+        after,
+        out_specs=VMEM,
+        out_shape=like((width // HSZ, tokens, tokens), F32),
+        cost_estimate=cost(tokens * tokens * width, 4 * tokens * width),
+        name="softmax_weights",
+    )
+
+
+def attention_grads_sum(q, k, v, prob, terms, after):
+    tokens, width = q.shape
     return call(
         backward_sum_kernel,
-        (q, k, v, *terms),
-        [spec] * (3 + len(terms)),
-        after,
-        grid=(tokens // PATCH, width // wide),
-        out_specs=[spec] * 3,
+        (q, k, v, prob, *terms),
+        [VMEM] * (4 + len(terms)),
+        after,
+        grid=(1,),
+        out_specs=[pl.BlockSpec(q.shape, lambda i: (0, 0))] * 3,
         out_shape=[like(q.shape)] * 3,
         cost_estimate=cost(5 * tokens * PATCH * width, 18 * tokens * width),
         name="attention_grads",
@@ -357,20 +375,25 @@
 
 
 def weight_parts_kernel(held_ref, got_ref, held_core_ref, got_core_ref, *refs):
-    cots, out_ref = refs[:4], refs[4]
-    half = out_ref.shape[0]
+    cots, outs = refs[:4], refs[4:]
+    half = held_core_ref.shape[2]
     cols = pl.ds(pl.multiple_of(position()[1] * half, half), half)
     left = [held_ref[0, :, cols], got_ref[:, cols], held_core_ref[0], got_core_ref[...]]
     right = jnp.concatenate([ref[...] for ref in cots], axis=0)
-    out_ref[...] = dot(jnp.concatenate(left, axis=0), right, TN).astype(out_ref.dtype)
-
-
-def weight_parts(j, heads, cots, dtype, after):
+    total = dot(jnp.concatenate(left, axis=0), right, TN)
+    at = 0
+    for ref in outs:
+        ref[...] = total[at : at + ref.shape[0]].astype(ref.dtype)
+        at += ref.shape[0]
+
+
+def weight_parts(j, heads, cots, dtype, parts, after):
     tokens, rows = heads[1].shape
     depth = cots[0].shape[1]
     wide = depth // 3 if depth % 384 == 0 else depth
     pair = lambda width: pl.BlockSpec((1, tokens, width), lambda i: (j, 0, 0))
     whole = lambda width: pl.BlockSpec((tokens, width), lambda i: (0, 0))
+    sizes = [n * rows // 64 for n in parts]
     return call(
         weight_parts_kernel,
         (*heads, *cots),
@@ -378,48 +401,39 @@
         + [pl.BlockSpec((tokens, wide), lambda i: (0, i))] * 4,
         after,
         grid=(depth // wide,),
-        out_specs=pl.BlockSpec((rows // 2, wide), lambda i: (0, i)),
-        out_shape=like((rows // 2, depth), dtype),
+        out_specs=[pl.BlockSpec((size, wide), lambda i: (0, i)) for size in sizes],
+        out_shape=[like((size, depth), dtype) for size in sizes],
         cost_estimate=cost(2 * tokens * rows * depth, 8 * tokens * (rows + depth) + rows * depth),
         name="weight_parts",
     )
 
 
-def weight_total(own, away, factor, rows, after):
+def weight_total(own, aways, factor, rows, after):
     half, depth = own.shape
-    cut = half // 2
-
-    def kernel(own_ref, away_ref, total_ref, out_ref, own, away, total, sems):
-        at = position()[1] * half
-        loads, stores = [], []
-        for i in (0, 1):
-            part = pl.ds(i * cut, cut)
-            loads.append(
-                copies([(own_ref.at[part], own.at[part]), (away_ref.at[part], away.at[part])], sems.at[i])
-            )
-        for i, load in enumerate(loads):
-            part = pl.ds(i * cut, cut)
-            for copy in load:
-                copy.wait()
-            total[part] = ((own[part] + away[part].astype(F32)) * factor).astype(BF16)
-            place = out_ref.at[pl.ds(pl.multiple_of(at + i * cut, cut), cut)]
-            stores += copies([(total.at[part], total_ref.at[part]), (total.at[part], place)], sems.at[2 + i])
+    starts = [sum(a.shape[0] for a in aways[:i]) for i in range(len(aways))]
+
+    def kernel(own_ref, *refs):
+        away_refs, (total_ref, out_ref, sems) = refs[: len(aways)], refs[len(aways) :]
+        base = position()[1] * half
+        stores = []
+        for i, (start, ref) in enumerate(zip(starts, away_refs)):
+            size = ref.shape[0]
+            part = pl.ds(start, size)
+            total_ref[part] = ((own_ref[part] + ref[...].astype(F32)) * factor).astype(BF16)
+            target = out_ref.at[pl.ds(pl.multiple_of(base + start, 16), size)]
+            stores.append(pltpu.make_async_copy(total_ref.at[part], target, sems.at[i]))
+            stores[-1].start()
         for copy in stores:
             copy.wait()
 
     return call(
         kernel,
-        (own, away),
-        [ANY] * 2,
-        after,
-        out_specs=[ANY] * 2,
+        (own, *aways),
+        [VMEM] * (1 + len(aways)),
+        after,
+        out_specs=[VMEM, ANY],
         out_shape=[like((half, depth)), like((rows, depth))],
-        scratch_shapes=[
-            pltpu.VMEM((half, depth), F32),
-            pltpu.VMEM((half, depth), BF16),
-            pltpu.VMEM((half, depth), BF16),
-            pltpu.SemaphoreType.DMA((4, 2)),
-        ],
+        scratch_shapes=[pltpu.SemaphoreType.DMA((len(aways),))],
         cost_estimate=cost(0, 10 * half * depth),
         name="weight_total",
     )
@@ -539,22 +553,25 @@
     got_three = tie(got_three, done)
     got_two = flip(tie(away_two, got_three), "row", 2)
     half, done = core_half(got_three)
+    away, done = weight_parts(1, [held, got_three, held_core, flip(half, "rep", 1)], cots, BF16, (25, 7), [done])
+    away = [flip(a, "row", 1) for a in away]
     second, done = plus(p2, far, [done])
     out, cross = line(second, (0, 1), (3, 2)), line(second, (1, 2), (2, 1))
-    away, done = weight_parts(1, [held, got_three, held_core, flip(half, "rep", 1)], cots, BF16, [done])
-    away = flip(away, "row", 1)
     besides = [*beside0, *beside1]
     projected, done = project([held, held], out_weight, besides, F32, [done])
     sent, done = project([got_two, got_three], out_weight, besides, BF16, [done])
     from_far = flip(sent, "row", 2)
+    prob, done = softmax_weights(queries, key_vectors, [done])
     near, done = plus(p1, cross, [done])
     mid, done = plus(p3, out, [done])
     near, mid = flip(near, "col", 1), line(mid, (1, 2), (2, 1))
     half, done = core_half(got_two, [done])
-    total, done = weight_parts(0, [held, got_two, held_core, flip(half, "rep", 1)], cots, F32, [done])
+    (total,), done = weight_parts(0, [held, got_two, held_core, flip(half, "rep", 1)], cots, F32, (32,), [done])
     projected, done = plus(projected, from_far, [done])
     (total, grad_weight), done = weight_total(total, away, factor, rows, [done, near, mid])
-    grads, done = attention_grads_sum(queries, key_vectors, value_vectors, (p0, near, mid), [done])
+    grads, done = attention_grads_sum(
+        queries, key_vectors, value_vectors, prob, (p0, near, mid), [done]
+    )
     grad_weight, _ = weight_fill(flip(total, "rep", 1), grad_weight, [done])
     return (projected, *grads, grad_weight)
 

time: 124 us -> 123 us (level)
  waiting for transfers between devices: 65.9 us -> 62.3 us
  starting transfers between devices: 29.7 us -> 32.5 us
    ppermute x20 -> x21, waiting for transfers between devices: 52.1 us -> 46.3 us  [flip(): lax.ppermute(x, axis, [(i, i ^ bit) for i in range(lax.axis_size(axis))])]
    ppermute x8, waiting for transfers between devices: 13.8 us -> 16 us  [line(): return lax.ppermute(x, 'col', pairs)]
    ppermute x20 -> x21, starting transfers between devices: 18.4 us -> 20 us  [flip(): lax.ppermute(x, axis, [(i, i ^ bit) for i in range(lax.axis_size(axis))])]
    pallas_call x25 -> x26, Pallas kernels: 25.7 us -> 25.6 us  [call(): pl.pallas_call(body, in_specs=[*in_specs, *[ANY] * len(after)], out_specs...]
  transfers between devices with their start and end apart: 28 -> 29, of which waited for: 12 -> 10; matrix products, arithmetic and copies ran while one was open for 1% -> 1% of each run, Pallas kernels for 16% -> 18%
where the time goes in v6:
time: 123 us
  waiting for transfers between devices  62.3 us (51%)
  starting transfers between devices  32.5 us (26%)
  Pallas kernels  25.6 us (21%)
  local copies, waits for them, and re-layouts  1.55 us (1%)
    ppermute x21, waiting for transfers between devices, flip(): lax.ppermute(x, axis, [(i, i ^ bit) for i in range(lax.axis_size(axis))])  46.3 us
    pallas_call x26, Pallas kernels, call(): pl.pallas_call(body, in_specs=[*in_specs, *[ANY] * len(after)], out_specs...  25.6 us
    ppermute x21, starting transfers between devices, flip(): lax.ppermute(x, axis, [(i, i ^ bit) for i in range(lax.axis_size(axis))])  20 us
    ppermute x8, waiting for transfers between devices, line(): return lax.ppermute(x, 'col', pairs)  16 us
    ppermute x8, starting transfers between devices, line(): return lax.ppermute(x, 'col', pairs)  12.5 us
  transfers between devices with their start and end apart: 29, of which 10 were waited for; matrix products, arithmetic and copies ran while one was open for 1% of the time, Pallas kernels for 18%

profile of v6, /device:TPU:0, one launch (start us, length us, event | category | flops | bytes accessed | tf_op | source)
XLA Modules:
  0.0 123.1 jit_solution(4272379894334520652)
XLA Ops:
  0.7 0.5 collective-permute-start.6
  1.2 2.6 %collective-permute-start.4 = (bf16[256,1536]{1,0:T(8,128)(2,1)}, bf16[256,1536]{1,0:T(8,128)(2,1)S(1)}, u32[]{:S(2)}, u32[]{:S(2)}) collective-permute-start(bf16[256,1536]{1,0:T(8,128)(2,1)} %refs_4_.5), channel_id=1, source_target_pairs={{0,16},{8,24},{16,0},{24,8},{1,17},{9,25},{17,1},{25,9},{2,18},{10... | collective-permute-start | bytes 2359304 | tf_op jit(solution)/shard_map/ppermute | solution.py:508
  3.8 1.5 %constant_dynamic-slice_fusion = (bf16[256,1536]{1,0:T(8,128)(2,1)S(1)}, bf16[256,1536]{1,0:T(8,128)(2,1)S(1)}) fusion(bf16[1024,1536]{1,0:T(8,128)(2,1)} %refs_7_.3, s32[]{:T(128)S(6)} %select_n.7, s32[]{:T(128)S(6)} %select_n.6), kind=kLoop, calls=%fused_computation | loop fusion | bytes 3145736 | tf_op jit(solution)/shard_map/dynamic_slice | solution.py:528
  5.2 1.6 %collective-permute-start.5 = (bf16[256,1536]{1,0:T(8,128)(2,1)S(1)}, bf16[256,1536]{1,0:T(8,128)(2,1)S(1)}, u32[]{:S(2)}, u32[]{:S(2)}) collective-permute-start(bf16[256,1536]{1,0:T(8,128)(2,1)S(1)} %get-tuple-element.118), channel_id=1, source_target_pairs={{0,8},{8,0},{16,24},{24,16},{1,9},{9,1},{17,25},{25,17},{2,10},{10... | collective-permute-start | bytes 2359304 | tf_op jit(solution)/shard_map/ppermute | solution.py:508
  6.8 1.5 %attention.1 = (bf16[256,1024]{1,0:T(8,128)(2,1)S(1)}, f32[8,128]{1,0:T(8,128)}) custom-call(bf16[256,1024]{1,0:T(8,128)(2,1)S(1)} %copy-done.1, bf16[256,1024]{1,0:T(8,128)(2,1)S(1)} %copy-done.2, bf16[256,1024]{1,0:T(8,128)(2,1)S(1)} %copy-done.3), custom_call_target="tpu_custom_call" | custom-call | flops 268435456 | bytes 2097152 | tf_op jit(solution)/shard_map/attention/pallas_call | solution.py:44
  8.3 0.8 collective-permute-start.1
  9.1 4.6 %collective-permute-start = (bf16[256,1024]{1,0:T(8,128)(2,1)S(1)}, bf16[256,1024]{1,0:T(8,128)(2,1)S(1)}, u32[]{:S(2)}, u32[]{:S(2)}) collective-permute-start(bf16[256,1024]{1,0:T(8,128)(2,1)S(1)} %get-tuple-element.61.refs_0_), channel_id=1, source_target_pairs={{0,2},{2,0},{4,6},{6,4},{1,3},{3,1},{5,7},{7,5},{8,10},{10,8},{12,... | collective-permute-start | bytes 1572872 | tf_op jit(solution)/shard_map/ppermute | solution.py:508
  13.7 11.7 %collective-permute-done.refs_1_ = bf16[256,1024]{1,0:T(8,128)(2,1)S(1)} collective-permute-done((bf16[256,1024]{1,0:T(8,128)(2,1)S(1)}, bf16[256,1024]{1,0:T(8,128)(2,1)S(1)}, u32[]{:S(2)}, u32[]{:S(2)}) %collective-permute-start) | collective-permute-done | bytes 524320 | tf_op jit(solution)/shard_map/ppermute | solution.py:508
  25.5 0.9 collective-permute-start.9
  26.4 0.7 collective-permute-start.3
  27.1 1.3 %collective-permute-start.2 = (bf16[256,1024]{1,0:T(8,128)(2,1)S(1)}, bf16[256,1024]{1,0:T(8,128)(2,1)S(1)}, u32[]{:S(2)}, u32[]{:S(2)}) collective-permute-start(bf16[256,1024]{1,0:T(8,128)(2,1)S(1)} %collective-permute-done.1.refs_2_.refs_5_), channel_id=1, source_target_pairs={{2,0},{4,6},{3,1},{5,7},{10,8},{12,14},{11,9},{13,15},{18,16},{20,... | collective-permute-start | bytes 1572872 | tf_op jit(solution)/shard_map/ppermute | solution.py:512
  28.4 3.1 %head_parts.2 = (bf16[256,1536]{1,0:T(8,128)(2,1)S(1)}, bf16[256,1536]{1,0:T(8,128)(2,1)S(1)}, f32[8,128]{1,0:T(8,128)S(1)}) custom-call(bf16[256,1536]{1,0:T(8,128)(2,1)S(1)} %copy-done.4, bf16[256,1536]{1,0:T(8,128)(2,1)S(1)} %collective-permute-done.4.refs_3_.refs_1_.refs_5_, bf16[256,1536]{1,0:T(8,128)(2,1)S(1)} %get-tuple-element.62.refs_2_, ...), custom_call_target="tpu_custom_call" | custom-call | flops 2415919104 | bytes 7864320 | tf_op jit(solution)/shard_map/head_parts/pallas_call | solution.py:44
  31.5 0.6 collective-permute-start.12
  32.1 13.4 %collective-permute-done.9.refs_0_ = bf16[256,1536]{1,0:T(8,128)(2,1)S(1)} collective-permute-done((bf16[256,1536]{1,0:T(8,128)(2,1)S(1)}, bf16[256,1536]{1,0:T(8,128)(2,1)S(1)}, u32[]{:S(2)}, u32[]{:S(2)}) %collective-permute-start.9) | collective-permute-done | bytes 786464 | tf_op jit(solution)/shard_map/ppermute | solution.py:508
  45.4 0.4 split.1
  45.9 0.5 collective-permute-start.11
  46.4 1.3 %collective-permute-start.8 = (bf16[256,1024]{1,0:T(8,128)(2,1)S(1)}, bf16[256,1024]{1,0:T(8,128)(2,1)S(1)}, u32[]{:S(2)}, u32[]{:S(2)}) collective-permute-start(bf16[256,1024]{1,0:T(8,128)(2,1)S(1)} %get-tuple-element.64.refs_1_.refs_3_), channel_id=1, source_target_pairs={{2,0},{4,6},{3,1},{5,7},{10,8},{12,14},{11,9},{13,15},{18,16},{20,... | collective-permute-start | bytes 1572872 | tf_op jit(solution)/shard_map/ppermute | solution.py:512
  47.7 0.5 collective-permute-done.11.refs_4_.refs_6_
  48.2 1.4 %head_parts.3 = (bf16[256,512]{1,0:T(8,128)(2,1)S(1)}, bf16[256,512]{1,0:T(8,128)(2,1)S(1)}, f32[8,128]{1,0:T(8,128)S(1)}) custom-call(bf16[256,1536]{1,0:T(8,128)(2,1)S(1)} %copy-done.4, bf16[256,1536]{1,0:T(8,128)(2,1)S(1)} %collective-permute-done.4.refs_3_.refs_1_.refs_5_, bf16[256,1536]{1,0:T(8,128)(2,1)S(1)} %get-tuple-element.65.refs_0_.refs_2_.refs_4_, ...), custom_call_target="tpu_custom_call" | custom-call | flops 805306368 | bytes 3670016 | tf_op jit(solution)/shard_map/head_parts/pallas_call | solution.py:44
  49.6 0.6 collective-permute-start.13
  50.2 12.0 %collective-permute-done.8.refs_4_ = bf16[256,1024]{1,0:T(8,128)(2,1)S(1)} collective-permute-done((bf16[256,1024]{1,0:T(8,128)(2,1)S(1)}, bf16[256,1024]{1,0:T(8,128)(2,1)S(1)}, u32[]{:S(2)}, u32[]{:S(2)}) %collective-permute-start.8) | collective-permute-done | bytes 524320 | tf_op jit(solution)/shard_map/ppermute | solution.py:512
  62.2 0.4 route_heads.1
  62.6 0.6 collective-permute-start.15
  63.3 0.5 collective-permute-start.16
  64.1 1.5 %collective-permute-start.14 = (bf16[256,1024]{1,0:T(8,128)(2,1)S(1)}, bf16[256,1024]{1,0:T(8,128)(2,1)S(1)}, u32[]{:S(2)}, u32[]{:S(2)}) collective-permute-start(bf16[256,1024]{1,0:T(8,128)(2,1)S(1)} %get-tuple-element.76.refs_0_), channel_id=1, source_target_pairs={{0,2},{6,4},{1,3},{7,5},{8,10},{14,12},{9,11},{15,13},{16,18},{22,... | collective-permute-start | bytes 1572872 | tf_op jit(solution)/shard_map/ppermute | solution.py:512
  65.6 10.1 %collective-permute-done.15.refs_0_ = bf16[256,1024]{1,0:T(8,128)(2,1)S(1)} collective-permute-done((bf16[256,1024]{1,0:T(8,128)(2,1)S(1)}, bf16[256,1024]{1,0:T(8,128)(2,1)S(1)}, u32[]{:S(2)}, u32[]{:S(2)}) %collective-permute-start.15) | collective-permute-done | bytes 524320 | tf_op jit(solution)/shard_map/ppermute | solution.py:508
  75.8 0.6 collective-permute-start.19
  76.4 0.9 collective-permute-done.17.refs_3_
  77.4 2.6 %weight_parts.2 = (bf16[400,1536]{1,0:T(8,128)(2,1)S(1)}, bf16[112,1536]{1,0:T(8,128)(2,1)S(1)}, f32[8,128]{1,0:T(8,128)S(1)}) custom-call(bf16[2,256,1024]{2,1,0:T(8,128)(2,1)S(1)} %get-tuple-element.71.refs_0_.refs_1_, bf16[256,1024]{1,0:T(8,128)(2,1)S(1)} %get-tuple-element.79.refs_0_.refs_1_, bf16[2,256,512]{2,1,0:T(8,128)(2,1)S(1)} %collective-permute-done.16.refs_2_, ...), custom_call_target="tpu_custom_call" | custom-call | flops 1610612736 | bytes 6815744 | tf_op jit(solution)/shard_map/weight_parts/pallas_call | solution.py:44
  80.0 1.0 collective-permute-start.26
  81.1 0.7 collective-permute-start.22
  81.8 5.6 %collective-permute-start.21 = (bf16[256,1024]{1,0:T(8,128)(2,1)S(1)}, bf16[256,1024]{1,0:T(8,128)(2,1)S(1)}, u32[]{:S(2)}, u32[]{:S(2)}) collective-permute-start(bf16[256,1024]{1,0:T(8,128)(2,1)S(1)} %get-tuple-element.91), channel_id=1, source_target_pairs={{0,2},{6,4},{1,3},{7,5},{8,10},{14,12},{9,11},{15,13},{16,18},{22,... | collective-permute-start | bytes 1572872 | tf_op jit(solution)/shard_map/ppermute | solution.py:512
  87.4 2.3 %project.2 = (f32[256,1536]{1,0:T(8,128)S(1)}, f32[8,128]{1,0:T(8,128)S(1)}) custom-call(bf16[2,256,1024]{2,1,0:T(8,128)(2,1)S(1)} %get-tuple-element.71.refs_0_.refs_1_, bf16[2,256,1024]{2,1,0:T(8,128)(2,1)S(1)} %get-tuple-element.71.refs_0_.refs_1_, bf16[256,1536]{1,0:T(8,128)(2,1)S(1)} %get-tuple-element.62.refs_2_, ...), custom_call_target="tpu_custom_call" | custom-call | flops 1610612736 | bytes 7864320 | tf_op jit(solution)/shard_map/project/pallas_call | solution.py:44
  89.6 0.5 collective-permute-done.19.refs_0_.refs_1_
  90.2 2.3 %project.3 = (bf16[256,1536]{1,0:T(8,128)(2,1)S(1)}, f32[8,128]{1,0:T(8,128)S(1)}) custom-call(bf16[256,1024]{1,0:T(8,128)(2,1)S(1)} %collective-permute-done.19.refs_0_.refs_1_, bf16[256,1024]{1,0:T(8,128)(2,1)S(1)} %get-tuple-element.79.refs_0_.refs_1_, bf16[256,1536]{1,0:T(8,128)(2,1)S(1)} %get-tuple-element.62.refs_2_, ...), custom_call_target="tpu_custom_call" | custom-call | flops 1610612736 | bytes 7864320 | tf_op jit(solution)/shard_map/project/pallas_call | solution.py:44
  92.5 0.6 collective-permute-start.20
  93.0 0.9 softmax_weights.1
  94.1 3.9 %collective-permute-done.21.refs_1_ = bf16[256,1024]{1,0:T(8,128)(2,1)S(1)} collective-permute-done((bf16[256,1024]{1,0:T(8,128)(2,1)S(1)}, bf16[256,1024]{1,0:T(8,128)(2,1)S(1)}, u32[]{:S(2)}, u32[]{:S(2)}) %collective-permute-start.21) | collective-permute-done | bytes 524320 | tf_op jit(solution)/shard_map/ppermute | solution.py:512
  98.3 0.7 collective-permute-start.25
  99.0 4.1 %collective-permute-start.24 = (bf16[256,1024]{1,0:T(8,128)(2,1)S(1)}, bf16[256,1024]{1,0:T(8,128)(2,1)S(1)}, u32[]{:S(2)}, u32[]{:S(2)}) collective-permute-start(bf16[256,1024]{1,0:T(8,128)(2,1)S(1)} %get-tuple-element.103), channel_id=1, source_target_pairs={{0,2},{2,0},{4,6},{6,4},{1,3},{3,1},{5,7},{7,5},{8,10},{10,8},{12,... | collective-permute-start | bytes 1572872 | tf_op jit(solution)/shard_map/ppermute | solution.py:508
  103.1 0.5 collective-permute-start.27
  103.6 2.7 %weight_parts.3 = (f32[512,1536]{1,0:T(8,128)S(1)}, f32[8,128]{1,0:T(8,128)S(1)}) custom-call(bf16[2,256,1024]{2,1,0:T(8,128)(2,1)S(1)} %get-tuple-element.71.refs_0_.refs_1_, bf16[256,1024]{1,0:T(8,128)(2,1)S(1)} %collective-permute-done.19.refs_0_.refs_1_, bf16[2,256,512]{2,1,0:T(8,128)(2,1)S(1)} %collective-permute-done.16.refs_2_, ...), custom_call_target="tpu_custom_call" | custom-call | flops 1610612736 | bytes 6815744 | tf_op jit(solution)/shard_map/weight_parts/pallas_call | solution.py:44
  106.3 5.3 %collective-permute-done.20.refs_1_ = bf16[256,1536]{1,0:T(8,128)(2,1)S(1)} collective-permute-done((bf16[256,1536]{1,0:T(8,128)(2,1)S(1)}, bf16[256,1536]{1,0:T(8,128)(2,1)S(1)}, u32[]{:S(2)}, u32[]{:S(2)}) %collective-permute-start.20) | collective-permute-done | bytes 786464 | tf_op jit(solution)/shard_map/ppermute | solution.py:508
  111.6 1.0 plus.7
  112.6 3.8 %collective-permute-done.27.refs_2_ = bf16[112,1536]{1,0:T(8,128)(2,1)S(1)} collective-permute-done((bf16[112,1536]{1,0:T(8,128)(2,1)S(1)}, bf16[112,1536]{1,0:T(8,128)(2,1)S(1)}, u32[]{:S(2)}, u32[]{:S(2)}) %collective-permute-start.27) | collective-permute-done | bytes 344096 | tf_op jit(solution)/shard_map/ppermute | solution.py:508
  116.5 1.4 %weight_total.1 = (bf16[512,1536]{1,0:T(8,128)(2,1)S(1)}, bf16[1024,1536]{1,0:T(8,128)(2,1)}, f32[8,128]{1,0:T(8,128)S(1)}) custom-call(f32[512,1536]{1,0:T(8,128)S(1)} %get-tuple-element.105.refs_0_, bf16[400,1536]{1,0:T(8,128)(2,1)S(1)} %collective-permute-done.26.refs_1_, bf16[112,1536]{1,0:T(8,128)(2,1)S(1)} %collective-permute-done.27.refs_2_, ...), custom_call_target="tpu_custom_call" | custom-call | bytes 7864320 | tf_op jit(solution)/shard_map/weight_total/pallas_call | solution.py:44
  118.0 3.8 %attention_grads.1 = (bf16[256,1024]{1,0:T(8,128)(2,1)}, bf16[256,1024]{1,0:T(8,128)(2,1)}, bf16[256,1024]{1,0:T(8,128)(2,1)}, f32[8,128]{1,0:T(8,128)S(1)}) custom-call(bf16[256,1024]{1,0:T(8,128)(2,1)S(1)} %copy-done.1, bf16[256,1024]{1,0:T(8,128)(2,1)S(1)} %copy-done.2, bf16[256,1024]{1,0:T(8,128)(2,1)S(1)} %copy-done.3, ...), custom_call_target="tpu_custom_call" | custom-call | flops 671088640 | bytes 4718592 | tf_op jit(solution)/shard_map/attention_grads/pallas_call | solution.py:44
  121.8 1.2 weight_fill.1
  (48 shorter events, 1.3 us)
Async XLA Ops:
  0.6 6.2 %copy-start.2 = (bf16[256,1024]{1,0:T(8,128)(2,1)S(1)}, bf16[256,1024]{1,0:T(8,128)(2,1)}, u32[]{:S(2)}) copy-start(bf16[256,1024]{1,0:T(8,128)(2,1)} %refs_1_.5) | copy-start | bytes 1572868
  0.6 6.2 %copy-start.1 = (bf16[256,1024]{1,0:T(8,128)(2,1)S(1)}, bf16[256,1024]{1,0:T(8,128)(2,1)}, u32[]{:S(2)}) copy-start(bf16[256,1024]{1,0:T(8,128)(2,1)} %refs_0_.9) | copy-start | bytes 1572868
  0.7 6.2 %copy-start.3 = (bf16[256,1024]{1,0:T(8,128)(2,1)S(1)}, bf16[256,1024]{1,0:T(8,128)(2,1)}, u32[]{:S(2)}) copy-start(bf16[256,1024]{1,0:T(8,128)(2,1)} %refs_2_.3) | copy-start | bytes 1572868
  0.7 24.7 %collective-permute-start.6 = (bf16[256,1536]{1,0:T(8,128)(2,1)}, bf16[256,1536]{1,0:T(8,128)(2,1)S(1)}, u32[]{:S(2)}, u32[]{:S(2)}) collective-permute-start(bf16[256,1536]{1,0:T(8,128)(2,1)} %refs_4_.5), channel_id=1, source_target_pairs={{0,1},{1,0},{2,3},{3,2},{4,5},{5,4},{6,7},{7,6},{8,9},{9,8},{10,11... | collective-permute-start | bytes 2359304 | tf_op jit(solution)/shard_map/ppermute | solution.py:508
  1.2 24.2 %collective-permute-start.4 = (bf16[256,1536]{1,0:T(8,128)(2,1)}, bf16[256,1536]{1,0:T(8,128)(2,1)S(1)}, u32[]{:S(2)}, u32[]{:S(2)}) collective-permute-start(bf16[256,1536]{1,0:T(8,128)(2,1)} %refs_4_.5), channel_id=1, source_target_pairs={{0,16},{8,24},{16,0},{24,8},{1,17},{9,25},{17,1},{25,9},{2,18},{10... | collective-permute-start | bytes 2359304 | tf_op jit(solution)/shard_map/ppermute | solution.py:508
  5.2 20.1 %collective-permute-start.5 = (bf16[256,1536]{1,0:T(8,128)(2,1)S(1)}, bf16[256,1536]{1,0:T(8,128)(2,1)S(1)}, u32[]{:S(2)}, u32[]{:S(2)}) collective-permute-start(bf16[256,1536]{1,0:T(8,128)(2,1)S(1)} %get-tuple-element.118), channel_id=1, source_target_pairs={{0,8},{8,0},{16,24},{24,16},{1,9},{9,1},{17,25},{25,17},{2,10},{10... | collective-permute-start | bytes 2359304 | tf_op jit(solution)/shard_map/ppermute | solution.py:508
  6.8 21.6 %copy-start.4 = (bf16[256,1536]{1,0:T(8,128)(2,1)S(1)}, bf16[256,1536]{1,0:T(8,128)(2,1)}, u32[]{:S(2)}) copy-start(bf16[256,1536]{1,0:T(8,128)(2,1)} %refs_4_.5) | copy-start | bytes 2359300
  8.3 20.1 %copy-start = (bf16[1024,1536]{1,0:T(8,128)(2,1)S(1)}, bf16[1024,1536]{1,0:T(8,128)(2,1)}, u32[]{:S(2)}) copy-start(bf16[1024,1536]{1,0:T(8,128)(2,1)} %refs_7_.3) | copy-start | bytes 9437188
  8.3 5.4 %collective-permute-start.1 = (bf16[256,1024]{1,0:T(8,128)(2,1)S(1)}, bf16[256,1024]{1,0:T(8,128)(2,1)S(1)}, u32[]{:S(2)}, u32[]{:S(2)}) collective-permute-start(bf16[256,1024]{1,0:T(8,128)(2,1)S(1)} %get-tuple-element.61.refs_0_), channel_id=1, source_target_pairs={{2,4},{4,2},{3,5},{5,3},{10,12},{12,10},{11,13},{13,11},{18,20},{2... | collective-permute-start | bytes 1572872 | tf_op jit(solution)/shard_map/ppermute | solution.py:512
  9.1 16.3 %collective-permute-start = (bf16[256,1024]{1,0:T(8,128)(2,1)S(1)}, bf16[256,1024]{1,0:T(8,128)(2,1)S(1)}, u32[]{:S(2)}, u32[]{:S(2)}) collective-permute-start(bf16[256,1024]{1,0:T(8,128)(2,1)S(1)} %get-tuple-element.61.refs_0_), channel_id=1, source_target_pairs={{0,2},{2,0},{4,6},{6,4},{1,3},{3,1},{5,7},{7,5},{8,10},{10,8},{12,... | collective-permute-start | bytes 1572872 | tf_op jit(solution)/shard_map/ppermute | solution.py:508
  25.4 3.0 %collective-permute-start.7 = (bf16[256,1536]{1,0:T(8,128)(2,1)S(1)}, bf16[256,1536]{1,0:T(8,128)(2,1)S(1)}, u32[]{:S(2)}, u32[]{:S(2)}) collective-permute-start(bf16[256,1536]{1,0:T(8,128)(2,1)S(1)} %get-tuple-element.62.refs_2_), channel_id=1, source_target_pairs={{0,1},{1,0},{2,3},{3,2},{4,5},{5,4},{6,7},{7,6},{8,9},{9,8},{10,11... | collective-permute-start | bytes 2359304 | tf_op jit(solution)/shard_map/ppermute | solution.py:508
  25.5 20.0 %collective-permute-start.9 = (bf16[256,1536]{1,0:T(8,128)(2,1)S(1)}, bf16[256,1536]{1,0:T(8,128)(2,1)S(1)}, u32[]{:S(2)}, u32[]{:S(2)}) collective-permute-start(bf16[256,1536]{1,0:T(8,128)(2,1)S(1)} %get-tuple-element.117), channel_id=1, source_target_pairs={{0,8},{8,0},{16,24},{24,16},{1,9},{9,1},{17,25},{25,17},{2,10},{10... | collective-permute-start | bytes 2359304 | tf_op jit(solution)/shard_map/ppermute | solution.py:508
  26.4 5.7 %collective-permute-start.3 = (bf16[256,1024]{1,0:T(8,128)(2,1)S(1)}, bf16[256,1024]{1,0:T(8,128)(2,1)S(1)}, u32[]{:S(2)}, u32[]{:S(2)}) collective-permute-start(bf16[256,1024]{1,0:T(8,128)(2,1)S(1)} %collective-permute-done.refs_1_), channel_id=1, source_target_pairs={{2,4},{4,2},{3,5},{5,3},{10,12},{12,10},{11,13},{13,11},{18,20},{2... | collective-permute-start | bytes 1572872 | tf_op jit(solution)/shard_map/ppermute | solution.py:512
  27.1 18.3 %collective-permute-start.2 = (bf16[256,1024]{1,0:T(8,128)(2,1)S(1)}, bf16[256,1024]{1,0:T(8,128)(2,1)S(1)}, u32[]{:S(2)}, u32[]{:S(2)}) collective-permute-start(bf16[256,1024]{1,0:T(8,128)(2,1)S(1)} %collective-permute-done.1.refs_2_.refs_5_), channel_id=1, source_target_pairs={{2,0},{4,6},{3,1},{5,7},{10,8},{12,14},{11,9},{13,15},{18,16},{20,... | collective-permute-start | bytes 1572872 | tf_op jit(solution)/shard_map/ppermute | solution.py:512
  31.5 30.7 %collective-permute-start.12 = (bf16[256,1536]{1,0:T(8,128)(2,1)S(1)}, bf16[256,1536]{1,0:T(8,128)(2,1)S(1)}, u32[]{:S(2)}, u32[]{:S(2)}) collective-permute-start(bf16[256,1536]{1,0:T(8,128)(2,1)S(1)} %get-tuple-element.69), channel_id=1, source_target_pairs={{0,16},{8,24},{16,0},{24,8},{1,17},{9,25},{17,1},{25,9},{2,18},{10... | collective-permute-start | bytes 2359304 | tf_op jit(solution)/shard_map/ppermute | solution.py:508
  45.8 1.9 %collective-permute-start.10 = (bf16[128,1536]{1,0:T(8,128)(2,1)S(1)}, bf16[128,1536]{1,0:T(8,128)(2,1)S(1)}, u32[]{:S(2)}, u32[]{:S(2)}) collective-permute-start(bf16[128,1536]{1,0:T(8,128)(2,1)S(1)} %get-tuple-element.66), channel_id=1, source_target_pairs={{0,1},{1,0},{2,3},{3,2},{4,5},{5,4},{6,7},{7,6},{8,9},{9,8},{10,11... | collective-permute-start | bytes 1179656 | tf_op jit(solution)/shard_map/ppermute | solution.py:508
  45.9 2.3 %collective-permute-start.11 = (bf16[128,1536]{1,0:T(8,128)(2,1)S(1)}, bf16[128,1536]{1,0:T(8,128)(2,1)S(1)}, u32[]{:S(2)}, u32[]{:S(2)}) collective-permute-start(bf16[128,1536]{1,0:T(8,128)(2,1)S(1)} %get-tuple-element.67), channel_id=1, source_target_pairs={{0,1},{1,0},{2,3},{3,2},{4,5},{5,4},{6,7},{7,6},{8,9},{9,8},{10,11... | collective-permute-start | bytes 1179656 | tf_op jit(solution)/shard_map/ppermute | solution.py:508
  46.4 15.8 %collective-permute-start.8 = (bf16[256,1024]{1,0:T(8,128)(2,1)S(1)}, bf16[256,1024]{1,0:T(8,128)(2,1)S(1)}, u32[]{:S(2)}, u32[]{:S(2)}) collective-permute-start(bf16[256,1024]{1,0:T(8,128)(2,1)S(1)} %get-tuple-element.64.refs_1_.refs_3_), channel_id=1, source_target_pairs={{2,0},{4,6},{3,1},{5,7},{10,8},{12,14},{11,9},{13,15},{18,16},{20,... | collective-permute-start | bytes 1572872 | tf_op jit(solution)/shard_map/ppermute | solution.py:512
  49.6 12.6 %collective-permute-start.13 = (bf16[256,512]{1,0:T(8,128)(2,1)S(1)}, bf16[256,512]{1,0:T(8,128)(2,1)S(1)}, u32[]{:S(2)}, u32[]{:S(2)}) collective-permute-start(bf16[256,512]{1,0:T(8,128)(2,1)S(1)} %get-tuple-element.70), channel_id=1, source_target_pairs={{0,16},{8,24},{16,0},{24,8},{1,17},{9,25},{17,1},{25,9},{2,18},{10... | collective-permute-start | bytes 786440 | tf_op jit(solution)/shard_map/ppermute | solution.py:508
  62.6 13.1 %collective-permute-start.15 = (bf16[256,1024]{1,0:T(8,128)(2,1)S(1)}, bf16[256,1024]{1,0:T(8,128)(2,1)S(1)}, u32[]{:S(2)}, u32[]{:S(2)}) collective-permute-start(bf16[256,1024]{1,0:T(8,128)(2,1)S(1)} %get-tuple-element.77), channel_id=1, source_target_pairs={{0,16},{8,24},{16,0},{24,8},{1,17},{9,25},{17,1},{25,9},{2,18},{10... | collective-permute-start | bytes 1572872 | tf_op jit(solution)/shard_map/ppermute | solution.py:508
  63.2 13.2 %collective-permute-start.18 = (bf16[256,1536]{1,0:T(8,128)(2,1)S(1)}, bf16[256,1536]{1,0:T(8,128)(2,1)S(1)}, u32[]{:S(2)}, u32[]{:S(2)}) collective-permute-start(bf16[256,1536]{1,0:T(8,128)(2,1)S(1)} %get-tuple-element.82), channel_id=1, source_target_pairs={{0,1},{1,0},{2,3},{3,2},{4,5},{5,4},{6,7},{7,6},{8,9},{9,8},{10,11... | collective-permute-start | bytes 2359304 | tf_op jit(solution)/shard_map/ppermute | solution.py:508
  63.3 13.1 %collective-permute-start.16 = (bf16[2,256,512]{2,1,0:T(8,128)(2,1)S(1)}, bf16[2,256,512]{2,1,0:T(8,128)(2,1)S(1)}, u32[]{:S(2)}, u32[]{:S(2)}) collective-permute-start(bf16[2,256,512]{2,1,0:T(8,128)(2,1)S(1)} %get-tuple-element.80), channel_id=1, source_target_pairs={{0,1},{1,0},{2,3},{3,2},{4,5},{5,4},{6,7},{7,6},{8,9},{9,8},{10,11... | collective-permute-start | bytes 1572872 | tf_op jit(solution)/shard_map/ppermute | solution.py:508
  64.1 16.9 %collective-permute-start.14 = (bf16[256,1024]{1,0:T(8,128)(2,1)S(1)}, bf16[256,1024]{1,0:T(8,128)(2,1)S(1)}, u32[]{:S(2)}, u32[]{:S(2)}) collective-permute-start(bf16[256,1024]{1,0:T(8,128)(2,1)S(1)} %get-tuple-element.76.refs_0_), channel_id=1, source_target_pairs={{0,2},{6,4},{1,3},{7,5},{8,10},{14,12},{9,11},{15,13},{16,18},{22,... | collective-permute-start | bytes 1572872 | tf_op jit(solution)/shard_map/ppermute | solution.py:512
  75.8 1.6 %collective-permute-start.17 = (bf16[256,512]{1,0:T(8,128)(2,1)S(1)}, bf16[256,512]{1,0:T(8,128)(2,1)S(1)}, u32[]{:S(2)}, u32[]{:S(2)}) collective-permute-start(bf16[256,512]{1,0:T(8,128)(2,1)S(1)} %get-tuple-element.81), channel_id=1, source_target_pairs={{0,1},{1,0},{2,3},{3,2},{4,5},{5,4},{6,7},{7,6},{8,9},{9,8},{10,11... | collective-permute-start | bytes 786440 | tf_op jit(solution)/shard_map/ppermute | solution.py:508
  75.8 14.3 %collective-permute-start.19 = (bf16[256,1024]{1,0:T(8,128)(2,1)S(1)}, bf16[256,1024]{1,0:T(8,128)(2,1)S(1)}, u32[]{:S(2)}, u32[]{:S(2)}) collective-permute-start(bf16[256,1024]{1,0:T(8,128)(2,1)S(1)} %get-tuple-element.88), channel_id=1, source_target_pairs={{0,16},{8,24},{16,0},{24,8},{1,17},{9,25},{17,1},{25,9},{2,18},{10... | collective-permute-start | bytes 1572872 | tf_op jit(solution)/shard_map/ppermute | solution.py:508
  80.0 36.5 %collective-permute-start.26 = (bf16[400,1536]{1,0:T(8,128)(2,1)S(1)}, bf16[400,1536]{1,0:T(8,128)(2,1)S(1)}, u32[]{:S(2)}, u32[]{:S(2)}) collective-permute-start(bf16[400,1536]{1,0:T(8,128)(2,1)S(1)} %get-tuple-element.106), channel_id=1, source_target_pairs={{0,8},{8,0},{16,24},{24,16},{1,9},{9,1},{17,25},{25,17},{2,10},{10... | collective-permute-start | bytes 3686408 | tf_op jit(solution)/shard_map/ppermute | solution.py:508
  81.1 12.9 %collective-permute-start.22 = (bf16[256,1024]{1,0:T(8,128)(2,1)S(1)}, bf16[256,1024]{1,0:T(8,128)(2,1)S(1)}, u32[]{:S(2)}, u32[]{:S(2)}) collective-permute-start(bf16[256,1024]{1,0:T(8,128)(2,1)S(1)} %get-tuple-element.91), channel_id=1, source_target_pairs={{2,4},{4,2},{3,5},{5,3},{10,12},{12,10},{11,13},{13,11},{18,20},{2... | collective-permute-start | bytes 1572872 | tf_op jit(solution)/shard_map/ppermute | solution.py:512
  81.8 16.3 %collective-permute-start.21 = (bf16[256,1024]{1,0:T(8,128)(2,1)S(1)}, bf16[256,1024]{1,0:T(8,128)(2,1)S(1)}, u32[]{:S(2)}, u32[]{:S(2)}) collective-permute-start(bf16[256,1024]{1,0:T(8,128)(2,1)S(1)} %get-tuple-element.91), channel_id=1, source_target_pairs={{0,2},{6,4},{1,3},{7,5},{8,10},{14,12},{9,11},{15,13},{16,18},{22,... | collective-permute-start | bytes 1572872 | tf_op jit(solution)/shard_map/ppermute | solution.py:512
  92.5 19.2 %collective-permute-start.20 = (bf16[256,1536]{1,0:T(8,128)(2,1)S(1)}, bf16[256,1536]{1,0:T(8,128)(2,1)S(1)}, u32[]{:S(2)}, u32[]{:S(2)}) collective-permute-start(bf16[256,1536]{1,0:T(8,128)(2,1)S(1)} %get-tuple-element.90), channel_id=1, source_target_pairs={{0,16},{8,24},{16,0},{24,8},{1,17},{9,25},{17,1},{25,9},{2,18},{10... | collective-permute-start | bytes 2359304 | tf_op jit(solution)/shard_map/ppermute | solution.py:508
  98.2 4.8 %collective-permute-start.23 = (bf16[256,512]{1,0:T(8,128)(2,1)S(1)}, bf16[256,512]{1,0:T(8,128)(2,1)S(1)}, u32[]{:S(2)}, u32[]{:S(2)}) collective-permute-start(bf16[256,512]{1,0:T(8,128)(2,1)S(1)} %get-tuple-element.97), channel_id=1, source_target_pairs={{0,1},{1,0},{2,3},{3,2},{4,5},{5,4},{6,7},{7,6},{8,9},{9,8},{10,11... | collective-permute-start | bytes 786440 | tf_op jit(solution)/shard_map/ppermute | solution.py:508
  98.3 18.2 %collective-permute-start.25 = (bf16[256,1024]{1,0:T(8,128)(2,1)S(1)}, bf16[256,1024]{1,0:T(8,128)(2,1)S(1)}, u32[]{:S(2)}, u32[]{:S(2)}) collective-permute-start(bf16[256,1024]{1,0:T(8,128)(2,1)S(1)} %get-tuple-element.104), channel_id=1, source_target_pairs={{2,4},{4,2},{3,5},{5,3},{10,12},{12,10},{11,13},{13,11},{18,20},{2... | collective-permute-start | bytes 1572872 | tf_op jit(solution)/shard_map/ppermute | solution.py:512
  99.0 17.5 %collective-permute-start.24 = (bf16[256,1024]{1,0:T(8,128)(2,1)S(1)}, bf16[256,1024]{1,0:T(8,128)(2,1)S(1)}, u32[]{:S(2)}, u32[]{:S(2)}) collective-permute-start(bf16[256,1024]{1,0:T(8,128)(2,1)S(1)} %get-tuple-element.103), channel_id=1, source_target_pairs={{0,2},{2,0},{4,6},{6,4},{1,3},{3,1},{5,7},{7,5},{8,10},{10,8},{12,... | collective-permute-start | bytes 1572872 | tf_op jit(solution)/shard_map/ppermute | solution.py:508
  103.1 13.4 %collective-permute-start.27 = (bf16[112,1536]{1,0:T(8,128)(2,1)S(1)}, bf16[112,1536]{1,0:T(8,128)(2,1)S(1)}, u32[]{:S(2)}, u32[]{:S(2)}) collective-permute-start(bf16[112,1536]{1,0:T(8,128)(2,1)S(1)} %get-tuple-element.107), channel_id=1, source_target_pairs={{0,8},{8,0},{16,24},{24,16},{1,9},{9,1},{17,25},{25,17},{2,10},{10... | collective-permute-start | bytes 1032200 | tf_op jit(solution)/shard_map/ppermute | solution.py:508
  117.9 3.9 %collective-permute-start.28 = (bf16[512,1536]{1,0:T(8,128)(2,1)S(1)}, bf16[512,1536]{1,0:T(8,128)(2,1)S(1)}, u32[]{:S(2)}, u32[]{:S(2)}) collective-permute-start(bf16[512,1536]{1,0:T(8,128)(2,1)S(1)} %get-tuple-element.113), channel_id=1, source_target_pairs={{0,1},{1,0},{2,3},{3,2},{4,5},{5,4},{6,7},{7,6},{8,9},{9,8},{10,11... | collective-permute-start | bytes 4718600 | tf_op jit(solution)/shard_map/ppermute | solution.py:508

commit v7 on v6

--- a/solution.py
+++ b/solution.py
@@ -131,12 +131,20 @@
 
 
 def backward_sum_kernel(q_ref, k_ref, v_ref, prob_ref, *refs):
+    terms, outs, stages, sems = refs[:-7], refs[-7:-4], refs[-4:-1], refs[-1]
+    stores, step = [], 2 * HSZ
     for lo in range(0, q_ref.shape[1], HSZ):
         cols = slice(lo, lo + HSZ)
-        g = sum(ref[:, cols].astype(F32) for ref in refs[:-3]).astype(BF16)
+        g = sum(ref[:, cols].astype(F32) for ref in terms).astype(BF16)
         got = backward_head(q_ref[:, cols], k_ref[:, cols], v_ref[:, cols], g, prob_ref[lo // HSZ])
-        for ref, value in zip(refs[-3:], got):
+        for ref, value in zip(stages, got):
             ref[:, cols] = value
+        if (lo + HSZ) % step == 0:
+            part = pl.ds(lo + HSZ - step, step)
+            pairs = [(a.at[:, part], b.at[:, part]) for a, b in zip(stages, outs)]
+            stores += copies(pairs, sems.at[lo // step])
+    for copy in stores:
+        copy.wait()
 
 
 def head_width(width):
@@ -202,9 +210,10 @@
         (q, k, v, prob, *terms),
         [VMEM] * (4 + len(terms)),
         after,
-        grid=(1,),
-        out_specs=[pl.BlockSpec(q.shape, lambda i: (0, 0))] * 3,
+        out_specs=[ANY] * 3,
         out_shape=[like(q.shape)] * 3,
+        scratch_shapes=[pltpu.VMEM(q.shape, BF16)] * 3
+        + [pltpu.SemaphoreType.DMA((width // (2 * HSZ), 3))],
         cost_estimate=cost(5 * tokens * PATCH * width, 18 * tokens * width),
         name="attention_grads",
     )

time: 123 us -> 123 us (level)
  no operation moved by 1% of the time
where the time goes in v7:
time: 123 us
  waiting for transfers between devices  62.3 us (51%)
  starting transfers between devices  32.5 us (26%)
  Pallas kernels  25.3 us (21%)
  local copies, waits for them, and re-layouts  1.55 us (1%)
    ppermute x21, waiting for transfers between devices, flip(): lax.ppermute(x, axis, [(i, i ^ bit) for i in range(lax.axis_size(axis))])  46.3 us
    pallas_call x26, Pallas kernels, call(): pl.pallas_call(body, in_specs=[*in_specs, *[ANY] * len(after)], out_specs...  25.3 us
    ppermute x21, starting transfers between devices, flip(): lax.ppermute(x, axis, [(i, i ^ bit) for i in range(lax.axis_size(axis))])  20 us
    ppermute x8, waiting for transfers between devices, line(): return lax.ppermute(x, 'col', pairs)  16 us
    ppermute x8, starting transfers between devices, line(): return lax.ppermute(x, 'col', pairs)  12.5 us
  transfers between devices with their start and end apart: 29, of which 10 were waited for; matrix products, arithmetic and copies ran while one was open for 1% of the time, Pallas kernels for 18%

profile of v7, /device:TPU:0, one launch (start us, length us, event | category | flops | bytes accessed | tf_op | source)
XLA Modules:
  0.0 122.9 jit_solution(6082687769120353471)
XLA Ops:
  0.7 0.5 collective-permute-start.6
  1.2 2.6 %collective-permute-start.4 = (bf16[256,1536]{1,0:T(8,128)(2,1)}, bf16[256,1536]{1,0:T(8,128)(2,1)S(1)}, u32[]{:S(2)}, u32[]{:S(2)}) collective-permute-start(bf16[256,1536]{1,0:T(8,128)(2,1)} %refs_4_.5), channel_id=1, source_target_pairs={{0,16},{8,24},{16,0},{24,8},{1,17},{9,25},{17,1},{25,9},{2,18},{10... | collective-permute-start | bytes 2359304 | tf_op jit(solution)/shard_map/ppermute | solution.py:517
  3.8 1.5 %constant_dynamic-slice_fusion = (bf16[256,1536]{1,0:T(8,128)(2,1)S(1)}, bf16[256,1536]{1,0:T(8,128)(2,1)S(1)}) fusion(bf16[1024,1536]{1,0:T(8,128)(2,1)} %refs_7_.3, s32[]{:T(128)S(6)} %select_n.7, s32[]{:T(128)S(6)} %select_n.6), kind=kLoop, calls=%fused_computation | loop fusion | bytes 3145736 | tf_op jit(solution)/shard_map/dynamic_slice | solution.py:537
  5.2 1.6 %collective-permute-start.5 = (bf16[256,1536]{1,0:T(8,128)(2,1)S(1)}, bf16[256,1536]{1,0:T(8,128)(2,1)S(1)}, u32[]{:S(2)}, u32[]{:S(2)}) collective-permute-start(bf16[256,1536]{1,0:T(8,128)(2,1)S(1)} %get-tuple-element.118), channel_id=1, source_target_pairs={{0,8},{8,0},{16,24},{24,16},{1,9},{9,1},{17,25},{25,17},{2,10},{10... | collective-permute-start | bytes 2359304 | tf_op jit(solution)/shard_map/ppermute | solution.py:517
  6.8 1.5 %attention.1 = (bf16[256,1024]{1,0:T(8,128)(2,1)S(1)}, f32[8,128]{1,0:T(8,128)}) custom-call(bf16[256,1024]{1,0:T(8,128)(2,1)S(1)} %copy-done.1, bf16[256,1024]{1,0:T(8,128)(2,1)S(1)} %copy-done.2, bf16[256,1024]{1,0:T(8,128)(2,1)S(1)} %copy-done.3), custom_call_target="tpu_custom_call" | custom-call | flops 268435456 | bytes 2097152 | tf_op jit(solution)/shard_map/attention/pallas_call | solution.py:44
  8.3 0.8 collective-permute-start.1
  9.1 4.6 %collective-permute-start = (bf16[256,1024]{1,0:T(8,128)(2,1)S(1)}, bf16[256,1024]{1,0:T(8,128)(2,1)S(1)}, u32[]{:S(2)}, u32[]{:S(2)}) collective-permute-start(bf16[256,1024]{1,0:T(8,128)(2,1)S(1)} %get-tuple-element.61.refs_0_), channel_id=1, source_target_pairs={{0,2},{2,0},{4,6},{6,4},{1,3},{3,1},{5,7},{7,5},{8,10},{10,8},{12,... | collective-permute-start | bytes 1572872 | tf_op jit(solution)/shard_map/ppermute | solution.py:517
  13.7 11.7 %collective-permute-done.refs_1_ = bf16[256,1024]{1,0:T(8,128)(2,1)S(1)} collective-permute-done((bf16[256,1024]{1,0:T(8,128)(2,1)S(1)}, bf16[256,1024]{1,0:T(8,128)(2,1)S(1)}, u32[]{:S(2)}, u32[]{:S(2)}) %collective-permute-start) | collective-permute-done | bytes 524320 | tf_op jit(solution)/shard_map/ppermute | solution.py:517
  25.5 0.9 collective-permute-start.9
  26.4 0.7 collective-permute-start.3
  27.1 1.3 %collective-permute-start.2 = (bf16[256,1024]{1,0:T(8,128)(2,1)S(1)}, bf16[256,1024]{1,0:T(8,128)(2,1)S(1)}, u32[]{:S(2)}, u32[]{:S(2)}) collective-permute-start(bf16[256,1024]{1,0:T(8,128)(2,1)S(1)} %collective-permute-done.1.refs_2_.refs_5_), channel_id=1, source_target_pairs={{2,0},{4,6},{3,1},{5,7},{10,8},{12,14},{11,9},{13,15},{18,16},{20,... | collective-permute-start | bytes 1572872 | tf_op jit(solution)/shard_map/ppermute | solution.py:521
  28.4 3.1 %head_parts.2 = (bf16[256,1536]{1,0:T(8,128)(2,1)S(1)}, bf16[256,1536]{1,0:T(8,128)(2,1)S(1)}, f32[8,128]{1,0:T(8,128)S(1)}) custom-call(bf16[256,1536]{1,0:T(8,128)(2,1)S(1)} %copy-done.4, bf16[256,1536]{1,0:T(8,128)(2,1)S(1)} %collective-permute-done.4.refs_3_.refs_1_.refs_5_, bf16[256,1536]{1,0:T(8,128)(2,1)S(1)} %get-tuple-element.62.refs_2_, ...), custom_call_target="tpu_custom_call" | custom-call | flops 2415919104 | bytes 7864320 | tf_op jit(solution)/shard_map/head_parts/pallas_call | solution.py:44
  31.5 0.6 collective-permute-start.12
  32.1 13.4 %collective-permute-done.9.refs_0_ = bf16[256,1536]{1,0:T(8,128)(2,1)S(1)} collective-permute-done((bf16[256,1536]{1,0:T(8,128)(2,1)S(1)}, bf16[256,1536]{1,0:T(8,128)(2,1)S(1)}, u32[]{:S(2)}, u32[]{:S(2)}) %collective-permute-start.9) | collective-permute-done | bytes 786464 | tf_op jit(solution)/shard_map/ppermute | solution.py:517
  45.4 0.4 split.1
  45.9 0.5 collective-permute-start.11
  46.4 1.3 %collective-permute-start.8 = (bf16[256,1024]{1,0:T(8,128)(2,1)S(1)}, bf16[256,1024]{1,0:T(8,128)(2,1)S(1)}, u32[]{:S(2)}, u32[]{:S(2)}) collective-permute-start(bf16[256,1024]{1,0:T(8,128)(2,1)S(1)} %get-tuple-element.64.refs_1_.refs_3_), channel_id=1, source_target_pairs={{2,0},{4,6},{3,1},{5,7},{10,8},{12,14},{11,9},{13,15},{18,16},{20,... | collective-permute-start | bytes 1572872 | tf_op jit(solution)/shard_map/ppermute | solution.py:521
  47.7 0.5 collective-permute-done.11.refs_4_.refs_6_
  48.2 1.4 %head_parts.3 = (bf16[256,512]{1,0:T(8,128)(2,1)S(1)}, bf16[256,512]{1,0:T(8,128)(2,1)S(1)}, f32[8,128]{1,0:T(8,128)S(1)}) custom-call(bf16[256,1536]{1,0:T(8,128)(2,1)S(1)} %copy-done.4, bf16[256,1536]{1,0:T(8,128)(2,1)S(1)} %collective-permute-done.4.refs_3_.refs_1_.refs_5_, bf16[256,1536]{1,0:T(8,128)(2,1)S(1)} %get-tuple-element.65.refs_0_.refs_2_.refs_4_, ...), custom_call_target="tpu_custom_call" | custom-call | flops 805306368 | bytes 3670016 | tf_op jit(solution)/shard_map/head_parts/pallas_call | solution.py:44
  49.6 0.6 collective-permute-start.13
  50.2 12.0 %collective-permute-done.8.refs_4_ = bf16[256,1024]{1,0:T(8,128)(2,1)S(1)} collective-permute-done((bf16[256,1024]{1,0:T(8,128)(2,1)S(1)}, bf16[256,1024]{1,0:T(8,128)(2,1)S(1)}, u32[]{:S(2)}, u32[]{:S(2)}) %collective-permute-start.8) | collective-permute-done | bytes 524320 | tf_op jit(solution)/shard_map/ppermute | solution.py:521
  62.2 0.4 route_heads.1
  62.6 0.6 collective-permute-start.15
  63.3 0.5 collective-permute-start.16
  64.1 1.5 %collective-permute-start.14 = (bf16[256,1024]{1,0:T(8,128)(2,1)S(1)}, bf16[256,1024]{1,0:T(8,128)(2,1)S(1)}, u32[]{:S(2)}, u32[]{:S(2)}) collective-permute-start(bf16[256,1024]{1,0:T(8,128)(2,1)S(1)} %get-tuple-element.76.refs_0_), channel_id=1, source_target_pairs={{0,2},{6,4},{1,3},{7,5},{8,10},{14,12},{9,11},{15,13},{16,18},{22,... | collective-permute-start | bytes 1572872 | tf_op jit(solution)/shard_map/ppermute | solution.py:521
  65.6 10.1 %collective-permute-done.15.refs_0_ = bf16[256,1024]{1,0:T(8,128)(2,1)S(1)} collective-permute-done((bf16[256,1024]{1,0:T(8,128)(2,1)S(1)}, bf16[256,1024]{1,0:T(8,128)(2,1)S(1)}, u32[]{:S(2)}, u32[]{:S(2)}) %collective-permute-start.15) | collective-permute-done | bytes 524320 | tf_op jit(solution)/shard_map/ppermute | solution.py:517
  75.8 0.6 collective-permute-start.19
  76.4 0.9 collective-permute-done.17.refs_3_
  77.4 2.6 %weight_parts.2 = (bf16[400,1536]{1,0:T(8,128)(2,1)S(1)}, bf16[112,1536]{1,0:T(8,128)(2,1)S(1)}, f32[8,128]{1,0:T(8,128)S(1)}) custom-call(bf16[2,256,1024]{2,1,0:T(8,128)(2,1)S(1)} %get-tuple-element.71.refs_0_.refs_1_, bf16[256,1024]{1,0:T(8,128)(2,1)S(1)} %get-tuple-element.79.refs_0_.refs_1_, bf16[2,256,512]{2,1,0:T(8,128)(2,1)S(1)} %collective-permute-done.16.refs_2_, ...), custom_call_target="tpu_custom_call" | custom-call | flops 1610612736 | bytes 6815744 | tf_op jit(solution)/shard_map/weight_parts/pallas_call | solution.py:44
  80.0 1.0 collective-permute-start.26
  81.1 0.7 collective-permute-start.22
  81.8 5.6 %collective-permute-start.21 = (bf16[256,1024]{1,0:T(8,128)(2,1)S(1)}, bf16[256,1024]{1,0:T(8,128)(2,1)S(1)}, u32[]{:S(2)}, u32[]{:S(2)}) collective-permute-start(bf16[256,1024]{1,0:T(8,128)(2,1)S(1)} %get-tuple-element.91), channel_id=1, source_target_pairs={{0,2},{6,4},{1,3},{7,5},{8,10},{14,12},{9,11},{15,13},{16,18},{22,... | collective-permute-start | bytes 1572872 | tf_op jit(solution)/shard_map/ppermute | solution.py:521
  87.4 2.3 %project.2 = (f32[256,1536]{1,0:T(8,128)S(1)}, f32[8,128]{1,0:T(8,128)S(1)}) custom-call(bf16[2,256,1024]{2,1,0:T(8,128)(2,1)S(1)} %get-tuple-element.71.refs_0_.refs_1_, bf16[2,256,1024]{2,1,0:T(8,128)(2,1)S(1)} %get-tuple-element.71.refs_0_.refs_1_, bf16[256,1536]{1,0:T(8,128)(2,1)S(1)} %get-tuple-element.62.refs_2_, ...), custom_call_target="tpu_custom_call" | custom-call | flops 1610612736 | bytes 7864320 | tf_op jit(solution)/shard_map/project/pallas_call | solution.py:44
  89.6 0.5 collective-permute-done.19.refs_0_.refs_1_
  90.2 2.3 %project.3 = (bf16[256,1536]{1,0:T(8,128)(2,1)S(1)}, f32[8,128]{1,0:T(8,128)S(1)}) custom-call(bf16[256,1024]{1,0:T(8,128)(2,1)S(1)} %collective-permute-done.19.refs_0_.refs_1_, bf16[256,1024]{1,0:T(8,128)(2,1)S(1)} %get-tuple-element.79.refs_0_.refs_1_, bf16[256,1536]{1,0:T(8,128)(2,1)S(1)} %get-tuple-element.62.refs_2_, ...), custom_call_target="tpu_custom_call" | custom-call | flops 1610612736 | bytes 7864320 | tf_op jit(solution)/shard_map/project/pallas_call | solution.py:44
  92.5 0.6 collective-permute-start.20
  93.0 0.9 softmax_weights.1
  94.1 3.9 %collective-permute-done.21.refs_1_ = bf16[256,1024]{1,0:T(8,128)(2,1)S(1)} collective-permute-done((bf16[256,1024]{1,0:T(8,128)(2,1)S(1)}, bf16[256,1024]{1,0:T(8,128)(2,1)S(1)}, u32[]{:S(2)}, u32[]{:S(2)}) %collective-permute-start.21) | collective-permute-done | bytes 524320 | tf_op jit(solution)/shard_map/ppermute | solution.py:521
  98.3 0.7 collective-permute-start.25
  99.0 4.1 %collective-permute-start.24 = (bf16[256,1024]{1,0:T(8,128)(2,1)S(1)}, bf16[256,1024]{1,0:T(8,128)(2,1)S(1)}, u32[]{:S(2)}, u32[]{:S(2)}) collective-permute-start(bf16[256,1024]{1,0:T(8,128)(2,1)S(1)} %get-tuple-element.103), channel_id=1, source_target_pairs={{0,2},{2,0},{4,6},{6,4},{1,3},{3,1},{5,7},{7,5},{8,10},{10,8},{12,... | collective-permute-start | bytes 1572872 | tf_op jit(solution)/shard_map/ppermute | solution.py:517
  103.1 0.5 collective-permute-start.27
  103.6 2.7 %weight_parts.3 = (f32[512,1536]{1,0:T(8,128)S(1)}, f32[8,128]{1,0:T(8,128)S(1)}) custom-call(bf16[2,256,1024]{2,1,0:T(8,128)(2,1)S(1)} %get-tuple-element.71.refs_0_.refs_1_, bf16[256,1024]{1,0:T(8,128)(2,1)S(1)} %collective-permute-done.19.refs_0_.refs_1_, bf16[2,256,512]{2,1,0:T(8,128)(2,1)S(1)} %collective-permute-done.16.refs_2_, ...), custom_call_target="tpu_custom_call" | custom-call | flops 1610612736 | bytes 6815744 | tf_op jit(solution)/shard_map/weight_parts/pallas_call | solution.py:44
  106.3 5.3 %collective-permute-done.20.refs_1_ = bf16[256,1536]{1,0:T(8,128)(2,1)S(1)} collective-permute-done((bf16[256,1536]{1,0:T(8,128)(2,1)S(1)}, bf16[256,1536]{1,0:T(8,128)(2,1)S(1)}, u32[]{:S(2)}, u32[]{:S(2)}) %collective-permute-start.20) | collective-permute-done | bytes 786464 | tf_op jit(solution)/shard_map/ppermute | solution.py:517
  111.6 1.0 plus.7
  112.6 3.8 %collective-permute-done.27.refs_2_ = bf16[112,1536]{1,0:T(8,128)(2,1)S(1)} collective-permute-done((bf16[112,1536]{1,0:T(8,128)(2,1)S(1)}, bf16[112,1536]{1,0:T(8,128)(2,1)S(1)}, u32[]{:S(2)}, u32[]{:S(2)}) %collective-permute-start.27) | collective-permute-done | bytes 344096 | tf_op jit(solution)/shard_map/ppermute | solution.py:517
  116.5 1.4 %weight_total.1 = (bf16[512,1536]{1,0:T(8,128)(2,1)S(1)}, bf16[1024,1536]{1,0:T(8,128)(2,1)}, f32[8,128]{1,0:T(8,128)S(1)}) custom-call(f32[512,1536]{1,0:T(8,128)S(1)} %get-tuple-element.105.refs_0_, bf16[400,1536]{1,0:T(8,128)(2,1)S(1)} %collective-permute-done.26.refs_1_, bf16[112,1536]{1,0:T(8,128)(2,1)S(1)} %collective-permute-done.27.refs_2_, ...), custom_call_target="tpu_custom_call" | custom-call | bytes 7864320 | tf_op jit(solution)/shard_map/weight_total/pallas_call | solution.py:44
  118.0 3.5 %attention_grads.1 = (bf16[256,1024]{1,0:T(8,128)(2,1)}, bf16[256,1024]{1,0:T(8,128)(2,1)}, bf16[256,1024]{1,0:T(8,128)(2,1)}, f32[8,128]{1,0:T(8,128)S(1)}) custom-call(bf16[256,1024]{1,0:T(8,128)(2,1)S(1)} %copy-done.1, bf16[256,1024]{1,0:T(8,128)(2,1)S(1)} %copy-done.2, bf16[256,1024]{1,0:T(8,128)(2,1)S(1)} %copy-done.3, ...), custom_call_target="tpu_custom_call" | custom-call | flops 671088640 | bytes 4718592 | tf_op jit(solution)/shard_map/attention_grads/pallas_call | solution.py:44
  121.6 1.2 weight_fill.1
  (48 shorter events, 1.3 us)
Async XLA Ops:
  0.6 6.2 %copy-start.2 = (bf16[256,1024]{1,0:T(8,128)(2,1)S(1)}, bf16[256,1024]{1,0:T(8,128)(2,1)}, u32[]{:S(2)}) copy-start(bf16[256,1024]{1,0:T(8,128)(2,1)} %refs_1_.5) | copy-start | bytes 1572868
  0.6 6.2 %copy-start.1 = (bf16[256,1024]{1,0:T(8,128)(2,1)S(1)}, bf16[256,1024]{1,0:T(8,128)(2,1)}, u32[]{:S(2)}) copy-start(bf16[256,1024]{1,0:T(8,128)(2,1)} %refs_0_.9) | copy-start | bytes 1572868
  0.7 6.2 %copy-start.3 = (bf16[256,1024]{1,0:T(8,128)(2,1)S(1)}, bf16[256,1024]{1,0:T(8,128)(2,1)}, u32[]{:S(2)}) copy-start(bf16[256,1024]{1,0:T(8,128)(2,1)} %refs_2_.3) | copy-start | bytes 1572868
  0.7 24.7 %collective-permute-start.6 = (bf16[256,1536]{1,0:T(8,128)(2,1)}, bf16[256,1536]{1,0:T(8,128)(2,1)S(1)}, u32[]{:S(2)}, u32[]{:S(2)}) collective-permute-start(bf16[256,1536]{1,0:T(8,128)(2,1)} %refs_4_.5), channel_id=1, source_target_pairs={{0,1},{1,0},{2,3},{3,2},{4,5},{5,4},{6,7},{7,6},{8,9},{9,8},{10,11... | collective-permute-start | bytes 2359304 | tf_op jit(solution)/shard_map/ppermute | solution.py:517
  1.2 24.2 %collective-permute-start.4 = (bf16[256,1536]{1,0:T(8,128)(2,1)}, bf16[256,1536]{1,0:T(8,128)(2,1)S(1)}, u32[]{:S(2)}, u32[]{:S(2)}) collective-permute-start(bf16[256,1536]{1,0:T(8,128)(2,1)} %refs_4_.5), channel_id=1, source_target_pairs={{0,16},{8,24},{16,0},{24,8},{1,17},{9,25},{17,1},{25,9},{2,18},{10... | collective-permute-start | bytes 2359304 | tf_op jit(solution)/shard_map/ppermute | solution.py:517
  5.2 20.1 %collective-permute-start.5 = (bf16[256,1536]{1,0:T(8,128)(2,1)S(1)}, bf16[256,1536]{1,0:T(8,128)(2,1)S(1)}, u32[]{:S(2)}, u32[]{:S(2)}) collective-permute-start(bf16[256,1536]{1,0:T(8,128)(2,1)S(1)} %get-tuple-element.118), channel_id=1, source_target_pairs={{0,8},{8,0},{16,24},{24,16},{1,9},{9,1},{17,25},{25,17},{2,10},{10... | collective-permute-start | bytes 2359304 | tf_op jit(solution)/shard_map/ppermute | solution.py:517
  6.8 21.6 %copy-start.4 = (bf16[256,1536]{1,0:T(8,128)(2,1)S(1)}, bf16[256,1536]{1,0:T(8,128)(2,1)}, u32[]{:S(2)}) copy-start(bf16[256,1536]{1,0:T(8,128)(2,1)} %refs_4_.5) | copy-start | bytes 2359300
  8.3 20.1 %copy-start = (bf16[1024,1536]{1,0:T(8,128)(2,1)S(1)}, bf16[1024,1536]{1,0:T(8,128)(2,1)}, u32[]{:S(2)}) copy-start(bf16[1024,1536]{1,0:T(8,128)(2,1)} %refs_7_.3) | copy-start | bytes 9437188
  8.3 5.4 %collective-permute-start.1 = (bf16[256,1024]{1,0:T(8,128)(2,1)S(1)}, bf16[256,1024]{1,0:T(8,128)(2,1)S(1)}, u32[]{:S(2)}, u32[]{:S(2)}) collective-permute-start(bf16[256,1024]{1,0:T(8,128)(2,1)S(1)} %get-tuple-element.61.refs_0_), channel_id=1, source_target_pairs={{2,4},{4,2},{3,5},{5,3},{10,12},{12,10},{11,13},{13,11},{18,20},{2... | collective-permute-start | bytes 1572872 | tf_op jit(solution)/shard_map/ppermute | solution.py:521
  9.1 16.3 %collective-permute-start = (bf16[256,1024]{1,0:T(8,128)(2,1)S(1)}, bf16[256,1024]{1,0:T(8,128)(2,1)S(1)}, u32[]{:S(2)}, u32[]{:S(2)}) collective-permute-start(bf16[256,1024]{1,0:T(8,128)(2,1)S(1)} %get-tuple-element.61.refs_0_), channel_id=1, source_target_pairs={{0,2},{2,0},{4,6},{6,4},{1,3},{3,1},{5,7},{7,5},{8,10},{10,8},{12,... | collective-permute-start | bytes 1572872 | tf_op jit(solution)/shard_map/ppermute | solution.py:517
  25.4 3.0 %collective-permute-start.7 = (bf16[256,1536]{1,0:T(8,128)(2,1)S(1)}, bf16[256,1536]{1,0:T(8,128)(2,1)S(1)}, u32[]{:S(2)}, u32[]{:S(2)}) collective-permute-start(bf16[256,1536]{1,0:T(8,128)(2,1)S(1)} %get-tuple-element.62.refs_2_), channel_id=1, source_target_pairs={{0,1},{1,0},{2,3},{3,2},{4,5},{5,4},{6,7},{7,6},{8,9},{9,8},{10,11... | collective-permute-start | bytes 2359304 | tf_op jit(solution)/shard_map/ppermute | solution.py:517
  25.5 20.0 %collective-permute-start.9 = (bf16[256,1536]{1,0:T(8,128)(2,1)S(1)}, bf16[256,1536]{1,0:T(8,128)(2,1)S(1)}, u32[]{:S(2)}, u32[]{:S(2)}) collective-permute-start(bf16[256,1536]{1,0:T(8,128)(2,1)S(1)} %get-tuple-element.117), channel_id=1, source_target_pairs={{0,8},{8,0},{16,24},{24,16},{1,9},{9,1},{17,25},{25,17},{2,10},{10... | collective-permute-start | bytes 2359304 | tf_op jit(solution)/shard_map/ppermute | solution.py:517
  26.4 5.7 %collective-permute-start.3 = (bf16[256,1024]{1,0:T(8,128)(2,1)S(1)}, bf16[256,1024]{1,0:T(8,128)(2,1)S(1)}, u32[]{:S(2)}, u32[]{:S(2)}) collective-permute-start(bf16[256,1024]{1,0:T(8,128)(2,1)S(1)} %collective-permute-done.refs_1_), channel_id=1, source_target_pairs={{2,4},{4,2},{3,5},{5,3},{10,12},{12,10},{11,13},{13,11},{18,20},{2... | collective-permute-start | bytes 1572872 | tf_op jit(solution)/shard_map/ppermute | solution.py:521
  27.1 18.3 %collective-permute-start.2 = (bf16[256,1024]{1,0:T(8,128)(2,1)S(1)}, bf16[256,1024]{1,0:T(8,128)(2,1)S(1)}, u32[]{:S(2)}, u32[]{:S(2)}) collective-permute-start(bf16[256,1024]{1,0:T(8,128)(2,1)S(1)} %collective-permute-done.1.refs_2_.refs_5_), channel_id=1, source_target_pairs={{2,0},{4,6},{3,1},{5,7},{10,8},{12,14},{11,9},{13,15},{18,16},{20,... | collective-permute-start | bytes 1572872 | tf_op jit(solution)/shard_map/ppermute | solution.py:521
  31.5 30.7 %collective-permute-start.12 = (bf16[256,1536]{1,0:T(8,128)(2,1)S(1)}, bf16[256,1536]{1,0:T(8,128)(2,1)S(1)}, u32[]{:S(2)}, u32[]{:S(2)}) collective-permute-start(bf16[256,1536]{1,0:T(8,128)(2,1)S(1)} %get-tuple-element.69), channel_id=1, source_target_pairs={{0,16},{8,24},{16,0},{24,8},{1,17},{9,25},{17,1},{25,9},{2,18},{10... | collective-permute-start | bytes 2359304 | tf_op jit(solution)/shard_map/ppermute | solution.py:517
  45.8 1.9 %collective-permute-start.10 = (bf16[128,1536]{1,0:T(8,128)(2,1)S(1)}, bf16[128,1536]{1,0:T(8,128)(2,1)S(1)}, u32[]{:S(2)}, u32[]{:S(2)}) collective-permute-start(bf16[128,1536]{1,0:T(8,128)(2,1)S(1)} %get-tuple-element.66), channel_id=1, source_target_pairs={{0,1},{1,0},{2,3},{3,2},{4,5},{5,4},{6,7},{7,6},{8,9},{9,8},{10,11... | collective-permute-start | bytes 1179656 | tf_op jit(solution)/shard_map/ppermute | solution.py:517
  45.9 2.3 %collective-permute-start.11 = (bf16[128,1536]{1,0:T(8,128)(2,1)S(1)}, bf16[128,1536]{1,0:T(8,128)(2,1)S(1)}, u32[]{:S(2)}, u32[]{:S(2)}) collective-permute-start(bf16[128,1536]{1,0:T(8,128)(2,1)S(1)} %get-tuple-element.67), channel_id=1, source_target_pairs={{0,1},{1,0},{2,3},{3,2},{4,5},{5,4},{6,7},{7,6},{8,9},{9,8},{10,11... | collective-permute-start | bytes 1179656 | tf_op jit(solution)/shard_map/ppermute | solution.py:517
  46.4 15.8 %collective-permute-start.8 = (bf16[256,1024]{1,0:T(8,128)(2,1)S(1)}, bf16[256,1024]{1,0:T(8,128)(2,1)S(1)}, u32[]{:S(2)}, u32[]{:S(2)}) collective-permute-start(bf16[256,1024]{1,0:T(8,128)(2,1)S(1)} %get-tuple-element.64.refs_1_.refs_3_), channel_id=1, source_target_pairs={{2,0},{4,6},{3,1},{5,7},{10,8},{12,14},{11,9},{13,15},{18,16},{20,... | collective-permute-start | bytes 1572872 | tf_op jit(solution)/shard_map/ppermute | solution.py:521
  49.6 12.6 %collective-permute-start.13 = (bf16[256,512]{1,0:T(8,128)(2,1)S(1)}, bf16[256,512]{1,0:T(8,128)(2,1)S(1)}, u32[]{:S(2)}, u32[]{:S(2)}) collective-permute-start(bf16[256,512]{1,0:T(8,128)(2,1)S(1)} %get-tuple-element.70), channel_id=1, source_target_pairs={{0,16},{8,24},{16,0},{24,8},{1,17},{9,25},{17,1},{25,9},{2,18},{10... | collective-permute-start | bytes 786440 | tf_op jit(solution)/shard_map/ppermute | solution.py:517
  62.6 13.1 %collective-permute-start.15 = (bf16[256,1024]{1,0:T(8,128)(2,1)S(1)}, bf16[256,1024]{1,0:T(8,128)(2,1)S(1)}, u32[]{:S(2)}, u32[]{:S(2)}) collective-permute-start(bf16[256,1024]{1,0:T(8,128)(2,1)S(1)} %get-tuple-element.77), channel_id=1, source_target_pairs={{0,16},{8,24},{16,0},{24,8},{1,17},{9,25},{17,1},{25,9},{2,18},{10... | collective-permute-start | bytes 1572872 | tf_op jit(solution)/shard_map/ppermute | solution.py:517
  63.2 13.2 %collective-permute-start.18 = (bf16[256,1536]{1,0:T(8,128)(2,1)S(1)}, bf16[256,1536]{1,0:T(8,128)(2,1)S(1)}, u32[]{:S(2)}, u32[]{:S(2)}) collective-permute-start(bf16[256,1536]{1,0:T(8,128)(2,1)S(1)} %get-tuple-element.82), channel_id=1, source_target_pairs={{0,1},{1,0},{2,3},{3,2},{4,5},{5,4},{6,7},{7,6},{8,9},{9,8},{10,11... | collective-permute-start | bytes 2359304 | tf_op jit(solution)/shard_map/ppermute | solution.py:517
  63.3 13.1 %collective-permute-start.16 = (bf16[2,256,512]{2,1,0:T(8,128)(2,1)S(1)}, bf16[2,256,512]{2,1,0:T(8,128)(2,1)S(1)}, u32[]{:S(2)}, u32[]{:S(2)}) collective-permute-start(bf16[2,256,512]{2,1,0:T(8,128)(2,1)S(1)} %get-tuple-element.80), channel_id=1, source_target_pairs={{0,1},{1,0},{2,3},{3,2},{4,5},{5,4},{6,7},{7,6},{8,9},{9,8},{10,11... | collective-permute-start | bytes 1572872 | tf_op jit(solution)/shard_map/ppermute | solution.py:517
  64.1 16.9 %collective-permute-start.14 = (bf16[256,1024]{1,0:T(8,128)(2,1)S(1)}, bf16[256,1024]{1,0:T(8,128)(2,1)S(1)}, u32[]{:S(2)}, u32[]{:S(2)}) collective-permute-start(bf16[256,1024]{1,0:T(8,128)(2,1)S(1)} %get-tuple-element.76.refs_0_), channel_id=1, source_target_pairs={{0,2},{6,4},{1,3},{7,5},{8,10},{14,12},{9,11},{15,13},{16,18},{22,... | collective-permute-start | bytes 1572872 | tf_op jit(solution)/shard_map/ppermute | solution.py:521
  75.8 1.6 %collective-permute-start.17 = (bf16[256,512]{1,0:T(8,128)(2,1)S(1)}, bf16[256,512]{1,0:T(8,128)(2,1)S(1)}, u32[]{:S(2)}, u32[]{:S(2)}) collective-permute-start(bf16[256,512]{1,0:T(8,128)(2,1)S(1)} %get-tuple-element.81), channel_id=1, source_target_pairs={{0,1},{1,0},{2,3},{3,2},{4,5},{5,4},{6,7},{7,6},{8,9},{9,8},{10,11... | collective-permute-start | bytes 786440 | tf_op jit(solution)/shard_map/ppermute | solution.py:517
  75.8 14.3 %collective-permute-start.19 = (bf16[256,1024]{1,0:T(8,128)(2,1)S(1)}, bf16[256,1024]{1,0:T(8,128)(2,1)S(1)}, u32[]{:S(2)}, u32[]{:S(2)}) collective-permute-start(bf16[256,1024]{1,0:T(8,128)(2,1)S(1)} %get-tuple-element.88), channel_id=1, source_target_pairs={{0,16},{8,24},{16,0},{24,8},{1,17},{9,25},{17,1},{25,9},{2,18},{10... | collective-permute-start | bytes 1572872 | tf_op jit(solution)/shard_map/ppermute | solution.py:517
  80.0 36.5 %collective-permute-start.26 = (bf16[400,1536]{1,0:T(8,128)(2,1)S(1)}, bf16[400,1536]{1,0:T(8,128)(2,1)S(1)}, u32[]{:S(2)}, u32[]{:S(2)}) collective-permute-start(bf16[400,1536]{1,0:T(8,128)(2,1)S(1)} %get-tuple-element.106), channel_id=1, source_target_pairs={{0,8},{8,0},{16,24},{24,16},{1,9},{9,1},{17,25},{25,17},{2,10},{10... | collective-permute-start | bytes 3686408 | tf_op jit(solution)/shard_map/ppermute | solution.py:517
  81.1 12.9 %collective-permute-start.22 = (bf16[256,1024]{1,0:T(8,128)(2,1)S(1)}, bf16[256,1024]{1,0:T(8,128)(2,1)S(1)}, u32[]{:S(2)}, u32[]{:S(2)}) collective-permute-start(bf16[256,1024]{1,0:T(8,128)(2,1)S(1)} %get-tuple-element.91), channel_id=1, source_target_pairs={{2,4},{4,2},{3,5},{5,3},{10,12},{12,10},{11,13},{13,11},{18,20},{2... | collective-permute-start | bytes 1572872 | tf_op jit(solution)/shard_map/ppermute | solution.py:521
  81.8 16.3 %collective-permute-start.21 = (bf16[256,1024]{1,0:T(8,128)(2,1)S(1)}, bf16[256,1024]{1,0:T(8,128)(2,1)S(1)}, u32[]{:S(2)}, u32[]{:S(2)}) collective-permute-start(bf16[256,1024]{1,0:T(8,128)(2,1)S(1)} %get-tuple-element.91), channel_id=1, source_target_pairs={{0,2},{6,4},{1,3},{7,5},{8,10},{14,12},{9,11},{15,13},{16,18},{22,... | collective-permute-start | bytes 1572872 | tf_op jit(solution)/shard_map/ppermute | solution.py:521
  92.5 19.2 %collective-permute-start.20 = (bf16[256,1536]{1,0:T(8,128)(2,1)S(1)}, bf16[256,1536]{1,0:T(8,128)(2,1)S(1)}, u32[]{:S(2)}, u32[]{:S(2)}) collective-permute-start(bf16[256,1536]{1,0:T(8,128)(2,1)S(1)} %get-tuple-element.90), channel_id=1, source_target_pairs={{0,16},{8,24},{16,0},{24,8},{1,17},{9,25},{17,1},{25,9},{2,18},{10... | collective-permute-start | bytes 2359304 | tf_op jit(solution)/shard_map/ppermute | solution.py:517
  98.2 4.8 %collective-permute-start.23 = (bf16[256,512]{1,0:T(8,128)(2,1)S(1)}, bf16[256,512]{1,0:T(8,128)(2,1)S(1)}, u32[]{:S(2)}, u32[]{:S(2)}) collective-permute-start(bf16[256,512]{1,0:T(8,128)(2,1)S(1)} %get-tuple-element.97), channel_id=1, source_target_pairs={{0,1},{1,0},{2,3},{3,2},{4,5},{5,4},{6,7},{7,6},{8,9},{9,8},{10,11... | collective-permute-start | bytes 786440 | tf_op jit(solution)/shard_map/ppermute | solution.py:517
  98.3 18.2 %collective-permute-start.25 = (bf16[256,1024]{1,0:T(8,128)(2,1)S(1)}, bf16[256,1024]{1,0:T(8,128)(2,1)S(1)}, u32[]{:S(2)}, u32[]{:S(2)}) collective-permute-start(bf16[256,1024]{1,0:T(8,128)(2,1)S(1)} %get-tuple-element.104), channel_id=1, source_target_pairs={{2,4},{4,2},{3,5},{5,3},{10,12},{12,10},{11,13},{13,11},{18,20},{2... | collective-permute-start | bytes 1572872 | tf_op jit(solution)/shard_map/ppermute | solution.py:521
  99.0 17.5 %collective-permute-start.24 = (bf16[256,1024]{1,0:T(8,128)(2,1)S(1)}, bf16[256,1024]{1,0:T(8,128)(2,1)S(1)}, u32[]{:S(2)}, u32[]{:S(2)}) collective-permute-start(bf16[256,1024]{1,0:T(8,128)(2,1)S(1)} %get-tuple-element.103), channel_id=1, source_target_pairs={{0,2},{2,0},{4,6},{6,4},{1,3},{3,1},{5,7},{7,5},{8,10},{10,8},{12,... | collective-permute-start | bytes 1572872 | tf_op jit(solution)/shard_map/ppermute | solution.py:517
  103.1 13.4 %collective-permute-start.27 = (bf16[112,1536]{1,0:T(8,128)(2,1)S(1)}, bf16[112,1536]{1,0:T(8,128)(2,1)S(1)}, u32[]{:S(2)}, u32[]{:S(2)}) collective-permute-start(bf16[112,1536]{1,0:T(8,128)(2,1)S(1)} %get-tuple-element.107), channel_id=1, source_target_pairs={{0,8},{8,0},{16,24},{24,16},{1,9},{9,1},{17,25},{25,17},{2,10},{10... | collective-permute-start | bytes 1032200 | tf_op jit(solution)/shard_map/ppermute | solution.py:517
  117.9 3.6 %collective-permute-start.28 = (bf16[512,1536]{1,0:T(8,128)(2,1)S(1)}, bf16[512,1536]{1,0:T(8,128)(2,1)S(1)}, u32[]{:S(2)}, u32[]{:S(2)}) collective-permute-start(bf16[512,1536]{1,0:T(8,128)(2,1)S(1)} %get-tuple-element.113), channel_id=1, source_target_pairs={{0,1},{1,0},{2,3},{3,2},{4,5},{5,4},{6,7},{7,6},{8,9},{9,8},{10,11... | collective-permute-start | bytes 4718600 | tf_op jit(solution)/shard_map/ppermute | solution.py:517
